TPU v7x, 32 devices: a whole 2x2x4 slice. The times are simulated.
32 devices in a mesh: dp: 2 (over x), stream: 4 (over y, core), head: 4 (over z).
Axes of the slice: x: 2, y: 2, z: 4, core: 2. Of those that a mesh axis runs over, the one named last changes fastest.
Arguments:
- history: bfloat16 [9, 4, 2048, 2048], P(None, 'dp', 'stream', 'head'), may hold values from -6 to 6
- seq_lens: int32 [4, 3], replicated, may hold values from 0 to 2048, as said below
- bucket_slot: int32 [4], replicated, may hold values from 0 to 3, each once
- w_mix_in: bfloat16 [2048, 36], P('head'), may hold values from -0.125 to 0.125
- w_mix_out: bfloat16 [36, 36], replicated, may hold values from -1 to 1
- mix_bias: float32 [4, 9], replicated, may hold values from -3 to 3
- ln_gain: float32 [4, 2048], P(None, 'head'), may hold values from 0.25 to 1.75
- ln_bias: float32 [4, 2048], P(None, 'head'), may hold values from -2 to 2
- w_qkv: bfloat16 [3, 2048, 2048], P(None, ('dp', 'stream'), 'head'), may hold values from -0.125 to 0.125
- w_attn_out: bfloat16 [2048, 2048], P('head', ('dp', 'stream')), may hold values from -3 to 3
- w_up: bfloat16 [2048, 8192], P(('dp', 'stream'), 'head'), may hold values from -0.125 to 0.125
- w_down: bfloat16 [8192, 2048], P('head', ('dp', 'stream')), may hold values from -0.0625 to 0.0625
- cotangent: bfloat16 [4, 2048, 2048], P('dp', 'stream', 'head'), may hold values from -6 to 6
Outputs:
- block_out: bfloat16 [4, 2048, 2048], P('dp', 'stream', 'head')
- mix_weights: float32 [4, 2048, 36], P('dp', 'stream')
- history_grad: float32 [9, 4, 2048, 2048], P(None, 'dp', 'stream', 'head')
- w_mix_in_grad: float32 [2048, 36], P('head')
- w_mix_out_grad: float32 [36, 36], replicated
- mix_bias_grad: float32 [4, 9], replicated
- ln_gain_grad: float32 [4, 2048], P(None, 'head')
- ln_bias_grad: float32 [4, 2048], P(None, 'head')
- w_qkv_grad: float32 [3, 2048, 2048], P(None, ('dp', 'stream'), 'head')
- w_attn_out_grad: float32 [2048, 2048], P('head', ('dp', 'stream'))
- w_up_grad: float32 [2048, 8192], P(('dp', 'stream'), 'head')
- w_down_grad: float32 [8192, 2048], P('head', ('dp', 'stream'))
Inputs may be any that keep to these rules, and one draw needn't show every extreme that they name: `seq_lens`: each bucket holds either one sequence of 1024 to 2048 tokens or two sequences of 1024 tokens each, in its first entries; the other entries are 0 and the places after the lengths' sum are padding. Slot k, the bucket of micro-batch k % 2 of dp member k // 2, takes the lengths of bucket bucket_slot[k]; every bucket is taken once.
All inputs are finite; a program needn't handle non-finite values.
Results may differ from a plain program's by a relative error of at most 0.02.
Values may be sent and summed in bfloat16 or wider, within the bound.
A program may use at most 216 MiB of HBM per device.

v0:
```python
import jax
import jax.numpy as jnp
from jax import lax
from jax.sharding import PartitionSpec as P

HD = 128
HIST = 9
ROT = 32


EPSILON = 1e-05
HIGHEST = lax.Precision.HIGHEST
MASKED = -1e30


def rotate(values_in, cosine, sine_table):
    half_width = cosine.shape[-1]
    first_part = values_in[..., :half_width]
    second = values_in[..., half_width : 2 * half_width]
    remain = values_in[..., 2 * half_width :]
    cos_heads = cosine[:, None, :]
    sin_heads = sine_table[:, None, :]
    return jnp.concatenate(
        [
            first_part * cos_heads - second * sin_heads,
            second * cos_heads + first_part * sin_heads,
            remain,
        ],
        axis=-1,
    )


def layout(lengths, length_total):
    bounds = jnp.cumsum(lengths)
    places = jnp.arange(length_total, dtype=jnp.int32)
    passed = (places[:, None] >= bounds[None, :]).astype(jnp.int32)
    segment = jnp.sum(passed, axis=1)
    starts = jnp.sum(passed * lengths[None, :], axis=1)
    return (segment, places - starts)


def angle_tables(position, rotary_dims):
    freq_index = jnp.arange(rotary_dims // 2, dtype=jnp.float32)
    inverse = 10000.0 ** (-2.0 * freq_index / rotary_dims)
    phases = position.astype(jnp.float32)[..., None] * inverse
    return (jnp.cos(phases), jnp.sin(phases))


def gelu_exact(values_in):
    return jax.nn.gelu(values_in, approximate=False)


def fetch_weights(w_qkv, w_attn_out, w_up, w_down):
    return (
        lax.all_gather(w_qkv, ("dp", "stream"), axis=1, tiled=True),
        lax.all_gather(w_attn_out, ("dp", "stream"), axis=1, tiled=True),
        lax.all_gather(w_up, ("dp", "stream"), axis=0, tiled=True),
        lax.all_gather(w_down, ("dp", "stream"), axis=1, tiled=True),
    )


def push_grads(grad_qkv, grad_attn_out, grad_up, grad_down):
    return (
        lax.psum_scatter(
            grad_qkv.astype(jnp.bfloat16), ("dp", "stream"), scatter_dimension=1, tiled=True
        ).astype(jnp.float32),
        lax.psum_scatter(
            grad_attn_out.astype(jnp.bfloat16), ("dp", "stream"), scatter_dimension=1, tiled=True
        ).astype(jnp.float32),
        lax.psum_scatter(
            grad_up.astype(jnp.bfloat16), ("dp", "stream"), scatter_dimension=0, tiled=True
        ).astype(jnp.float32),
        lax.psum_scatter(
            grad_down.astype(jnp.bfloat16), ("dp", "stream"), scatter_dimension=1, tiled=True
        ).astype(jnp.float32),
    )


def shards(
    history,
    seq_lens,
    bucket_slot,
    w_mix_in,
    w_mix_out,
    mix_bias,
    ln_gain,
    ln_bias,
    w_qkv,
    w_attn_out,
    w_up,
    w_down,
    cotangent,
):
    members = lax.axis_size("stream")
    member = lax.axis_index("stream")
    micro_count = history.shape[1]
    quarter = history.shape[2]
    feat_local = history.shape[3]
    bucket_len = quarter * members
    model_width = feat_local * lax.axis_size("head")
    heads_here = feat_local // HD
    score_scale = HD ** (-0.5)
    slot_base = lax.axis_index("dp") * micro_count
    slot_ids = jnp.arange(bucket_slot.shape[0], dtype=jnp.int32)
    row_start = member * quarter
    places = jnp.arange(bucket_len, dtype=jnp.int32)
    query_places = row_start + jnp.arange(quarter, dtype=jnp.int32)
    w_mix_in_f = w_mix_in.astype(jnp.float32)
    w_mix_out_f = w_mix_out.astype(jnp.float32)
    bias_flat = mix_bias.reshape(-1)
    acc_w1 = jnp.zeros(w_mix_in.shape, jnp.float32)
    acc_w2 = jnp.zeros(w_mix_out.shape, jnp.float32)
    acc_bias = jnp.zeros(bias_flat.shape, jnp.float32)
    acc_gain = jnp.zeros(ln_gain.shape, jnp.float32)
    acc_shift = jnp.zeros(ln_bias.shape, jnp.float32)
    big_acc = tuple(
        (
            jnp.zeros(weight_item.shape, jnp.float32)
            for weight_item in (w_qkv, w_attn_out, w_up, w_down)
        )
    )
    outputs = []
    mixes = []
    hist_grads = []
    for micro_index in range(micro_count):
        gathered = fetch_weights(w_qkv, w_attn_out, w_up, w_down)
        qkv_full, attn_out_full, up_full, down_full = gathered
        bucket = jnp.sum(jnp.where(slot_ids == slot_base + micro_index, bucket_slot, 0))
        lengths = jnp.sum(jnp.where(slot_ids[:, None] == bucket, seq_lens, 0), axis=0)
        segment, position = layout(lengths, bucket_len)
        query_seg = lax.dynamic_slice_in_dim(segment, row_start, quarter)
        query_pos = lax.dynamic_slice_in_dim(position, row_start, quarter)
        valid_rows = (query_seg < 3).astype(jnp.float32)
        cosine, sine_table = angle_tables(query_pos, ROT)
        allowed = (query_seg[:, None] == segment[None, :]) & (
            places[None, :] <= query_places[:, None]
        )
        history_block = history[:, micro_index]
        current = history_block[HIST - 1]
        current_f = current.astype(jnp.float32)
        partial_value = jnp.dot(current, w_mix_in, preferred_element_type=jnp.float32)
        mix_sum, square_sum = lax.psum(
            (partial_value, jnp.sum(current_f * current_f, axis=1)), "head"
        )
        rms_scale = lax.rsqrt(square_sum / model_width + EPSILON)[:, None]
        mix_pre = mix_sum * rms_scale
        mix_hidden = gelu_exact(mix_pre)
        mix_weights = jnp.dot(mix_hidden, w_mix_out_f, precision=HIGHEST) + bias_flat
        weights_four = mix_weights.reshape(quarter, 4, HIST)
        streams = jnp.zeros((4, quarter, feat_local), jnp.float32)
        for layer_index in range(HIST):
            streams = (
                streams
                + jnp.transpose(weights_four[:, :, layer_index])[:, :, None]
                * history_block[layer_index].astype(jnp.float32)[None]
            )
        stat_sum, stat_square = lax.psum(
            (jnp.sum(streams, axis=2), jnp.sum(streams * streams, axis=2)), "head"
        )
        row_means = (stat_sum / model_width)[:, :, None]
        inv_std = lax.rsqrt(stat_square[:, :, None] / model_width - row_means * row_means + EPSILON)
        centered = (streams - row_means) * inv_std
        normed = (centered * ln_gain[:, None, :] + ln_bias[:, None, :]).astype(jnp.bfloat16)
        full_streams = lax.all_gather(normed, "head", axis=2, tiled=True)
        query_pre = jnp.dot(full_streams[0], qkv_full[0], preferred_element_type=jnp.float32)
        key_pre = jnp.dot(full_streams[1], qkv_full[1], preferred_element_type=jnp.float32)
        value_pre = jnp.dot(full_streams[2], qkv_full[2], preferred_element_type=jnp.float32)
        up_pre = jnp.dot(full_streams[3], up_full, preferred_element_type=jnp.float32)
        gated_up = gelu_exact(up_pre).astype(jnp.bfloat16)
        queries = rotate(query_pre.reshape(quarter, heads_here, HD), cosine, sine_table).astype(
            jnp.bfloat16
        )
        key_local = (
            rotate(key_pre.reshape(quarter, heads_here, HD), cosine, sine_table)
            .astype(jnp.bfloat16)
            .reshape(quarter, feat_local)
        )
        value_local = value_pre.astype(jnp.bfloat16)
        key_rows, value_rows = (
            lax.all_gather(key_local, "stream", axis=0, tiled=True),
            lax.all_gather(value_local, "stream", axis=0, tiled=True),
        )
        key_heads = key_rows.reshape(bucket_len, heads_here, HD)
        value_heads = value_rows.reshape(bucket_len, heads_here, HD)
        scores = (
            jnp.einsum("qhd,khd->hqk", queries, key_heads, preferred_element_type=jnp.float32)
            * score_scale
        )
        scores = jnp.where(allowed[None], scores, MASKED)
        row_top = jnp.max(scores, axis=2, keepdims=True)
        exponent = jnp.exp(scores - row_top)
        row_total = jnp.sum(exponent, axis=2, keepdims=True)
        log_total = row_top + jnp.log(row_total)
        prob_bf = (exponent / row_total).astype(jnp.bfloat16)
        attended = jnp.einsum(
            "hqk,khd->qhd", prob_bf, value_heads, preferred_element_type=jnp.float32
        )
        attended = (
            (attended * valid_rows[:, None, None]).astype(jnp.bfloat16).reshape(quarter, feat_local)
        )
        combined = jnp.dot(attended, attn_out_full, preferred_element_type=jnp.float32) + jnp.dot(
            gated_up, down_full, preferred_element_type=jnp.float32
        )
        branch = lax.psum_scatter(
            combined.astype(jnp.bfloat16), "head", scatter_dimension=1, tiled=True
        ).astype(jnp.float32)
        output = valid_rows[:, None] * (streams[3] + branch)
        outputs.append(output.astype(jnp.bfloat16))
        mixes.append(mix_weights)
        cot_rows = cotangent[micro_index].astype(jnp.float32) * valid_rows[:, None]
        out_full = lax.all_gather(cot_rows.astype(jnp.bfloat16), "head", axis=1, tiled=True)
        d_attended = jnp.einsum(
            "qd,fd->qf", out_full, attn_out_full, preferred_element_type=jnp.float32
        ).astype(jnp.bfloat16)
        d_attended = d_attended * valid_rows[:, None].astype(jnp.bfloat16)
        grad_attn_out = jnp.einsum(
            "qf,qd->fd", attended, out_full, preferred_element_type=jnp.float32
        )
        d_gated = jnp.einsum("qd,fd->qf", out_full, down_full, preferred_element_type=jnp.float32)
        grad_down = jnp.einsum("qf,qd->fd", gated_up, out_full, preferred_element_type=jnp.float32)
        unused_out, gelu_back = jax.vjp(gelu_exact, up_pre)
        d_up = gelu_back(d_gated)[0].astype(jnp.bfloat16)
        grad_up = jnp.einsum("qd,qf->df", full_streams[3], d_up, preferred_element_type=jnp.float32)
        d_stream_up = jnp.einsum("qf,df->qd", d_up, up_full, preferred_element_type=jnp.float32)
        d_out_heads = d_attended.reshape(quarter, heads_here, HD)
        scores_again = (
            jnp.einsum("qhd,khd->hqk", queries, key_heads, preferred_element_type=jnp.float32)
            * score_scale
        )
        scores_again = jnp.where(allowed[None], scores_again, MASKED)
        probs_f = jnp.exp(scores_again - log_total)
        d_probs = jnp.einsum(
            "qhd,khd->hqk", d_out_heads, value_heads, preferred_element_type=jnp.float32
        )
        d_scores = (probs_f * (d_probs - jnp.sum(probs_f * d_probs, axis=2, keepdims=True))).astype(
            jnp.bfloat16
        )
        d_queries = (
            jnp.einsum("hqk,khd->qhd", d_scores, key_heads, preferred_element_type=jnp.float32)
            * score_scale
        )
        d_keys = (
            jnp.einsum("hqk,qhd->khd", d_scores, queries, preferred_element_type=jnp.float32)
            * score_scale
        )
        d_values = jnp.einsum(
            "hqk,qhd->khd", prob_bf, d_out_heads, preferred_element_type=jnp.float32
        )
        key_part, value_part = (
            lax.psum_scatter(
                d_keys.reshape(bucket_len, feat_local).astype(jnp.bfloat16),
                "stream",
                scatter_dimension=0,
                tiled=True,
            ).astype(jnp.float32),
            lax.psum_scatter(
                d_values.reshape(bucket_len, feat_local).astype(jnp.bfloat16),
                "stream",
                scatter_dimension=0,
                tiled=True,
            ).astype(jnp.float32),
        )
        d_query_pre = (
            rotate(d_queries, cosine, -sine_table).astype(jnp.bfloat16).reshape(quarter, feat_local)
        )
        d_key_pre = (
            rotate(key_part.reshape(quarter, heads_here, HD), cosine, -sine_table)
            .astype(jnp.bfloat16)
            .reshape(quarter, feat_local)
        )
        d_value_pre = value_part.astype(jnp.bfloat16)
        grad_qkv = jnp.stack(
            [
                jnp.einsum(
                    "qd,qf->df", full_streams[0], d_query_pre, preferred_element_type=jnp.float32
                ),
                jnp.einsum(
                    "qd,qf->df", full_streams[1], d_key_pre, preferred_element_type=jnp.float32
                ),
                jnp.einsum(
                    "qd,qf->df", full_streams[2], d_value_pre, preferred_element_type=jnp.float32
                ),
            ]
        )
        d_norm_full = jnp.stack(
            [
                jnp.einsum(
                    "qf,df->qd", d_query_pre, qkv_full[0], preferred_element_type=jnp.float32
                ),
                jnp.einsum("qf,df->qd", d_key_pre, qkv_full[1], preferred_element_type=jnp.float32),
                jnp.einsum(
                    "qf,df->qd", d_value_pre, qkv_full[2], preferred_element_type=jnp.float32
                ),
                d_stream_up,
            ]
        )
        stream_grad = lax.psum_scatter(
            d_norm_full.astype(jnp.bfloat16), "head", scatter_dimension=2, tiled=True
        ).astype(jnp.float32)
        d_centered = stream_grad * ln_gain[:, None, :]
        sum_grad, sum_cross = lax.psum(
            (jnp.sum(d_centered, axis=2), jnp.sum(d_centered * centered, axis=2)), "head"
        )
        d_streams = inv_std * (
            d_centered
            - sum_grad[:, :, None] / model_width
            - centered * sum_cross[:, :, None] / model_width
        )
        acc_gain = acc_gain + jnp.sum(stream_grad * centered, axis=1)
        acc_shift = acc_shift + jnp.sum(stream_grad, axis=1)
        d_streams = jnp.concatenate([d_streams[:3], (d_streams[3] + cot_rows)[None]], axis=0)
        layer_grads = []
        d_mix_parts = []
        for layer_index in range(HIST):
            layer_f = history_block[layer_index].astype(jnp.float32)
            layer_grads.append(
                jnp.sum(
                    jnp.transpose(weights_four[:, :, layer_index])[:, :, None] * d_streams, axis=0
                )
            )
            d_mix_parts.append(jnp.sum(d_streams * layer_f[None], axis=2))
        d_mix_local = jnp.transpose(jnp.stack(d_mix_parts, axis=-1), (1, 0, 2)).reshape(
            quarter, 4 * HIST
        )
        d_mix = lax.psum(d_mix_local.astype(jnp.bfloat16), "head").astype(jnp.float32)
        acc_bias = acc_bias + jnp.sum(d_mix, axis=0)
        acc_w2 = acc_w2 + jnp.dot(jnp.transpose(mix_hidden), d_mix, precision=HIGHEST)
        d_hidden = jnp.dot(d_mix, jnp.transpose(w_mix_out_f), precision=HIGHEST)
        unused_mix, gelu_mix_back = jax.vjp(gelu_exact, mix_pre)
        d_pre = gelu_mix_back(d_hidden)[0]
        normed_in = current_f * rms_scale
        acc_w1 = acc_w1 + jnp.dot(jnp.transpose(normed_in), d_pre, precision=HIGHEST)
        d_normed_in = jnp.dot(d_pre, jnp.transpose(w_mix_in_f), precision=HIGHEST)
        cross = jnp.sum(d_pre * mix_pre, axis=1, keepdims=True)
        d_current = rms_scale * (d_normed_in - normed_in * cross / model_width)
        layer_grads[HIST - 1] = layer_grads[HIST - 1] + d_current
        hist_grads.append(jnp.stack(layer_grads))
        reduced = push_grads(grad_qkv, grad_attn_out, grad_up, grad_down)
        big_acc = (
            big_acc[0] + reduced[0],
            big_acc[1] + reduced[1],
            big_acc[2] + reduced[2],
            big_acc[3] + reduced[3],
        )
    grad_w1, grad_w2, grad_bias, grad_gain, grad_shift = (
        lax.psum(acc_w1.astype(jnp.bfloat16), ("dp", "stream")).astype(jnp.float32),
        lax.psum(acc_w2.astype(jnp.bfloat16), ("dp", "stream")).astype(jnp.float32),
        lax.psum(acc_bias.astype(jnp.bfloat16), ("dp", "stream")).astype(jnp.float32),
        lax.psum(acc_gain.astype(jnp.bfloat16), ("dp", "stream")).astype(jnp.float32),
        lax.psum(acc_shift.astype(jnp.bfloat16), ("dp", "stream")).astype(jnp.float32),
    )
    block_out = jnp.stack(outputs, axis=0)
    mix_out = jnp.stack(mixes, axis=0)
    history_grad = jnp.stack(hist_grads, axis=1)
    return (
        block_out,
        mix_out,
        history_grad,
        grad_w1,
        grad_w2,
        grad_bias.reshape(mix_bias.shape),
        grad_gain,
        grad_shift,
        big_acc[0],
        big_acc[1],
        big_acc[2],
        big_acc[3],
    )


def solution(mesh):
    return jax.shard_map(
        shards,
        mesh=mesh,
        in_specs=(
            P(None, "dp", "stream", "head"),
            P(),
            P(),
            P("head", None),
            P(),
            P(),
            P(None, "head"),
            P(None, "head"),
            P(None, ("dp", "stream"), "head"),
            P("head", ("dp", "stream")),
            P(("dp", "stream"), "head"),
            P("head", ("dp", "stream")),
            P("dp", "stream", "head"),
        ),
        out_specs=(
            P("dp", "stream", "head"),
            P("dp", "stream", None),
            P(None, "dp", "stream", "head"),
            P("head", None),
            P(),
            P(),
            P(None, "head"),
            P(None, "head"),
            P(None, ("dp", "stream"), "head"),
            P("head", ("dp", "stream")),
            P(("dp", "stream"), "head"),
            P("head", ("dp", "stream")),
        ),
        check_vma=False,
    )
```

profile of v0, /device:TPU:8, one launch (start us, length us, event | category | flops | bytes accessed | tf_op | source)
XLA Modules:
  0.0 1921.1 jit_solution(4292910003922224556)
XLA Ops:
  105.8 130.9 %all-gather.13.cloned.1.call-done = bf16[4,512,2048]{2,1,0:T(8,128)(2,1)} async-done(((bf16[4,512,512]{2,1,0:T(8,128)(2,1)}), bf16[4,512,2048]{2,1,0:T(8,128)(2,1)}) %all-gather.13.cloned.1.call-update) | async-done | bytes 8388624 | tf_op jit(solution)/shard_map/all_gather | solution.py:164
  250.0 136.5 %all-gather.27.cloned.1.call-done = bf16[4,512,2048]{2,1,0:T(8,128)(2,1)} async-done(((bf16[4,512,512]{2,1,0:T(8,128)(2,1)}), bf16[4,512,2048]{2,1,0:T(8,128)(2,1)}) %all-gather.27.cloned.1.call-update) | async-done | bytes 8388624 | tf_op jit(solution)/shard_map/all_gather | solution.py:164
  401.4 32.7 %all-gather.33.cloned.1.call-done = bf16[512,2048]{1,0:T(8,128)(2,1)} async-done(((bf16[512,512]{1,0:T(8,128)(2,1)}), bf16[512,2048]{1,0:T(8,128)(2,1)}) %all-gather.33.cloned.1.call-update) | async-done | bytes 2097168 | tf_op jit(solution)/shard_map/all_gather | solution.py:211
  434.1 30.3 %all-gather.21.cloned.1.call-done = bf16[512,2048]{1,0:T(8,128)(2,1)} async-done(((bf16[512,256]{1,0:T(8,128)(2,1)}), bf16[512,2048]{1,0:T(8,128)(2,1)}) %all-gather.21.cloned.1.call-update) | async-done | bytes 2097168 | tf_op jit(solution)/shard_map/all_gather | solution.py:56
  469.3 19.2 all-gather.19.cloned.1.call-done
  526.1 16.1 multiply_convert_fusion.1
  563.1 19.9 %all-gather.31.cloned.1.call-done = bf16[2048,512]{0,1:T(8,128)(2,1)} async-done(((bf16[512,512]{0,1:T(8,128)(2,1)}), bf16[2048,512]{0,1:T(8,128)(2,1)}) %all-gather.31.cloned.1.call-update) | async-done | bytes 2097168 | tf_op jit(solution)/shard_map/all_gather | solution.py:180
  621.7 15.9 multiply_convert_fusion
  647.9 15.9 all-gather.23.cloned.1.call-done
  684.2 37.5 %all-gather.25.cloned.1.call-done = bf16[2048,2048]{1,0:T(8,128)(2,1)} async-done(((bf16[2048,256]{1,0:T(8,128)(2,1)}), bf16[2048,2048]{1,0:T(8,128)(2,1)}) %all-gather.25.cloned.1.call-update) | async-done | bytes 8388624 | tf_op jit(solution)/shard_map/all_gather | solution.py:58
  721.7 19.0 add_convert_fusion.1
  773.9 18.7 add_convert_fusion
  948.7 43.1 %reduce-scatter.17.cloned.1.call-done = bf16[512,512]{1,0:T(8,128)(2,1)} async-done(((bf16[512,2048]{1,0:T(8,128)(2,1)}), bf16[512,512]{1,0:T(8,128)(2,1)}) %reduce-scatter.17.cloned.1.call-update) | async-done | bytes 524304 | tf_op jit(solution)/shard_map/reduce_scatter | solution.py:204
  993.3 44.1 %reduce-scatter.19.cloned.1.call-done = bf16[512,512]{1,0:T(8,128)(2,1)} async-done(((bf16[512,2048]{1,0:T(8,128)(2,1)}), bf16[512,512]{1,0:T(8,128)(2,1)}) %reduce-scatter.19.cloned.1.call-update) | async-done | bytes 524304 | tf_op jit(solution)/shard_map/reduce_scatter | solution.py:204
  1040.0 72.3 %reduce-scatter.41.cloned.1.call-done = bf16[256,2048]{1,0:T(8,128)(2,1)} async-done(((bf16[2048,2048]{1,0:T(8,128)(2,1)}), bf16[256,2048]{1,0:T(8,128)(2,1)}) %reduce-scatter.41.cloned.1.call-update) | async-done | bytes 1048592 | tf_op jit(solution)/shard_map/reduce_scatter | solution.py:70
  1112.3 74.5 %reduce-scatter.43.cloned.1.call-done = bf16[256,2048]{1,0:T(8,128)(2,1)} async-done(((bf16[2048,2048]{1,0:T(8,128)(2,1)}), bf16[256,2048]{1,0:T(8,128)(2,1)}) %reduce-scatter.43.cloned.1.call-update) | async-done | bytes 1048592 | tf_op jit(solution)/shard_map/reduce_scatter | solution.py:70
  1190.0 71.6 %reduce-scatter.45.cloned.1.call-done = bf16[2048,256]{1,0:T(8,128)(2,1)} async-done(((bf16[2048,2048]{1,0:T(8,128)(2,1)}), bf16[2048,256]{1,0:T(8,128)(2,1)}) %reduce-scatter.45.cloned.1.call-update) | async-done | bytes 1048592 | tf_op jit(solution)/shard_map/reduce_scatter | solution.py:73
  1261.6 74.7 %reduce-scatter.47.cloned.1.call-done = bf16[2048,256]{1,0:T(8,128)(2,1)} async-done(((bf16[2048,2048]{1,0:T(8,128)(2,1)}), bf16[2048,256]{1,0:T(8,128)(2,1)}) %reduce-scatter.47.cloned.1.call-update) | async-done | bytes 1048592 | tf_op jit(solution)/shard_map/reduce_scatter | solution.py:73
  1339.4 62.1 %reduce-scatter.33.cloned.1.call-done = bf16[3,256,512]{2,1,0:T(8,128)(2,1)} async-done(((bf16[3,2048,512]{2,1,0:T(8,128)(2,1)}), bf16[3,256,512]{2,1,0:T(8,128)(2,1)}) %reduce-scatter.33.cloned.1.call-update) | async-done | bytes 786448 | tf_op jit(solution)/shard_map/reduce_scatter | solution.py:64
  1401.5 65.0 %reduce-scatter.35.cloned.1.call-done = bf16[3,256,512]{2,1,0:T(8,128)(2,1)} async-done(((bf16[3,2048,512]{2,1,0:T(8,128)(2,1)}), bf16[3,256,512]{2,1,0:T(8,128)(2,1)}) %reduce-scatter.35.cloned.1.call-update) | async-done | bytes 786448 | tf_op jit(solution)/shard_map/reduce_scatter | solution.py:64
  1469.2 143.8 %reduce-scatter.31.cloned.1.call-done = bf16[4,512,512]{2,1,0:T(8,128)(2,1)} async-done(((bf16[4,512,2048]{2,1,0:T(8,128)(2,1)}), bf16[4,512,512]{2,1,0:T(8,128)(2,1)}) %reduce-scatter.31.cloned.1.call-update) | async-done | bytes 2097168 | tf_op jit(solution)/shard_map/reduce_scatter | solution.py:297
  1613.0 148.0 %reduce-scatter.25.cloned.1.call-done = bf16[4,512,512]{2,1,0:T(8,128)(2,1)} async-done(((bf16[4,512,2048]{2,1,0:T(8,128)(2,1)}), bf16[4,512,512]{2,1,0:T(8,128)(2,1)}) %reduce-scatter.25.cloned.1.call-update) | async-done | bytes 2097168 | tf_op jit(solution)/shard_map/reduce_scatter | solution.py:297
  1838.6 18.6 all-reduce.11.cloned.1.call-done
  1866.8 23.0 %all-reduce.4 = (bf16[512,36]{0,1:T(8,128)(2,1)S(1)}, bf16[36,36]{1,0:T(8,128)(2,1)S(1)}, bf16[4,9]{1,0:T(4,128)(2,1)S(1)}, bf16[4,512]{1,0:T(4,128)(2,1)S(1)}, bf16[4,512]{1,0:T(4,128)(2,1)S(1)}) all-reduce(bf16[512,36]{0,1:T(8,128)(2,1)S(1)} %fusion.116, ...), channel_id=1, replica_groups=mesh['dp'=2,'stream'=4,'head'=4] {'dp','stream'}, use_global_device_ids=true, to_apply=%region_86.87 | all-reduce | flops 23860 | bytes 95440 | tf_op jit(solution)/shard_map/psum | solution.py:346
  (612 shorter events, 568.9 us)
Async XLA Ops:
  88.5 298.0 %all-gather.27.cloned.1.call-start = ((), (), s32[]{:S(2)}) async-start(), calls=%async_computation.24 | async-start | bytes 10485760 | tf_op jit(solution)/shard_map/all_gather | solution.py:164
  89.1 345.0 %all-gather.33.cloned.1.call-start = ((), (), s32[]{:S(2)}) async-start(), calls=%async_computation.28 | async-start | bytes 2621440 | tf_op jit(solution)/shard_map/all_gather | solution.py:211
  93.3 371.1 %all-gather.21.cloned.1.call-start = ((), (), s32[]{:S(2)}) async-start(), calls=%async_computation.20 | async-start | bytes 2359296 | tf_op jit(solution)/shard_map/all_gather | solution.py:56
  94.1 394.5 %all-gather.19.cloned.1.call-start = ((), (), s32[]{:S(2)}) async-start(), calls=%async_computation.19 | async-start | bytes 2621440 | tf_op jit(solution)/shard_map/all_gather | solution.py:180
  244.5 268.0 %all-gather.17.cloned.1.call-start = ((), (), s32[]{:S(2)}) async-start(), calls=%async_computation.18 | async-start | bytes 2621440 | tf_op jit(solution)/shard_map/all_gather | solution.py:181
  249.1 309.2 %all-gather.35.cloned.1.call-start = ((), (), s32[]{:S(2)}) async-start(), calls=%async_computation.32 | async-start | bytes 2621440 | tf_op jit(solution)/shard_map/all_gather | solution.py:211
  249.7 333.3 %all-gather.31.cloned.1.call-start = ((), (), s32[]{:S(2)}) async-start(), calls=%async_computation.26 | async-start | bytes 2621440 | tf_op jit(solution)/shard_map/all_gather | solution.py:180
  398.0 265.8 %all-gather.23.cloned.1.call-start = ((), (), s32[]{:S(2)}) async-start(), calls=%async_computation.21 | async-start | bytes 9437184 | tf_op jit(solution)/shard_map/all_gather | solution.py:57
  398.6 323.1 %all-gather.25.cloned.1.call-start = ((), (), s32[]{:S(2)}) async-start(), calls=%async_computation.22 | async-start | bytes 9437184 | tf_op jit(solution)/shard_map/all_gather | solution.py:58
  399.3 453.3 %reduce-scatter.21.cloned.1.call-start = ((), (), s32[]{:S(2)}) async-start(), calls=%async_computation.29 | async-start | bytes 2621440 | tf_op jit(solution)/shard_map/reduce_scatter | solution.py:250
  546.5 316.0 %reduce-scatter.23.cloned.1.call-start = ((), (), s32[]{:S(2)}) async-start(), calls=%async_computation.30 | async-start | bytes 2621440 | tf_op jit(solution)/shard_map/reduce_scatter | solution.py:256
  600.9 276.4 %reduce-scatter.27.cloned.1.call-start = ((), (), s32[]{:S(2)}) async-start(), calls=%async_computation.33 | async-start | bytes 2621440 | tf_op jit(solution)/shard_map/reduce_scatter | solution.py:250
  647.9 292.4 %reduce-scatter.37.cloned.1.call-start = ((), (), s32[]{:S(2)}) async-start(), calls=%async_computation.38 | async-start | bytes 2359296 | tf_op jit(solution)/shard_map/reduce_scatter | solution.py:67
  683.8 263.0 %reduce-scatter.39.cloned.1.call-start = ((), (), s32[]{:S(2)}) async-start(), calls=%async_computation.39 | async-start | bytes 2359296 | tf_op jit(solution)/shard_map/reduce_scatter | solution.py:67
  773.6 263.8 %reduce-scatter.19.cloned.1.call-start = ((), (), s32[]{:S(2)}) async-start(), calls=%async_computation.27 | async-start | bytes 2621440 | tf_op jit(solution)/shard_map/reduce_scatter | solution.py:204
  803.9 308.3 %reduce-scatter.41.cloned.1.call-start = ((), (), s32[]{:S(2)}) async-start(), calls=%async_computation.40 | async-start | bytes 9437184 | tf_op jit(solution)/shard_map/reduce_scatter | solution.py:70
  814.5 372.3 %reduce-scatter.43.cloned.1.call-start = ((), (), s32[]{:S(2)}) async-start(), calls=%async_computation.41 | async-start | bytes 9437184 | tf_op jit(solution)/shard_map/reduce_scatter | solution.py:70
  824.6 437.1 %reduce-scatter.45.cloned.1.call-start = ((), (), s32[]{:S(2)}) async-start(), calls=%async_computation.42 | async-start | bytes 9437184 | tf_op jit(solution)/shard_map/reduce_scatter | solution.py:73
  834.6 501.7 %reduce-scatter.47.cloned.1.call-start = ((), (), s32[]{:S(2)}) async-start(), calls=%async_computation.43 | async-start | bytes 9437184 | tf_op jit(solution)/shard_map/reduce_scatter | solution.py:73
  844.6 556.8 %reduce-scatter.33.cloned.1.call-start = ((), (), s32[]{:S(2)}) async-start(), calls=%async_computation.36 | async-start | bytes 7077888 | tf_op jit(solution)/shard_map/reduce_scatter | solution.py:64
  868.9 597.6 %reduce-scatter.35.cloned.1.call-start = ((), (), s32[]{:S(2)}) async-start(), calls=%async_computation.37 | async-start | bytes 7077888 | tf_op jit(solution)/shard_map/reduce_scatter | solution.py:64
  893.2 719.9 %reduce-scatter.31.cloned.1.call-start = ((), (), s32[]{:S(2)}) async-start(), calls=%async_computation.35 | async-start | bytes 10485760 | tf_op jit(solution)/shard_map/reduce_scatter | solution.py:297
  915.8 845.3 %reduce-scatter.25.cloned.1.call-start = ((), (), s32[]{:S(2)}) async-start(), calls=%async_computation.31 | async-start | bytes 10485760 | tf_op jit(solution)/shard_map/reduce_scatter | solution.py:297
  938.6 918.6 %all-reduce.11.cloned.1.call-start = ((), (), s32[]{:S(2)}) async-start(), calls=%async_computation.45 | async-start | bytes 163840 | tf_op jit(solution)/shard_map/psum | solution.py:325
  (168 other events, 6871.1 us)
Sparse Core Ops, SparseCore 0:
  12.8 35.8 all-reduce.8
  1821.2 35.9 all-reduce.10
Sparse Core Ops, SparseCore 1:
  15.1 46.5 all-gather.14
  88.6 148.1 all-gather.12
  238.8 147.6 all-gather.26
  388.8 45.3 all-gather.32
  436.2 28.2 all-gather.20
  514.0 44.2 all-gather.34
  609.6 54.2 all-gather.22
  665.9 55.8 all-gather.24
  724.2 31.3 reduce-scatter.20
  758.2 31.3 reduce-scatter.22
  792.3 31.3 reduce-scatter.26
  826.2 31.3 reduce-scatter.28
  861.2 41.1 reduce-scatter.36
  905.7 41.1 reduce-scatter.38
  949.1 42.6 reduce-scatter.16
  994.7 42.7 reduce-scatter.18
  1041.1 71.1 reduce-scatter.40
  1115.6 71.1 reduce-scatter.42
  1190.5 71.1 reduce-scatter.44
  1265.1 71.1 reduce-scatter.46
  1339.9 61.5 reduce-scatter.32
  1404.9 61.5 reduce-scatter.34
  1468.9 144.0 reduce-scatter.30
  1615.9 145.1 reduce-scatter.24
  (4 shorter events, 89.8 us)
where the time goes:
time: 1930 us; the launch traced here: 1920 us
  waiting for transfers between devices  1300 us (67%)
  matrix products  303 us (16%)
  other arithmetic  165 us (9%)
  local copies, waits for them, and re-layouts  70.5 us (4%)
  blocking collectives  62.3 us (3%)
    reduce_scatter x2, waiting for transfers between devices, shards(): lax.psum_scatter(d_norm_full.astype(jnp.bfloat16), 'head', scatter_dimens...  292 us
    all_gather x2, waiting for transfers between devices, shards(): full_streams = lax.all_gather(normed, 'head', axis=2, tiled=True)  267 us
    reduce_scatter x2, waiting for transfers between devices, push_grads(): lax.psum_scatter(grad_up.astype(jnp.bfloat16), ('dp', 'stream'), scatter_...  147 us
    reduce_scatter x2, waiting for transfers between devices, push_grads(): lax.psum_scatter(grad_down.astype(jnp.bfloat16), ('dp', 'stream'), scatte...  146 us
    reduce_scatter x2, waiting for transfers between devices, push_grads(): lax.psum_scatter(grad_qkv.astype(jnp.bfloat16), ('dp', 'stream'), scatter...  127 us
    reduce_scatter x2, waiting for transfers between devices, shards(): lax.psum_scatter(combined.astype(jnp.bfloat16), 'head', scatter_dimension...  87.1 us
    unnamed x376, local copies, waits for them, and re-layouts  52.2 us
    all_gather x2, waiting for transfers between devices, shards(): lax.all_gather(cot_rows.astype(jnp.bfloat16), 'head', axis=1, tiled=True)  44.4 us
  transfers between devices with their start and end apart: 30, of which 24 were waited for; matrix products, arithmetic and copies ran while one was open for 23% of the time, Pallas kernels for 0%

commit v1 on v0

v1 whole, which is shorter than its diff:
```python
import functools

import jax
import jax.numpy as jnp
from jax import lax
from jax.experimental import pallas as pl
from jax.experimental.pallas import tpu as pltpu
from jax.sharding import PartitionSpec as P

HD = 128
HIST = 9
ROT = 32

EPSILON = 1e-05
HIGHEST = lax.Precision.HIGHEST
MASKED = -1e30
F32 = jnp.float32
BF16 = jnp.bfloat16

SWAP_X = [(0, 1), (1, 0)]
SWAP_Y = [(0, 2), (2, 0), (1, 3), (3, 1)]
SWAP_CORE = [(0, 1), (1, 0), (2, 3), (3, 2)]


def dot(a, b):
    return jnp.dot(a, b, preferred_element_type=F32)


def dot_nt(a, b):
    return lax.dot_general(a, b, (((1,), (1,)), ((), ())), preferred_element_type=F32)


def dot_tn(a, b):
    return lax.dot_general(a, b, (((0,), (0,)), ((), ())), preferred_element_type=F32)


def gelu_exact(values_in):
    return jax.nn.gelu(values_in, approximate=False)


def over_x(a):
    return lax.ppermute(a, "dp", SWAP_X)


def over_y(a):
    return lax.ppermute(a, "stream", SWAP_Y)


def over_core(a):
    return lax.ppermute(a, "stream", SWAP_CORE)


def paired():
    return lax.axis_size("dp") == 2 and lax.axis_size("stream") == 4


def gather_weight(shard, axis):
    if not paired():
        return lax.all_gather(shard, ("dp", "stream"), axis=axis, tiled=True)
    place = lax.axis_index("dp") * 4 + lax.axis_index("stream")
    width = shard.shape[axis]
    full_shape = list(shard.shape)
    full_shape[axis] = width * 8
    near_x = over_x(shard)
    near_y = over_y(shard)
    half = shard.shape[-2] // 2
    low = lax.slice_in_dim(near_x, 0, half, axis=shard.ndim - 2)
    high = lax.slice_in_dim(near_y, half, 2 * half, axis=shard.ndim - 2)
    far = jnp.concatenate([over_y(low), over_x(high)], axis=shard.ndim - 2)
    full = jnp.zeros(full_shape, shard.dtype)
    for flip, block in ((0, shard), (4, near_x), (2, near_y), (6, far)):
        full = lax.dynamic_update_slice_in_dim(full, block, (place ^ flip) * width, axis)
        full = lax.dynamic_update_slice_in_dim(
            full, over_core(block), (place ^ flip ^ 1) * width, axis
        )
    return full


def scatter_product(rows, columns):
    if not paired():
        return lax.psum_scatter(
            dot_tn(rows, columns).astype(BF16),
            ("dp", "stream"),
            scatter_dimension=0,
            tiled=True,
        ).astype(F32)
    tokens, model_width = rows.shape
    width = model_width // 8
    stream = lax.axis_index("stream")
    x, y, core = lax.axis_index("dp"), stream // 2, stream % 2
    split = rows.reshape(tokens, 4, 2, width)
    mine = lax.dynamic_index_in_dim(split, core, 2, keepdims=False).reshape(tokens, 4 * width)
    other = lax.dynamic_index_in_dim(split, 1 - core, 2, keepdims=False).reshape(tokens, 4 * width)
    received = over_core(dot_tn(other, columns).astype(BF16))
    chip = (dot_tn(mine, columns) + received.astype(F32)).astype(BF16)
    half = columns.shape[1] // 2
    chip = chip.reshape(2, 2, width, 2 * half)
    first, second = chip[..., :half], chip[..., half:]

    def pick(a, index, axis):
        return lax.dynamic_index_in_dim(a, index, axis, keepdims=False)

    def add(a, b):
        return a.astype(F32) + b.astype(F32)

    first_x = add(pick(first, x, 0), over_x(pick(first, 1 - x, 0))).astype(BF16)
    second_y = add(pick(second, y, 1), over_y(pick(second, 1 - y, 1))).astype(BF16)
    first_out = add(pick(first_x, y, 0), over_y(pick(first_x, 1 - y, 0)))
    second_out = add(pick(second_y, x, 0), over_x(pick(second_y, 1 - x, 0)))
    return jnp.concatenate([first_out, second_out], axis=1)


def attention_kernel(place_ref, q_ref, do_ref, start_ref, *refs):
    blocks = (len(refs) - 4) // 4
    k_refs, v_refs = refs[:blocks], refs[blocks : 2 * blocks]
    o_ref, dq_ref = refs[2 * blocks : 2 * blocks + 2]
    dk_refs = refs[2 * blocks + 2 : 3 * blocks + 2]
    dv_refs = refs[3 * blocks + 2 : 4 * blocks + 2]
    s_ref, dp_ref = refs[4 * blocks + 2 :]
    rows = q_ref.shape[1]
    scale = HD ** (-0.5)
    member = place_ref[0]
    q, d_out = q_ref[0], do_ref[0]
    start = start_ref[0]
    top = jnp.full((rows, 1), MASKED, F32)
    t = member * rows + lax.broadcasted_iota(jnp.int32, (rows, rows), 0)
    for j in range(blocks):
        u = place_ref[j] * rows + lax.broadcasted_iota(jnp.int32, (rows, rows), 1)
        allowed = (u <= t) & (u >= start)
        s_ref[j] = jnp.where(allowed, dot_nt(q, k_refs[j][0]) * scale, MASKED)
        top = jnp.maximum(top, jnp.max(s_ref[j], axis=1, keepdims=True))
    total = jnp.zeros((rows, 1), F32)
    for j in range(blocks):
        e = jnp.exp(s_ref[j] - top)
        s_ref[j] = e
        total = total + jnp.sum(e, axis=1, keepdims=True)
    inverse = 1.0 / total
    out = jnp.zeros((rows, HD), F32)
    delta = jnp.zeros((rows, 1), F32)
    for j in range(blocks):
        p = s_ref[j] * inverse
        s_ref[j] = p
        p_bf = p.astype(BF16)
        out = out + dot(p_bf, v_refs[j][0])
        dv_refs[j][0] = dot_tn(p_bf, d_out).astype(BF16)
        d_p = dot_nt(d_out, v_refs[j][0])
        dp_ref[j] = d_p
        delta = delta + jnp.sum(p * d_p, axis=1, keepdims=True)
    o_ref[0] = out.astype(BF16)
    d_q = jnp.zeros((rows, HD), F32)
    for j in range(blocks):
        d_s = (s_ref[j] * (dp_ref[j] - delta)).astype(BF16)
        d_q = d_q + dot(d_s, k_refs[j][0])
        dk_refs[j][0] = (dot_tn(d_s, q) * scale).astype(BF16)
    dq_ref[0] = d_q * scale


def attention(places, queries, d_attended, starts, keys, values):
    micro, rows, feats = queries.shape
    blocks = len(keys)
    tile = pl.BlockSpec((1, rows, HD), lambda b, h: (b, 0, h))
    like = lambda dtype: jax.ShapeDtypeStruct((micro, rows, feats), dtype)
    return pl.pallas_call(
        attention_kernel,
        grid=(micro, feats // HD),
        in_specs=[pl.BlockSpec(memory_space=pltpu.SMEM), tile, tile]
        + [pl.BlockSpec((1, rows, 1), lambda b, h: (b, 0, 0))]
        + [tile] * (2 * blocks),
        out_specs=[tile] * (2 + 2 * blocks),
        out_shape=[like(BF16), like(F32)] + [like(BF16)] * (2 * blocks),
        scratch_shapes=[
            pltpu.VMEM((blocks, rows, rows), F32),
            pltpu.VMEM((blocks, rows, rows), F32),
        ],
        compiler_params=pltpu.CompilerParams(vmem_limit_bytes=40 * 1024 * 1024),
        cost_estimate=pl.CostEstimate(
            flops=12 * micro * feats * rows * rows * blocks,
            bytes_accessed=micro * rows * feats * 2 * (4 + 4 * blocks),
            transcendentals=micro * rows * rows * blocks * feats // HD,
        ),
        name="attention_both_ways",
    )(places, queries, d_attended, starts, *keys, *values)


def exchange_rows(local):
    if lax.axis_size("stream") != 4:
        raise ValueError("stream")
    across = lax.ppermute(local, "stream", [(0, 2), (1, 3)])
    beside = over_core(local)
    return (local, beside, across, over_core(across))


def reduce_rows(parts):
    add = lambda a, b: a.astype(F32) + b.astype(F32)
    across = add(parts[2], over_core(parts[3])).astype(BF16)
    return add(
        add(parts[0], over_core(parts[1])), lax.ppermute(across, "stream", [(2, 0), (3, 1)])
    )


def rotate(values_in, cosine, sine, sign):
    tokens, feats = values_in.shape
    rest = HD - ROT
    ones, zeros = jnp.ones((tokens, rest), F32), jnp.zeros((tokens, rest), F32)
    none = jnp.zeros_like(sine)
    heads = feats // HD
    keep = jnp.tile(jnp.concatenate([cosine, cosine, ones], axis=1), (1, heads))
    left = jnp.tile(jnp.concatenate([-sign * sine, none, zeros], axis=1), (1, heads))
    right = jnp.tile(jnp.concatenate([none, sign * sine, zeros], axis=1), (1, heads))
    h = ROT // 2
    return (
        values_in * keep
        + jnp.roll(values_in, -h, axis=1) * left
        + jnp.roll(values_in, h, axis=1) * right
    )


def shards(
    history,
    seq_lens,
    bucket_slot,
    w_mix_in,
    w_mix_out,
    mix_bias,
    ln_gain,
    ln_bias,
    w_qkv,
    w_attn_out,
    w_up,
    w_down,
    cotangent,
):
    member = lax.axis_index("stream")
    micro, quarter, feats = history.shape[1:]
    tokens = micro * quarter
    model_width = feats * lax.axis_size("head")
    slot_base = lax.axis_index("dp") * micro
    slot_ids = jnp.arange(bucket_slot.shape[0], dtype=jnp.int32)
    query_places = member * quarter + jnp.arange(quarter, dtype=jnp.int32)
    w_mix_in_f = w_mix_in.astype(F32)
    w_mix_out_f = w_mix_out.astype(F32)

    segments, starts = [], []
    for index in range(micro):
        bucket = jnp.sum(jnp.where(slot_ids == slot_base + index, bucket_slot, 0))
        lengths = jnp.sum(jnp.where(slot_ids[:, None] == bucket, seq_lens, 0), axis=0)
        bounds = jnp.cumsum(lengths)
        passed = (query_places[:, None] >= bounds[None, :]).astype(jnp.int32)
        segments.append(jnp.sum(passed, axis=1))
        starts.append(jnp.sum(passed * lengths[None, :], axis=1))
    valid = (jnp.concatenate(segments) < 3).astype(F32)[:, None]
    starts = jnp.concatenate(starts)
    position = jnp.tile(query_places, micro) - starts
    frequency = jnp.arange(ROT // 2, dtype=F32)
    phases = position.astype(F32)[:, None] * (10000.0 ** (-2.0 * frequency / ROT))
    cosine, sine = jnp.cos(phases), jnp.sin(phases)

    cot_rows = cotangent.reshape(tokens, feats).astype(F32) * valid
    out_full = lax.all_gather(cot_rows.astype(BF16), "head", axis=1, tiled=True)
    wq, wk, wv = (gather_weight(w_qkv[i], 0) for i in range(3))
    w_out_full = gather_weight(w_attn_out, 1)
    up_full = gather_weight(w_up, 0)
    down_full = gather_weight(w_down, 1)

    history = history.reshape(HIST, tokens, feats)
    current = history[HIST - 1]
    current_f = current.astype(F32)
    mix_sum, square_sum = lax.psum(
        (dot(current, w_mix_in), jnp.sum(current_f * current_f, axis=1)), "head"
    )
    rms_scale = lax.rsqrt(square_sum / model_width + EPSILON)[:, None]
    mix_pre = mix_sum * rms_scale
    mix_hidden = gelu_exact(mix_pre)
    mix_weights = jnp.dot(mix_hidden, w_mix_out_f, precision=HIGHEST) + mix_bias.reshape(-1)
    weights_four = mix_weights.reshape(tokens, 4, HIST)
    streams = jnp.zeros((4, tokens, feats), F32)
    for layer in range(HIST):
        streams = (
            streams
            + jnp.transpose(weights_four[:, :, layer])[:, :, None]
            * history[layer].astype(F32)[None]
        )
    stat_sum, stat_square = lax.psum(
        (jnp.sum(streams, axis=2), jnp.sum(streams * streams, axis=2)), "head"
    )
    row_means = (stat_sum / model_width)[:, :, None]
    inv_std = lax.rsqrt(stat_square[:, :, None] / model_width - row_means * row_means + EPSILON)
    centered = (streams - row_means) * inv_std
    normed = (centered * ln_gain[:, None, :] + ln_bias[:, None, :]).astype(BF16)

    def all_features(stream):
        return lax.all_gather(normed[stream], "head", axis=1, tiled=True)

    k_in, v_in, q_in, up_in = all_features(1), all_features(2), all_features(0), all_features(3)

    keys = rotate(dot(k_in, wk), cosine, sine, 1.0).astype(BF16)
    values = dot(v_in, wv).astype(BF16)
    queries = rotate(dot(q_in, wq), cosine, sine, 1.0).astype(BF16)
    d_attended = dot_nt(out_full, w_out_full).astype(BF16) * valid.astype(BF16)
    by_micro = lambda a: a.reshape(micro, quarter, feats)
    key_blocks = exchange_rows(by_micro(keys))
    value_blocks = exchange_rows(by_micro(values))
    places = member ^ jnp.arange(4, dtype=jnp.int32)
    results = attention(
        places,
        by_micro(queries),
        by_micro(d_attended),
        starts.reshape(micro, quarter, 1),
        key_blocks,
        value_blocks,
    )
    attended, d_queries = results[0].reshape(tokens, feats), results[1].reshape(tokens, feats)
    attended = attended * valid.astype(BF16)
    d_keys = reduce_rows(results[2:6]).reshape(tokens, feats)
    d_values = reduce_rows(results[6:10]).reshape(tokens, feats)
    d_query_pre = rotate(d_queries, cosine, sine, -1.0).astype(BF16)
    d_key_pre = rotate(d_keys, cosine, sine, -1.0).astype(BF16)
    d_value_pre = d_values.astype(BF16)

    up_pre = dot(up_in, up_full)
    gated_up = gelu_exact(up_pre).astype(BF16)
    _, gelu_back = jax.vjp(gelu_exact, up_pre)
    d_up = gelu_back(dot_nt(out_full, down_full))[0].astype(BF16)

    def to_owner(partial):
        return lax.psum_scatter(
            partial.astype(BF16), "head", scatter_dimension=1, tiled=True
        ).astype(F32)

    g_up = to_owner(dot_nt(d_up, up_full))
    g_query = to_owner(dot_nt(d_query_pre, wq))
    g_key = to_owner(dot_nt(d_key_pre, wk))
    g_value = to_owner(dot_nt(d_value_pre, wv))
    branch = to_owner(dot(attended, w_out_full) + dot(gated_up, down_full))
    block_out = (valid * (streams[3] + branch)).astype(BF16)

    grad_up = scatter_product(up_in, d_up)
    grad_down = scatter_product(out_full, gated_up).T
    grad_attn_out = scatter_product(out_full, attended).T
    grad_qkv = jnp.stack(
        [
            scatter_product(q_in, d_query_pre),
            scatter_product(k_in, d_key_pre),
            scatter_product(v_in, d_value_pre),
        ]
    )

    stream_grad = jnp.stack([g_query, g_key, g_value, g_up])
    d_centered = stream_grad * ln_gain[:, None, :]
    sum_grad, sum_cross = lax.psum(
        (jnp.sum(d_centered, axis=2), jnp.sum(d_centered * centered, axis=2)), "head"
    )
    d_streams = inv_std * (
        d_centered
        - sum_grad[:, :, None] / model_width
        - centered * sum_cross[:, :, None] / model_width
    )
    grad_gain = jnp.sum(stream_grad * centered, axis=1)
    grad_shift = jnp.sum(stream_grad, axis=1)
    d_streams = jnp.concatenate([d_streams[:3], (d_streams[3] + cot_rows)[None]], axis=0)
    layer_grads = []
    d_mix_parts = []
    for layer in range(HIST):
        layer_f = history[layer].astype(F32)
        layer_grads.append(
            jnp.sum(jnp.transpose(weights_four[:, :, layer])[:, :, None] * d_streams, axis=0)
        )
        d_mix_parts.append(jnp.sum(d_streams * layer_f[None], axis=2))
    d_mix_local = jnp.transpose(jnp.stack(d_mix_parts, axis=-1), (1, 0, 2)).reshape(
        tokens, 4 * HIST
    )
    d_mix = lax.psum(d_mix_local.astype(BF16), "head").astype(F32)
    grad_bias = jnp.sum(d_mix, axis=0)
    grad_w2 = jnp.dot(mix_hidden.T, d_mix, precision=HIGHEST)
    d_hidden = jnp.dot(d_mix, w_mix_out_f.T, precision=HIGHEST)
    _, gelu_mix_back = jax.vjp(gelu_exact, mix_pre)
    d_pre = gelu_mix_back(d_hidden)[0]
    normed_in = current_f * rms_scale
    grad_w1 = jnp.dot(normed_in.T, d_pre, precision=HIGHEST)
    d_normed_in = jnp.dot(d_pre, w_mix_in_f.T, precision=HIGHEST)
    cross = jnp.sum(d_pre * mix_pre, axis=1, keepdims=True)
    layer_grads[HIST - 1] = layer_grads[HIST - 1] + rms_scale * (
        d_normed_in - normed_in * cross / model_width
    )
    history_grad = jnp.stack(layer_grads).reshape(HIST, micro, quarter, feats)
    small = [
        lax.psum(a.astype(BF16), ("dp", "stream")).astype(F32)
        for a in (grad_w1, grad_w2, grad_bias, grad_gain, grad_shift)
    ]
    return (
        block_out.reshape(micro, quarter, feats),
        mix_weights.reshape(micro, quarter, 4 * HIST),
        history_grad,
        small[0],
        small[1],
        small[2].reshape(mix_bias.shape),
        small[3],
        small[4],
        grad_qkv,
        grad_attn_out,
        grad_up,
        grad_down,
    )


def solution(mesh):
    return jax.shard_map(
        shards,
        mesh=mesh,
        in_specs=(
            P(None, "dp", "stream", "head"),
            P(),
            P(),
            P("head", None),
            P(),
            P(),
            P(None, "head"),
            P(None, "head"),
            P(None, ("dp", "stream"), "head"),
            P("head", ("dp", "stream")),
            P(("dp", "stream"), "head"),
            P("head", ("dp", "stream")),
            P("dp", "stream", "head"),
        ),
        out_specs=(
            P("dp", "stream", "head"),
            P("dp", "stream", None),
            P(None, "dp", "stream", "head"),
            P("head", None),
            P(),
            P(),
            P(None, "head"),
            P(None, "head"),
            P(None, ("dp", "stream"), "head"),
            P("head", ("dp", "stream")),
            P(("dp", "stream"), "head"),
            P("head", ("dp", "stream")),
        ),
        check_vma=False,
    )
```

time: 1930 us -> 1280 us (0.66)
  waiting for transfers between devices: 1300 us -> 348 us
  local copies, waits for them, and re-layouts: 70.5 us -> 387 us
  matrix products: 303 us -> 189 us
  starting transfers between devices: 3.93 us -> 76.5 us
  Pallas kernels: 0 us -> 44.1 us
  other arithmetic: 165 us -> 136 us
    reduce_scatter x16 -> x5, waiting for transfers between devices: 806 us -> 0.02 us  [to_owner(): lax.psum_scatter(partial.astype(BF16), 'head', scatter_dimension=1, tiled...]
    all_gather x12 -> x5, waiting for transfers between devices: 454 us -> 157 us  [the longest x4 157 us: all_features(): return lax.all_gather(normed[stream], 'head', axis=1, tiled=True)]
    ppermute x0 -> x90, waiting for transfers between devices: none -> 166 us  [the longest x24 83.8 us: over_x(): return lax.ppermute(a, 'dp', SWAP_X)]
    dot_general x60 -> x30, matrix products: 303 us -> 189 us  [the longest x6 67 us: dot_nt(): lax.dot_general(a, b, (((1,), (1,)), ((), ())), preferred_element_type=F32)]
    unnamed x376 -> x361, local copies, waits for them, and re-layouts: 52.2 us -> 164 us
    ppermute x0 -> x90, starting transfers between devices: none -> 75.5 us  [the longest x24 29.4 us: over_y(): return lax.ppermute(a, 'stream', SWAP_Y)]
    dynamic_slice x0 -> x9, local copies, waits for them, and re-layouts: none -> 60.7 us  [the longest x3 32.7 us: scatter_product(): lax.dynamic_index_in_dim(split, 1 - core, 2, keepdims=False)]
    reshape x3 -> x10, local copies, waits for them, and re-layouts: 0.11 us -> 46 us  [the longest x5 39.1 us: scatter_product(): split = rows.reshape(tokens, 4, 2, width)]
  transfers between devices with their start and end apart: 30 -> 102, of which waited for: 24 -> 38; matrix products, arithmetic and copies ran while one was open for 23% -> 48% of each run, Pallas kernels for 0% -> 0%
where the time goes in v1:
time: 1280 us; the launch traced here: 1260 us
  local copies, waits for them, and re-layouts  387 us (30%)
  waiting for transfers between devices  348 us (27%)
  matrix products  189 us (15%)
  other arithmetic  136 us (11%)
  starting transfers between devices  76.5 us (6%)
  blocking collectives  67.1 us (5%)
  Pallas kernels  44.1 us (3%)
  between operations  17.4 us (1%)
    unnamed x361, local copies, waits for them, and re-layouts  164 us
    all_gather x4, waiting for transfers between devices, all_features(): return lax.all_gather(normed[stream], 'head', axis=1, tiled=True)  157 us
    ppermute x24, waiting for transfers between devices, over_x(): return lax.ppermute(a, 'dp', SWAP_X)  83.8 us
    dot_general x6, matrix products, dot_nt(): lax.dot_general(a, b, (((1,), (1,)), ((), ())), preferred_element_type=F32)  67 us
    dot_general x7, matrix products, dot(): return jnp.dot(a, b, preferred_element_type=F32)  60.8 us
    dot_general x12, matrix products, dot_tn(): lax.dot_general(a, b, (((0,), (0,)), ((), ())), preferred_element_type=F32)  51.9 us
    ppermute x24, waiting for transfers between devices, over_y(): return lax.ppermute(a, 'stream', SWAP_Y)  48.1 us
    pallas_call x1, Pallas kernels, attention(): pl.pallas_call(attention_kernel, grid=(micro, feats // HD), in_specs=[pl....  44.1 us
  transfers between devices with their start and end apart: 102, of which 38 were waited for; matrix products, arithmetic and copies ran while one was open for 48% of the time, Pallas kernels for 0%

profile of v1, /device:TPU:8, one launch (start us, length us, event | category | flops | bytes accessed | tf_op | source)
XLA Modules:
  0.0 1264.4 jit_solution(2587914713941707674)
XLA Ops:
  54.6 13.5 %fusion.90 = (f32[4,1024]{1,0:T(4,128)S(1)}, f32[4,1024]{1,0:T(4,128)S(1)}, f32[4,1024,512]{2,1,0:T(8,128)}) fusion(f32[1024,512]{1,0:T(8,128)S(1)} %convert_element_type.633, f32[4,1024]{1,0:T(4,128)S(1)} %get-tuple-element.175, f32[1024,512]{1,0:T(8,128)} %convert.94, f32[4,1024]{1,0:T(4,128)S(1)} %get-tuple-element.176, f32[1024,512]{1,0:T(8,128)} %convert.93, ...), kind=kLoop, calls=%fused_computation.372 | loop fusion | flops 41934848 | bytes 27443200 | tf_op jit(solution)/shard_map/reduce_sum | solution.py:284
  68.1 17.4 %all-reduce.1 = (f32[4,1024]{1,0:T(4,128)S(1)}, f32[4,1024]{1,0:T(4,128)S(1)}) all-reduce(f32[4,1024]{1,0:T(4,128)S(1)} %get-tuple-element.53, f32[4,1024]{1,0:T(4,128)S(1)} %get-tuple-element.52), channel_id=1, replica_groups=mesh['dp'=2,'stream'=4,'head'=4] {'head'}, use_global_device_ids=true, to_apply=%region_14.15 | all-reduce | flops 8192 | bytes 65536 | tf_op jit(solution)/shard_map/psum | solution.py:283
  174.6 16.4 %collective-permute-done.39 = bf16[256,2048]{1,0:T(8,128)(2,1)S(1)} collective-permute-done((bf16[256,2048]{1,0:T(8,128)(2,1)S(1)}, bf16[256,2048]{1,0:T(8,128)(2,1)S(1)}, u32[]{:S(2)}, u32[]{:S(2)}) %collective-permute-start.39) | collective-permute-done | bytes 1048608 | tf_op jit(solution)/shard_map/ppermute | solution.py:42
  197.2 15.3 %collective-permute-done.47 = bf16[2048,256]{1,0:T(8,128)(2,1)S(1)} collective-permute-done((bf16[2048,256]{1,0:T(8,128)(2,1)S(1)}, bf16[2048,256]{1,0:T(8,128)(2,1)S(1)}, u32[]{:S(2)}, u32[]{:S(2)}) %collective-permute-start.47) | collective-permute-done | bytes 1048608 | tf_op jit(solution)/shard_map/ppermute | solution.py:42
  224.7 15.2 %collective-permute-done.51 = bf16[1024,256]{1,0:T(8,128)(2,1)S(1)} collective-permute-done((bf16[1024,256]{1,0:T(8,128)(2,1)S(1)}, bf16[1024,256]{1,0:T(8,128)(2,1)S(1)}, u32[]{:S(2)}, u32[]{:S(2)}) %collective-permute-start.51) | collective-permute-done | bytes 524320 | tf_op jit(solution)/shard_map/ppermute | solution.py:46
  263.4 30.1 %all-gather.12.cloned.1.call-done = bf16[1,1024,2048]{2,1,0:T(8,128)(2,1)} async-done(((bf16[1,1024,512]{2,1,0:T(8,128)(2,1)}), bf16[1,1024,2048]{2,1,0:T(8,128)(2,1)}) %all-gather.12.cloned.1.call-update) | async-done | bytes 4194320 | tf_op jit(solution)/shard_map/all_gather | solution.py:292
  293.5 15.6 %fusion.19 = f32[1024,512]{0,1:T(8,128)S(1)} fusion(bf16[2048,512]{1,0:T(8,128)(2,1)} %constant_dynamic-update-slice_fusion.70, bf16[1,1024,2048]{2,1,0:T(8,128)(2,1)} %all-gather.12.cloned.1.call-done), kind=kOutput, calls=%fused_computation.63 | convolution fusion | flops 2147483648 | bytes 8388608 | tf_op jit(solution)/shard_map/dot_general | solution.py:26
  319.7 55.2 %all-gather.16.cloned.1.call-done = bf16[1,1024,2048]{2,1,0:T(8,128)(2,1)} async-done(((bf16[1,1024,512]{2,1,0:T(8,128)(2,1)}), bf16[1,1024,2048]{2,1,0:T(8,128)(2,1)}) %all-gather.16.cloned.1.call-update) | async-done | bytes 4194320 | tf_op jit(solution)/shard_map/all_gather | solution.py:292
  384.7 71.5 %all-gather.18.cloned.1.call-done = bf16[1,1024,2048]{2,1,0:T(8,128)(2,1)} async-done(((bf16[1,1024,512]{2,1,0:T(8,128)(2,1)}), bf16[1,1024,2048]{2,1,0:T(8,128)(2,1)}) %all-gather.18.cloned.1.call-update) | async-done | bytes 4194320 | tf_op jit(solution)/shard_map/all_gather | solution.py:292
  456.3 12.6 fusion.13
  468.9 32.5 %add_convert_fusion.2 = (bf16[1024,2048]{1,0:T(8,128)(2,1)}, f32[1024,2048]{1,0:T(8,128)}) fusion(f32[1024,2048]{1,0:T(8,128)S(1)} %fusion.13, bf16[1024,2048]{1,0:T(8,128)(2,1)S(1)} %copy-done.65, bf16[2048,2048]{1,0:T(8,128)(2,1)} %constant_dynamic-update-slice_fusion.30), kind=kOutput, calls=%fused_computation.32 | convolution fusion | flops 8740929536 | bytes 33554432 | tf_op jit(solution)/shard_map/dot_general | solution.py:30
  511.6 15.6 %fusion.110 = f32[1024,2048]{1,0:T(8,128)} fusion(bf16[1024,2048]{1,0:T(8,128)(2,1)S(1)} %multiply_convert_fusion, bf16[2048,2048]{1,0:T(8,128)(2,1)} %constant_dynamic-update-slice_fusion.30), kind=kOutput, calls=%fused_computation.391 | convolution fusion | flops 8589934592 | bytes 20971520 | tf_op jit(solution)/shard_map/dot_general | solution.py:26
  528.6 44.1 %attention_both_ways.1 = (bf16[2,512,512]{2,1,0:T(8,128)(2,1)S(1)}, f32[2,512,512]{2,1,0:T(8,128)}, bf16[2,512,512]{2,1,0:T(8,128)(2,1)S(1)}, bf16[2,512,512]{2,...) custom-call(s32[4]{0:T(128)S(1)} %iota_xor_fusion.place_ref, ...), custom_call_target="tpu_custom_call" | custom-call | flops 12884901888 | bytes 20971520 | tf_op jit(solution)/shard_map/attention_both_ways/pallas_call | solution.py:163
  584.7 13.9 %convolution_convert_fusion = bf16[1024,2048]{1,0:T(8,128)(2,1)} fusion(bf16[1024,2048]{1,0:T(8,128)(2,1)} %get-tuple-element.76, bf16[2048,2048]{1,0:T(8,128)(2,1)} %constant_dynamic-update-slice_fusion.38), kind=kOutput, calls=%fused_computation.65 | convolution fusion | flops 8592031744 | bytes 16777216 | tf_op jit(solution)/shard_map/dot_general | solution.py:30
  604.5 25.8 %collective-permute-done.59 = bf16[2,512,512]{2,1,0:T(8,128)(2,1)S(1)} collective-permute-done((bf16[2,512,512]{2,1,0:T(8,128)(2,1)S(1)}, bf16[2,512,512]{2,1,0:T(8,128)(2,1)S(1)}, u32[]{:S(2)}, u32[]{:S(2)}) %collective-permute-start.59) | collective-permute-done | bytes 1048608 | tf_op jit(solution)/shard_map/ppermute | solution.py:197
  671.0 11.4 constant_dynamic-slice_fusion.11
  711.4 11.4 constant_dynamic-slice_fusion.4
  753.3 11.5 constant_dynamic-slice_fusion.13
  840.0 11.4 constant_dynamic-slice_fusion.16
  1057.7 22.6 %collective-permute-done.74 = bf16[256,256]{1,0:T(8,128)(2,1)S(1)} collective-permute-done((bf16[256,256]{1,0:T(8,128)(2,1)S(1)}, bf16[256,256]{1,0:T(8,128)(2,1)S(1)}, u32[]{:S(2)}, u32[]{:S(2)}) %collective-permute-start.74) | collective-permute-done | bytes 131104 | tf_op jit(solution)/shard_map/ppermute | solution.py:42
  1121.4 17.4 %all-reduce = (f32[4,1024]{1,0:T(4,128)S(1)}, f32[4,1024]{1,0:T(4,128)S(1)}) all-reduce(f32[4,1024]{1,0:T(4,128)S(1)} %get-tuple-element.33, f32[4,1024]{1,0:T(4,128)S(1)} %get-tuple-element.54), channel_id=1, replica_groups=mesh['dp'=2,'stream'=4,'head'=4] {'head'}, use_global_device_ids=true, to_apply=%region_25.26 | all-reduce | flops 8192 | bytes 65536 | tf_op jit(solution)/shard_map/psum | solution.py:350
  1160.7 17.0 %multiply_reduce_fusion.1 = (bf16[4,1024]{1,0:T(4,128)(2,1)S(1)}, f32[1024,512]{1,0:T(8,128)}, f32[1024,512]{1,0:T(8,128)}, f32[1024,512]{1,0:T(8,128)}, bf16[4,...) fusion(f32[1024,512]{1,0:T(8,128)} %convert.94, ...), kind=kLoop, calls=%fused_computation.15 | loop fusion | flops 48218112 | bytes 33718272 | tf_op jit(solution)/shard_map/reduce_sum | solution.py:368
  1198.9 18.8 %all-reduce.8.cloned.1.call-done = bf16[1024,36]{0,1:T(8,128)(2,1)} async-done(((bf16[1024,36]{0,1:T(8,128)(2,1)}), bf16[1024,36]{0,1:T(8,128)(2,1)}) %all-reduce.8.cloned.1.call-update) | async-done | bytes 73744 | tf_op jit(solution)/shard_map/psum | solution.py:372
  1226.9 23.3 %all-reduce.2 = (bf16[512,36]{0,1:T(8,128)(2,1)S(1)}, bf16[36,36]{1,0:T(8,128)(2,1)S(1)}, bf16[4,9]{1,0:T(4,128)(2,1)S(1)}, bf16[4,512]{1,0:T(4,128)(2,1)S(1)}, bf16[4,512]{1,0:T(4,128)(2,1)S(1)}) all-reduce(bf16[512,36]{0,1:T(8,128)(2,1)S(1)} %fusion.53, ...), channel_id=1, replica_groups=mesh['dp'=2,'stream'=4,'head'=4] {'dp','stream'}, use_global_device_ids=true, to_apply=%region_46.47 | all-reduce | flops 23860 | bytes 95440 | tf_op jit(solution)/shard_map/psum | solution.py:387
  (841 shorter events, 707.5 us)
Async XLA Ops:
  15.2 237.3 %all-gather.10.cloned.1.call-start = ((), (), s32[]{:S(2)}) async-start(), calls=%async_computation.6 | async-start | bytes 5242880 | tf_op jit(solution)/shard_map/all_gather | solution.py:259
  19.7 238.3 %all-gather.14.cloned.1.call-start = ((), (), s32[]{:S(2)}) async-start(), calls=%async_computation.14 | async-start | bytes 5242880 | tf_op jit(solution)/shard_map/all_gather | solution.py:292
  92.1 201.4 %all-gather.12.cloned.1.call-start = ((), (), s32[]{:S(2)}) async-start(), calls=%async_computation.13 | async-start | bytes 5242880 | tf_op jit(solution)/shard_map/all_gather | solution.py:292
  92.7 282.2 %all-gather.16.cloned.1.call-start = ((), (), s32[]{:S(2)}) async-start(), calls=%async_computation.15 | async-start | bytes 5242880 | tf_op jit(solution)/shard_map/all_gather | solution.py:292
  93.3 363.0 %all-gather.18.cloned.1.call-start = ((), (), s32[]{:S(2)}) async-start(), calls=%async_computation.16 | async-start | bytes 5242880 | tf_op jit(solution)/shard_map/all_gather | solution.py:292
  121.3 988.8 %reduce-scatter.6.cloned.1.call-start = ((), (), s32[]{:S(2)}) async-start(), calls=%async_computation.7 | async-start | bytes 5242880 | tf_op jit(solution)/shard_map/reduce_scatter | solution.py:326
  169.3 50.4 %collective-permute-start.38 = (bf16[256,2048]{1,0:T(8,128)(2,1)S(1)}, bf16[256,2048]{1,0:T(8,128)(2,1)S(1)}, u32[]{:S(2)}, u32[]{:S(2)}) collective-permute-start(bf16[256,2048]{1,0:T(8,128)(2,1)S(1)} %copy-done.98), channel_id=1, source_target_pairs={{0,4},{4,0},{8,12},{12,8},{1,5},{5,1},{9,13},{13,9},{2,6},{6,2},{1... | collective-permute-start | bytes 3145736 | tf_op jit(solution)/shard_map/ppermute | solution.py:50
  316.0 211.2 %collective-permute-start.24 = (bf16[2,512,512]{2,1,0:T(8,128)(2,1)}, bf16[2,512,512]{2,1,0:T(8,128)(2,1)}, u32[]{:S(2)}, u32[]{:S(2)}) collective-permute-start(bf16[2,512,512]{2,1,0:T(8,128)(2,1)} %bitcast.35.refs_0_), channel_id=1, source_target_pairs={{0,4},{4,0},{8,12},{12,8},{1,5},{5,1},{9,13},{13,9},{2,6},{6,2},{1... | collective-permute-start | bytes 3145736 | tf_op jit(solution)/shard_map/ppermute | solution.py:50
  316.0 195.0 %collective-permute-start.25 = (bf16[2,512,512]{2,1,0:T(8,128)(2,1)}, bf16[2,512,512]{2,1,0:T(8,128)(2,1)S(1)}, u32[]{:S(2)}, u32[]{:S(2)}) collective-permute-start(bf16[2,512,512]{2,1,0:T(8,128)(2,1)} %bitcast.35.refs_0_), channel_id=1, source_target_pairs={{0,8},{4,12},{1,9},{5,13},{2,10},{6,14},{3,11},{7,15},{16,24},{20,... | collective-permute-start | bytes 3145736 | tf_op jit(solution)/shard_map/ppermute | solution.py:188
  381.0 146.1 %collective-permute-start.35 = (bf16[2,512,512]{2,1,0:T(8,128)(2,1)}, bf16[2,512,512]{2,1,0:T(8,128)(2,1)}, u32[]{:S(2)}, u32[]{:S(2)}) collective-permute-start(bf16[2,512,512]{2,1,0:T(8,128)(2,1)} %bitcast.38.refs_4_), channel_id=1, source_target_pairs={{0,4},{4,0},{8,12},{12,8},{1,5},{5,1},{9,13},{13,9},{2,6},{6,2},{1... | collective-permute-start | bytes 3145736 | tf_op jit(solution)/shard_map/ppermute | solution.py:50
  381.0 130.0 %collective-permute-start.36 = (bf16[2,512,512]{2,1,0:T(8,128)(2,1)}, bf16[2,512,512]{2,1,0:T(8,128)(2,1)S(1)}, u32[]{:S(2)}, u32[]{:S(2)}) collective-permute-start(bf16[2,512,512]{2,1,0:T(8,128)(2,1)} %bitcast.38.refs_4_), channel_id=1, source_target_pairs={{0,8},{4,12},{1,9},{5,13},{2,10},{6,14},{3,11},{7,15},{16,24},{20,... | collective-permute-start | bytes 3145736 | tf_op jit(solution)/shard_map/ppermute | solution.py:188
  584.7 528.6 %reduce-scatter.14.cloned.1.call-start = ((), (), s32[]{:S(2)}) async-start(), calls=%async_computation.11 | async-start | bytes 5242880 | tf_op jit(solution)/shard_map/reduce_scatter | solution.py:326
  598.6 514.6 %reduce-scatter.12.cloned.1.call-start = ((), (), s32[]{:S(2)}) async-start(), calls=%async_computation.10 | async-start | bytes 5242880 | tf_op jit(solution)/shard_map/reduce_scatter | solution.py:326
  637.8 475.5 %reduce-scatter.10.cloned.1.call-start = ((), (), s32[]{:S(2)}) async-start(), calls=%async_computation.9 | async-start | bytes 5242880 | tf_op jit(solution)/shard_map/reduce_scatter | solution.py:326
  671.0 78.5 %collective-permute-start.55 = (bf16[2,512,512]{2,1,0:T(8,128)(2,1)}, bf16[2,512,512]{2,1,0:T(8,128)(2,1)}, u32[]{:S(2)}, u32[]{:S(2)}) collective-permute-start(bf16[2,512,512]{2,1,0:T(8,128)(2,1)} %copy-done.7), channel_id=1, source_target_pairs={{0,4},{4,0},{8,12},{12,8},{1,5},{5,1},{9,13},{13,9},{2,6},{6,2},{1... | collective-permute-start | bytes 3145736 | tf_op jit(solution)/shard_map/ppermute | solution.py:50
  796.0 317.2 %reduce-scatter.8.cloned.1.call-start = ((), (), s32[]{:S(2)}) async-start(), calls=%async_computation.8 | async-start | bytes 5242880 | tf_op jit(solution)/shard_map/reduce_scatter | solution.py:326
  820.3 155.0 %collective-permute-start.80 = (bf16[1024,2048]{1,0:T(8,128)(2,1)}, bf16[1024,2048]{1,0:T(8,128)(2,1)}, u32[]{:S(2)}, u32[]{:S(2)}) collective-permute-start(bf16[1024,2048]{1,0:T(8,128)(2,1)} %convolution_convert_fusion.5), channel_id=1, source_target_pairs={{0,4},{4,0},{8,12},{12,8},{1,5},{5,1},{9,13},{13,9},{2,6},{6,2},{1... | collective-permute-start | bytes 12582920 | tf_op jit(solution)/shard_map/ppermute | solution.py:50
  840.0 95.1 %collective-permute-start.78 = (bf16[2,256,256]{1,2,0:T(8,128)(2,1)}, bf16[2,256,256]{1,2,0:T(8,128)(2,1)}, u32[]{:S(2)}, u32[]{:S(2)}) collective-permute-start(bf16[2,256,256]{1,2,0:T(8,128)(2,1)} %bitcast.128), channel_id=1, source_target_pairs={{0,8},{8,0},{4,12},{12,4},{1,9},{9,1},{5,13},{13,5},{2,10},{10,2},... | collective-permute-start | bytes 786440 | tf_op jit(solution)/shard_map/ppermute | solution.py:46
  925.4 63.3 %collective-permute-start.85 = (bf16[1024,2048]{1,0:T(8,128)(2,1)}, bf16[1024,2048]{1,0:T(8,128)(2,1)}, u32[]{:S(2)}, u32[]{:S(2)}) collective-permute-start(bf16[1024,2048]{1,0:T(8,128)(2,1)} %convolution_convert_fusion.4), channel_id=1, source_target_pairs={{0,4},{4,0},{8,12},{12,8},{1,5},{5,1},{9,13},{13,9},{2,6},{6,2},{1... | collective-permute-start | bytes 12582920 | tf_op jit(solution)/shard_map/ppermute | solution.py:50
  975.2 242.5 %all-reduce.8.cloned.1.call-start = ((), (), s32[]{:S(2)}) async-start(), calls=%async_computation.12 | async-start | bytes 163840 | tf_op jit(solution)/shard_map/psum | solution.py:372
  1044.7 61.8 %collective-permute-start.84 = (bf16[256,1024]{1,0:T(8,128)(2,1)S(1)}, bf16[256,1024]{1,0:T(8,128)(2,1)S(1)}, u32[]{:S(2)}, u32[]{:S(2)}) collective-permute-start(bf16[256,1024]{1,0:T(8,128)(2,1)S(1)} %dynamic-slice_bitcast_fusion.4), channel_id=1, source_target_pairs={{0,16},{16,0},{1,17},{17,1},{2,18},{18,2},{3,19},{19,3},{4,20},{20... | collective-permute-start | bytes 1572872 | tf_op jit(solution)/shard_map/ppermute | solution.py:42
  1046.7 59.9 %collective-permute-start.82 = (bf16[256,1024]{1,0:T(8,128)(2,1)S(1)}, bf16[256,1024]{1,0:T(8,128)(2,1)S(1)}, u32[]{:S(2)}, u32[]{:S(2)}) collective-permute-start(bf16[256,1024]{1,0:T(8,128)(2,1)S(1)} %dynamic-slice_bitcast_fusion.5), channel_id=1, source_target_pairs={{0,8},{8,0},{4,12},{12,4},{1,9},{9,1},{5,13},{13,5},{2,10},{10,2},... | collective-permute-start | bytes 1572872 | tf_op jit(solution)/shard_map/ppermute | solution.py:46
  1050.3 56.6 %collective-permute-start.89 = (bf16[256,1024]{0,1:T(8,128)(2,1)S(1)}, bf16[256,1024]{0,1:T(8,128)(2,1)S(1)}, u32[]{:S(2)}, u32[]{:S(2)}) collective-permute-start(bf16[256,1024]{0,1:T(8,128)(2,1)S(1)} %dynamic-slice_bitcast_fusion.2), channel_id=1, source_target_pairs={{0,16},{16,0},{1,17},{17,1},{2,18},{18,2},{3,19},{19,3},{4,20},{20... | collective-permute-start | bytes 1572872 | tf_op jit(solution)/shard_map/ppermute | solution.py:42
  1052.4 54.7 %collective-permute-start.87 = (bf16[256,1024]{0,1:T(8,128)(2,1)S(1)}, bf16[256,1024]{0,1:T(8,128)(2,1)S(1)}, u32[]{:S(2)}, u32[]{:S(2)}) collective-permute-start(bf16[256,1024]{0,1:T(8,128)(2,1)S(1)} %dynamic-slice_bitcast_fusion.3), channel_id=1, source_target_pairs={{0,8},{8,0},{4,12},{12,4},{1,9},{9,1},{5,13},{13,5},{2,10},{10,2},... | collective-permute-start | bytes 1572872 | tf_op jit(solution)/shard_map/ppermute | solution.py:46
  (235 other events, 3139.1 us)
Sparse Core Ops, SparseCore 0:
  15.3 35.6 all-reduce.5
  52.7 78.8 all-gather.9
  133.3 79.3 all-gather.13
  214.1 79.2 all-gather.11
  295.5 79.2 all-gather.15
  377.0 79.2 all-gather.17
  584.8 77.9 reduce-scatter.5
  665.1 77.2 reduce-scatter.13
  744.8 77.2 reduce-scatter.11
  824.2 77.2 reduce-scatter.9
  975.3 79.0 reduce-scatter.7
  1183.4 34.2 all-reduce.7

commit v2 on v1

--- a/solution.py
+++ b/solution.py
@@ -54,48 +54,56 @@
     return lax.axis_size("dp") == 2 and lax.axis_size("stream") == 4
 
 
+def place_kernel(order_ref, near_ref, beside_ref, out_ref):
+    step = pl.program_id(0)
+    half = pl.num_programs(0) // 2
+
+    @pl.when(step < half)
+    def _():
+        out_ref[...] = near_ref[0]
+
+    @pl.when(step >= half)
+    def _():
+        out_ref[...] = beside_ref[0]
+
+
 def gather_weight(shard, axis):
     if not paired():
         return lax.all_gather(shard, ("dp", "stream"), axis=axis, tiled=True)
     place = lax.axis_index("dp") * 4 + lax.axis_index("stream")
-    width = shard.shape[axis]
-    full_shape = list(shard.shape)
-    full_shape[axis] = width * 8
-    near_x = over_x(shard)
-    near_y = over_y(shard)
-    half = shard.shape[-2] // 2
-    low = lax.slice_in_dim(near_x, 0, half, axis=shard.ndim - 2)
-    high = lax.slice_in_dim(near_y, half, 2 * half, axis=shard.ndim - 2)
-    far = jnp.concatenate([over_y(low), over_x(high)], axis=shard.ndim - 2)
-    full = jnp.zeros(full_shape, shard.dtype)
-    for flip, block in ((0, shard), (4, near_x), (2, near_y), (6, far)):
-        full = lax.dynamic_update_slice_in_dim(full, block, (place ^ flip) * width, axis)
-        full = lax.dynamic_update_slice_in_dim(
-            full, over_core(block), (place ^ flip ^ 1) * width, axis
-        )
-    return full
-
-
-def scatter_product(rows, columns):
+    row = jnp.stack([shard, over_x(shard)])
+    near = jnp.concatenate([row, over_y(row)])
+    beside = over_core(near)
+    flips = jnp.array([0, 4, 2, 6, 1, 5, 3, 7], jnp.int32)
+    full_shape = tuple(n * 8 if i == axis else n for i, n in enumerate(shard.shape))
+    at = lambda k: tuple(k if i == axis else 0 for i in range(shard.ndim))
+    inner = (0,) * shard.ndim
+    return pl.pallas_call(
+        place_kernel,
+        grid_spec=pltpu.PrefetchScalarGridSpec(
+            num_scalar_prefetch=1,
+            grid=(8,),
+            in_specs=[
+                pl.BlockSpec((1,) + shard.shape, lambda k, order: (jnp.minimum(k, 3),) + inner),
+                pl.BlockSpec((1,) + shard.shape, lambda k, order: (jnp.maximum(k - 4, 0),) + inner),
+            ],
+            out_specs=pl.BlockSpec(shard.shape, lambda k, order: at(order[k])),
+        ),
+        out_shape=jax.ShapeDtypeStruct(full_shape, shard.dtype),
+        compiler_params=pltpu.CompilerParams(vmem_limit_bytes=40 * 1024 * 1024),
+        cost_estimate=pl.CostEstimate(flops=0, bytes_accessed=32 * shard.size, transcendentals=0),
+        name="weight_in_order",
+    )(place ^ flips, near, beside)
+
+
+def scatter_sum(partial):
     if not paired():
         return lax.psum_scatter(
-            dot_tn(rows, columns).astype(BF16),
-            ("dp", "stream"),
-            scatter_dimension=0,
-            tiled=True,
+            partial, ("dp", "stream"), scatter_dimension=0, tiled=True
         ).astype(F32)
-    tokens, model_width = rows.shape
-    width = model_width // 8
+    rows, columns = partial.shape
     stream = lax.axis_index("stream")
     x, y, core = lax.axis_index("dp"), stream // 2, stream % 2
-    split = rows.reshape(tokens, 4, 2, width)
-    mine = lax.dynamic_index_in_dim(split, core, 2, keepdims=False).reshape(tokens, 4 * width)
-    other = lax.dynamic_index_in_dim(split, 1 - core, 2, keepdims=False).reshape(tokens, 4 * width)
-    received = over_core(dot_tn(other, columns).astype(BF16))
-    chip = (dot_tn(mine, columns) + received.astype(F32)).astype(BF16)
-    half = columns.shape[1] // 2
-    chip = chip.reshape(2, 2, width, 2 * half)
-    first, second = chip[..., :half], chip[..., half:]
 
     def pick(a, index, axis):
         return lax.dynamic_index_in_dim(a, index, axis, keepdims=False)
@@ -103,14 +111,96 @@
     def add(a, b):
         return a.astype(F32) + b.astype(F32)
 
-    first_x = add(pick(first, x, 0), over_x(pick(first, 1 - x, 0))).astype(BF16)
-    second_y = add(pick(second, y, 1), over_y(pick(second, 1 - y, 1))).astype(BF16)
-    first_out = add(pick(first_x, y, 0), over_y(pick(first_x, 1 - y, 0)))
-    second_out = add(pick(second_y, x, 0), over_x(pick(second_y, 1 - x, 0)))
-    return jnp.concatenate([first_out, second_out], axis=1)
-
-
-def attention_kernel(place_ref, q_ref, do_ref, start_ref, *refs):
+    split = partial.reshape(4, 2, rows // 8, columns)
+    chip = add(pick(split, core, 1), over_core(pick(split, 1 - core, 1))).astype(BF16)
+    chip = chip.reshape(2, 2, rows // 8, columns)
+    line = add(pick(chip, x, 0), over_x(pick(chip, 1 - x, 0))).astype(BF16)
+    return add(pick(line, y, 0), over_y(pick(line, 1 - y, 0)))
+
+
+def head_sum_kernel(members, x_ref, out_ref, slots, send_sem, recv_sem):
+    z = lax.axis_index("head")
+    barrier = pltpu.get_barrier_semaphore()
+    for k in range(1, members):
+        pl.semaphore_signal(
+            barrier,
+            inc=1,
+            device_id={"head": lax.rem(z + k, members)},
+            device_id_type=pl.DeviceIdType.MESH,
+        )
+    pl.semaphore_wait(barrier, members - 1)
+    copies = []
+    for k in range(1, members):
+        copy = pltpu.make_async_remote_copy(
+            src_ref=x_ref,
+            dst_ref=slots.at[z],
+            send_sem=send_sem.at[k - 1],
+            recv_sem=recv_sem.at[k - 1],
+            device_id={"head": lax.rem(z + k, members)},
+            device_id_type=pl.DeviceIdType.MESH,
+        )
+        copy.start()
+        copies.append(copy)
+    slots[z] = x_ref[...]
+    for copy in copies:
+        copy.wait()
+    total = slots[0]
+    for k in range(1, members):
+        total = total + slots[k]
+    out_ref[...] = total
+
+
+def head_sum(x, collective_id):
+    members = lax.axis_size("head")
+    return pl.pallas_call(
+        functools.partial(head_sum_kernel, members),
+        out_shape=jax.ShapeDtypeStruct(x.shape, F32),
+        in_specs=[pl.BlockSpec(memory_space=pltpu.VMEM)],
+        out_specs=pl.BlockSpec(memory_space=pltpu.VMEM),
+        scratch_shapes=[
+            pltpu.VMEM((members,) + x.shape, F32),
+            pltpu.SemaphoreType.DMA((members - 1,)),
+            pltpu.SemaphoreType.DMA((members - 1,)),
+        ],
+        compiler_params=pltpu.CompilerParams(collective_id=collective_id, has_side_effects=True),
+        name="sum_over_head",
+    )(x)
+
+
+def turn(v, keep, left, right):
+    h = ROT // 2
+    return v * keep + pltpu.roll(v, HD - h, 1) * left + pltpu.roll(v, h, 1) * right
+
+
+def rotate_kernel(sign, v_ref, keep_ref, left_ref, right_ref, out_ref):
+    for head in range(v_ref.shape[1] // HD):
+        part = pl.ds(head * HD, HD)
+        out_ref[:, part] = turn(
+            v_ref[:, part], keep_ref[...], sign * left_ref[...], sign * right_ref[...]
+        ).astype(BF16)
+
+
+def rotate(values_in, tables, sign):
+    tokens, feats = values_in.shape
+    block = min(tokens, 256)
+    table = pl.BlockSpec((block, HD), lambda i: (i, 0))
+    wide = pl.BlockSpec((block, feats), lambda i: (i, 0))
+    return pl.pallas_call(
+        functools.partial(rotate_kernel, sign),
+        grid=(tokens // block,),
+        in_specs=[wide, table, table, table],
+        out_specs=wide,
+        out_shape=jax.ShapeDtypeStruct((tokens, feats), BF16),
+        cost_estimate=pl.CostEstimate(
+            flops=5 * tokens * feats, bytes_accessed=8 * tokens * feats, transcendentals=0
+        ),
+        name="rotate_heads",
+    )(values_in, *tables)
+
+
+def attention_kernel(
+    place_ref, q_ref, do_ref, start_ref, valid_ref, keep_ref, left_ref, right_ref, *refs
+):
     blocks = (len(refs) - 4) // 4
     k_refs, v_refs = refs[:blocks], refs[blocks : 2 * blocks]
     o_ref, dq_ref = refs[2 * blocks : 2 * blocks + 2]
@@ -120,7 +210,9 @@
     rows = q_ref.shape[1]
     scale = HD ** (-0.5)
     member = place_ref[0]
-    q, d_out = q_ref[0], do_ref[0]
+    keep, left, right = keep_ref[0], left_ref[0], right_ref[0]
+    q = turn(q_ref[0], keep, left, right).astype(BF16)
+    d_out = do_ref[0]
     start = start_ref[0]
     top = jnp.full((rows, 1), MASKED, F32)
     t = member * rows + lax.broadcasted_iota(jnp.int32, (rows, rows), 0)
@@ -146,16 +238,16 @@
         d_p = dot_nt(d_out, v_refs[j][0])
         dp_ref[j] = d_p
         delta = delta + jnp.sum(p * d_p, axis=1, keepdims=True)
-    o_ref[0] = out.astype(BF16)
+    o_ref[0] = (out * valid_ref[0]).astype(BF16)
     d_q = jnp.zeros((rows, HD), F32)
     for j in range(blocks):
         d_s = (s_ref[j] * (dp_ref[j] - delta)).astype(BF16)
         d_q = d_q + dot(d_s, k_refs[j][0])
         dk_refs[j][0] = (dot_tn(d_s, q) * scale).astype(BF16)
-    dq_ref[0] = d_q * scale
-
-
-def attention(places, queries, d_attended, starts, keys, values):
+    dq_ref[0] = turn(d_q * scale, keep, -left, -right).astype(BF16)
+
+
+def attention(places, queries, d_attended, starts, valid, tables, keys, values):
     micro, rows, feats = queries.shape
     blocks = len(keys)
     tile = pl.BlockSpec((1, rows, HD), lambda b, h: (b, 0, h))
@@ -164,10 +256,11 @@
         attention_kernel,
         grid=(micro, feats // HD),
         in_specs=[pl.BlockSpec(memory_space=pltpu.SMEM), tile, tile]
-        + [pl.BlockSpec((1, rows, 1), lambda b, h: (b, 0, 0))]
+        + [pl.BlockSpec((1, rows, 1), lambda b, h: (b, 0, 0))] * 2
+        + [pl.BlockSpec((1, rows, HD), lambda b, h: (b, 0, 0))] * 3
         + [tile] * (2 * blocks),
         out_specs=[tile] * (2 + 2 * blocks),
-        out_shape=[like(BF16), like(F32)] + [like(BF16)] * (2 * blocks),
+        out_shape=[like(BF16)] * (2 + 2 * blocks),
         scratch_shapes=[
             pltpu.VMEM((blocks, rows, rows), F32),
             pltpu.VMEM((blocks, rows, rows), F32),
@@ -179,7 +272,7 @@
             transcendentals=micro * rows * rows * blocks * feats // HD,
         ),
         name="attention_both_ways",
-    )(places, queries, d_attended, starts, *keys, *values)
+    )(places, queries, d_attended, starts, valid, *tables, *keys, *values)
 
 
 def exchange_rows(local):
@@ -195,23 +288,6 @@
     across = add(parts[2], over_core(parts[3])).astype(BF16)
     return add(
         add(parts[0], over_core(parts[1])), lax.ppermute(across, "stream", [(2, 0), (3, 1)])
-    )
-
-
-def rotate(values_in, cosine, sine, sign):
-    tokens, feats = values_in.shape
-    rest = HD - ROT
-    ones, zeros = jnp.ones((tokens, rest), F32), jnp.zeros((tokens, rest), F32)
-    none = jnp.zeros_like(sine)
-    heads = feats // HD
-    keep = jnp.tile(jnp.concatenate([cosine, cosine, ones], axis=1), (1, heads))
-    left = jnp.tile(jnp.concatenate([-sign * sine, none, zeros], axis=1), (1, heads))
-    right = jnp.tile(jnp.concatenate([none, sign * sine, zeros], axis=1), (1, heads))
-    h = ROT // 2
-    return (
-        values_in * keep
-        + jnp.roll(values_in, -h, axis=1) * left
-        + jnp.roll(values_in, h, axis=1) * right
     )
 
 
@@ -254,22 +330,29 @@
     frequency = jnp.arange(ROT // 2, dtype=F32)
     phases = position.astype(F32)[:, None] * (10000.0 ** (-2.0 * frequency / ROT))
     cosine, sine = jnp.cos(phases), jnp.sin(phases)
+    plain = jnp.zeros((tokens, HD - ROT), F32)
+    none = jnp.zeros_like(sine)
+    tables = (
+        jnp.concatenate([cosine, cosine, plain + 1.0], axis=1),
+        jnp.concatenate([-sine, none, plain], axis=1),
+        jnp.concatenate([none, sine, plain], axis=1),
+    )
 
     cot_rows = cotangent.reshape(tokens, feats).astype(F32) * valid
     out_full = lax.all_gather(cot_rows.astype(BF16), "head", axis=1, tiled=True)
-    wq, wk, wv = (gather_weight(w_qkv[i], 0) for i in range(3))
-    w_out_full = gather_weight(w_attn_out, 1)
+    wq, wk, wv = gather_weight(w_qkv, 1)
+    both_full = gather_weight(jnp.concatenate([w_attn_out, w_down]), 1)
+    w_out_full, down_full = both_full[:feats], both_full[feats:]
     up_full = gather_weight(w_up, 0)
-    down_full = gather_weight(w_down, 1)
 
     history = history.reshape(HIST, tokens, feats)
     current = history[HIST - 1]
     current_f = current.astype(F32)
-    mix_sum, square_sum = lax.psum(
-        (dot(current, w_mix_in), jnp.sum(current_f * current_f, axis=1)), "head"
-    )
-    rms_scale = lax.rsqrt(square_sum / model_width + EPSILON)[:, None]
-    mix_pre = mix_sum * rms_scale
+    mixed = lax.dot_general(w_mix_in, current, (((0,), (1,)), ((), ())), preferred_element_type=F32)
+    square = jnp.sum(current_f * current_f, axis=1)[None]
+    mixed = head_sum(jnp.concatenate([mixed, square]), 0).T
+    rms_scale = lax.rsqrt(mixed[:, 4 * HIST :] / model_width + EPSILON)
+    mix_pre = mixed[:, : 4 * HIST] * rms_scale
     mix_hidden = gelu_exact(mix_pre)
     mix_weights = jnp.dot(mix_hidden, w_mix_out_f, precision=HIGHEST) + mix_bias.reshape(-1)
     weights_four = mix_weights.reshape(tokens, 4, HIST)
@@ -280,9 +363,10 @@
             + jnp.transpose(weights_four[:, :, layer])[:, :, None]
             * history[layer].astype(F32)[None]
         )
-    stat_sum, stat_square = lax.psum(
-        (jnp.sum(streams, axis=2), jnp.sum(streams * streams, axis=2)), "head"
-    )
+    stats = head_sum(
+        jnp.concatenate([jnp.sum(streams, axis=2), jnp.sum(streams * streams, axis=2)]), 1
+    )
+    stat_sum, stat_square = stats[:4], stats[4:]
     row_means = (stat_sum / model_width)[:, :, None]
     inv_std = lax.rsqrt(stat_square[:, :, None] / model_width - row_means * row_means + EPSILON)
     centered = (streams - row_means) * inv_std
@@ -291,11 +375,11 @@
     def all_features(stream):
         return lax.all_gather(normed[stream], "head", axis=1, tiled=True)
 
-    k_in, v_in, q_in, up_in = all_features(1), all_features(2), all_features(0), all_features(3)
-
-    keys = rotate(dot(k_in, wk), cosine, sine, 1.0).astype(BF16)
+    k_in, v_in, q_in, up_in = (all_features(s) for s in (1, 2, 0, 3))
+
+    keys = rotate(dot(k_in, wk), tables, 1.0)
     values = dot(v_in, wv).astype(BF16)
-    queries = rotate(dot(q_in, wq), cosine, sine, 1.0).astype(BF16)
+    queries = dot(q_in, wq)
     d_attended = dot_nt(out_full, w_out_full).astype(BF16) * valid.astype(BF16)
     by_micro = lambda a: a.reshape(micro, quarter, feats)
     key_blocks = exchange_rows(by_micro(keys))
@@ -306,21 +390,22 @@
         by_micro(queries),
         by_micro(d_attended),
         starts.reshape(micro, quarter, 1),
+        valid.reshape(micro, quarter, 1),
+        tuple(a.reshape(micro, quarter, HD) for a in tables),
         key_blocks,
         value_blocks,
     )
-    attended, d_queries = results[0].reshape(tokens, feats), results[1].reshape(tokens, feats)
-    attended = attended * valid.astype(BF16)
+    attended, d_query_pre = results[0].reshape(tokens, feats), results[1].reshape(tokens, feats)
     d_keys = reduce_rows(results[2:6]).reshape(tokens, feats)
     d_values = reduce_rows(results[6:10]).reshape(tokens, feats)
-    d_query_pre = rotate(d_queries, cosine, sine, -1.0).astype(BF16)
-    d_key_pre = rotate(d_keys, cosine, sine, -1.0).astype(BF16)
+    d_key_pre = rotate(d_keys, tables, -1.0)
     d_value_pre = d_values.astype(BF16)
 
     up_pre = dot(up_in, up_full)
-    gated_up = gelu_exact(up_pre).astype(BF16)
-    _, gelu_back = jax.vjp(gelu_exact, up_pre)
-    d_up = gelu_back(dot_nt(out_full, down_full))[0].astype(BF16)
+    below = 0.5 * (1.0 + lax.erf(up_pre * 0.5**0.5))
+    slope = below + up_pre * jnp.exp(-0.5 * up_pre * up_pre) * (2.0 * jnp.pi) ** -0.5
+    gated_up, slope = lax.optimization_barrier(((up_pre * below).astype(BF16), slope))
+    d_up = (dot_nt(out_full, down_full) * slope).astype(BF16)
 
     def to_owner(partial):
         return lax.psum_scatter(
@@ -334,22 +419,29 @@
     branch = to_owner(dot(attended, w_out_full) + dot(gated_up, down_full))
     block_out = (valid * (streams[3] + branch)).astype(BF16)
 
-    grad_up = scatter_product(up_in, d_up)
-    grad_down = scatter_product(out_full, gated_up).T
-    grad_attn_out = scatter_product(out_full, attended).T
-    grad_qkv = jnp.stack(
-        [
-            scatter_product(q_in, d_query_pre),
-            scatter_product(k_in, d_key_pre),
-            scatter_product(v_in, d_value_pre),
-        ]
-    )
+    product = lambda a, b: dot_tn(a, b).astype(BF16)
+    grad_up = scatter_sum(product(up_in, d_up))
+    grad_down = scatter_sum(product(out_full, gated_up)).T
+    grads = scatter_sum(
+        jnp.concatenate(
+            [
+                product(q_in, d_query_pre),
+                product(k_in, d_key_pre),
+                product(v_in, d_value_pre),
+                product(out_full, attended),
+            ],
+            axis=1,
+        )
+    )
+    grad_qkv = jnp.stack([grads[:, i * feats : (i + 1) * feats] for i in range(3)])
+    grad_attn_out = grads[:, 3 * feats :].T
 
     stream_grad = jnp.stack([g_query, g_key, g_value, g_up])
     d_centered = stream_grad * ln_gain[:, None, :]
-    sum_grad, sum_cross = lax.psum(
-        (jnp.sum(d_centered, axis=2), jnp.sum(d_centered * centered, axis=2)), "head"
-    )
+    sums = head_sum(
+        jnp.concatenate([jnp.sum(d_centered, axis=2), jnp.sum(d_centered * centered, axis=2)]), 2
+    )
+    sum_grad, sum_cross = sums[:4], sums[4:]
     d_streams = inv_std * (
         d_centered
         - sum_grad[:, :, None] / model_width
@@ -369,7 +461,7 @@
     d_mix_local = jnp.transpose(jnp.stack(d_mix_parts, axis=-1), (1, 0, 2)).reshape(
         tokens, 4 * HIST
     )
-    d_mix = lax.psum(d_mix_local.astype(BF16), "head").astype(F32)
+    d_mix = head_sum(d_mix_local.T, 3).T
     grad_bias = jnp.sum(d_mix, axis=0)
     grad_w2 = jnp.dot(mix_hidden.T, d_mix, precision=HIGHEST)
     d_hidden = jnp.dot(d_mix, w_mix_out_f.T, precision=HIGHEST)

time: 1280 us -> 1110 us (0.87)
  local copies, waits for them, and re-layouts: 387 us -> 179 us
  Pallas kernels: 44.1 us -> 132 us
  waiting for transfers between devices: 348 us -> 421 us
  starting transfers between devices: 76.5 us -> 21.8 us
  blocking collectives: 67.1 us -> 23.5 us
  matrix products: 189 us -> 155 us
  other arithmetic: 136 us -> 150 us
    all_gather x4, waiting for transfers between devices: 157 us -> 54.1 us  [all_features(): return lax.all_gather(normed[stream], 'head', axis=1, tiled=True)]
    pallas_call x0 -> x9, Pallas kernels: none -> 87.1 us  [the longest x4 51.2 us: head_sum(): pl.pallas_call(functools.partial(head_sum_kernel, members), out_shape=jax...]
    ppermute x24 -> x6, waiting for transfers between devices: 83.8 us -> 169 us  [over_x(): return lax.ppermute(a, 'dp', SWAP_X)]
    ppermute x24 -> x6, waiting for transfers between devices: 48.1 us -> 128 us  [over_y(): return lax.ppermute(a, 'stream', SWAP_Y)]
    unnamed x361 -> x264, local copies, waits for them, and re-layouts: 164 us -> 89.6 us
    dynamic_slice x5 -> x0, local copies, waits for them, and re-layouts: 55.6 us -> none  [the longest x3 32.7 us: scatter_product(): lax.dynamic_index_in_dim(split, 1 - core, 2, keepdims=False)]
    psum x3 -> x0, blocking collectives: 43.8 us -> none  [the longest x1 17.4 us: shards(): lax.psum((jnp.sum(streams, axis=2), jnp.sum(streams * streams, axis=2)),...]
    all_gather x1, waiting for transfers between devices: 0.01 us -> 38.3 us  [shards(): out_full = lax.all_gather(cot_rows.astype(BF16), 'head', axis=1, tiled=True)]
  transfers between devices with their start and end apart: 102 -> 40, of which waited for: 38 -> 13; matrix products, arithmetic and copies ran while one was open for 48% -> 30% of each run, Pallas kernels for 0% -> 3%
where the time goes in v2:
time: 1110 us; the launch traced here: 1100 us
  waiting for transfers between devices  421 us (38%)
  local copies, waits for them, and re-layouts  179 us (16%)
  matrix products  155 us (14%)
  other arithmetic  150 us (14%)
  Pallas kernels  132 us (12%)
  blocking collectives  23.5 us (2%)
  starting transfers between devices  21.8 us (2%)
  between operations  16.5 us (1%)
    ppermute x6, waiting for transfers between devices, over_x(): return lax.ppermute(a, 'dp', SWAP_X)  169 us
    ppermute x6, waiting for transfers between devices, over_y(): return lax.ppermute(a, 'stream', SWAP_Y)  128 us
    unnamed x264, local copies, waits for them, and re-layouts  89.6 us
    dot_general x6, matrix products, dot(): return jnp.dot(a, b, preferred_element_type=F32)  54.7 us
    all_gather x4, waiting for transfers between devices, all_features(): return lax.all_gather(normed[stream], 'head', axis=1, tiled=True)  54.1 us
    pallas_call x4, Pallas kernels, head_sum(): pl.pallas_call(functools.partial(head_sum_kernel, members), out_shape=jax...  51.2 us
    dot_general x6, matrix products, dot_nt(): lax.dot_general(a, b, (((1,), (1,)), ((), ())), preferred_element_type=F32)  51.1 us
    pallas_call x1, Pallas kernels, attention(): pl.pallas_call(attention_kernel, grid=(micro, feats // HD), in_specs=[pl....  45.3 us
  transfers between devices with their start and end apart: 40, of which 13 were waited for; matrix products, arithmetic and copies ran while one was open for 30% of the time, Pallas kernels for 3%

profile of v2, /device:TPU:8, one launch (start us, length us, event | category | flops | bytes accessed | tf_op | source)
XLA Modules:
  0.0 1098.9 jit_solution(14317692818801488989)
XLA Ops:
  17.3 19.2 %sum_over_head.4 = f32[37,1024]{1,0:T(8,128)} custom-call(f32[37,1024]{1,0:T(8,128)} %pad_maximum_fusion.10.x_ref), custom_call_target="tpu_custom_call" | custom-call | tf_op jit(solution)/shard_map/sum_over_head/pallas_call | solution.py:155
  80.9 64.1 %collective-permute-done = bf16[3,256,512]{2,1,0:T(8,128)(2,1)} collective-permute-done((bf16[3,256,512]{2,1,0:T(8,128)(2,1)S(1)}, bf16[3,256,512]{2,1,0:T(8,128)(2,1)}, u32[]{:S(2)}, u32[]{:S(2)}) %collective-permute-start) | collective-permute-done | bytes 786464 | tf_op jit(solution)/shard_map/ppermute | solution.py:42
  161.4 23.7 %collective-permute-done.1 = bf16[2,3,256,512]{3,2,1,0:T(8,128)(2,1)} collective-permute-done((bf16[2,3,256,512]{3,2,1,0:T(8,128)(2,1)}, bf16[2,3,256,512]{3,2,1,0:T(8,128)(2,1)}, u32[]{:S(2)}, u32[]{:S(2)}) %collective-permute-start.1) | collective-permute-done | bytes 1572896 | tf_op jit(solution)/shard_map/ppermute | solution.py:46
  190.3 39.7 %collective-permute-done.13 = bf16[2,256,2048]{2,1,0:T(8,128)(2,1)} collective-permute-done((bf16[2,256,2048]{2,1,0:T(8,128)(2,1)}, bf16[2,256,2048]{2,1,0:T(8,128)(2,1)}, u32[]{:S(2)}, u32[]{:S(2)}) %collective-permute-start.13) | collective-permute-done | bytes 2097184 | tf_op jit(solution)/shard_map/ppermute | solution.py:46
  236.8 45.5 %collective-permute-done.4 = bf16[2,2560,256]{2,1,0:T(8,128)(2,1)} collective-permute-done((bf16[2,2560,256]{2,1,0:T(8,128)(2,1)}, bf16[2,2560,256]{2,1,0:T(8,128)(2,1)}, u32[]{:S(2)}, u32[]{:S(2)}) %collective-permute-start.4) | collective-permute-done | bytes 2621472 | tf_op jit(solution)/shard_map/ppermute | solution.py:46
  342.6 54.1 %all-gather.18.cloned.1.call-done = bf16[1,1024,2048]{2,1,0:T(8,128)(2,1)} async-done(((bf16[1,1024,512]{2,1,0:T(8,128)(2,1)}), bf16[1,1024,2048]{2,1,0:T(8,128)(2,1)}) %all-gather.18.cloned.1.call-update) | async-done | bytes 4194320 | tf_op jit(solution)/shard_map/all_gather | solution.py:376
  396.7 16.6 %fusion.10 = (f32[1024,2048]{1,0:T(8,128)}, bf16[1024,2048]{1,0:T(8,128)(2,1)S(1)}) fusion(bf16[2048,2048]{1,0:T(8,128)(2,1)} %weight_in_order.5, bf16[1,1024,2048]{2,1,0:T(8,128)(2,1)} %all-gather.18.cloned.1.call-done), kind=kOutput, calls=%fused_computation.13 | convolution fusion | flops 8610906112 | bytes 25165824 | tf_op jit(solution)/shard_map/dot_general | solution.py:26
  425.8 13.3 %fusion.16 = f32[1024,2048]{1,0:T(8,128)} fusion(bf16[1024,2048]{1,0:T(8,128)(2,1)S(1)} %get-tuple-element.25, bf16[2560,2048]{1,0:T(8,128)(2,1)} %weight_in_order.4), kind=kOutput, calls=%fused_computation.52 | convolution fusion | flops 8589934592 | bytes 20971520 | tf_op jit(solution)/shard_map/dot_general | solution.py:26
  439.2 38.3 %all-gather.10.cloned.1.call-done = bf16[1024,2048]{1,0:T(8,128)(2,1)} async-done(((bf16[1024,512]{1,0:T(8,128)(2,1)}), bf16[1024,2048]{1,0:T(8,128)(2,1)}) %all-gather.10.cloned.1.call-update) | async-done | bytes 4194320 | tf_op jit(solution)/shard_map/all_gather | solution.py:342
  482.9 45.3 %attention_both_ways.1 = (bf16[2,512,512]{2,1,0:T(8,128)(2,1)S(1)}, bf16[2,512,512]{2,1,0:T(8,128)(2,1)S(1)}, bf16[2,512,512]{2,1,0:T(8,128)(2,1)S(1)}, bf16[2,5...) custom-call(s32[4]{0:T(128)S(1)} %iota_xor_fusion.place_ref, ...), custom_call_target="tpu_custom_call" | custom-call | flops 12884901888 | bytes 20971520 | tf_op jit(solution)/shard_map/attention_both_ways/pallas_call | solution.py:255
  546.4 14.8 %multiply_convert_fusion = bf16[1024,2048]{1,0:T(8,128)(2,1)S(1)} fusion(f32[1024,2048]{1,0:T(8,128)} %get-tuple-element.35, bf16[1024,2048]{1,0:T(8,128)(2,1)} %all-gather.10.cloned.1.call-done, bf16[2560,2048]{1,0:T(8,128)(2,1)} %weight_in_order.4), kind=kOutput, calls=%fused_computation.40 | convolution fusion | flops 8594128896 | bytes 25165824 | tf_op jit(solution)/shard_map/dot_general | solution.py:30
  563.2 12.9 %convolution_convert_fusion.2 = bf16[1024,2048]{1,0:T(8,128)(2,1)} fusion(bf16[1024,2048]{1,0:T(8,128)(2,1)S(1)} %multiply_convert_fusion, bf16[2048,2048]{1,0:T(8,128)(2,1)} %weight_in_order.5), kind=kOutput, calls=%fused_computation.78 | convolution fusion | flops 8592031744 | bytes 16777216 | tf_op jit(solution)/shard_map/dot_general | solution.py:30
  645.1 18.5 %collective-permute-done.17 = bf16[2,512,512]{2,1,0:T(8,128)(2,1)S(1)} collective-permute-done((bf16[2,512,512]{2,1,0:T(8,128)(2,1)S(1)}, bf16[2,512,512]{2,1,0:T(8,128)(2,1)S(1)}, u32[]{:S(2)}, u32[]{:S(2)}) %collective-permute-start.17) | collective-permute-done | bytes 1048608 | tf_op jit(solution)/shard_map/ppermute | solution.py:290
  682.6 14.5 %reshape.485 = bf16[4,2,256,2048]{2,1,0,3:T(2,128)(2,1)} reshape(bf16[2048,2048]{0,1:T(8,128)(2,1)} %pad_maximum_fusion.1) | data formatting | bytes 16777216 | tf_op jit(solution)/shard_map/reshape | solution.py:114
  697.1 20.2 %constant_dynamic-slice_fusion.3 = (bf16[4,1,256,2048]{2,1,0,3:T(2,128)(2,1)}, bf16[4,1,256,2048]{2,1,0,3:T(2,128)(2,1)}) fusion(bf16[4,2,256,2048]{2,1,0,3:T(2,128)(2,1)} %reshape.485, s32[]{:T(128)S(6)} %select_n.69, s32[]{:T(128)S(6)} %select_n.70), kind=kLoop, calls=%fused_computation.208 | loop fusion | bytes 16777224 | tf_op jit(solution)/shard_map/jit(dynamic_index_in_dim)/dynamic_slice | solution.py:109
  717.3 20.1 %copy.88 = bf16[4,1,256,2048]{3,2,0,1:T(8,128)(2,1)} copy(bf16[4,1,256,2048]{2,1,0,3:T(2,128)(2,1)} %get-tuple-element.147) | data formatting | bytes 8388608
  743.3 20.1 %copy.87 = bf16[4,1,256,2048]{3,2,0,1:T(8,128)(2,1)} copy(bf16[4,1,256,2048]{2,1,0,3:T(2,128)(2,1)} %get-tuple-element.146) | data formatting | bytes 8388608
  803.0 26.5 %collective-permute-done.28 = bf16[2,256,2048]{1,2,0:T(8,128)(2,1)} collective-permute-done((bf16[2,256,2048]{1,2,0:T(8,128)(2,1)}, bf16[2,256,2048]{1,2,0:T(8,128)(2,1)}, u32[]{:S(2)}, u32[]{:S(2)}) %collective-permute-start.28) | collective-permute-done | bytes 2097184 | tf_op jit(solution)/shard_map/ppermute | solution.py:42
  837.2 37.2 %collective-permute-done.25 = bf16[2,256,2048]{2,1,0:T(8,128)(2,1)} collective-permute-done((bf16[2,256,2048]{2,1,0:T(8,128)(2,1)}, bf16[2,256,2048]{2,1,0:T(8,128)(2,1)}, u32[]{:S(2)}, u32[]{:S(2)}) %collective-permute-start.25) | collective-permute-done | bytes 2097184 | tf_op jit(solution)/shard_map/ppermute | solution.py:42
  877.7 41.3 %collective-permute-done.22 = bf16[2,256,2048]{1,2,0:T(8,128)(2,1)} collective-permute-done((bf16[2,256,2048]{1,2,0:T(8,128)(2,1)}, bf16[2,256,2048]{1,2,0:T(8,128)(2,1)}, u32[]{:S(2)}, u32[]{:S(2)}) %collective-permute-start.22) | collective-permute-done | bytes 2097184 | tf_op jit(solution)/shard_map/ppermute | solution.py:42
  928.8 18.8 %collective-permute-done.23 = bf16[256,2048]{0,1:T(8,128)(2,1)} collective-permute-done((bf16[256,2048]{0,1:T(8,128)(2,1)}, bf16[256,2048]{0,1:T(8,128)(2,1)}, u32[]{:S(2)}, u32[]{:S(2)}) %collective-permute-start.23) | collective-permute-done | bytes 1048608 | tf_op jit(solution)/shard_map/ppermute | solution.py:46
  993.7 17.7 %multiply_reduce_fusion.1 = (f32[4,1024]{1,0:T(4,128)}, f32[1024,512]{1,0:T(8,128)}, f32[1024,512]{1,0:T(8,128)}, f32[1024,512]{1,0:T(8,128)}, f32[4,1024]{1,0:T...) fusion(f32[1024,512]{1,0:T(8,128)} %copy-done.24, ...), kind=kLoop, calls=%fused_computation.23 | loop fusion | flops 48218112 | bytes 33751040 | tf_op jit(solution)/shard_map/reduce_sum | solution.py:460
  1027.0 16.6 %sum_over_head.7 = f32[36,1024]{1,0:T(8,128)} custom-call(f32[36,1024]{1,0:T(8,128)} %bitcast.330), custom_call_target="tpu_custom_call" | custom-call | tf_op jit(solution)/shard_map/sum_over_head/pallas_call | solution.py:155
  1050.9 23.5 %all-reduce = (bf16[512,36]{0,1:T(8,128)(2,1)S(1)}, bf16[36,36]{1,0:T(8,128)(2,1)S(1)}, bf16[4,9]{1,0:T(4,128)(2,1)S(1)}, bf16[4,512]{1,0:T(4,128)(2,1)S(1)}, bf16[4,512]{1,0:T(4,128)(2,1)S(1)}) all-reduce(bf16[512,36]{0,1:T(8,128)(2,1)S(1)} %fusion.69, ...), channel_id=1, replica_groups=mesh['dp'=2,'stream'=4,'head'=4] {'dp','stream'}, use_global_device_ids=true, to_apply=%region_39.40 | all-reduce | flops 23860 | bytes 95440 | tf_op jit(solution)/shard_map/psum | solution.py:479
  (491 shorter events, 420.0 us)
Async XLA Ops:
  7.2 295.2 %all-gather.16.cloned.1.call-start = ((), (), s32[]{:S(2)}) async-start(), calls=%async_computation.13 | async-start | bytes 5242880 | tf_op jit(solution)/shard_map/all_gather | solution.py:376
  74.4 237.1 %all-gather.14.cloned.1.call-start = ((), (), s32[]{:S(2)}) async-start(), calls=%async_computation.12 | async-start | bytes 5242880 | tf_op jit(solution)/shard_map/all_gather | solution.py:376
  75.1 250.2 %all-gather.12.cloned.1.call-start = ((), (), s32[]{:S(2)}) async-start(), calls=%async_computation.11 | async-start | bytes 5242880 | tf_op jit(solution)/shard_map/all_gather | solution.py:376
  75.9 320.8 %all-gather.18.cloned.1.call-start = ((), (), s32[]{:S(2)}) async-start(), calls=%async_computation.14 | async-start | bytes 5242880 | tf_op jit(solution)/shard_map/all_gather | solution.py:376
  76.5 401.0 %all-gather.10.cloned.1.call-start = ((), (), s32[]{:S(2)}) async-start(), calls=%async_computation.5 | async-start | bytes 5242880 | tf_op jit(solution)/shard_map/all_gather | solution.py:342
  152.0 78.0 %collective-permute-start.13 = (bf16[2,256,2048]{2,1,0:T(8,128)(2,1)}, bf16[2,256,2048]{2,1,0:T(8,128)(2,1)}, u32[]{:S(2)}, u32[]{:S(2)}) collective-permute-start(bf16[2,256,2048]{2,1,0:T(8,128)(2,1)} %pad_maximum_fusion.7), channel_id=1, source_target_pairs={{0,8},{8,0},{4,12},{12,4},{1,9},{9,1},{5,13},{13,5},{2,10},{10,2},... | collective-permute-start | bytes 6291464 | tf_op jit(solution)/shard_map/ppermute | solution.py:46
  154.5 127.9 %collective-permute-start.4 = (bf16[2,2560,256]{2,1,0:T(8,128)(2,1)}, bf16[2,2560,256]{2,1,0:T(8,128)(2,1)}, u32[]{:S(2)}, u32[]{:S(2)}) collective-permute-start(bf16[2,2560,256]{2,1,0:T(8,128)(2,1)} %pad_maximum_fusion.6), channel_id=1, source_target_pairs={{0,8},{8,0},{4,12},{12,4},{1,9},{9,1},{5,13},{13,5},{2,10},{10,2},... | collective-permute-start | bytes 7864328 | tf_op jit(solution)/shard_map/ppermute | solution.py:46
  161.1 764.6 %reduce-scatter.6.cloned.1.call-start = ((), (), s32[]{:S(2)}) async-start(), calls=%async_computation.6 | async-start | bytes 5242880 | tf_op jit(solution)/shard_map/reduce_scatter | solution.py:411
  187.3 107.8 %collective-permute-start.2 = (bf16[4,3,256,512]{3,2,1,0:T(8,128)(2,1)S(1)}, bf16[4,3,256,512]{3,2,1,0:T(8,128)(2,1)}, u32[]{:S(2)}, u32[]{:S(2)}) collective-permute-start(bf16[4,3,256,512]{3,2,1,0:T(8,128)(2,1)S(1)} %pad_maximum_fusion.5.near_ref), channel_id=1, source_target_pairs={{0,4},{4,0},{8,12},{12,8},{1,5},{5,1},{9,13},{13,9},{2,6},{6,2},{1... | collective-permute-start | bytes 9437192 | tf_op jit(solution)/shard_map/ppermute | solution.py:50
  233.8 98.7 %collective-permute-start.14 = (bf16[4,256,2048]{2,1,0:T(8,128)(2,1)}, bf16[4,256,2048]{2,1,0:T(8,128)(2,1)}, u32[]{:S(2)}, u32[]{:S(2)}) collective-permute-start(bf16[4,256,2048]{2,1,0:T(8,128)(2,1)} %pad_maximum_fusion.3.near_ref), channel_id=1, source_target_pairs={{0,4},{4,0},{8,12},{12,8},{1,5},{5,1},{9,13},{13,9},{2,6},{6,2},{1... | collective-permute-start | bytes 12582920 | tf_op jit(solution)/shard_map/ppermute | solution.py:50
  287.0 126.9 %collective-permute-start.5 = (bf16[4,2560,256]{2,1,0:T(8,128)(2,1)}, bf16[4,2560,256]{2,1,0:T(8,128)(2,1)}, u32[]{:S(2)}, u32[]{:S(2)}) collective-permute-start(bf16[4,2560,256]{2,1,0:T(8,128)(2,1)} %pad_maximum_fusion.2.near_ref), channel_id=1, source_target_pairs={{0,4},{4,0},{8,12},{12,8},{1,5},{5,1},{9,13},{13,9},{2,6},{6,2},{1... | collective-permute-start | bytes 15728648 | tf_op jit(solution)/shard_map/ppermute | solution.py:50
  307.7 105.7 %collective-permute-start.10 = (bf16[2,512,512]{2,1,0:T(8,128)(2,1)S(1)}, bf16[2,512,512]{2,1,0:T(8,128)(2,1)S(1)}, u32[]{:S(2)}, u32[]{:S(2)}) collective-permute-start(bf16[2,512,512]{2,1,0:T(8,128)(2,1)S(1)} %bitcast.353), channel_id=1, source_target_pairs={{0,8},{4,12},{1,9},{5,13},{2,10},{6,14},{3,11},{7,15},{16,24},{20,... | collective-permute-start | bytes 3145736 | tf_op jit(solution)/shard_map/ppermute | solution.py:281
  311.1 171.7 %collective-permute-start.9 = (bf16[2,512,512]{2,1,0:T(8,128)(2,1)S(1)}, bf16[2,512,512]{2,1,0:T(8,128)(2,1)}, u32[]{:S(2)}, u32[]{:S(2)}) collective-permute-start(bf16[2,512,512]{2,1,0:T(8,128)(2,1)S(1)} %bitcast.354), channel_id=1, source_target_pairs={{0,4},{4,0},{8,12},{12,8},{1,5},{5,1},{9,13},{13,9},{2,6},{6,2},{1... | collective-permute-start | bytes 3145736 | tf_op jit(solution)/shard_map/ppermute | solution.py:50
  322.5 91.0 %collective-permute-start.7 = (bf16[2,512,512]{2,1,0:T(8,128)(2,1)}, bf16[2,512,512]{2,1,0:T(8,128)(2,1)}, u32[]{:S(2)}, u32[]{:S(2)}) collective-permute-start(bf16[2,512,512]{2,1,0:T(8,128)(2,1)} %bitcast.325), channel_id=1, source_target_pairs={{0,8},{4,12},{1,9},{5,13},{2,10},{6,14},{3,11},{7,15},{16,24},{20,... | collective-permute-start | bytes 3145736 | tf_op jit(solution)/shard_map/ppermute | solution.py:281
  332.5 150.4 %collective-permute-start.6 = (bf16[2,512,512]{2,1,0:T(8,128)(2,1)S(1)}, bf16[2,512,512]{2,1,0:T(8,128)(2,1)}, u32[]{:S(2)}, u32[]{:S(2)}) collective-permute-start(bf16[2,512,512]{2,1,0:T(8,128)(2,1)S(1)} %bitcast.327), channel_id=1, source_target_pairs={{0,4},{4,0},{8,12},{12,8},{1,5},{5,1},{9,13},{13,9},{2,6},{6,2},{1... | collective-permute-start | bytes 3145736 | tf_op jit(solution)/shard_map/ppermute | solution.py:50
  540.1 411.7 %reduce-scatter.8.cloned.1.call-start = ((), (), s32[]{:S(2)}) async-start(), calls=%async_computation.7 | async-start | bytes 5242880 | tf_op jit(solution)/shard_map/reduce_scatter | solution.py:411
  546.4 405.4 %reduce-scatter.14.cloned.1.call-start = ((), (), s32[]{:S(2)}) async-start(), calls=%async_computation.10 | async-start | bytes 5242880 | tf_op jit(solution)/shard_map/reduce_scatter | solution.py:411
  576.1 375.7 %reduce-scatter.12.cloned.1.call-start = ((), (), s32[]{:S(2)}) async-start(), calls=%async_computation.9 | async-start | bytes 5242880 | tf_op jit(solution)/shard_map/reduce_scatter | solution.py:411
  599.6 163.8 %collective-permute-start.27 = (bf16[4,256,2048]{2,1,0:T(8,128)(2,1)}, bf16[4,256,2048]{2,1,0:T(8,128)(2,1)}, u32[]{:S(2)}, u32[]{:S(2)}) collective-permute-start(bf16[4,256,2048]{2,1,0:T(8,128)(2,1)} %dynamic-slice_bitcast_fusion), channel_id=1, source_target_pairs={{0,4},{4,0},{8,12},{12,8},{1,5},{5,1},{9,13},{13,9},{2,6},{6,2},{1... | collective-permute-start | bytes 12582920 | tf_op jit(solution)/shard_map/ppermute | solution.py:50
  615.7 336.1 %reduce-scatter.10.cloned.1.call-start = ((), (), s32[]{:S(2)}) async-start(), calls=%async_computation.8 | async-start | bytes 5242880 | tf_op jit(solution)/shard_map/reduce_scatter | solution.py:411
  634.3 148.1 %collective-permute-start.24 = (bf16[4,256,2048]{2,1,0:T(8,128)(2,1)}, bf16[4,256,2048]{2,1,0:T(8,128)(2,1)}, u32[]{:S(2)}, u32[]{:S(2)}) collective-permute-start(bf16[4,256,2048]{2,1,0:T(8,128)(2,1)} %dynamic-slice_bitcast_fusion.1), channel_id=1, source_target_pairs={{0,4},{4,0},{8,12},{12,8},{1,5},{5,1},{9,13},{13,9},{2,6},{6,2},{1... | collective-permute-start | bytes 12582920 | tf_op jit(solution)/shard_map/ppermute | solution.py:50
  789.3 85.1 %collective-permute-start.25 = (bf16[2,256,2048]{2,1,0:T(8,128)(2,1)}, bf16[2,256,2048]{2,1,0:T(8,128)(2,1)}, u32[]{:S(2)}, u32[]{:S(2)}) collective-permute-start(bf16[2,256,2048]{2,1,0:T(8,128)(2,1)} %dynamic-slice_bitcast_fusion.3), channel_id=1, source_target_pairs={{0,16},{16,0},{1,17},{17,1},{2,18},{18,2},{3,19},{19,3},{4,20},{20... | collective-permute-start | bytes 6291464 | tf_op jit(solution)/shard_map/ppermute | solution.py:42
  800.2 118.8 %collective-permute-start.22 = (bf16[2,256,2048]{1,2,0:T(8,128)(2,1)}, bf16[2,256,2048]{1,2,0:T(8,128)(2,1)}, u32[]{:S(2)}, u32[]{:S(2)}) collective-permute-start(bf16[2,256,2048]{1,2,0:T(8,128)(2,1)} %bitcast.322), channel_id=1, source_target_pairs={{0,16},{16,0},{1,17},{17,1},{2,18},{18,2},{3,19},{19,3},{4,20},{20... | collective-permute-start | bytes 6291464 | tf_op jit(solution)/shard_map/ppermute | solution.py:42
  833.3 89.2 %collective-permute-start.29 = (bf16[256,2048]{0,1:T(8,128)(2,1)}, bf16[256,2048]{0,1:T(8,128)(2,1)S(1)}, u32[]{:S(2)}, u32[]{:S(2)}) collective-permute-start(bf16[256,2048]{0,1:T(8,128)(2,1)} %dynamic-slice_bitcast_fusion.4), channel_id=1, source_target_pairs={{0,8},{8,0},{4,12},{12,4},{1,9},{9,1},{5,13},{13,5},{2,10},{10,2},... | collective-permute-start | bytes 3145736 | tf_op jit(solution)/shard_map/ppermute | solution.py:46
  (140 other events, 2262.7 us)
Sparse Core Ops, SparseCore 0:
  74.5 79.5 all-gather.15
  155.7 79.2 all-gather.13
  236.6 79.2 all-gather.11
  317.4 79.2 all-gather.17
  398.1 79.2 all-gather.9
  540.2 77.9 reduce-scatter.5
  620.6 77.2 reduce-scatter.7
  700.2 77.2 reduce-scatter.13
  779.9 77.2 reduce-scatter.11
  859.3 77.2 reduce-scatter.9

commit v3 on v2

--- a/solution.py
+++ b/solution.py
@@ -67,11 +67,11 @@
         out_ref[...] = beside_ref[0]
 
 
-def gather_weight(shard, axis):
+def gather_weight(shard, near_x, axis):
     if not paired():
         return lax.all_gather(shard, ("dp", "stream"), axis=axis, tiled=True)
     place = lax.axis_index("dp") * 4 + lax.axis_index("stream")
-    row = jnp.stack([shard, over_x(shard)])
+    row = jnp.stack([shard, near_x])
     near = jnp.concatenate([row, over_y(row)])
     beside = over_core(near)
     flips = jnp.array([0, 4, 2, 6, 1, 5, 3, 7], jnp.int32)
@@ -96,12 +96,11 @@
     )(place ^ flips, near, beside)
 
 
-def scatter_sum(partial):
+def scatter_parts(partial):
     if not paired():
-        return lax.psum_scatter(
-            partial, ("dp", "stream"), scatter_dimension=0, tiled=True
-        ).astype(F32)
-    rows, columns = partial.shape
+        whole = lax.psum_scatter(partial, ("dp", "stream"), scatter_dimension=1, tiled=True)
+        return whole, jnp.zeros_like(whole)
+    count, rows, columns = partial.shape
     stream = lax.axis_index("stream")
     x, y, core = lax.axis_index("dp"), stream // 2, stream % 2
 
@@ -109,13 +108,36 @@
         return lax.dynamic_index_in_dim(a, index, axis, keepdims=False)
 
     def add(a, b):
-        return a.astype(F32) + b.astype(F32)
-
-    split = partial.reshape(4, 2, rows // 8, columns)
-    chip = add(pick(split, core, 1), over_core(pick(split, 1 - core, 1))).astype(BF16)
-    chip = chip.reshape(2, 2, rows // 8, columns)
-    line = add(pick(chip, x, 0), over_x(pick(chip, 1 - x, 0))).astype(BF16)
-    return add(pick(line, y, 0), over_y(pick(line, 1 - y, 0)))
+        return (a.astype(F32) + b.astype(F32)).astype(BF16)
+
+    split = partial.reshape(count, 4, 2, rows // 8, columns)
+    chip = add(pick(split, core, 2), over_core(pick(split, 1 - core, 2)))
+    chip = chip.reshape(count, 2, 2, rows // 8, columns)
+    line = add(pick(chip, x, 1), over_x(pick(chip, 1 - x, 1)))
+    return pick(line, y, 1), over_y(pick(line, 1 - y, 1))
+
+
+def add_kernel(turned, a_ref, b_ref, out_ref):
+    total = a_ref[...].astype(F32) + b_ref[...].astype(F32)
+    out_ref[...] = total.T if turned else total
+
+
+def add_terms(a, b, turned):
+    rows, columns = a.shape
+    block = min(512, columns)
+    return pl.pallas_call(
+        functools.partial(add_kernel, turned),
+        grid=(columns // block,),
+        in_specs=[pl.BlockSpec((rows, block), lambda i: (0, i))] * 2,
+        out_specs=pl.BlockSpec((block, rows), lambda i: (i, 0))
+        if turned
+        else pl.BlockSpec((rows, block), lambda i: (0, i)),
+        out_shape=jax.ShapeDtypeStruct((columns, rows) if turned else (rows, columns), F32),
+        cost_estimate=pl.CostEstimate(
+            flops=rows * columns, bytes_accessed=8 * rows * columns, transcendentals=0
+        ),
+        name="add_terms",
+    )(a, b)
 
 
 def head_sum_kernel(members, x_ref, out_ref, slots, send_sem, recv_sem):
@@ -291,6 +313,175 @@
     )
 
 
+def columns_of(pieces, rows):
+    lane = lax.broadcasted_iota(jnp.int32, (rows, 128), 1)
+    out = jnp.zeros((rows, 128), F32)
+    for index, piece in enumerate(pieces):
+        out = jnp.where(lane == index, piece, out)
+    return out
+
+
+def row_sum(a):
+    return jnp.sum(a, axis=1, keepdims=True)
+
+
+def early_kernel(streams_ref, stats_ref, cot_ref, history_ref, out_ref):
+    stats = stats_ref[...]
+    cot = cot_ref[...].astype(F32)
+    plain, crossed, direct = [], [], []
+    layers = [history_ref[j].astype(F32) for j in range(HIST)]
+    for layer in layers:
+        plain.append(row_sum(layer))
+        direct.append(row_sum(cot * layer))
+    for s in range(4):
+        centered = (streams_ref[s] - stats[:, s : s + 1]) * stats[:, 4 + s : 5 + s]
+        for layer in layers:
+            crossed.append(row_sum(centered * layer))
+    out_ref[...] = columns_of(crossed + plain + direct, stats.shape[0])
+
+
+def early_sums(streams, stats, cot, history):
+    _, tokens, feats = streams.shape
+    block = min(128, tokens)
+    return pl.pallas_call(
+        early_kernel,
+        grid=(tokens // block,),
+        in_specs=[
+            pl.BlockSpec((4, block, feats), lambda i: (0, i, 0)),
+            pl.BlockSpec((block, 8), lambda i: (i, 0)),
+            pl.BlockSpec((block, feats), lambda i: (i, 0)),
+            pl.BlockSpec((HIST, block, feats), lambda i: (0, i, 0)),
+        ],
+        out_specs=pl.BlockSpec((block, 128), lambda i: (i, 0)),
+        out_shape=jax.ShapeDtypeStruct((tokens, 128), F32),
+        compiler_params=pltpu.CompilerParams(vmem_limit_bytes=40 * 1024 * 1024),
+        cost_estimate=pl.CostEstimate(
+            flops=110 * tokens * feats, bytes_accessed=36 * tokens * feats, transcendentals=0
+        ),
+        name="early_sums",
+    )(streams, stats, cot, history)
+
+
+def sums_kernel(g0, g1, g2, g3, streams_ref, stats_ref, gain_ref, history_ref, out_ref, edge_ref):
+    stats = stats_ref[...]
+    rows = stats.shape[0]
+
+    @pl.when(pl.program_id(0) == 0)
+    def _():
+        edge_ref[...] = jnp.zeros_like(edge_ref)
+
+    firsts, seconds, dots = [], [], []
+    for s, g_ref in enumerate((g0, g1, g2, g3)):
+        g = g_ref[...].astype(F32)
+        centered = (streams_ref[s] - stats[:, s : s + 1]) * stats[:, 4 + s : 5 + s]
+        edge_ref[s : s + 1] += jnp.sum(g * centered, axis=0, keepdims=True)
+        edge_ref[4 + s : 5 + s] += jnp.sum(g, axis=0, keepdims=True)
+        scaled = g * gain_ref[s : s + 1]
+        firsts.append(row_sum(scaled))
+        seconds.append(row_sum(scaled * centered))
+        for j in range(HIST):
+            dots.append(row_sum(scaled * history_ref[j].astype(F32)))
+    out_ref[...] = columns_of(dots + firsts + seconds, rows)
+
+
+def gradient_sums(grads, streams, stats, gain, history):
+    _, tokens, feats = streams.shape
+    block = min(128, tokens)
+    wide = pl.BlockSpec((block, feats), lambda i: (i, 0))
+    sums, edges = pl.pallas_call(
+        sums_kernel,
+        grid=(tokens // block,),
+        in_specs=[wide] * 4
+        + [
+            pl.BlockSpec((4, block, feats), lambda i: (0, i, 0)),
+            pl.BlockSpec((block, 8), lambda i: (i, 0)),
+            pl.BlockSpec((4, feats), lambda i: (0, 0)),
+            pl.BlockSpec((HIST, block, feats), lambda i: (0, i, 0)),
+        ],
+        out_specs=[
+            pl.BlockSpec((block, 128), lambda i: (i, 0)),
+            pl.BlockSpec((8, feats), lambda i: (0, 0)),
+        ],
+        out_shape=[
+            jax.ShapeDtypeStruct((tokens, 128), F32),
+            jax.ShapeDtypeStruct((8, feats), F32),
+        ],
+        compiler_params=pltpu.CompilerParams(vmem_limit_bytes=40 * 1024 * 1024),
+        cost_estimate=pl.CostEstimate(
+            flops=110 * tokens * feats, bytes_accessed=42 * tokens * feats, transcendentals=0
+        ),
+        name="gradient_sums",
+    )(*grads, streams, stats, gain, history)
+    return sums[:, : 4 * HIST + 8], edges
+
+
+def mix_gradient(sums, early, stats, model_width):
+    n = 4 * HIST
+    first, second = sums[n : n + 4] / model_width, sums[n + 4 : n + 8] / model_width
+    spread = lambda a: jnp.repeat(a, HIST, axis=0)
+    crossed, plain, direct = early[:n], early[n : n + HIST], early[n + HIST : n + 2 * HIST]
+    d_mix = spread(stats.T[4:]) * (
+        sums[:n] - spread(first) * jnp.tile(plain, (4, 1)) - spread(second) * crossed
+    )
+    d_mix = d_mix + jnp.concatenate([jnp.zeros_like(d_mix[: 3 * HIST]), direct])
+    return d_mix, jnp.concatenate([first, second])
+
+
+def history_kernel(
+    g0, g1, g2, g3, streams_ref, stats_ref, gain_ref, cot_ref, current_ref, columns_ref, d_ref, w_ref, out_ref
+):
+    n = 4 * HIST
+    stats, columns = stats_ref[...], columns_ref[...]
+    column = lambda i: columns[:, i : i + 1]
+    d_streams = []
+    for s, g_ref in enumerate((g0, g1, g2, g3)):
+        inverse = stats[:, 4 + s : 5 + s]
+        centered = (streams_ref[s] - stats[:, s : s + 1]) * inverse
+        scaled = g_ref[...].astype(F32) * gain_ref[s : s + 1]
+        d_streams.append(inverse * (scaled - column(n + s) - centered * column(n + 4 + s)))
+    d_streams[3] = d_streams[3] + cot_ref[...].astype(F32)
+    for j in range(HIST):
+        total = column(j) * d_streams[0]
+        for s in range(1, 4):
+            total = total + column(s * HIST + j) * d_streams[s]
+        if j == HIST - 1:
+            total = total + jnp.dot(
+                d_ref[...], w_ref[...], precision=HIGHEST, preferred_element_type=F32
+            )
+            total = total - current_ref[...].astype(F32) * column(n + 9)
+        out_ref[j] = total
+
+
+def history_gradient(grads, streams, stats, gain, cot, current, columns, d_scaled, w_rows):
+    _, tokens, feats = streams.shape
+    block = min(128, tokens)
+    wide = pl.BlockSpec((block, feats), lambda i: (i, 0))
+    narrow = lambda a: pl.BlockSpec((block, a.shape[1]), lambda i: (i, 0))
+    fixed = lambda a: pl.BlockSpec(a.shape, lambda i: (0, 0))
+    return pl.pallas_call(
+        history_kernel,
+        grid=(tokens // block,),
+        in_specs=[wide] * 4
+        + [
+            pl.BlockSpec((4, block, feats), lambda i: (0, i, 0)),
+            narrow(stats),
+            fixed(gain),
+            wide,
+            wide,
+            narrow(columns),
+            narrow(d_scaled),
+            fixed(w_rows),
+        ],
+        out_specs=pl.BlockSpec((HIST, block, feats), lambda i: (0, i, 0)),
+        out_shape=jax.ShapeDtypeStruct((HIST, tokens, feats), F32),
+        compiler_params=pltpu.CompilerParams(vmem_limit_bytes=40 * 1024 * 1024),
+        cost_estimate=pl.CostEstimate(
+            flops=110 * tokens * feats, bytes_accessed=64 * tokens * feats, transcendentals=0
+        ),
+        name="history_gradient",
+    )(*grads, streams, stats, gain, cot, current, columns, d_scaled, w_rows)
+
+
 def shards(
     history,
     seq_lens,
@@ -340,10 +531,8 @@
 
     cot_rows = cotangent.reshape(tokens, feats).astype(F32) * valid
     out_full = lax.all_gather(cot_rows.astype(BF16), "head", axis=1, tiled=True)
-    wq, wk, wv = gather_weight(w_qkv, 1)
-    both_full = gather_weight(jnp.concatenate([w_attn_out, w_down]), 1)
-    w_out_full, down_full = both_full[:feats], both_full[feats:]
-    up_full = gather_weight(w_up, 0)
+    w_both = jnp.concatenate([w_attn_out, w_down])
+    near_x = tuple(over_x(w) if paired() else w[:1] for w in (w_qkv, w_both, w_up))
 
     history = history.reshape(HIST, tokens, feats)
     current = history[HIST - 1]
@@ -367,10 +556,21 @@
         jnp.concatenate([jnp.sum(streams, axis=2), jnp.sum(streams * streams, axis=2)]), 1
     )
     stat_sum, stat_square = stats[:4], stats[4:]
+    stat_sum, stat_square, out_full, near_x = lax.optimization_barrier(
+        (stat_sum, stat_square, out_full, near_x)
+    )
     row_means = (stat_sum / model_width)[:, :, None]
     inv_std = lax.rsqrt(stat_square[:, :, None] / model_width - row_means * row_means + EPSILON)
     centered = (streams - row_means) * inv_std
+    row_stats = jnp.concatenate([row_means[..., 0], inv_std[..., 0]]).T
+    early = early_sums(streams, row_stats, cot_rows.astype(BF16), history)
+    early = head_sum(early[:, : 6 * HIST].T, 2)
     normed = (centered * ln_gain[:, None, :] + ln_bias[:, None, :]).astype(BF16)
+
+    wq, wk, wv = gather_weight(w_qkv, near_x[0], 1)
+    both_full = gather_weight(w_both, near_x[1], 1)
+    w_out_full, down_full = both_full[:feats], both_full[feats:]
+    up_full = gather_weight(w_up, near_x[2], 0)
 
     def all_features(stream):
         return lax.all_gather(normed[stream], "head", axis=1, tiled=True)
@@ -420,74 +620,64 @@
     block_out = (valid * (streams[3] + branch)).astype(BF16)
 
     product = lambda a, b: dot_tn(a, b).astype(BF16)
-    grad_up = scatter_sum(product(up_in, d_up))
-    grad_down = scatter_sum(product(out_full, gated_up)).T
-    grads = scatter_sum(
-        jnp.concatenate(
+    up_terms = scatter_parts(product(up_in, d_up)[None])
+    down_terms = scatter_parts(product(out_full, gated_up)[None])
+    grad_up = add_terms(up_terms[0][0], up_terms[1][0], False)
+    grad_down = add_terms(down_terms[0][0], down_terms[1][0], True)
+    terms = scatter_parts(
+        jnp.stack(
             [
                 product(q_in, d_query_pre),
                 product(k_in, d_key_pre),
                 product(v_in, d_value_pre),
                 product(out_full, attended),
-            ],
-            axis=1,
+            ]
         )
     )
-    grad_qkv = jnp.stack([grads[:, i * feats : (i + 1) * feats] for i in range(3)])
-    grad_attn_out = grads[:, 3 * feats :].T
-
-    stream_grad = jnp.stack([g_query, g_key, g_value, g_up])
-    d_centered = stream_grad * ln_gain[:, None, :]
-    sums = head_sum(
-        jnp.concatenate([jnp.sum(d_centered, axis=2), jnp.sum(d_centered * centered, axis=2)]), 2
-    )
-    sum_grad, sum_cross = sums[:4], sums[4:]
-    d_streams = inv_std * (
-        d_centered
-        - sum_grad[:, :, None] / model_width
-        - centered * sum_cross[:, :, None] / model_width
-    )
-    grad_gain = jnp.sum(stream_grad * centered, axis=1)
-    grad_shift = jnp.sum(stream_grad, axis=1)
-    d_streams = jnp.concatenate([d_streams[:3], (d_streams[3] + cot_rows)[None]], axis=0)
-    layer_grads = []
-    d_mix_parts = []
-    for layer in range(HIST):
-        layer_f = history[layer].astype(F32)
-        layer_grads.append(
-            jnp.sum(jnp.transpose(weights_four[:, :, layer])[:, :, None] * d_streams, axis=0)
-        )
-        d_mix_parts.append(jnp.sum(d_streams * layer_f[None], axis=2))
-    d_mix_local = jnp.transpose(jnp.stack(d_mix_parts, axis=-1), (1, 0, 2)).reshape(
-        tokens, 4 * HIST
-    )
-    d_mix = head_sum(d_mix_local.T, 3).T
-    grad_bias = jnp.sum(d_mix, axis=0)
-    grad_w2 = jnp.dot(mix_hidden.T, d_mix, precision=HIGHEST)
-    d_hidden = jnp.dot(d_mix, w_mix_out_f.T, precision=HIGHEST)
-    _, gelu_mix_back = jax.vjp(gelu_exact, mix_pre)
-    d_pre = gelu_mix_back(d_hidden)[0]
-    normed_in = current_f * rms_scale
-    grad_w1 = jnp.dot(normed_in.T, d_pre, precision=HIGHEST)
-    d_normed_in = jnp.dot(d_pre, w_mix_in_f.T, precision=HIGHEST)
-    cross = jnp.sum(d_pre * mix_pre, axis=1, keepdims=True)
-    layer_grads[HIST - 1] = layer_grads[HIST - 1] + rms_scale * (
-        d_normed_in - normed_in * cross / model_width
-    )
-    history_grad = jnp.stack(layer_grads).reshape(HIST, micro, quarter, feats)
-    small = [
-        lax.psum(a.astype(BF16), ("dp", "stream")).astype(F32)
-        for a in (grad_w1, grad_w2, grad_bias, grad_gain, grad_shift)
-    ]
+    grad_qkv = terms[0][:3].astype(F32) + terms[1][:3].astype(F32)
+    grad_attn_out = add_terms(terms[0][3], terms[1][3], True)
+
+    grads = (g_query, g_key, g_value, g_up)
+    sums, gain_shift = gradient_sums(grads, streams, row_stats, ln_gain, history)
+    sums = head_sum(sums.T, 3)
+    d_mix, coefs = mix_gradient(sums, early, row_stats, model_width)
+    d_hidden = jnp.dot(w_mix_out_f, d_mix, precision=HIGHEST)
+    mix_pre_t = mix_pre.T
+    below_mix = 0.5 * (1.0 + lax.erf(mix_pre_t * 0.5**0.5))
+    density = jnp.exp(-0.5 * mix_pre_t * mix_pre_t) * (2.0 * jnp.pi) ** -0.5
+    d_pre = d_hidden * (below_mix + mix_pre_t * density)
+    cross = jnp.sum(d_pre * mix_pre_t, axis=0, keepdims=True)
+    rms_row = rms_scale.T
+    grad_w1 = jnp.dot(d_pre * rms_row, current_f, precision=HIGHEST)
+    grad_w2 = jnp.dot(mix_hidden.T, d_mix.T, precision=HIGHEST)
+    grad_bias = jnp.sum(d_mix, axis=1)
+    wide = lambda a: jnp.pad(a, ((0, 0), (0, feats - a.shape[1])))
+    small = jnp.concatenate([grad_w1, gain_shift, wide(grad_w2), wide(grad_bias[None])])
+    small = lax.psum(small.astype(BF16), ("dp", "stream")).astype(F32)
+    n = 4 * HIST
+    columns = jnp.concatenate(
+        [mix_weights.T, coefs, rms_row, rms_row * rms_row * cross / model_width]
+    ).T
+    history_grad = history_gradient(
+        grads,
+        streams,
+        row_stats,
+        ln_gain,
+        cot_rows.astype(BF16),
+        current,
+        columns,
+        (d_pre * rms_row).T,
+        w_mix_in_f.T,
+    ).reshape(HIST, micro, quarter, feats)
     return (
         block_out.reshape(micro, quarter, feats),
         mix_weights.reshape(micro, quarter, 4 * HIST),
         history_grad,
-        small[0],
-        small[1],
-        small[2].reshape(mix_bias.shape),
-        small[3],
-        small[4],
+        small[:n].T,
+        small[n + 8 : 2 * n + 8, :n],
+        small[2 * n + 8, :n].reshape(mix_bias.shape),
+        small[n : n + 4],
+        small[n + 4 : n + 8],
         grad_qkv,
         grad_attn_out,
         grad_up,

time: 1110 us -> 1020 us (0.919)
  Pallas kernels: 132 us -> 241 us
  local copies, waits for them, and re-layouts: 179 us -> 96.9 us
  other arithmetic: 150 us -> 100 us
  waiting for transfers between devices: 421 us -> 385 us
  blocking collectives: 23.5 us -> 0 us
  matrix products: 155 us -> 142 us
    pallas_call x0 -> x6, Pallas kernels: none -> 58.8 us  [the longest x1 17.1 us: history_gradient(): pl.pallas_call(history_kernel, grid=(tokens // block,), in_specs=[wide] *...]
    ppermute x6, waiting for transfers between devices: 169 us -> 111 us  [over_x(): return lax.ppermute(a, 'dp', SWAP_X)]
    pallas_call x4, Pallas kernels: 51.2 us -> 101 us  [head_sum(): pl.pallas_call(functools.partial(head_sum_kernel, members), out_shape=jax...]
    unnamed x264 -> x202, local copies, waits for them, and re-layouts: 89.6 us -> 47 us
    reduce_sum x5 -> x1, other arithmetic: 35.7 us -> 1.45 us  [shards(): grad_bias = jnp.sum(d_mix, axis=1)]
    all_gather x1, waiting for transfers between devices: 38.3 us -> 12.4 us  [shards(): out_full = lax.all_gather(cot_rows.astype(BF16), 'head', axis=1, tiled=True)]
    psum x1 -> x0, blocking collectives: 23.5 us -> none  [shards(): lax.psum(a.astype(BF16), ('dp', 'stream')).astype(F32)]
    dynamic_slice x3 -> x1, local copies, waits for them, and re-layouts: 24.4 us -> 2.76 us  [pick(): return lax.dynamic_index_in_dim(a, index, axis, keepdims=False)]
  transfers between devices with their start and end apart: 40 -> 41, of which waited for: 13 -> 12; matrix products, arithmetic and copies ran while one was open for 30% -> 27% of each run, Pallas kernels for 3% -> 20%
where the time goes in v3:
time: 1020 us; the launch traced here: 1010 us
  waiting for transfers between devices  385 us (38%)
  Pallas kernels  241 us (24%)
  matrix products  142 us (14%)
  other arithmetic  100 us (10%)
  local copies, waits for them, and re-layouts  96.9 us (10%)
  starting transfers between devices  25.8 us (3%)
  between operations  15.8 us (2%)
    ppermute x6, waiting for transfers between devices, over_y(): return lax.ppermute(a, 'stream', SWAP_Y)  131 us
    ppermute x6, waiting for transfers between devices, over_x(): return lax.ppermute(a, 'dp', SWAP_X)  111 us
    pallas_call x4, Pallas kernels, head_sum(): pl.pallas_call(functools.partial(head_sum_kernel, members), out_shape=jax...  101 us
    all_gather x4, waiting for transfers between devices, all_features(): return lax.all_gather(normed[stream], 'head', axis=1, tiled=True)  60.9 us
    dot_general x6, matrix products, dot(): return jnp.dot(a, b, preferred_element_type=F32)  53.9 us
    dot_general x6, matrix products, dot_nt(): lax.dot_general(a, b, (((1,), (1,)), ((), ())), preferred_element_type=F32)  47.2 us
    unnamed x202, local copies, waits for them, and re-layouts  47 us
    ppermute x2, waiting for transfers between devices, reduce_rows(): lax.ppermute(across, 'stream', [(2, 0), (3, 1)])  45.1 us
  transfers between devices with their start and end apart: 41, of which 12 were waited for; matrix products, arithmetic and copies ran while one was open for 27% of the time, Pallas kernels for 20%

profile of v3, /device:TPU:8, one launch (start us, length us, event | category | flops | bytes accessed | tf_op | source)
XLA Modules:
  0.0 1007.1 jit_solution(11115747669504887187)
XLA Ops:
  29.7 37.3 %sum_over_head.4 = f32[37,1024]{1,0:T(8,128)} custom-call(f32[37,1024]{1,0:T(8,128)} %pad_maximum_fusion.7.x_ref), custom_call_target="tpu_custom_call" | custom-call | tf_op jit(solution)/shard_map/sum_over_head/pallas_call | solution.py:177
  85.7 11.3 %sum_over_head.5 = f32[8,1024]{1,0:T(8,128)} custom-call(f32[8,1024]{1,0:T(8,128)} %pad_maximum_fusion.8.x_ref), custom_call_target="tpu_custom_call" | custom-call | tf_op jit(solution)/shard_map/sum_over_head/pallas_call | solution.py:177
  97.8 12.4 %all-gather.10.cloned.1.call-done = bf16[1024,2048]{1,0:T(8,128)(2,1)} async-done(((bf16[1024,512]{1,0:T(8,128)(2,1)}), bf16[1024,2048]{1,0:T(8,128)(2,1)}) %all-gather.10.cloned.1.call-update) | async-done | bytes 4194320 | tf_op jit(solution)/shard_map/all_gather | solution.py:533
  124.4 45.1 %collective-permute-done.13 = bf16[2,256,2048]{2,1,0:T(8,128)(2,1)} collective-permute-done((bf16[2,256,2048]{2,1,0:T(8,128)(2,1)}, bf16[2,256,2048]{2,1,0:T(8,128)(2,1)}, u32[]{:S(2)}, u32[]{:S(2)}) %collective-permute-start.13) | collective-permute-done | bytes 2097184 | tf_op jit(solution)/shard_map/ppermute | solution.py:46
  173.1 51.6 %collective-permute-done.5 = bf16[2,2560,256]{2,1,0:T(8,128)(2,1)S(1)} collective-permute-done((bf16[2,2560,256]{2,1,0:T(8,128)(2,1)S(1)}, bf16[2,2560,256]{2,1,0:T(8,128)(2,1)S(1)}, u32[]{:S(2)}, u32[]{:S(2)}) %collective-permute-start.5) | collective-permute-done | bytes 2621472 | tf_op jit(solution)/shard_map/ppermute | solution.py:46
  232.1 34.8 %collective-permute-done.3 = bf16[2,3,256,512]{3,2,1,0:T(8,128)(2,1)} collective-permute-done((bf16[2,3,256,512]{3,2,1,0:T(8,128)(2,1)S(1)}, bf16[2,3,256,512]{3,2,1,0:T(8,128)(2,1)}, u32[]{:S(2)}, u32[]{:S(2)}) %collective-permute-start.3) | collective-permute-done | bytes 1572896 | tf_op jit(solution)/shard_map/ppermute | solution.py:46
  279.3 17.2 %fusion.3 = (f32[1024,2048]{1,0:T(8,128)}, bf16[1024,2048]{1,0:T(8,128)(2,1)}) fusion(bf16[2048,2048]{1,0:T(8,128)(2,1)} %weight_in_order.5, bf16[1,1024,2048]{2,1,0:T(8,128)(2,1)} %all-gather.18.cloned.1.call-done), kind=kOutput, calls=%fused_computation.4 | convolution fusion | flops 8610906112 | bytes 25165824 | tf_op jit(solution)/shard_map/dot_general | solution.py:26
  296.5 12.3 %weight_in_order.4 = bf16[2560,2048]{1,0:T(8,128)(2,1)} custom-call(s32[8]{0:T(128)S(1)} %broadcast_xor_fusion.order_ref, bf16[4,2560,256]{2,1,0:T(8,128)(2,1)} %pad_maximum_fusion.1.near_ref, bf16[4,2560,256]{2,1,0:T(8,128)(2,1)} %collective-permute-done.6.beside_ref), custom_call_target="tpu_custom_call" | custom-call | bytes 20971520 | tf_op jit(solution)/shard_map/weight_in_order/pallas_call | solution.py:81
  308.8 14.8 %multiply_convert_fusion = bf16[1024,2048]{1,0:T(8,128)(2,1)} fusion(f32[1024,2048]{1,0:T(8,128)} %get-tuple-element.49, bf16[1024,2048]{1,0:T(8,128)(2,1)S(1)} %copy-done.81, bf16[2560,2048]{1,0:T(8,128)(2,1)} %weight_in_order.4), kind=kOutput, calls=%fused_computation.12 | convolution fusion | flops 8594128896 | bytes 25165824 | tf_op jit(solution)/shard_map/dot_general | solution.py:30
  323.6 12.0 %convolution_convert_fusion.2 = bf16[1024,2048]{1,0:T(8,128)(2,1)} fusion(bf16[1024,2048]{1,0:T(8,128)(2,1)} %multiply_convert_fusion, bf16[2048,2048]{1,0:T(8,128)(2,1)S(1)} %bitcast.310), kind=kOutput, calls=%fused_computation.50 | convolution fusion | flops 8592031744 | bytes 16777216 | tf_op jit(solution)/shard_map/dot_general | solution.py:30
  380.5 60.9 %all-gather.12.cloned.1.call-done = bf16[1,1024,2048]{2,1,0:T(8,128)(2,1)} async-done(((bf16[1,1024,512]{2,1,0:T(8,128)(2,1)}), bf16[1,1024,2048]{2,1,0:T(8,128)(2,1)}) %all-gather.12.cloned.1.call-update) | async-done | bytes 4194320 | tf_op jit(solution)/shard_map/all_gather | solution.py:576
  463.7 44.9 %attention_both_ways.1 = (bf16[2,512,512]{2,1,0:T(8,128)(2,1)S(1)}, bf16[2,512,512]{2,1,0:T(8,128)(2,1)S(1)}, bf16[2,512,512]{2,1,0:T(8,128)(2,1)S(1)}, bf16[2,5...) custom-call(s32[4]{0:T(128)S(1)} %iota_xor_fusion.place_ref, ...), custom_call_target="tpu_custom_call" | custom-call | flops 12884901888 | bytes 20971520 | tf_op jit(solution)/shard_map/attention_both_ways/pallas_call | solution.py:277
  534.1 26.0 %collective-permute-done.20 = bf16[2,512,512]{2,1,0:T(8,128)(2,1)S(1)} collective-permute-done((bf16[2,512,512]{2,1,0:T(8,128)(2,1)}, bf16[2,512,512]{2,1,0:T(8,128)(2,1)S(1)}, u32[]{:S(2)}, u32[]{:S(2)}) %collective-permute-start.20) | collective-permute-done | bytes 1048608 | tf_op jit(solution)/shard_map/ppermute | solution.py:312
  569.1 12.5 %convolution_convert_fusion = bf16[2048,2048]{1,0:T(8,128)(2,1)S(1)} fusion(bf16[1024,2048]{1,0:T(8,128)(2,1)} %all-gather.10.cloned.1.call-done, bf16[1024,2048]{1,0:T(8,128)(2,1)} %get-tuple-element.39), kind=kOutput, calls=%fused_computation.19 | convolution fusion | flops 8594128896 | bytes 16777216 | tf_op jit(solution)/shard_map/dot_general | solution.py:34
  612.9 19.1 %collective-permute-done.17 = bf16[2,512,512]{2,1,0:T(8,128)(2,1)S(1)} collective-permute-done((bf16[2,512,512]{2,1,0:T(8,128)(2,1)S(1)}, bf16[2,512,512]{2,1,0:T(8,128)(2,1)S(1)}, u32[]{:S(2)}, u32[]{:S(2)}) %collective-permute-start.17) | collective-permute-done | bytes 1048608 | tf_op jit(solution)/shard_map/ppermute | solution.py:312
  684.4 29.5 %collective-permute-done.28 = bf16[1,2,256,2048]{3,2,1,0:T(8,128)(2,1)} collective-permute-done((bf16[1,2,256,2048]{3,2,1,0:T(8,128)(2,1)}, bf16[1,2,256,2048]{3,2,1,0:T(8,128)(2,1)}, u32[]{:S(2)}, u32[]{:S(2)}) %collective-permute-start.28) | collective-permute-done | bytes 2097184 | tf_op jit(solution)/shard_map/ppermute | solution.py:42
  718.4 40.4 %collective-permute-done.25 = bf16[1,2,256,2048]{3,2,1,0:T(8,128)(2,1)} collective-permute-done((bf16[1,2,256,2048]{3,2,1,0:T(8,128)(2,1)}, bf16[1,2,256,2048]{3,2,1,0:T(8,128)(2,1)}, u32[]{:S(2)}, u32[]{:S(2)}) %collective-permute-start.25) | collective-permute-done | bytes 2097184 | tf_op jit(solution)/shard_map/ppermute | solution.py:42
  762.8 40.6 %collective-permute-done.22 = bf16[4,2,256,512]{3,2,0,1:T(8,128)(2,1)S(1)} collective-permute-done((bf16[4,2,256,512]{3,2,0,1:T(8,128)(2,1)}, bf16[4,2,256,512]{3,2,0,1:T(8,128)(2,1)S(1)}, u32[]{:S(2)}, u32[]{:S(2)}) %collective-permute-start.22) | collective-permute-done | bytes 2097184 | tf_op jit(solution)/shard_map/ppermute | solution.py:42
  811.0 16.0 %early_sums.1 = f32[1024,128]{1,0:T(8,128)S(1)} custom-call(f32[4,1024,512]{2,1,0:T(8,128)S(1)} %copy-done.1, f32[1024,8]{1,0:T(8,128)S(1)} %bitcast.288, bf16[1024,512]{1,0:T(8,128)(2,1)S(1)} %copy-done.10, bf16[9,1024,512]{2,1,0:T(8,128)(2,1)} %bitcast.298), custom_call_target="tpu_custom_call" | custom-call | flops 57671680 | bytes 18874368 | tf_op jit(solution)/shard_map/early_sums/pallas_call | solution.py:346
  827.8 31.2 %sum_over_head.7 = f32[54,1024]{1,0:T(8,128)} custom-call(f32[54,1024]{1,0:T(8,128)} %bitcast.334), custom_call_target="tpu_custom_call" | custom-call | tf_op jit(solution)/shard_map/sum_over_head/pallas_call | solution.py:177
  890.6 15.7 %gradient_sums.1 = (f32[1024,128]{1,0:T(8,128)S(1)}, f32[8,512]{1,0:T(8,128)S(1)}) custom-call(f32[1024,512]{1,0:T(8,128)S(1)} %copy-done.4, f32[1024,512]{1,0:T(8,128)S(1)} %convert_element_type.421.g1, f32[1024,512]{1,0:T(8,128)S(1)} %copy-done.6, f32[1024,512]{1,0:T(8,128)S(1)} %convert_element_type.434.g3, ...), custom_call_target="tpu_custom_call" | custom-call | flops 57671680 | bytes 22020096 | tf_op jit(solution)/shard_map/gradient_sums/pallas_call | solution.py:391
  909.0 21.1 %sum_over_head.6 = f32[44,1024]{1,0:T(8,128)} custom-call(f32[44,1024]{1,0:T(8,128)} %slice_bitcast_fusion.10.x_ref), custom_call_target="tpu_custom_call" | custom-call | tf_op jit(solution)/shard_map/sum_over_head/pallas_call | solution.py:177
  957.6 17.1 %history_gradient.1 = f32[9,1024,512]{2,1,0:T(8,128)} custom-call(f32[1024,512]{1,0:T(8,128)S(1)} %copy-done.5, f32[1024,512]{1,0:T(8,128)S(1)} %copy-done.9, f32[1024,512]{1,0:T(8,128)S(1)} %copy-done.7, f32[1024,512]{1,0:T(8,128)S(1)} %convert_element_type.434.g3, f32[4,1024,512]{2,1,0:T(8,128)} %get-tuple-element.92.streams_ref, f32[1024,8]{1,0:T(8,128)S(1)} %bitcast.290, ...), custom_call_target="tpu_custom_call" | custom-call | flops 57671680 | bytes 33554432 | tf_op jit(solution)/shard_map/history_gradient/pallas_call | solution.py:461
  974.7 20.6 %all-reduce.5.cloned.1.call-done = bf16[81,512]{1,0:T(8,128)(2,1)} async-done(((bf16[81,512]{1,0:T(8,128)(2,1)}), bf16[81,512]{1,0:T(8,128)(2,1)}) %all-reduce.5.cloned.1.call-update) | async-done | bytes 82960 | tf_op jit(solution)/shard_map/psum | solution.py:656
  (431 shorter events, 347.1 us)
Async XLA Ops:
  7.2 103.0 %all-gather.10.cloned.1.call-start = ((), (), s32[]{:S(2)}) async-start(), calls=%async_computation.5 | async-start | bytes 5242880 | tf_op jit(solution)/shard_map/all_gather | solution.py:533
  7.3 90.6 %collective-permute-start = (bf16[3,256,512]{2,1,0:T(8,128)(2,1)}, bf16[3,256,512]{2,1,0:T(8,128)(2,1)}, u32[]{:S(2)}, u32[]{:S(2)}) collective-permute-start(bf16[3,256,512]{2,1,0:T(8,128)(2,1)} %param.24), channel_id=1, source_target_pairs={{0,16},{16,0},{1,17},{17,1},{2,18},{18,2},{3,19},{19,3},{4,20},{20... | collective-permute-start | bytes 2359304 | tf_op jit(solution)/shard_map/ppermute | solution.py:42
  16.4 262.9 %all-gather.18.cloned.1.call-start = ((), (), s32[]{:S(2)}) async-start(), calls=%async_computation.15 | async-start | bytes 5242880 | tf_op jit(solution)/shard_map/all_gather | solution.py:576
  16.4 81.4 %collective-permute-start.2 = (bf16[256,2048]{1,0:T(8,128)(2,1)}, bf16[256,2048]{1,0:T(8,128)(2,1)}, u32[]{:S(2)}, u32[]{:S(2)}) collective-permute-start(bf16[256,2048]{1,0:T(8,128)(2,1)} %param.26), channel_id=1, source_target_pairs={{0,16},{16,0},{1,17},{17,1},{2,18},{18,2},{3,19},{19,3},{4,20},{20... | collective-permute-start | bytes 3145736 | tf_op jit(solution)/shard_map/ppermute | solution.py:42
  18.1 79.7 %collective-permute-start.1 = (bf16[2560,256]{1,0:T(8,128)(2,1)S(1)}, bf16[2560,256]{1,0:T(8,128)(2,1)}, u32[]{:S(2)}, u32[]{:S(2)}) collective-permute-start(bf16[2560,256]{1,0:T(8,128)(2,1)S(1)} %constant_dynamic-update-slice_fusion), channel_id=1, source_target_pairs={{0,16},{16,0},{1,17},{17,1},{2,18},{18,2},{3,19},{19,3},{4,20},{20... | collective-permute-start | bytes 3932168 | tf_op jit(solution)/shard_map/ppermute | solution.py:42
  117.2 234.7 %all-gather.16.cloned.1.call-start = ((), (), s32[]{:S(2)}) async-start(), calls=%async_computation.14 | async-start | bytes 5242880 | tf_op jit(solution)/shard_map/all_gather | solution.py:576
  117.9 244.7 %all-gather.14.cloned.1.call-start = ((), (), s32[]{:S(2)}) async-start(), calls=%async_computation.13 | async-start | bytes 5242880 | tf_op jit(solution)/shard_map/all_gather | solution.py:576
  122.5 318.9 %all-gather.12.cloned.1.call-start = ((), (), s32[]{:S(2)}) async-start(), calls=%async_computation.12 | async-start | bytes 5242880 | tf_op jit(solution)/shard_map/all_gather | solution.py:576
  124.1 100.6 %collective-permute-start.5 = (bf16[2,2560,256]{2,1,0:T(8,128)(2,1)S(1)}, bf16[2,2560,256]{2,1,0:T(8,128)(2,1)S(1)}, u32[]{:S(2)}, u32[]{:S(2)}) collective-permute-start(bf16[2,2560,256]{2,1,0:T(8,128)(2,1)S(1)} %pad_maximum_fusion.4), channel_id=1, source_target_pairs={{0,8},{8,0},{4,12},{12,4},{1,9},{9,1},{5,13},{13,5},{2,10},{10,2},... | collective-permute-start | bytes 7864328 | tf_op jit(solution)/shard_map/ppermute | solution.py:46
  173.1 96.0 %collective-permute-start.14 = (bf16[4,256,2048]{2,1,0:T(8,128)(2,1)}, bf16[4,256,2048]{2,1,0:T(8,128)(2,1)}, u32[]{:S(2)}, u32[]{:S(2)}) collective-permute-start(bf16[4,256,2048]{2,1,0:T(8,128)(2,1)} %pad_maximum_fusion.2.near_ref), channel_id=1, source_target_pairs={{0,4},{4,0},{8,12},{12,8},{1,5},{5,1},{9,13},{13,9},{2,6},{6,2},{1... | collective-permute-start | bytes 12582920 | tf_op jit(solution)/shard_map/ppermute | solution.py:50
  231.8 636.7 %reduce-scatter.14.cloned.1.call-start = ((), (), s32[]{:S(2)}) async-start(), calls=%async_computation.10 | async-start | bytes 5242880 | tf_op jit(solution)/shard_map/reduce_scatter | solution.py:611
  269.0 75.5 %collective-permute-start.4 = (bf16[4,3,256,512]{3,2,1,0:T(8,128)(2,1)S(1)}, bf16[4,3,256,512]{3,2,1,0:T(8,128)(2,1)}, u32[]{:S(2)}, u32[]{:S(2)}) collective-permute-start(bf16[4,3,256,512]{3,2,1,0:T(8,128)(2,1)S(1)} %pad_maximum_fusion.3.near_ref), channel_id=1, source_target_pairs={{0,4},{4,0},{8,12},{12,8},{1,5},{5,1},{9,13},{13,9},{2,6},{6,2},{1... | collective-permute-start | bytes 9437192 | tf_op jit(solution)/shard_map/ppermute | solution.py:50
  335.6 536.1 %reduce-scatter.6.cloned.1.call-start = ((), (), s32[]{:S(2)}) async-start(), calls=%async_computation.6 | async-start | bytes 5242880 | tf_op jit(solution)/shard_map/reduce_scatter | solution.py:611
  358.1 89.9 %collective-permute-start.11 = (bf16[2,512,512]{2,1,0:T(8,128)(2,1)}, bf16[2,512,512]{2,1,0:T(8,128)(2,1)}, u32[]{:S(2)}, u32[]{:S(2)}) collective-permute-start(bf16[2,512,512]{2,1,0:T(8,128)(2,1)} %bitcast.46.refs_4_), channel_id=1, source_target_pairs={{0,8},{4,12},{1,9},{5,13},{2,10},{6,14},{3,11},{7,15},{16,24},{20,... | collective-permute-start | bytes 3145736 | tf_op jit(solution)/shard_map/ppermute | solution.py:303
  380.0 82.4 %collective-permute-start.10 = (bf16[2,512,512]{2,1,0:T(8,128)(2,1)}, bf16[2,512,512]{2,1,0:T(8,128)(2,1)}, u32[]{:S(2)}, u32[]{:S(2)}) collective-permute-start(bf16[2,512,512]{2,1,0:T(8,128)(2,1)} %bitcast.46.refs_4_), channel_id=1, source_target_pairs={{0,4},{4,0},{8,12},{12,8},{1,5},{5,1},{9,13},{13,9},{2,6},{6,2},{1... | collective-permute-start | bytes 3145736 | tf_op jit(solution)/shard_map/ppermute | solution.py:50
  380.0 82.4 %collective-permute-start.7 = (bf16[2,512,512]{2,1,0:T(8,128)(2,1)}, bf16[2,512,512]{2,1,0:T(8,128)(2,1)}, u32[]{:S(2)}, u32[]{:S(2)}) collective-permute-start(bf16[2,512,512]{2,1,0:T(8,128)(2,1)} %bitcast.43.refs_0_), channel_id=1, source_target_pairs={{0,4},{4,0},{8,12},{12,8},{1,5},{5,1},{9,13},{13,9},{2,6},{6,2},{1... | collective-permute-start | bytes 3145736 | tf_op jit(solution)/shard_map/ppermute | solution.py:50
  521.5 355.1 %reduce-scatter.8.cloned.1.call-start = ((), (), s32[]{:S(2)}) async-start(), calls=%async_computation.7 | async-start | bytes 5242880 | tf_op jit(solution)/shard_map/reduce_scatter | solution.py:611
  527.8 356.4 %reduce-scatter.12.cloned.1.call-start = ((), (), s32[]{:S(2)}) async-start(), calls=%async_computation.9 | async-start | bytes 5242880 | tf_op jit(solution)/shard_map/reduce_scatter | solution.py:611
  569.0 318.0 %reduce-scatter.10.cloned.1.call-start = ((), (), s32[]{:S(2)}) async-start(), calls=%async_computation.8 | async-start | bytes 5242880 | tf_op jit(solution)/shard_map/reduce_scatter | solution.py:611
  657.9 337.4 %all-reduce.5.cloned.1.call-start = ((), (), s32[]{:S(2)}) async-start(), calls=%async_computation.11 | async-start | bytes 180224 | tf_op jit(solution)/shard_map/psum | solution.py:656
  673.7 85.1 %collective-permute-start.25 = (bf16[1,2,256,2048]{3,2,1,0:T(8,128)(2,1)}, bf16[1,2,256,2048]{3,2,1,0:T(8,128)(2,1)}, u32[]{:S(2)}, u32[]{:S(2)}) collective-permute-start(bf16[1,2,256,2048]{3,2,1,0:T(8,128)(2,1)} %dynamic-slice_bitcast_fusion.3), channel_id=1, source_target_pairs={{0,16},{16,0},{1,17},{17,1},{2,18},{18,2},{3,19},{19,3},{4,20},{20... | collective-permute-start | bytes 6291464 | tf_op jit(solution)/shard_map/ppermute | solution.py:42
  683.3 120.1 %collective-permute-start.22 = (bf16[4,2,256,512]{3,2,0,1:T(8,128)(2,1)}, bf16[4,2,256,512]{3,2,0,1:T(8,128)(2,1)S(1)}, u32[]{:S(2)}, u32[]{:S(2)}) collective-permute-start(bf16[4,2,256,512]{3,2,0,1:T(8,128)(2,1)} %dynamic-slice_bitcast_fusion.4), channel_id=1, source_target_pairs={{0,16},{16,0},{1,17},{17,1},{2,18},{18,2},{3,19},{19,3},{4,20},{20... | collective-permute-start | bytes 6291464 | tf_op jit(solution)/shard_map/ppermute | solution.py:42
  718.4 142.2 %collective-permute-start.29 = (bf16[1,256,2048]{2,1,0:T(8,128)(2,1)}, bf16[1,256,2048]{2,1,0:T(8,128)(2,1)}, u32[]{:S(2)}, u32[]{:S(2)}) collective-permute-start(bf16[1,256,2048]{2,1,0:T(8,128)(2,1)} %get-tuple-element.110), channel_id=1, source_target_pairs={{0,8},{8,0},{4,12},{12,4},{1,9},{9,1},{5,13},{13,5},{2,10},{10,2},... | collective-permute-start | bytes 3145736 | tf_op jit(solution)/shard_map/ppermute | solution.py:46
  762.8 102.0 %collective-permute-start.26 = (bf16[1,256,2048]{2,1,0:T(8,128)(2,1)}, bf16[1,256,2048]{2,1,0:T(8,128)(2,1)}, u32[]{:S(2)}, u32[]{:S(2)}) collective-permute-start(bf16[1,256,2048]{2,1,0:T(8,128)(2,1)} %get-tuple-element.112), channel_id=1, source_target_pairs={{0,8},{8,0},{4,12},{12,4},{1,9},{9,1},{5,13},{13,5},{2,10},{10,2},... | collective-permute-start | bytes 3145736 | tf_op jit(solution)/shard_map/ppermute | solution.py:46
  (115 other events, 1878.6 us)
Sparse Core Ops, SparseCore 0:
  16.5 93.6 all-gather.9
  117.3 80.4 all-gather.17
  200.0 79.2 all-gather.15
  281.3 79.2 all-gather.13
  362.1 79.2 all-gather.11
  443.5 77.9 reduce-scatter.13
  523.9 77.2 reduce-scatter.5
  603.5 77.2 reduce-scatter.7
  683.2 77.2 reduce-scatter.11
  762.7 89.0 reduce-scatter.9
  943.9 51.3 all-reduce.4

commit v4 on v3

--- a/solution.py
+++ b/solution.py
@@ -67,29 +67,48 @@
         out_ref[...] = beside_ref[0]
 
 
-def gather_weight(shard, near_x, axis):
-    if not paired():
-        return lax.all_gather(shard, ("dp", "stream"), axis=axis, tiled=True)
+def gather_weight(shard, axis):
+    return lax.all_gather(shard, ("dp", "stream"), axis=axis, tiled=True)
+
+
+def lined():
+    return paired() and lax.axis_size("head") == 4
+
+
+def swap_head(a):
+    at = lambda x, y, core, z: (x * 4 + y * 2 + core) * 4 + z
+    pairs = [
+        (at(x, y, core, z), at(z // 2, z % 2, core, 2 * x + y))
+        for x in range(2)
+        for y in range(2)
+        for core in range(2)
+        for z in range(4)
+    ]
+    return lax.ppermute(a, ("dp", "stream", "head"), pairs)
+
+
+def row_weight(shard, near):
     place = lax.axis_index("dp") * 4 + lax.axis_index("stream")
-    row = jnp.stack([shard, near_x])
-    near = jnp.concatenate([row, over_y(row)])
     beside = over_core(near)
     flips = jnp.array([0, 4, 2, 6, 1, 5, 3, 7], jnp.int32)
-    full_shape = tuple(n * 8 if i == axis else n for i, n in enumerate(shard.shape))
-    at = lambda k: tuple(k if i == axis else 0 for i in range(shard.ndim))
-    inner = (0,) * shard.ndim
+    count, rows, columns = shard.shape
+    piece = (1, count, rows, columns)
+    inner = (0, 0, 0)
     return pl.pallas_call(
         place_kernel,
         grid_spec=pltpu.PrefetchScalarGridSpec(
             num_scalar_prefetch=1,
             grid=(8,),
             in_specs=[
-                pl.BlockSpec((1,) + shard.shape, lambda k, order: (jnp.minimum(k, 3),) + inner),
-                pl.BlockSpec((1,) + shard.shape, lambda k, order: (jnp.maximum(k - 4, 0),) + inner),
+                pl.BlockSpec(piece, lambda k, order: (jnp.minimum(k, 3),) + inner),
+                pl.BlockSpec(piece, lambda k, order: (jnp.maximum(k - 4, 0),) + inner),
             ],
-            out_specs=pl.BlockSpec(shard.shape, lambda k, order: at(order[k])),
+            out_specs=pl.BlockSpec(
+                shard.shape,
+                lambda k, order: (0, lax.rem(order[k], 2), lax.div(order[k], 2)),
+            ),
         ),
-        out_shape=jax.ShapeDtypeStruct(full_shape, shard.dtype),
+        out_shape=jax.ShapeDtypeStruct((count, 2 * rows, 4 * columns), shard.dtype),
         compiler_params=pltpu.CompilerParams(vmem_limit_bytes=40 * 1024 * 1024),
         cost_estimate=pl.CostEstimate(flops=0, bytes_accessed=32 * shard.size, transcendentals=0),
         name="weight_in_order",
@@ -138,6 +157,231 @@
         ),
         name="add_terms",
     )(a, b)
+
+
+def exchange_kernel(units, axes, *refs):
+    count = len(axes)
+    partials, shard_refs = refs[:units], refs[units : units + count]
+    outs = refs[units + count : 2 * units + count]
+    fulls = refs[2 * units + count : 2 * units + 2 * count]
+    held, got, load_sem, send_sem, recv_sem, own_sem, near_send, near_recv = refs[
+        2 * units + 2 * count :
+    ]
+    x, stream, z = lax.axis_index("dp"), lax.axis_index("stream"), lax.axis_index("head")
+    core = lax.rem(stream, 2)
+    other_x, other_y, other_core = 1 - x, lax.rem(stream + 2, 4), stream + 1 - 2 * core
+    line = ({"head": lax.rem(z + 1, 4)}, {"head": lax.rem(z + 3, 4)})
+    to_x, to_y, to_core = {"dp": other_x}, {"stream": other_y}, {"stream": other_core}
+    place = x * 4 + stream
+    place_x, place_y = other_x * 4 + stream, x * 4 + other_y
+    place_far = other_x * 4 + other_y
+    beside = lambda at: at + 1 - 2 * core
+
+    barrier = pltpu.get_barrier_semaphore()
+    peers = line + ((to_x, to_y, to_core) if count else ())
+    for peer in peers:
+        pl.semaphore_signal(barrier, inc=1, device_id=peer, device_id_type=pl.DeviceIdType.MESH)
+    pl.semaphore_wait(barrier, len(peers))
+
+    def region(w, at, part=None):
+        full, width = fulls[w], shard_refs[w].shape[axes[w]]
+        rows = shard_refs[w].shape[0]
+        start, size = (0, rows) if part is None else (part * (rows // 2), rows // 2)
+        if axes[w] == 0:
+            return full.at[pl.ds(pl.multiple_of(at * width + start, size), size)]
+        return full.at[pl.ds(start, size), pl.ds(pl.multiple_of(at * width, width), width)]
+
+    def near(w, index, source, target, peer):
+        return pltpu.make_async_remote_copy(
+            src_ref=source,
+            dst_ref=target,
+            send_sem=near_send.at[w, index],
+            recv_sem=near_recv.at[w, index],
+            device_id=peer,
+            device_id_type=pl.DeviceIdType.MESH,
+        )
+
+    def pass_on(w, index, at, peer, part=None):
+        return near(w, index, region(w, at, part), region(w, at, part), peer)
+
+    def first(w):
+        target = region(w, place)
+        pltpu.make_async_copy(shard_refs[w], target, own_sem.at[w]).start()
+        for index, peer in enumerate((to_x, to_y, to_core)):
+            near(w, index, shard_refs[w], target, peer).start()
+
+    def second(w):
+        pass_on(w, 0, place_x, to_x).wait_recv()
+        pass_on(w, 4, place_x, to_y, 0).start()
+        pass_on(w, 3, place_x, to_core).start()
+        pass_on(w, 1, place_y, to_y).wait_recv()
+        pass_on(w, 6, place_y, to_x, 1).start()
+        pass_on(w, 5, place_y, to_core).start()
+
+    def third(w):
+        pass_on(w, 4, place_far, to_y, 0).wait_recv()
+        pass_on(w, 7, place_far, to_core, 0).start()
+        pass_on(w, 6, place_far, to_x, 1).wait_recv()
+        pass_on(w, 8, place_far, to_core, 1).start()
+
+    def last(w):
+        for index, at, part in (
+            (2, place, None),
+            (3, place_x, None),
+            (5, place_y, None),
+            (7, place_far, 0),
+            (8, place_far, 1),
+        ):
+            pass_on(w, index, beside(at), to_core, part).wait_recv()
+        pltpu.make_async_copy(shard_refs[w], region(w, place), own_sem.at[w]).wait()
+        for index in (0, 1, 2):
+            near(w, index, shard_refs[w], region(w, place), to_core).wait_send()
+        for index, at, part in (
+            (3, place_x, None),
+            (4, place_x, 0),
+            (5, place_y, None),
+            (6, place_y, 1),
+            (7, place_far, 0),
+            (8, place_far, 1),
+        ):
+            pass_on(w, index, at, to_core, part).wait_send()
+
+    feats = held.shape[-1]
+    chunk = send_sem.shape[-1]
+    step_rows = held.shape[2] // chunk
+
+    def load(u, b):
+        return pltpu.make_async_copy(
+            partials[u].at[:, b * feats : (b + 1) * feats], held.at[u, b], load_sem.at[u, b]
+        )
+
+    for u in range(units):
+        for b in range(4):
+            load(u, b).start()
+    for w in range(count):
+        first(w)
+    for u in range(units):
+        for b in range(4):
+            load(u, b).wait()
+
+    def part(c):
+        return pl.ds(pl.multiple_of(c * step_rows, step_rows), step_rows)
+
+    def hop(way, u, step, block, c):
+        return pltpu.make_async_remote_copy(
+            src_ref=held.at[u, block, part(c)],
+            dst_ref=got.at[way, u, step, part(c)],
+            send_sem=send_sem.at[way, u, step, c],
+            recv_sem=recv_sem.at[way, u, step, c],
+            device_id=line[way],
+            device_id_type=pl.DeviceIdType.MESH,
+        )
+
+    ways = ((0, z), (1, 3 - z))
+
+    def block_at(way, step):
+        return 3 - step + z if way == 0 else step + z - 3
+
+    def line_step(step):
+        def body(c, carry):
+            for way, rank in ways:
+
+                @pl.when(rank <= step)
+                def _():
+                    block = block_at(way, step)
+                    for u in range(units):
+                        if step > 0:
+
+                            @pl.when(rank > 0)
+                            def _():
+                                hop(way, u, step - 1, block, c).wait_recv()
+                                total = held[u, block, part(c)].astype(F32) + got[
+                                    way, u, step - 1, part(c)
+                                ].astype(F32)
+                                held[u, block, part(c)] = total.astype(BF16)
+
+                        hop(way, u, step, block, c).start()
+
+            return carry
+
+        lax.fori_loop(0, chunk, body, 0)
+
+    line_step(0)
+    for w in range(min(count, 2)):
+        second(w)
+    line_step(1)
+    for w in range(2, count):
+        second(w)
+    line_step(2)
+    for w in range(count):
+        third(w)
+
+    def finish(c, carry):
+        for u in range(units):
+            outs[u][part(c)] = held[u, z, part(c)].astype(F32)
+            for way, rank in ways:
+
+                @pl.when(rank > 0)
+                def _():
+                    hop(way, u, 2, z, c).wait_recv()
+                    outs[u][part(c)] += got[way, u, 2, part(c)].astype(F32)
+
+        return carry
+
+    lax.fori_loop(0, chunk, finish, 0)
+    for w in range(count):
+        last(w)
+
+    def drain(c, carry):
+        for step in range(3):
+            for way, rank in ways:
+
+                @pl.when(rank <= step)
+                def _():
+                    for u in range(units):
+                        hop(way, u, step, block_at(way, step), c).wait_send()
+
+        return carry
+
+    lax.fori_loop(0, chunk, drain, 0)
+
+
+def exchange(partials, shards_in, axes, collective_id):
+    units, count = len(partials), len(shards_in)
+    tokens, feats = partials[0].shape[0], partials[0].shape[1] // 4
+    chunk = 4
+    full = [
+        jax.ShapeDtypeStruct(tuple(n * 8 if i == axis else n for i, n in enumerate(w.shape)), BF16)
+        for w, axis in zip(shards_in, axes)
+    ]
+    anywhere = pl.BlockSpec(memory_space=pl.ANY)
+    sems = pltpu.SemaphoreType.DMA
+    results = pl.pallas_call(
+        functools.partial(exchange_kernel, units, axes),
+        in_specs=[anywhere] * (units + count),
+        out_specs=[pl.BlockSpec(memory_space=pltpu.VMEM)] * units + [anywhere] * count,
+        out_shape=[jax.ShapeDtypeStruct((tokens, feats), F32)] * units + full,
+        scratch_shapes=[
+            pltpu.VMEM((units, 4, tokens, feats), BF16),
+            pltpu.VMEM((2, units, 3, tokens, feats), BF16),
+            sems((units, 4)),
+            sems((2, units, 3, chunk)),
+            sems((2, units, 3, chunk)),
+            sems((max(count, 1),)),
+            sems((max(count, 1), 9)),
+            sems((max(count, 1), 9)),
+        ],
+        compiler_params=pltpu.CompilerParams(
+            collective_id=collective_id,
+            has_side_effects=True,
+            vmem_limit_bytes=48 * 1024 * 1024,
+        ),
+        cost_estimate=pl.CostEstimate(
+            flops=0, bytes_accessed=600 * 1024 * 1024, transcendentals=0
+        ),
+        name="exchange",
+    )(*partials, *shards_in)
+    return results[:units], results[units:]
 
 
 def head_sum_kernel(members, x_ref, out_ref, slots, send_sem, recv_sem):
@@ -325,8 +569,7 @@
     return jnp.sum(a, axis=1, keepdims=True)
 
 
-def early_kernel(streams_ref, stats_ref, cot_ref, history_ref, out_ref):
-    stats = stats_ref[...]
+def early_kernel(streams_ref, cot_ref, history_ref, out_ref):
     cot = cot_ref[...].astype(F32)
     plain, crossed, direct = [], [], []
     layers = [history_ref[j].astype(F32) for j in range(HIST)]
@@ -334,13 +577,12 @@
         plain.append(row_sum(layer))
         direct.append(row_sum(cot * layer))
     for s in range(4):
-        centered = (streams_ref[s] - stats[:, s : s + 1]) * stats[:, 4 + s : 5 + s]
         for layer in layers:
-            crossed.append(row_sum(centered * layer))
-    out_ref[...] = columns_of(crossed + plain + direct, stats.shape[0])
-
-
-def early_sums(streams, stats, cot, history):
+            crossed.append(row_sum(streams_ref[s] * layer))
+    out_ref[...] = columns_of(crossed + plain + direct, cot.shape[0])
+
+
+def early_sums(streams, cot, history):
     _, tokens, feats = streams.shape
     block = min(128, tokens)
     return pl.pallas_call(
@@ -348,7 +590,6 @@
         grid=(tokens // block,),
         in_specs=[
             pl.BlockSpec((4, block, feats), lambda i: (0, i, 0)),
-            pl.BlockSpec((block, 8), lambda i: (i, 0)),
             pl.BlockSpec((block, feats), lambda i: (i, 0)),
             pl.BlockSpec((HIST, block, feats), lambda i: (0, i, 0)),
         ],
@@ -359,7 +600,7 @@
             flops=110 * tokens * feats, bytes_accessed=36 * tokens * feats, transcendentals=0
         ),
         name="early_sums",
-    )(streams, stats, cot, history)
+    )(streams, cot, history)
 
 
 def sums_kernel(g0, g1, g2, g3, streams_ref, stats_ref, gain_ref, history_ref, out_ref, edge_ref):
@@ -420,9 +661,10 @@
     first, second = sums[n : n + 4] / model_width, sums[n + 4 : n + 8] / model_width
     spread = lambda a: jnp.repeat(a, HIST, axis=0)
     crossed, plain, direct = early[:n], early[n : n + HIST], early[n + HIST : n + 2 * HIST]
-    d_mix = spread(stats.T[4:]) * (
-        sums[:n] - spread(first) * jnp.tile(plain, (4, 1)) - spread(second) * crossed
-    )
+    means, inverse = spread(stats.T[:4]), spread(stats.T[4:])
+    plain = jnp.tile(plain, (4, 1))
+    crossed = (crossed - means * plain) * inverse
+    d_mix = inverse * (sums[:n] - spread(first) * plain - spread(second) * crossed)
     d_mix = d_mix + jnp.concatenate([jnp.zeros_like(d_mix[: 3 * HIST]), direct])
     return d_mix, jnp.concatenate([first, second])
 
@@ -532,7 +774,8 @@
     cot_rows = cotangent.reshape(tokens, feats).astype(F32) * valid
     out_full = lax.all_gather(cot_rows.astype(BF16), "head", axis=1, tiled=True)
     w_both = jnp.concatenate([w_attn_out, w_down])
-    near_x = tuple(over_x(w) if paired() else w[:1] for w in (w_qkv, w_both, w_up))
+    duplex = lined()
+    kv_near = swap_head(w_qkv[1:]) if duplex else w_qkv[:1]
 
     history = history.reshape(HIST, tokens, feats)
     current = history[HIST - 1]
@@ -540,6 +783,10 @@
     mixed = lax.dot_general(w_mix_in, current, (((0,), (1,)), ((), ())), preferred_element_type=F32)
     square = jnp.sum(current_f * current_f, axis=1)[None]
     mixed = head_sum(jnp.concatenate([mixed, square]), 0).T
+    mixed, kv_near = lax.optimization_barrier((mixed, kv_near))
+    if duplex:
+        kv_near = jnp.stack([kv_near, over_x(kv_near)])
+        kv_near = jnp.concatenate([kv_near, over_y(kv_near)])
     rms_scale = lax.rsqrt(mixed[:, 4 * HIST :] / model_width + EPSILON)
     mix_pre = mixed[:, : 4 * HIST] * rms_scale
     mix_hidden = gelu_exact(mix_pre)
@@ -556,29 +803,39 @@
         jnp.concatenate([jnp.sum(streams, axis=2), jnp.sum(streams * streams, axis=2)]), 1
     )
     stat_sum, stat_square = stats[:4], stats[4:]
-    stat_sum, stat_square, out_full, near_x = lax.optimization_barrier(
-        (stat_sum, stat_square, out_full, near_x)
+    early = early_sums(streams, cot_rows.astype(BF16), history)
+    stat_sum, stat_square, out_full, kv_near, early = lax.optimization_barrier(
+        (stat_sum, stat_square, out_full, kv_near, early)
     )
     row_means = (stat_sum / model_width)[:, :, None]
     inv_std = lax.rsqrt(stat_square[:, :, None] / model_width - row_means * row_means + EPSILON)
     centered = (streams - row_means) * inv_std
     row_stats = jnp.concatenate([row_means[..., 0], inv_std[..., 0]]).T
-    early = early_sums(streams, row_stats, cot_rows.astype(BF16), history)
-    early = head_sum(early[:, : 6 * HIST].T, 2)
+    early = lax.psum(early[:, : 6 * HIST].T, "head")
     normed = (centered * ln_gain[:, None, :] + ln_bias[:, None, :]).astype(BF16)
-
-    wq, wk, wv = gather_weight(w_qkv, near_x[0], 1)
-    both_full = gather_weight(w_both, near_x[1], 1)
-    w_out_full, down_full = both_full[:feats], both_full[feats:]
-    up_full = gather_weight(w_up, near_x[2], 0)
 
     def all_features(stream):
         return lax.all_gather(normed[stream], "head", axis=1, tiled=True)
 
-    k_in, v_in, q_in, up_in = (all_features(s) for s in (1, 2, 0, 3))
-
-    keys = rotate(dot(k_in, wk), tables, 1.0)
-    values = dot(v_in, wv).astype(BF16)
+    if duplex:
+        w_kv = row_weight(w_qkv[1:], kv_near)
+        k_in, v_in, up_in, q_in = normed[1], normed[2], all_features(3), all_features(0)
+        (key_pre, value_pre), (wq, up_full, both_full) = exchange(
+            [dot(k_in, w_kv[0]).astype(BF16), dot(v_in, w_kv[1]).astype(BF16)],
+            [w_qkv[0], w_up, w_both],
+            (0, 0, 1),
+            4,
+        )
+    else:
+        wq, wk, wv = gather_weight(w_qkv, 1)
+        both_full = gather_weight(w_both, 1)
+        up_full = gather_weight(w_up, 0)
+        k_in, v_in, q_in, up_in = (all_features(s) for s in (1, 2, 0, 3))
+        key_pre, value_pre = dot(k_in, wk), dot(v_in, wv)
+    w_out_full, down_full = both_full[:feats], both_full[feats:]
+
+    keys = rotate(key_pre, tables, 1.0)
+    values = value_pre.astype(BF16)
     queries = dot(q_in, wq)
     d_attended = dot_nt(out_full, w_out_full).astype(BF16) * valid.astype(BF16)
     by_micro = lambda a: a.reshape(micro, quarter, feats)
@@ -613,10 +870,21 @@
         ).astype(F32)
 
     g_up = to_owner(dot_nt(d_up, up_full))
-    g_query = to_owner(dot_nt(d_query_pre, wq))
-    g_key = to_owner(dot_nt(d_key_pre, wk))
-    g_value = to_owner(dot_nt(d_value_pre, wv))
-    branch = to_owner(dot(attended, w_out_full) + dot(gated_up, down_full))
+    combined = dot(attended, w_out_full) + dot(gated_up, down_full)
+    if duplex:
+        partials = [dot_nt(d_query_pre, wq).astype(BF16), combined.astype(BF16)]
+        partials, d_key_pre, d_value_pre = lax.optimization_barrier(
+            (partials, d_key_pre, d_value_pre)
+        )
+        (g_query, branch), _ = exchange(partials, [], (), 5)
+        d_key_full = lax.all_gather(d_key_pre, "head", axis=1, tiled=True)
+        d_value_full = lax.all_gather(d_value_pre, "head", axis=1, tiled=True)
+        g_key, g_value = dot_nt(d_key_full, w_kv[0]), dot_nt(d_value_full, w_kv[1])
+    else:
+        g_query = to_owner(dot_nt(d_query_pre, wq))
+        g_key = to_owner(dot_nt(d_key_pre, wk))
+        g_value = to_owner(dot_nt(d_value_pre, wv))
+        branch = to_owner(combined)
     block_out = (valid * (streams[3] + branch)).astype(BF16)
 
     product = lambda a, b: dot_tn(a, b).astype(BF16)
@@ -624,18 +892,30 @@
     down_terms = scatter_parts(product(out_full, gated_up)[None])
     grad_up = add_terms(up_terms[0][0], up_terms[1][0], False)
     grad_down = add_terms(down_terms[0][0], down_terms[1][0], True)
-    terms = scatter_parts(
-        jnp.stack(
-            [
-                product(q_in, d_query_pre),
-                product(k_in, d_key_pre),
-                product(v_in, d_value_pre),
-                product(out_full, attended),
-            ]
+    if duplex:
+        by_head = lambda a, b: jnp.concatenate(
+            [product(a, b[:, i * feats : (i + 1) * feats]) for i in range(4)]
         )
-    )
-    grad_qkv = terms[0][:3].astype(F32) + terms[1][:3].astype(F32)
-    grad_attn_out = add_terms(terms[0][3], terms[1][3], True)
+        terms = scatter_parts(
+            jnp.stack([by_head(k_in, d_key_full), by_head(v_in, d_value_full)])
+        )
+        kv = swap_head((terms[0].astype(F32) + terms[1].astype(F32)).astype(BF16)).astype(F32)
+        terms = scatter_parts(jnp.stack([product(q_in, d_query_pre), product(out_full, attended)]))
+        grad_query = terms[0][:1].astype(F32) + terms[1][:1].astype(F32)
+        grad_qkv = jnp.concatenate([grad_query, kv])
+    else:
+        terms = scatter_parts(
+            jnp.stack(
+                [
+                    product(q_in, d_query_pre),
+                    product(k_in, d_key_pre),
+                    product(v_in, d_value_pre),
+                    product(out_full, attended),
+                ]
+            )
+        )
+        grad_qkv = terms[0][:3].astype(F32) + terms[1][:3].astype(F32)
+    grad_attn_out = add_terms(terms[0][-1], terms[1][-1], True)
 
     grads = (g_query, g_key, g_value, g_up)
     sums, gain_shift = gradient_sums(grads, streams, row_stats, ln_gain, history)

time: 1020 us -> 1260 us (1.24)
  Pallas kernels: 241 us -> 710 us
  waiting for transfers between devices: 385 us -> 140 us
  starting transfers between devices: 25.8 us -> 41.5 us
    pallas_call x3, Pallas kernels: 27.2 us -> 522 us  [the longest x2 517 us: exchange(): pl.pallas_call(functools.partial(exchange_kernel, units, axes), in_specs=...]
    ppermute x6 -> x5, waiting for transfers between devices: 131 us -> 11.5 us  [over_y(): return lax.ppermute(a, 'stream', SWAP_Y)]
    ppermute x6 -> x5, waiting for transfers between devices: 111 us -> 28.8 us  [over_x(): return lax.ppermute(a, 'dp', SWAP_X)]
    all_gather x4 -> x2, waiting for transfers between devices: 60.9 us -> 0.01 us  [all_features(): return lax.all_gather(normed[stream], 'head', axis=1, tiled=True)]
    ppermute x0 -> x2, waiting for transfers between devices: none -> 28.6 us  [swap_head(): return lax.ppermute(a, ('dp', 'stream', 'head'), pairs)]
    ppermute x2, waiting for transfers between devices: 0.01 us -> 21.2 us  [exchange_rows(): across = lax.ppermute(local, 'stream', [(0, 2), (1, 3)])]
    pallas_call x4 -> x3, Pallas kernels: 101 us -> 80.3 us  [head_sum(): pl.pallas_call(functools.partial(head_sum_kernel, members), out_shape=jax...]
    unnamed x202 -> x197, local copies, waits for them, and re-layouts: 47 us -> 36 us
  transfers between devices with their start and end apart: 41 -> 37, of which waited for: 12 -> 9; matrix products, arithmetic and copies ran while one was open for 27% -> 23% of each run, Pallas kernels for 20% -> 57%
where the time goes in v4:
time: 1260 us; the launch traced here: 1250 us
  Pallas kernels  710 us (56%)
  matrix products  147 us (12%)
  waiting for transfers between devices  140 us (11%)
  other arithmetic  109 us (9%)
  local copies, waits for them, and re-layouts  87.3 us (7%)
  starting transfers between devices  41.5 us (3%)
  between operations  16.2 us (1%)
    pallas_call x2, Pallas kernels, exchange(): pl.pallas_call(functools.partial(exchange_kernel, units, axes), in_specs=...  517 us
    pallas_call x3, Pallas kernels, head_sum(): pl.pallas_call(functools.partial(head_sum_kernel, members), out_shape=jax...  80.3 us
    dot_general x6, matrix products, dot(): return jnp.dot(a, b, preferred_element_type=F32)  50.9 us
    dot_general x6, matrix products, dot_nt(): lax.dot_general(a, b, (((1,), (1,)), ((), ())), preferred_element_type=F32)  47.6 us
    pallas_call x1, Pallas kernels, attention(): pl.pallas_call(attention_kernel, grid=(micro, feats // HD), in_specs=[pl....  44.6 us
    dot_general x12, matrix products, dot_tn(): lax.dot_general(a, b, (((0,), (0,)), ((), ())), preferred_element_type=F32)  41.9 us
    unnamed x197, local copies, waits for them, and re-layouts  36 us
    ppermute x2, waiting for transfers between devices, reduce_rows(): lax.ppermute(across, 'stream', [(2, 0), (3, 1)])  32.6 us
  transfers between devices with their start and end apart: 37, of which 9 were waited for; matrix products, arithmetic and copies ran while one was open for 23% of the time, Pallas kernels for 57%

profile of v4, /device:TPU:8, one launch (start us, length us, event | category | flops | bytes accessed | tf_op | source)
XLA Modules:
  0.0 1251.3 jit_solution(17845441799115624417)
XLA Ops:
  36.8 51.0 %sum_over_head.3 = f32[37,1024]{1,0:T(8,128)} custom-call(f32[37,1024]{1,0:T(8,128)} %pad_maximum_fusion.6.x_ref), custom_call_target="tpu_custom_call" | custom-call | tf_op jit(solution)/shard_map/sum_over_head/pallas_call | solution.py:421
  103.2 10.3 collective-permute-done.1
  116.4 13.3 %fusion.107 = (f32[4,1024]{1,0:T(4,128)S(1)}, f32[4,1024]{1,0:T(4,128)S(1)}, f32[4,1024,512]{2,1,0:T(8,128)}) fusion(f32[1024,512]{1,0:T(8,128)} %bitcast_convert_fusion.8, f32[4,1024]{1,0:T(4,128)S(1)} %get-tuple-element.178, f32[1024,512]{1,0:T(8,128)} %get-tuple-element.170, f32[4,1024]{1,0:T(4,128)S(1)} %get-tuple-element.179, ...), kind=kLoop, calls=%fused_computation.260 | loop fusion | flops 41934848 | bytes 27443200 | tf_op jit(solution)/shard_map/reduce_sum | solution.py:803
  142.4 11.8 early_sums.1
  186.3 261.4 %exchange.2 = (f32[1024,512]{1,0:T(8,128)S(1)}, f32[1024,512]{1,0:T(8,128)}, bf16[2048,512]{1,0:T(8,128)(2,1)}, bf16[2048,2048]{1,0:T(8,128)(2,1)}, bf16[2560,2048]{1,0:T(8,128)(2,1)}) custom-call(bf16[1024,2048]{1,0:T(8,128)(2,1)} %convolution_convert_fusion.5.refs_0_, bf16[1024,2048]{1,0:T(8,128)(2,1)} %convolution_convert_fusion.4.refs_1_, ...), custom_call_target="tpu_custom_call" | custom-call | bytes 629145600 | tf_op jit(solution)/shard_map/exchange/pallas_call | solution.py:359
  467.6 10.0 all-gather.12.cloned.1.call-start
  478.3 21.2 %collective-permute-done.5.refs_2_ = bf16[2,512,512]{2,1,0:T(8,128)(2,1)} collective-permute-done((bf16[2,512,512]{2,1,0:T(8,128)(2,1)}, bf16[2,512,512]{2,1,0:T(8,128)(2,1)}, u32[]{:S(2)}, u32[]{:S(2)}) %collective-permute-start.5) | collective-permute-done | bytes 1048608 | tf_op jit(solution)/shard_map/ppermute | solution.py:547
  513.4 44.6 %attention_both_ways.1 = (bf16[2,512,512]{2,1,0:T(8,128)(2,1)S(1)}, bf16[2,512,512]{2,1,0:T(8,128)(2,1)S(1)}, bf16[2,512,512]{2,1,0:T(8,128)(2,1)S(1)}, bf16[2,5...) custom-call(s32[4]{0:T(128)S(1)} %iota_xor_fusion.place_ref, ...), custom_call_target="tpu_custom_call" | custom-call | flops 12884901888 | bytes 20971520 | tf_op jit(solution)/shard_map/attention_both_ways/pallas_call | solution.py:521
  562.0 16.7 %fusion.3 = (f32[1024,2048]{1,0:T(8,128)}, bf16[1024,2048]{1,0:T(8,128)(2,1)S(1)}) fusion(bf16[2048,2048]{1,0:T(8,128)(2,1)} %get-tuple-element.56, bf16[1,1024,2048]{2,1,0:T(8,128)(2,1)} %all-gather.16.cloned.1.call-done), kind=kOutput, calls=%fused_computation.4 | convolution fusion | flops 8610906112 | bytes 25165824 | tf_op jit(solution)/shard_map/dot_general | solution.py:26
  578.7 13.0 %fusion.8 = f32[1024,2048]{1,0:T(8,128)S(1)} fusion(bf16[1024,2048]{1,0:T(8,128)(2,1)S(1)} %get-tuple-element.57, bf16[2560,2048]{1,0:T(8,128)(2,1)} %get-tuple-element.51), kind=kOutput, calls=%fused_computation.20 | convolution fusion | flops 8589934592 | bytes 20971520 | tf_op jit(solution)/shard_map/dot_general | solution.py:26
  607.7 17.8 %collective-permute-done.12 = bf16[2,512,512]{2,1,0:T(8,128)(2,1)S(1)} collective-permute-done((bf16[2,512,512]{2,1,0:T(8,128)(2,1)S(1)}, bf16[2,512,512]{2,1,0:T(8,128)(2,1)S(1)}, u32[]{:S(2)}, u32[]{:S(2)}) %collective-permute-start.12) | collective-permute-done | bytes 1048608 | tf_op jit(solution)/shard_map/ppermute | solution.py:556
  633.0 14.8 %collective-permute-done.15 = bf16[2,512,512]{2,1,0:T(8,128)(2,1)} collective-permute-done((bf16[2,512,512]{2,1,0:T(8,128)(2,1)S(1)}, bf16[2,512,512]{2,1,0:T(8,128)(2,1)}, u32[]{:S(2)}, u32[]{:S(2)}) %collective-permute-start.15) | collective-permute-done | bytes 1048608 | tf_op jit(solution)/shard_map/ppermute | solution.py:556
  651.0 15.5 %multiply_convert_fusion = bf16[1024,2048]{1,0:T(8,128)(2,1)} fusion(f32[1024,2048]{1,0:T(8,128)} %get-tuple-element.72, bf16[1024,2048]{1,0:T(8,128)(2,1)} %all-gather.8.cloned.1.call-done, bf16[2560,2048]{1,0:T(8,128)(2,1)} %get-tuple-element.51), kind=kOutput, calls=%fused_computation.9 | convolution fusion | flops 8594128896 | bytes 25165824 | tf_op jit(solution)/shard_map/dot_general | solution.py:30
  666.5 12.1 convolution_convert_fusion
  686.6 9.8 convolution_convert_fusion.1
  710.5 13.9 %convolution_convert_fusion.2 = bf16[1024,2048]{1,0:T(8,128)(2,1)} fusion(bf16[1024,2048]{1,0:T(8,128)(2,1)} %multiply_convert_fusion, bf16[2048,2048]{1,0:T(8,128)(2,1)} %get-tuple-element.56), kind=kOutput, calls=%fused_computation.47 | convolution fusion | flops 8592031744 | bytes 16777216 | tf_op jit(solution)/shard_map/dot_general | solution.py:30
  743.6 9.5 collective-permute-done.17
  758.0 255.4 %exchange.3 = (f32[1024,512]{1,0:T(8,128)S(1)}, f32[1024,512]{1,0:T(8,128)S(1)}) custom-call(bf16[1024,2048]{1,0:T(8,128)(2,1)} %convolution_convert_fusion.3.refs_0_, bf16[1024,2048]{1,0:T(8,128)(2,1)} %add_convert_fusion.refs_1_), custom_call_target="tpu_custom_call" | custom-call | bytes 629145600 | tf_op jit(solution)/shard_map/exchange/pallas_call | solution.py:359
  1056.1 11.5 collective-permute-done.25
  1081.0 15.7 %gradient_sums.1 = (f32[1024,128]{1,0:T(8,128)S(1)}, f32[8,512]{1,0:T(8,128)S(1)}) custom-call(f32[1024,512]{1,0:T(8,128)S(1)} %copy-done.7, f32[1024,512]{1,0:T(8,128)S(1)} %fusion.40.g1, f32[1024,512]{1,0:T(8,128)S(1)} %fusion.41.g2, f32[1024,512]{1,0:T(8,128)S(1)} %convert_element_type.482.g3, f32[4,1024,512]{2,1,0:T(8,128)} %get-tuple-element.116.streams_ref, ...), custom_call_target="tpu_custom_call" | custom-call | flops 57671680 | bytes 22020096 | tf_op jit(solution)/shard_map/gradient_sums/pallas_call | solution.py:632
  1097.6 20.6 %sum_over_head.5 = f32[44,1024]{1,0:T(8,128)} custom-call(f32[44,1024]{1,0:T(8,128)} %slice_bitcast_fusion.22.x_ref), custom_call_target="tpu_custom_call" | custom-call | tf_op jit(solution)/shard_map/sum_over_head/pallas_call | solution.py:421
  1168.7 17.1 %history_gradient.1 = f32[9,1024,512]{2,1,0:T(8,128)} custom-call(f32[1024,512]{1,0:T(8,128)S(1)} %copy-done.8, f32[1024,512]{1,0:T(8,128)S(1)} %copy-done.12, f32[1024,512]{1,0:T(8,128)S(1)} %copy-done.10, f32[1024,512]{1,0:T(8,128)S(1)} %convert_element_type.482.g3, f32[4,1024,512]{2,1,0:T(8,128)} %get-tuple-element.116.streams_ref, ...), custom_call_target="tpu_custom_call" | custom-call | flops 57671680 | bytes 33554432 | tf_op jit(solution)/shard_map/history_gradient/pallas_call | solution.py:703
  1185.8 16.6 %all-reduce.8.cloned.1.call-done = bf16[81,512]{1,0:T(8,128)(2,1)} async-done(((bf16[81,512]{1,0:T(8,128)(2,1)}), bf16[81,512]{1,0:T(8,128)(2,1)}) %all-reduce.8.cloned.1.call-update) | async-done | bytes 82960 | tf_op jit(solution)/shard_map/psum | solution.py:936
  1212.9 28.6 %collective-permute-done.22 = bf16[2,256,512]{2,1,0:T(8,128)(2,1)S(1)} collective-permute-done((bf16[2,256,512]{2,1,0:T(8,128)(2,1)S(1)}, bf16[2,256,512]{2,1,0:T(8,128)(2,1)S(1)}, u32[]{:S(2)}, u32[]{:S(2)}) %collective-permute-start.22) | collective-permute-done | bytes 524320 | tf_op jit(solution)/shard_map/ppermute | solution.py:87
  (428 shorter events, 322.9 us)
Async XLA Ops:
  7.2 148.5 %all-gather.8.cloned.1.call-start = ((), (), s32[]{:S(2)}) async-start(), calls=%async_computation.1 | async-start | bytes 5242880 | tf_op jit(solution)/shard_map/all_gather | solution.py:775
  9.1 84.2 %collective-permute-start = (bf16[2,256,512]{2,1,0:T(8,128)(2,1)}, bf16[2,256,512]{2,1,0:T(8,128)(2,1)S(1)}, u32[]{:S(2)}, u32[]{:S(2)}) collective-permute-start(bf16[2,256,512]{2,1,0:T(8,128)(2,1)} %slice.189), channel_id=1, source_target_pairs={{0,0},{1,8},{2,16},{3,24},{4,4},{5,12},{6,20},{7,28},{8,1},{9,9},{... | collective-permute-start | bytes 1572872 | tf_op jit(solution)/shard_map/ppermute | solution.py:87
  19.4 486.3 %all-gather.14.cloned.1.call-start = ((), (), s32[]{:S(2)}) async-start(), calls=%async_computation.7 | async-start | bytes 5242880 | tf_op jit(solution)/shard_map/all_gather | solution.py:818
  115.8 38.4 %collective-permute-start.2 = (bf16[2,2,256,512]{3,2,1,0:T(8,128)(2,1)}, bf16[2,2,256,512]{3,2,1,0:T(8,128)(2,1)}, u32[]{:S(2)}, u32[]{:S(2)}) collective-permute-start(bf16[2,2,256,512]{3,2,1,0:T(8,128)(2,1)} %pad_maximum_fusion.5), channel_id=1, source_target_pairs={{0,8},{8,0},{4,12},{12,4},{1,9},{9,1},{5,13},{13,5},{2,10},{10,2},... | collective-permute-start | bytes 3145736 | tf_op jit(solution)/shard_map/ppermute | solution.py:46
  163.6 398.4 %all-gather.16.cloned.1.call-start = ((), (), s32[]{:S(2)}) async-start(), calls=%async_computation.8 | async-start | bytes 5242880 | tf_op jit(solution)/shard_map/all_gather | solution.py:818
  164.3 592.0 %all-reduce.6.cloned.1.call-start = ((), (), s32[]{:S(2)}) async-start(), calls=%async_computation.5 | async-start | bytes 458752 | tf_op jit(solution)/shard_map/psum | solution.py:814
  459.9 39.6 %collective-permute-start.5 = (bf16[2,512,512]{2,1,0:T(8,128)(2,1)}, bf16[2,512,512]{2,1,0:T(8,128)(2,1)}, u32[]{:S(2)}, u32[]{:S(2)}) collective-permute-start(bf16[2,512,512]{2,1,0:T(8,128)(2,1)} %bitcast.348), channel_id=1, source_target_pairs={{0,8},{4,12},{1,9},{5,13},{2,10},{6,14},{3,11},{7,15},{16,24},{20,... | collective-permute-start | bytes 3145736 | tf_op jit(solution)/shard_map/ppermute | solution.py:547
  467.6 558.8 %all-gather.12.cloned.1.call-start = ((), (), s32[]{:S(2)}) async-start(), calls=%async_computation.3 | async-start | bytes 5242880 | tf_op jit(solution)/shard_map/all_gather | solution.py:881
  561.0 46.8 %collective-permute-start.10 = (bf16[2,512,512]{2,1,0:T(8,128)(2,1)}, bf16[2,512,512]{2,1,0:T(8,128)(2,1)}, u32[]{:S(2)}, u32[]{:S(2)}) collective-permute-start(bf16[2,512,512]{2,1,0:T(8,128)(2,1)} %get-tuple-element.59), channel_id=1, source_target_pairs={{0,4},{4,0},{8,12},{12,8},{1,5},{5,1},{9,13},{13,9},{2,6},{6,2},{1... | collective-permute-start | bytes 3145736 | tf_op jit(solution)/shard_map/ppermute | solution.py:50
  561.5 71.5 %collective-permute-start.13 = (bf16[2,512,512]{2,1,0:T(8,128)(2,1)}, bf16[2,512,512]{2,1,0:T(8,128)(2,1)}, u32[]{:S(2)}, u32[]{:S(2)}) collective-permute-start(bf16[2,512,512]{2,1,0:T(8,128)(2,1)} %get-tuple-element.63), channel_id=1, source_target_pairs={{0,4},{4,0},{8,12},{12,8},{1,5},{5,1},{9,13},{13,9},{2,6},{6,2},{1... | collective-permute-start | bytes 3145736 | tf_op jit(solution)/shard_map/ppermute | solution.py:50
  562.0 37.0 %collective-permute-start.14 = (bf16[2,512,512]{2,1,0:T(8,128)(2,1)}, bf16[2,512,512]{2,1,0:T(8,128)(2,1)}, u32[]{:S(2)}, u32[]{:S(2)}) collective-permute-start(bf16[2,512,512]{2,1,0:T(8,128)(2,1)} %get-tuple-element.65), channel_id=1, source_target_pairs={{0,4},{4,0},{8,12},{12,8},{1,5},{5,1},{9,13},{13,9},{2,6},{6,2},{1... | collective-permute-start | bytes 3145736 | tf_op jit(solution)/shard_map/ppermute | solution.py:50
  600.6 47.3 %collective-permute-start.15 = (bf16[2,512,512]{2,1,0:T(8,128)(2,1)S(1)}, bf16[2,512,512]{2,1,0:T(8,128)(2,1)}, u32[]{:S(2)}, u32[]{:S(2)}) collective-permute-start(bf16[2,512,512]{2,1,0:T(8,128)(2,1)S(1)} %add_convert_fusion.3), channel_id=1, source_target_pairs={{8,0},{12,4},{9,1},{13,5},{10,2},{14,6},{11,3},{15,7},{24,16},{28,... | collective-permute-start | bytes 3145736 | tf_op jit(solution)/shard_map/ppermute | solution.py:556
  650.9 384.6 %all-gather.10.cloned.1.call-start = ((), (), s32[]{:S(2)}) async-start(), calls=%async_computation.2 | async-start | bytes 5242880 | tf_op jit(solution)/shard_map/all_gather | solution.py:880
  666.5 405.1 %reduce-scatter.2.cloned.1.call-start = ((), (), s32[]{:S(2)}) async-start(), calls=%async_computation.4 | async-start | bytes 5242880 | tf_op jit(solution)/shard_map/reduce_scatter | solution.py:868
  684.9 43.7 %collective-permute-start.26 = (bf16[1,4,256,2048]{3,2,1,0:T(8,128)(2,1)}, bf16[1,4,256,2048]{3,2,1,0:T(8,128)(2,1)}, u32[]{:S(2)}, u32[]{:S(2)}) collective-permute-start(bf16[1,4,256,2048]{3,2,1,0:T(8,128)(2,1)} %dynamic-slice_bitcast_fusion), channel_id=1, source_target_pairs={{0,4},{4,0},{8,12},{12,8},{1,5},{5,1},{9,13},{13,9},{2,6},{6,2},{1... | collective-permute-start | bytes 12582920 | tf_op jit(solution)/shard_map/ppermute | solution.py:50
  702.3 35.0 %collective-permute-start.23 = (bf16[1,4,256,2048]{3,2,1,0:T(8,128)(2,1)}, bf16[1,4,256,2048]{3,2,1,0:T(8,128)(2,1)}, u32[]{:S(2)}, u32[]{:S(2)}) collective-permute-start(bf16[1,4,256,2048]{3,2,1,0:T(8,128)(2,1)} %dynamic-slice_bitcast_fusion.1), channel_id=1, source_target_pairs={{0,4},{4,0},{8,12},{12,8},{1,5},{5,1},{9,13},{13,9},{2,6},{6,2},{1... | collective-permute-start | bytes 12582920 | tf_op jit(solution)/shard_map/ppermute | solution.py:50
  724.4 478.1 %all-reduce.8.cloned.1.call-start = ((), (), s32[]{:S(2)}) async-start(), calls=%async_computation.6 | async-start | bytes 180224 | tf_op jit(solution)/shard_map/psum | solution.py:936
  736.3 279.7 %collective-permute-start.27 = (bf16[1,2,256,2048]{3,2,1,0:T(8,128)(2,1)}, bf16[1,2,256,2048]{3,2,1,0:T(8,128)(2,1)}, u32[]{:S(2)}, u32[]{:S(2)}) collective-permute-start(bf16[1,2,256,2048]{3,2,1,0:T(8,128)(2,1)} %dynamic-slice_bitcast_fusion.2), channel_id=1, source_target_pairs={{0,16},{16,0},{1,17},{17,1},{2,18},{18,2},{3,19},{19,3},{4,20},{20... | collective-permute-start | bytes 6291464 | tf_op jit(solution)/shard_map/ppermute | solution.py:42
  742.7 279.3 %collective-permute-start.24 = (bf16[1,2,256,2048]{3,2,1,0:T(8,128)(2,1)}, bf16[1,2,256,2048]{3,2,1,0:T(8,128)(2,1)}, u32[]{:S(2)}, u32[]{:S(2)}) collective-permute-start(bf16[1,2,256,2048]{3,2,1,0:T(8,128)(2,1)} %dynamic-slice_bitcast_fusion.3), channel_id=1, source_target_pairs={{0,16},{16,0},{1,17},{17,1},{2,18},{18,2},{3,19},{19,3},{4,20},{20... | collective-permute-start | bytes 6291464 | tf_op jit(solution)/shard_map/ppermute | solution.py:42
  754.3 261.0 %collective-permute-start.18 = (bf16[2,256,512]{2,1,0:T(8,128)(2,1)}, bf16[2,256,512]{2,1,0:T(8,128)(2,1)S(1)}, u32[]{:S(2)}, u32[]{:S(2)}) collective-permute-start(bf16[2,256,512]{2,1,0:T(8,128)(2,1)} %dynamic-slice_bitcast_fusion.11), channel_id=1, source_target_pairs={{0,8},{8,0},{4,12},{12,4},{1,9},{9,1},{5,13},{13,5},{2,10},{10,2},... | collective-permute-start | bytes 1572872 | tf_op jit(solution)/shard_map/ppermute | solution.py:46
  1026.0 41.5 %collective-permute-start.25 = (bf16[1,256,2048]{2,1,0:T(8,128)(2,1)}, bf16[1,256,2048]{2,1,0:T(8,128)(2,1)}, u32[]{:S(2)}, u32[]{:S(2)}) collective-permute-start(bf16[1,256,2048]{2,1,0:T(8,128)(2,1)} %get-tuple-element.132), channel_id=1, source_target_pairs={{0,8},{8,0},{4,12},{12,4},{1,9},{9,1},{5,13},{13,5},{2,10},{10,2},... | collective-permute-start | bytes 3145736 | tf_op jit(solution)/shard_map/ppermute | solution.py:46
  1045.1 73.9 %collective-permute-start.19 = (bf16[2,4,256,512]{3,2,1,0:T(8,128)(2,1)}, bf16[2,4,256,512]{3,2,1,0:T(8,128)(2,1)}, u32[]{:S(2)}, u32[]{:S(2)}) collective-permute-start(bf16[2,4,256,512]{3,2,1,0:T(8,128)(2,1)} %fusion.27), channel_id=1, source_target_pairs={{0,4},{4,0},{8,12},{12,8},{1,5},{5,1},{9,13},{13,9},{2,6},{6,2},{1... | collective-permute-start | bytes 6291464 | tf_op jit(solution)/shard_map/ppermute | solution.py:50
  1150.6 52.8 %collective-permute-start.21 = (bf16[2,256,512]{2,1,0:T(8,128)(2,1)}, bf16[2,256,512]{2,1,0:T(8,128)(2,1)}, u32[]{:S(2)}, u32[]{:S(2)}) collective-permute-start(bf16[2,256,512]{2,1,0:T(8,128)(2,1)} %dynamic-slice_bitcast_fusion.10), channel_id=1, source_target_pairs={{0,8},{8,0},{4,12},{12,4},{1,9},{9,1},{5,13},{13,5},{2,10},{10,2},... | collective-permute-start | bytes 1572872 | tf_op jit(solution)/shard_map/ppermute | solution.py:46
  1204.7 36.8 %collective-permute-start.22 = (bf16[2,256,512]{2,1,0:T(8,128)(2,1)S(1)}, bf16[2,256,512]{2,1,0:T(8,128)(2,1)S(1)}, u32[]{:S(2)}, u32[]{:S(2)}) collective-permute-start(bf16[2,256,512]{2,1,0:T(8,128)(2,1)S(1)} %fusion.59), channel_id=1, source_target_pairs={{0,0},{1,8},{2,16},{3,24},{4,4},{5,12},{6,20},{7,28},{8,1},{9,9},{... | collective-permute-start | bytes 1572872 | tf_op jit(solution)/shard_map/ppermute | solution.py:87
  (110 other events, 1626.2 us)
Sparse Core Ops, SparseCore 0:
  19.5 104.7 all-gather.7
  163.7 125.4 all-gather.13
  291.4 148.8 all-gather.15
  467.7 34.9 all-reduce.5
  651.0 78.1 all-gather.11
  731.2 124.4 all-gather.9
  858.1 139.4 reduce-scatter.1
  1152.7 49.7 all-reduce.7

commit v5 on v4

--- a/solution.py
+++ b/solution.py
@@ -159,14 +159,14 @@
     )(a, b)
 
 
-def exchange_kernel(units, axes, *refs):
+def exchange_kernel(units, whole, axes, *refs):
     count = len(axes)
-    partials, shard_refs = refs[:units], refs[units : units + count]
-    outs = refs[units + count : 2 * units + count]
-    fulls = refs[2 * units + count : 2 * units + 2 * count]
-    held, got, load_sem, send_sem, recv_sem, own_sem, near_send, near_recv = refs[
-        2 * units + 2 * count :
-    ]
+    inputs, refs = refs[: units + whole + count], refs[units + whole + count :]
+    partials, pieces, shard_refs = inputs[:units], inputs[units : units + whole], inputs[units + whole :]
+    outputs, refs = refs[: units + whole + count], refs[units + whole + count :]
+    outs, wides, fulls = outputs[:units], outputs[units : units + whole], outputs[units + whole :]
+    held, got, load_sem, send_sem, recv_sem, own_sem, near_send, near_recv = refs[:8]
+    piece_own, piece_send, piece_recv = refs[8:]
     x, stream, z = lax.axis_index("dp"), lax.axis_index("stream"), lax.axis_index("head")
     core = lax.rem(stream, 2)
     other_x, other_y, other_core = 1 - x, lax.rem(stream + 2, 4), stream + 1 - 2 * core
@@ -260,6 +260,15 @@
             load(u, b).start()
     for w in range(count):
         first(w)
+
+    def columns(block):
+        return pl.ds(pl.multiple_of(block * feats, feats), feats)
+
+    def keep(v):
+        return pltpu.make_async_copy(pieces[v], wides[v].at[:, columns(z)], piece_own.at[v])
+
+    for v in range(whole):
+        keep(v).start()
     for u in range(units):
         for b in range(4):
             load(u, b).wait()
@@ -279,6 +288,20 @@
 
     ways = ((0, z), (1, 3 - z))
 
+    def relay(way, v, step, block, c):
+        target = wides[v].at[part(c), columns(block)]
+        return pltpu.make_async_remote_copy(
+            src_ref=pieces[v].at[part(c)] if step == 0 else target,
+            dst_ref=target,
+            send_sem=piece_send.at[way, v, step, c],
+            recv_sem=piece_recv.at[way, v, step, c],
+            device_id=line[way],
+            device_id_type=pl.DeviceIdType.MESH,
+        )
+
+    def piece_at(way, step):
+        return z - step if way == 0 else z + step
+
     def block_at(way, step):
         return 3 - step + z if way == 0 else step + z - 3
 
@@ -301,6 +324,14 @@
                                 held[u, block, part(c)] = total.astype(BF16)
 
                         hop(way, u, step, block, c).start()
+
+                @pl.when((rank >= step) & (rank < 3))
+                def _():
+                    block = piece_at(way, step)
+                    for v in range(whole):
+                        if step > 0:
+                            relay(way, v, step - 1, block, c).wait_recv()
+                        relay(way, v, step, block, c).start()
 
             return carry
 
@@ -326,6 +357,14 @@
                     hop(way, u, 2, z, c).wait_recv()
                     outs[u][part(c)] += got[way, u, 2, part(c)].astype(F32)
 
+        for way, rank in ways:
+
+            @pl.when(rank == 3)
+            def _():
+                for v in range(whole):
+                    for step in range(3):
+                        relay(way, v, step, piece_at(way, step + 1), c).wait_recv()
+
         return carry
 
     lax.fori_loop(0, chunk, finish, 0)
@@ -341,13 +380,20 @@
                     for u in range(units):
                         hop(way, u, step, block_at(way, step), c).wait_send()
 
+                @pl.when((rank >= step) & (rank < 3))
+                def _():
+                    for v in range(whole):
+                        relay(way, v, step, piece_at(way, step), c).wait_send()
+
         return carry
 
     lax.fori_loop(0, chunk, drain, 0)
-
-
-def exchange(partials, shards_in, axes, collective_id):
-    units, count = len(partials), len(shards_in)
+    for v in range(whole):
+        keep(v).wait()
+
+
+def exchange(partials, pieces, shards_in, axes, collective_id):
+    units, whole, count = len(partials), len(pieces), len(shards_in)
     tokens, feats = partials[0].shape[0], partials[0].shape[1] // 4
     chunk = 4
     full = [
@@ -357,10 +403,12 @@
     anywhere = pl.BlockSpec(memory_space=pl.ANY)
     sems = pltpu.SemaphoreType.DMA
     results = pl.pallas_call(
-        functools.partial(exchange_kernel, units, axes),
-        in_specs=[anywhere] * (units + count),
-        out_specs=[pl.BlockSpec(memory_space=pltpu.VMEM)] * units + [anywhere] * count,
-        out_shape=[jax.ShapeDtypeStruct((tokens, feats), F32)] * units + full,
+        functools.partial(exchange_kernel, units, whole, axes),
+        in_specs=[anywhere] * (units + whole + count),
+        out_specs=[pl.BlockSpec(memory_space=pltpu.VMEM)] * units + [anywhere] * (whole + count),
+        out_shape=[jax.ShapeDtypeStruct((tokens, feats), F32)] * units
+        + [jax.ShapeDtypeStruct((tokens, 4 * feats), BF16)] * whole
+        + full,
         scratch_shapes=[
             pltpu.VMEM((units, 4, tokens, feats), BF16),
             pltpu.VMEM((2, units, 3, tokens, feats), BF16),
@@ -370,6 +418,9 @@
             sems((max(count, 1),)),
             sems((max(count, 1), 9)),
             sems((max(count, 1), 9)),
+            sems((whole,)),
+            sems((2, whole, 3, chunk)),
+            sems((2, whole, 3, chunk)),
         ],
         compiler_params=pltpu.CompilerParams(
             collective_id=collective_id,
@@ -380,8 +431,8 @@
             flops=0, bytes_accessed=600 * 1024 * 1024, transcendentals=0
         ),
         name="exchange",
-    )(*partials, *shards_in)
-    return results[:units], results[units:]
+    )(*partials, *pieces, *shards_in)
+    return results[:units], results[units : units + whole], results[units + whole :]
 
 
 def head_sum_kernel(members, x_ref, out_ref, slots, send_sem, recv_sem):
@@ -430,6 +481,50 @@
         ],
         compiler_params=pltpu.CompilerParams(collective_id=collective_id, has_side_effects=True),
         name="sum_over_head",
+    )(x)
+
+
+def plane_sum_kernel(x_ref, out_ref, got, send_sem, recv_sem):
+    x, stream = lax.axis_index("dp"), lax.axis_index("stream")
+    peers = (
+        {"stream": stream + 1 - 2 * lax.rem(stream, 2)},
+        {"stream": lax.rem(stream + 2, 4)},
+        {"dp": 1 - x},
+    )
+    barrier = pltpu.get_barrier_semaphore()
+    for peer in peers:
+        pl.semaphore_signal(barrier, inc=1, device_id=peer, device_id_type=pl.DeviceIdType.MESH)
+    pl.semaphore_wait(barrier, 3)
+    out_ref[...] = x_ref[...]
+    for step, peer in enumerate(peers):
+        copy = pltpu.make_async_remote_copy(
+            src_ref=out_ref,
+            dst_ref=got.at[step],
+            send_sem=send_sem.at[step],
+            recv_sem=recv_sem.at[step],
+            device_id=peer,
+            device_id_type=pl.DeviceIdType.MESH,
+        )
+        copy.start()
+        copy.wait()
+        out_ref[...] += got[step]
+
+
+def plane_sum(x, collective_id):
+    if not paired():
+        return lax.psum(x.astype(BF16), ("dp", "stream")).astype(F32)
+    return pl.pallas_call(
+        plane_sum_kernel,
+        out_shape=jax.ShapeDtypeStruct(x.shape, F32),
+        in_specs=[pl.BlockSpec(memory_space=pltpu.VMEM)],
+        out_specs=pl.BlockSpec(memory_space=pltpu.VMEM),
+        scratch_shapes=[
+            pltpu.VMEM((3,) + x.shape, F32),
+            pltpu.SemaphoreType.DMA((3,)),
+            pltpu.SemaphoreType.DMA((3,)),
+        ],
+        compiler_params=pltpu.CompilerParams(collective_id=collective_id, has_side_effects=True),
+        name="sum_over_plane",
     )(x)
 
 
@@ -569,6 +664,46 @@
     return jnp.sum(a, axis=1, keepdims=True)
 
 
+def streams_kernel(weights_ref, history_ref, streams_ref, stats_ref):
+    weights = weights_ref[...]
+    layers = [history_ref[j].astype(F32) for j in range(HIST)]
+    sums, squares = [], []
+    for s in range(4):
+        total = weights[:, s * HIST : s * HIST + 1] * layers[0]
+        for j in range(1, HIST):
+            total = total + weights[:, s * HIST + j : s * HIST + j + 1] * layers[j]
+        streams_ref[s] = total
+        sums.append(row_sum(total))
+        squares.append(row_sum(total * total))
+    stats_ref[...] = columns_of(sums + squares, weights.shape[0])
+
+
+def mix_streams(weights, history):
+    _, tokens, feats = history.shape
+    block = min(128, tokens)
+    return pl.pallas_call(
+        streams_kernel,
+        grid=(tokens // block,),
+        in_specs=[
+            pl.BlockSpec((block, weights.shape[1]), lambda i: (i, 0)),
+            pl.BlockSpec((HIST, block, feats), lambda i: (0, i, 0)),
+        ],
+        out_specs=[
+            pl.BlockSpec((4, block, feats), lambda i: (0, i, 0)),
+            pl.BlockSpec((block, 128), lambda i: (i, 0)),
+        ],
+        out_shape=[
+            jax.ShapeDtypeStruct((4, tokens, feats), F32),
+            jax.ShapeDtypeStruct((tokens, 128), F32),
+        ],
+        compiler_params=pltpu.CompilerParams(vmem_limit_bytes=40 * 1024 * 1024),
+        cost_estimate=pl.CostEstimate(
+            flops=80 * tokens * feats, bytes_accessed=34 * tokens * feats, transcendentals=0
+        ),
+        name="mix_streams",
+    )(weights, history)
+
+
 def early_kernel(streams_ref, cot_ref, history_ref, out_ref):
     cot = cot_ref[...].astype(F32)
     plain, crossed, direct = [], [], []
@@ -772,7 +907,7 @@
     )
 
     cot_rows = cotangent.reshape(tokens, feats).astype(F32) * valid
-    out_full = lax.all_gather(cot_rows.astype(BF16), "head", axis=1, tiled=True)
+    cot_bf = cot_rows.astype(BF16)
     w_both = jnp.concatenate([w_attn_out, w_down])
     duplex = lined()
     kv_near = swap_head(w_qkv[1:]) if duplex else w_qkv[:1]
@@ -783,7 +918,8 @@
     mixed = lax.dot_general(w_mix_in, current, (((0,), (1,)), ((), ())), preferred_element_type=F32)
     square = jnp.sum(current_f * current_f, axis=1)[None]
     mixed = head_sum(jnp.concatenate([mixed, square]), 0).T
-    mixed, kv_near = lax.optimization_barrier((mixed, kv_near))
+    mixed, kv_near, cot_bf = lax.optimization_barrier((mixed, kv_near, cot_bf))
+    out_full = lax.all_gather(cot_bf, "head", axis=1, tiled=True)
     if duplex:
         kv_near = jnp.stack([kv_near, over_x(kv_near)])
         kv_near = jnp.concatenate([kv_near, over_y(kv_near)])
@@ -791,22 +927,11 @@
     mix_pre = mixed[:, : 4 * HIST] * rms_scale
     mix_hidden = gelu_exact(mix_pre)
     mix_weights = jnp.dot(mix_hidden, w_mix_out_f, precision=HIGHEST) + mix_bias.reshape(-1)
-    weights_four = mix_weights.reshape(tokens, 4, HIST)
-    streams = jnp.zeros((4, tokens, feats), F32)
-    for layer in range(HIST):
-        streams = (
-            streams
-            + jnp.transpose(weights_four[:, :, layer])[:, :, None]
-            * history[layer].astype(F32)[None]
-        )
-    stats = head_sum(
-        jnp.concatenate([jnp.sum(streams, axis=2), jnp.sum(streams * streams, axis=2)]), 1
-    )
+    streams, stats = mix_streams(mix_weights, history)
+    stats = head_sum(stats[:, :8].T, 1)
     stat_sum, stat_square = stats[:4], stats[4:]
-    early = early_sums(streams, cot_rows.astype(BF16), history)
-    stat_sum, stat_square, out_full, kv_near, early = lax.optimization_barrier(
-        (stat_sum, stat_square, out_full, kv_near, early)
-    )
+    early = early_sums(streams, cot_bf, history)
+    stat_sum, stat_square, kv_near = lax.optimization_barrier((stat_sum, stat_square, kv_near))
     row_means = (stat_sum / model_width)[:, :, None]
     inv_std = lax.rsqrt(stat_square[:, :, None] / model_width - row_means * row_means + EPSILON)
     centered = (streams - row_means) * inv_std
@@ -819,9 +944,12 @@
 
     if duplex:
         w_kv = row_weight(w_qkv[1:], kv_near)
-        k_in, v_in, up_in, q_in = normed[1], normed[2], all_features(3), all_features(0)
-        (key_pre, value_pre), (wq, up_full, both_full) = exchange(
-            [dot(k_in, w_kv[0]).astype(BF16), dot(v_in, w_kv[1]).astype(BF16)],
+        k_in, v_in = normed[1], normed[2]
+        partials = [dot(k_in, w_kv[0]).astype(BF16), dot(v_in, w_kv[1]).astype(BF16)]
+        partials, out_full = lax.optimization_barrier((partials, out_full))
+        (key_pre, value_pre), (up_in, q_in), (wq, up_full, both_full) = exchange(
+            partials,
+            [normed[3], normed[0]],
             [w_qkv[0], w_up, w_both],
             (0, 0, 1),
             4,
@@ -842,6 +970,21 @@
     key_blocks = exchange_rows(by_micro(keys))
     value_blocks = exchange_rows(by_micro(values))
     places = member ^ jnp.arange(4, dtype=jnp.int32)
+
+    def to_owner(partial):
+        return lax.psum_scatter(
+            partial.astype(BF16), "head", scatter_dimension=1, tiled=True
+        ).astype(F32)
+
+    up_pre = dot(up_in, up_full)
+    below = 0.5 * (1.0 + lax.erf(up_pre * 0.5**0.5))
+    slope = below + up_pre * jnp.exp(-0.5 * up_pre * up_pre) * (2.0 * jnp.pi) ** -0.5
+    gated_up, slope = lax.optimization_barrier(((up_pre * below).astype(BF16), slope))
+    d_up = (dot_nt(out_full, down_full) * slope).astype(BF16)
+    d_up_in = dot_nt(d_up, up_full).astype(BF16)
+    queries, d_up, gated_up, d_up_in = lax.optimization_barrier((queries, d_up, gated_up, d_up_in))
+    g_up = to_owner(d_up_in)
+
     results = attention(
         places,
         by_micro(queries),
@@ -858,27 +1001,12 @@
     d_key_pre = rotate(d_keys, tables, -1.0)
     d_value_pre = d_values.astype(BF16)
 
-    up_pre = dot(up_in, up_full)
-    below = 0.5 * (1.0 + lax.erf(up_pre * 0.5**0.5))
-    slope = below + up_pre * jnp.exp(-0.5 * up_pre * up_pre) * (2.0 * jnp.pi) ** -0.5
-    gated_up, slope = lax.optimization_barrier(((up_pre * below).astype(BF16), slope))
-    d_up = (dot_nt(out_full, down_full) * slope).astype(BF16)
-
-    def to_owner(partial):
-        return lax.psum_scatter(
-            partial.astype(BF16), "head", scatter_dimension=1, tiled=True
-        ).astype(F32)
-
-    g_up = to_owner(dot_nt(d_up, up_full))
     combined = dot(attended, w_out_full) + dot(gated_up, down_full)
     if duplex:
         partials = [dot_nt(d_query_pre, wq).astype(BF16), combined.astype(BF16)]
-        partials, d_key_pre, d_value_pre = lax.optimization_barrier(
-            (partials, d_key_pre, d_value_pre)
+        (g_query, branch), (d_key_full, d_value_full), _ = exchange(
+            partials, [d_key_pre, d_value_pre], [], (), 5
         )
-        (g_query, branch), _ = exchange(partials, [], (), 5)
-        d_key_full = lax.all_gather(d_key_pre, "head", axis=1, tiled=True)
-        d_value_full = lax.all_gather(d_value_pre, "head", axis=1, tiled=True)
         g_key, g_value = dot_nt(d_key_full, w_kv[0]), dot_nt(d_value_full, w_kv[1])
     else:
         g_query = to_owner(dot_nt(d_query_pre, wq))
@@ -933,7 +1061,7 @@
     grad_bias = jnp.sum(d_mix, axis=1)
     wide = lambda a: jnp.pad(a, ((0, 0), (0, feats - a.shape[1])))
     small = jnp.concatenate([grad_w1, gain_shift, wide(grad_w2), wide(grad_bias[None])])
-    small = lax.psum(small.astype(BF16), ("dp", "stream")).astype(F32)
+    small = plane_sum(small, 6)
     n = 4 * HIST
     columns = jnp.concatenate(
         [mix_weights.T, coefs, rms_row, rms_row * rms_row * cross / model_width]
@@ -943,7 +1071,7 @@
         streams,
         row_stats,
         ln_gain,
-        cot_rows.astype(BF16),
+        cot_bf,
         current,
         columns,
         (d_pre * rms_row).T,

time: 1260 us -> 1190 us (0.944)
  waiting for transfers between devices: 140 us -> 231 us
  Pallas kernels: 710 us -> 622 us
  other arithmetic: 109 us -> 73 us
  starting transfers between devices: 41.5 us -> 25.8 us
  matrix products: 147 us -> 133 us
    ppermute x5, waiting for transfers between devices: 28.8 us -> 120 us  [over_x(): return lax.ppermute(a, 'dp', SWAP_X)]
    pallas_call x2 -> x4, Pallas kernels: 517 us -> 437 us  [the longest x2 407 us: exchange(): pl.pallas_call(functools.partial(exchange_kernel, units, whole, axes), in...]
    all_gather x5 -> x1, waiting for transfers between devices: 0.03 us -> 44.5 us  [shards(): out_full = lax.all_gather(cot_bf, 'head', axis=1, tiled=True)]
    ppermute x2, waiting for transfers between devices: 28.6 us -> 0.01 us  [swap_head(): return lax.ppermute(a, ('dp', 'stream', 'head'), pairs)]
    ppermute x2, waiting for transfers between devices: 21.2 us -> 0.01 us  [exchange_rows(): across = lax.ppermute(local, 'stream', [(0, 2), (1, 3)])]
    ppermute x5, waiting for transfers between devices: 11.5 us -> 30.3 us  [over_y(): return lax.ppermute(a, 'stream', SWAP_Y)]
    convert_element_type x7 -> x1, other arithmetic: 17 us -> 0.32 us  [shards(): cot_bf = cot_rows.astype(BF16)]
    psum x1 -> x0, waiting for transfers between devices: 16.6 us -> none  [shards(): small = lax.psum(small.astype(BF16), ('dp', 'stream')).astype(F32)]
  transfers between devices with their start and end apart: 37 -> 32, of which waited for: 9 -> 10; matrix products, arithmetic and copies ran while one was open for 23% -> 19% of each run, Pallas kernels for 57% -> 27%
where the time goes in v5:
time: 1190 us; the launch traced here: 1180 us
  Pallas kernels  622 us (52%)
  waiting for transfers between devices  231 us (19%)
  matrix products  133 us (11%)
  local copies, waits for them, and re-layouts  80 us (7%)
  other arithmetic  73 us (6%)
  starting transfers between devices  25.8 us (2%)
  between operations  15.4 us (1%)
    pallas_call x2, Pallas kernels, exchange(): pl.pallas_call(functools.partial(exchange_kernel, units, whole, axes), in...  407 us
    ppermute x5, waiting for transfers between devices, over_x(): return lax.ppermute(a, 'dp', SWAP_X)  120 us
    pallas_call x3, Pallas kernels, head_sum(): pl.pallas_call(functools.partial(head_sum_kernel, members), out_shape=jax...  70.6 us
    dot_general x6, matrix products, dot(): return jnp.dot(a, b, preferred_element_type=F32)  52.2 us
    pallas_call x1, Pallas kernels, attention(): pl.pallas_call(attention_kernel, grid=(micro, feats // HD), in_specs=[pl....  45.1 us
    all_gather x1, waiting for transfers between devices, shards(): out_full = lax.all_gather(cot_bf, 'head', axis=1, tiled=True)  44.5 us
    dot_general x6, matrix products, dot_nt(): lax.dot_general(a, b, (((1,), (1,)), ((), ())), preferred_element_type=F32)  42.6 us
    ppermute x2, waiting for transfers between devices, reduce_rows(): lax.ppermute(across, 'stream', [(2, 0), (3, 1)])  36.3 us
  transfers between devices with their start and end apart: 32, of which 10 were waited for; matrix products, arithmetic and copies ran while one was open for 19% of the time, Pallas kernels for 27%

profile of v5, /device:TPU:8, one launch (start us, length us, event | category | flops | bytes accessed | tf_op | source)
XLA Modules:
  0.0 1180.8 jit_solution(515087949307997182)
XLA Ops:
  19.3 38.4 %sum_over_head.3 = f32[37,1024]{1,0:T(8,128)} custom-call(f32[37,1024]{1,0:T(8,128)} %pad_maximum_fusion.6.x_ref), custom_call_target="tpu_custom_call" | custom-call | tf_op jit(solution)/shard_map/sum_over_head/pallas_call | solution.py:472
  64.2 12.5 %mix_streams.1 = (f32[4,1024,512]{2,1,0:T(8,128)S(1)}, f32[1024,128]{1,0:T(8,128)S(1)}) custom-call(f32[1024,36]{1,0:T(8,128)S(1)} %convolution_add_fusion.weights_ref, bf16[9,1024,512]{2,1,0:T(8,128)(2,1)} %bitcast.239), custom_call_target="tpu_custom_call" | custom-call | flops 41943040 | bytes 17825792 | tf_op jit(solution)/shard_map/mix_streams/pallas_call | solution.py:684
  76.7 12.6 %early_sums.1 = f32[1024,128]{1,0:T(8,128)S(1)} custom-call(f32[4,1024,512]{2,1,0:T(8,128)S(1)} %get-tuple-element.53.streams_ref, bf16[1024,512]{1,0:T(8,128)(2,1)S(1)} %fusion.26.cot_ref, bf16[9,1024,512]{2,1,0:T(8,128)(2,1)} %bitcast.240), custom_call_target="tpu_custom_call" | custom-call | flops 57671680 | bytes 18874368 | tf_op jit(solution)/shard_map/early_sums/pallas_call | solution.py:723
  115.2 13.2 %sum_over_head.4 = f32[8,1024]{1,0:T(8,128)} custom-call(f32[8,1024]{1,0:T(8,128)} %slice_bitcast_fusion.25.x_ref), custom_call_target="tpu_custom_call" | custom-call | tf_op jit(solution)/shard_map/sum_over_head/pallas_call | solution.py:472
  167.3 44.5 %all-gather.2.cloned.1.call-done = bf16[1024,2048]{1,0:T(8,128)(2,1)} async-done(((bf16[1024,512]{1,0:T(8,128)(2,1)}), bf16[1024,2048]{1,0:T(8,128)(2,1)}) %all-gather.2.cloned.1.call-update) | async-done | bytes 4194320 | tf_op jit(solution)/shard_map/all_gather | solution.py:922
  214.2 205.4 %exchange.2 = (f32[1024,512]{1,0:T(8,128)}, f32[1024,512]{1,0:T(8,128)}, bf16[1024,2048]{1,0:T(8,128)(2,1)}, bf16[1024,2048]{1,0:T(8,128)(2,1)}, bf16[2048,512]{...) custom-call(bf16[1024,2048]{1,0:T(8,128)(2,1)} %convolution_convert_fusion.5.refs_0_, ...), custom_call_target="tpu_custom_call" | custom-call | bytes 629145600 | tf_op jit(solution)/shard_map/exchange/pallas_call | solution.py:405
  432.6 17.9 %fusion.3 = (f32[1024,2048]{1,0:T(8,128)}, bf16[1024,2048]{1,0:T(8,128)(2,1)}) fusion(bf16[1024,2048]{1,0:T(8,128)(2,1)} %get-tuple-element.66, bf16[2048,2048]{1,0:T(8,128)(2,1)} %get-tuple-element.67), kind=kOutput, calls=%fused_computation.4 | convolution fusion | flops 8610906112 | bytes 25165824 | tf_op jit(solution)/shard_map/dot_general | solution.py:26
  450.6 12.1 %multiply_convert_fusion = bf16[1024,2048]{1,0:T(8,128)(2,1)} fusion(f32[1024,2048]{1,0:T(8,128)} %get-tuple-element.68, bf16[1024,2048]{1,0:T(8,128)(2,1)S(1)} %copy-done.64, bf16[2560,2048]{1,0:T(8,128)(2,1)S(1)} %bitcast.294), kind=kOutput, calls=%fused_computation.10 | convolution fusion | flops 8594128896 | bytes 25165824 | tf_op jit(solution)/shard_map/dot_general | solution.py:30
  462.7 14.0 %convolution_convert_fusion.3 = bf16[1024,2048]{1,0:T(8,128)(2,1)} fusion(bf16[1024,2048]{1,0:T(8,128)(2,1)} %multiply_convert_fusion, bf16[2048,2048]{1,0:T(8,128)(2,1)} %get-tuple-element.67), kind=kOutput, calls=%fused_computation.39 | convolution fusion | flops 8592031744 | bytes 16777216 | tf_op jit(solution)/shard_map/dot_general | solution.py:30
  482.7 9.8 convolution_convert_fusion
  498.8 11.2 convolution_convert_fusion.1
  510.6 11.2 fusion.6
  532.8 45.1 %attention_both_ways.1 = (bf16[2,512,512]{2,1,0:T(8,128)(2,1)S(1)}, bf16[2,512,512]{2,1,0:T(8,128)(2,1)S(1)}, bf16[2,512,512]{2,1,0:T(8,128)(2,1)S(1)}, bf16[2,5...) custom-call(s32[4]{0:T(128)S(1)} %iota_xor_fusion.place_ref, ...), custom_call_target="tpu_custom_call" | custom-call | flops 12884901888 | bytes 20971520 | tf_op jit(solution)/shard_map/attention_both_ways/pallas_call | solution.py:616
  602.9 16.1 %collective-permute-done.12 = bf16[2,512,512]{2,1,0:T(8,128)(2,1)S(1)} collective-permute-done((bf16[2,512,512]{2,1,0:T(8,128)(2,1)S(1)}, bf16[2,512,512]{2,1,0:T(8,128)(2,1)S(1)}, u32[]{:S(2)}, u32[]{:S(2)}) %collective-permute-start.12) | collective-permute-done | bytes 1048608 | tf_op jit(solution)/shard_map/ppermute | solution.py:651
  620.8 20.2 %collective-permute-done.15 = bf16[2,512,512]{2,1,0:T(8,128)(2,1)S(1)} collective-permute-done((bf16[2,512,512]{2,1,0:T(8,128)(2,1)S(1)}, bf16[2,512,512]{2,1,0:T(8,128)(2,1)S(1)}, u32[]{:S(2)}, u32[]{:S(2)}) %collective-permute-start.15) | collective-permute-done | bytes 1048608 | tf_op jit(solution)/shard_map/ppermute | solution.py:651
  647.1 201.3 %exchange.3 = (f32[1024,512]{1,0:T(8,128)S(1)}, f32[1024,512]{1,0:T(8,128)}, bf16[1024,2048]{1,0:T(8,128)(2,1)}, bf16[1024,2048]{1,0:T(8,128)(2,1)}) custom-call(bf16[1024,2048]{1,0:T(8,128)(2,1)} %convolution_convert_fusion.2.refs_0_, bf16[1024,2048]{1,0:T(8,128)(2,1)} %add_convert_fusion.refs_1_, bf16[1024,512]{1,0:T(8,128)(2,1)S(1)} %copy-done.20, ...), custom_call_target="tpu_custom_call" | custom-call | bytes 629145600 | tf_op jit(solution)/shard_map/exchange/pallas_call | solution.py:405
  884.5 9.8 collective-permute-done.17
  900.1 39.1 %collective-permute-done.27 = bf16[1,2,256,2048]{3,2,1,0:T(8,128)(2,1)} collective-permute-done((bf16[1,2,256,2048]{3,2,1,0:T(8,128)(2,1)}, bf16[1,2,256,2048]{3,2,1,0:T(8,128)(2,1)}, u32[]{:S(2)}, u32[]{:S(2)}) %collective-permute-start.27) | collective-permute-done | bytes 2097184 | tf_op jit(solution)/shard_map/ppermute | solution.py:42
  942.6 62.0 %collective-permute-done.20 = bf16[2,2,256,512]{3,2,0,1:T(8,128)(2,1)S(1)} collective-permute-done((bf16[2,2,256,512]{3,2,0,1:T(8,128)(2,1)S(1)}, bf16[2,2,256,512]{3,2,0,1:T(8,128)(2,1)S(1)}, u32[]{:S(2)}, u32[]{:S(2)}) %collective-permute-start.20) | collective-permute-done | bytes 1048608 | tf_op jit(solution)/shard_map/ppermute | solution.py:42
  1034.7 16.1 %collective-permute-done.25 = bf16[1,256,2048]{2,1,0:T(8,128)(2,1)} collective-permute-done((bf16[1,256,2048]{2,1,0:T(8,128)(2,1)}, bf16[1,256,2048]{2,1,0:T(8,128)(2,1)}, u32[]{:S(2)}, u32[]{:S(2)}) %collective-permute-start.25) | collective-permute-done | bytes 1048608 | tf_op jit(solution)/shard_map/ppermute | solution.py:46
  1063.3 15.0 %gradient_sums.1 = (f32[1024,128]{1,0:T(8,128)S(1)}, f32[8,512]{1,0:T(8,128)S(1)}) custom-call(f32[1024,512]{1,0:T(8,128)S(1)} %copy-done.8, f32[1024,512]{1,0:T(8,128)S(1)} %copy-done.12, f32[1024,512]{1,0:T(8,128)S(1)} %copy-done.10, f32[1024,512]{1,0:T(8,128)S(1)} %convert_element_type.371.g3, f32[4,1024,512]{2,1,0:T(8,128)} %copy-done.1, ...), custom_call_target="tpu_custom_call" | custom-call | flops 57671680 | bytes 22020096 | tf_op jit(solution)/shard_map/gradient_sums/pallas_call | solution.py:767
  1079.2 19.0 %sum_over_head.5 = f32[44,1024]{1,0:T(8,128)} custom-call(f32[44,1024]{1,0:T(8,128)} %slice_bitcast_fusion.23.x_ref), custom_call_target="tpu_custom_call" | custom-call | tf_op jit(solution)/shard_map/sum_over_head/pallas_call | solution.py:472
  1114.2 17.8 %sum_over_plane.1 = f32[81,512]{1,0:T(8,128)} custom-call(f32[81,512]{1,0:T(8,128)} %select_maximum_fusion.x_ref), custom_call_target="tpu_custom_call" | custom-call | tf_op jit(solution)/shard_map/sum_over_plane/pallas_call | solution.py:516
  1156.9 17.1 %history_gradient.1 = f32[9,1024,512]{2,1,0:T(8,128)} custom-call(f32[1024,512]{1,0:T(8,128)S(1)} %copy-done.9, f32[1024,512]{1,0:T(8,128)S(1)} %copy-done.13, f32[1024,512]{1,0:T(8,128)S(1)} %copy-done.11, f32[1024,512]{1,0:T(8,128)S(1)} %convert_element_type.371.g3, f32[4,1024,512]{2,1,0:T(8,128)} %copy-done.1, f32[1024,8]{1,0:T(8,128)S(1)} %copy-done.16, ...), custom_call_target="tpu_custom_call" | custom-call | flops 57671680 | bytes 33554432 | tf_op jit(solution)/shard_map/history_gradient/pallas_call | solution.py:838
  (402 shorter events, 284.2 us)
Async XLA Ops:
  7.2 133.9 %all-reduce.5.cloned.1.call-start = ((), (), s32[]{:S(2)}) async-start(), calls=%async_computation.3 | async-start | bytes 1048576 | tf_op jit(solution)/shard_map/psum | solution.py:939
  9.2 51.8 %collective-permute-start = (bf16[2,256,512]{2,1,0:T(8,128)(2,1)}, bf16[2,256,512]{2,1,0:T(8,128)(2,1)}, u32[]{:S(2)}, u32[]{:S(2)}) collective-permute-start(bf16[2,256,512]{2,1,0:T(8,128)(2,1)} %slice.132), channel_id=1, source_target_pairs={{0,0},{1,8},{2,16},{3,24},{4,4},{5,12},{6,20},{7,28},{8,1},{9,9},{... | collective-permute-start | bytes 1572872 | tf_op jit(solution)/shard_map/ppermute | solution.py:87
  90.2 121.6 %all-gather.2.cloned.1.call-start = ((), (), s32[]{:S(2)}) async-start(), calls=%async_computation.1 | async-start | bytes 5242880 | tf_op jit(solution)/shard_map/all_gather | solution.py:922
  91.1 965.9 %reduce-scatter.2.cloned.1.call-start = ((), (), s32[]{:S(2)}) async-start(), calls=%async_computation.2 | async-start | bytes 5242880 | tf_op jit(solution)/shard_map/reduce_scatter | solution.py:975
  111.5 23.6 %collective-permute-start.2 = (bf16[2,2,256,512]{3,2,1,0:T(8,128)(2,1)}, bf16[2,2,256,512]{3,2,1,0:T(8,128)(2,1)}, u32[]{:S(2)}, u32[]{:S(2)}) collective-permute-start(bf16[2,2,256,512]{3,2,1,0:T(8,128)(2,1)} %pad_maximum_fusion.5), channel_id=1, source_target_pairs={{0,8},{8,0},{4,12},{12,4},{1,9},{9,1},{5,13},{13,5},{2,10},{10,2},... | collective-permute-start | bytes 3145736 | tf_op jit(solution)/shard_map/ppermute | solution.py:46
  424.2 85.7 %collective-permute-start.5 = (bf16[2,512,512]{2,1,0:T(8,128)(2,1)}, bf16[2,512,512]{2,1,0:T(8,128)(2,1)}, u32[]{:S(2)}, u32[]{:S(2)}) collective-permute-start(bf16[2,512,512]{2,1,0:T(8,128)(2,1)} %bitcast.273), channel_id=1, source_target_pairs={{0,8},{4,12},{1,9},{5,13},{2,10},{6,14},{3,11},{7,15},{16,24},{20,... | collective-permute-start | bytes 3145736 | tf_op jit(solution)/shard_map/ppermute | solution.py:642
  428.6 102.8 %collective-permute-start.4 = (bf16[2,512,512]{2,1,0:T(8,128)(2,1)}, bf16[2,512,512]{2,1,0:T(8,128)(2,1)}, u32[]{:S(2)}, u32[]{:S(2)}) collective-permute-start(bf16[2,512,512]{2,1,0:T(8,128)(2,1)} %bitcast.274), channel_id=1, source_target_pairs={{0,4},{4,0},{8,12},{12,8},{1,5},{5,1},{9,13},{13,9},{2,6},{6,2},{1... | collective-permute-start | bytes 3145736 | tf_op jit(solution)/shard_map/ppermute | solution.py:50
  429.7 80.8 %collective-permute-start.8 = (bf16[2,512,512]{2,1,0:T(8,128)(2,1)}, bf16[2,512,512]{2,1,0:T(8,128)(2,1)}, u32[]{:S(2)}, u32[]{:S(2)}) collective-permute-start(bf16[2,512,512]{2,1,0:T(8,128)(2,1)} %bitcast.30.refs_4_), channel_id=1, source_target_pairs={{0,8},{4,12},{1,9},{5,13},{2,10},{6,14},{3,11},{7,15},{16,24},{20,... | collective-permute-start | bytes 3145736 | tf_op jit(solution)/shard_map/ppermute | solution.py:642
  432.1 99.3 %collective-permute-start.7 = (bf16[2,512,512]{2,1,0:T(8,128)(2,1)}, bf16[2,512,512]{2,1,0:T(8,128)(2,1)}, u32[]{:S(2)}, u32[]{:S(2)}) collective-permute-start(bf16[2,512,512]{2,1,0:T(8,128)(2,1)} %bitcast.30.refs_4_), channel_id=1, source_target_pairs={{0,4},{4,0},{8,12},{12,8},{1,5},{5,1},{9,13},{13,9},{2,6},{6,2},{1... | collective-permute-start | bytes 3145736 | tf_op jit(solution)/shard_map/ppermute | solution.py:50
  498.8 370.2 %collective-permute-start.26 = (bf16[1,4,256,2048]{3,2,1,0:T(8,128)(2,1)}, bf16[1,4,256,2048]{3,2,1,0:T(8,128)(2,1)}, u32[]{:S(2)}, u32[]{:S(2)}) collective-permute-start(bf16[1,4,256,2048]{3,2,1,0:T(8,128)(2,1)} %dynamic-slice_bitcast_fusion), channel_id=1, source_target_pairs={{0,4},{4,0},{8,12},{12,8},{1,5},{5,1},{9,13},{13,9},{2,6},{6,2},{1... | collective-permute-start | bytes 12582920 | tf_op jit(solution)/shard_map/ppermute | solution.py:50
  583.4 37.4 %collective-permute-start.13 = (bf16[2,512,512]{2,1,0:T(8,128)(2,1)S(1)}, bf16[2,512,512]{2,1,0:T(8,128)(2,1)S(1)}, u32[]{:S(2)}, u32[]{:S(2)}) collective-permute-start(bf16[2,512,512]{2,1,0:T(8,128)(2,1)S(1)} %get-tuple-element.81), channel_id=1, source_target_pairs={{0,4},{4,0},{8,12},{12,8},{1,5},{5,1},{9,13},{13,9},{2,6},{6,2},{1... | collective-permute-start | bytes 3145736 | tf_op jit(solution)/shard_map/ppermute | solution.py:50
  591.2 27.9 %collective-permute-start.12 = (bf16[2,512,512]{2,1,0:T(8,128)(2,1)S(1)}, bf16[2,512,512]{2,1,0:T(8,128)(2,1)S(1)}, u32[]{:S(2)}, u32[]{:S(2)}) collective-permute-start(bf16[2,512,512]{2,1,0:T(8,128)(2,1)S(1)} %add_convert_fusion.4), channel_id=1, source_target_pairs={{8,0},{12,4},{9,1},{13,5},{10,2},{14,6},{11,3},{15,7},{24,16},{28,... | collective-permute-start | bytes 3145736 | tf_op jit(solution)/shard_map/ppermute | solution.py:651
  592.8 48.2 %collective-permute-start.15 = (bf16[2,512,512]{2,1,0:T(8,128)(2,1)S(1)}, bf16[2,512,512]{2,1,0:T(8,128)(2,1)S(1)}, u32[]{:S(2)}, u32[]{:S(2)}) collective-permute-start(bf16[2,512,512]{2,1,0:T(8,128)(2,1)S(1)} %add_convert_fusion.3), channel_id=1, source_target_pairs={{8,0},{12,4},{9,1},{13,5},{10,2},{14,6},{11,3},{15,7},{24,16},{28,... | collective-permute-start | bytes 3145736 | tf_op jit(solution)/shard_map/ppermute | solution.py:651
  602.5 276.8 %collective-permute-start.23 = (bf16[1,4,256,2048]{3,2,1,0:T(8,128)(2,1)}, bf16[1,4,256,2048]{3,2,1,0:T(8,128)(2,1)}, u32[]{:S(2)}, u32[]{:S(2)}) collective-permute-start(bf16[1,4,256,2048]{3,2,1,0:T(8,128)(2,1)} %dynamic-slice_bitcast_fusion.1), channel_id=1, source_target_pairs={{0,4},{4,0},{8,12},{12,8},{1,5},{5,1},{9,13},{13,9},{2,6},{6,2},{1... | collective-permute-start | bytes 12582920 | tf_op jit(solution)/shard_map/ppermute | solution.py:50
  619.1 245.5 %collective-permute-start.16 = (bf16[2,4,256,512]{3,2,1,0:T(8,128)(2,1)}, bf16[2,4,256,512]{3,2,1,0:T(8,128)(2,1)}, u32[]{:S(2)}, u32[]{:S(2)}) collective-permute-start(bf16[2,4,256,512]{3,2,1,0:T(8,128)(2,1)} %fusion.21), channel_id=1, source_target_pairs={{0,4},{4,0},{8,12},{12,8},{1,5},{5,1},{9,13},{13,9},{2,6},{6,2},{1... | collective-permute-start | bytes 6291464 | tf_op jit(solution)/shard_map/ppermute | solution.py:50
  859.5 36.2 %collective-permute-start.19 = (bf16[2,4,256,512]{3,2,1,0:T(8,128)(2,1)}, bf16[2,4,256,512]{3,2,1,0:T(8,128)(2,1)}, u32[]{:S(2)}, u32[]{:S(2)}) collective-permute-start(bf16[2,4,256,512]{3,2,1,0:T(8,128)(2,1)} %fusion.17), channel_id=1, source_target_pairs={{0,4},{4,0},{8,12},{12,8},{1,5},{5,1},{9,13},{13,9},{2,6},{6,2},{1... | collective-permute-start | bytes 6291464 | tf_op jit(solution)/shard_map/ppermute | solution.py:50
  867.8 26.4 %collective-permute-start.17 = (bf16[2,2,256,512]{3,2,1,0:T(8,128)(2,1)}, bf16[2,2,256,512]{3,2,1,0:T(8,128)(2,1)}, u32[]{:S(2)}, u32[]{:S(2)}) collective-permute-start(bf16[2,2,256,512]{3,2,1,0:T(8,128)(2,1)} %dynamic-slice_bitcast_fusion.9), channel_id=1, source_target_pairs={{0,16},{16,0},{1,17},{17,1},{2,18},{18,2},{3,19},{19,3},{4,20},{20... | collective-permute-start | bytes 3145736 | tf_op jit(solution)/shard_map/ppermute | solution.py:42
  874.1 65.0 %collective-permute-start.27 = (bf16[1,2,256,2048]{3,2,1,0:T(8,128)(2,1)}, bf16[1,2,256,2048]{3,2,1,0:T(8,128)(2,1)}, u32[]{:S(2)}, u32[]{:S(2)}) collective-permute-start(bf16[1,2,256,2048]{3,2,1,0:T(8,128)(2,1)} %dynamic-slice_bitcast_fusion.2), channel_id=1, source_target_pairs={{0,16},{16,0},{1,17},{17,1},{2,18},{18,2},{3,19},{19,3},{4,20},{20... | collective-permute-start | bytes 6291464 | tf_op jit(solution)/shard_map/ppermute | solution.py:42
  883.5 121.5 %collective-permute-start.24 = (bf16[1,2,256,2048]{3,2,1,0:T(8,128)(2,1)S(1)}, bf16[1,2,256,2048]{3,2,1,0:T(8,128)(2,1)S(1)}, u32[]{:S(2)}, u32[]{:S(2)}) collective-permute-start(bf16[1,2,256,2048]{3,2,1,0:T(8,128)(2,1)S(1)} %dynamic-slice_bitcast_fusion.3), channel_id=1, source_target_pairs={{0,16},{16,0},{1,17},{17,1},{2,18},{18,2},{3,19},{19,3},{4,20},{20... | collective-permute-start | bytes 6291464 | tf_op jit(solution)/shard_map/ppermute | solution.py:42
  898.0 106.5 %collective-permute-start.20 = (bf16[2,2,256,512]{3,2,0,1:T(8,128)(2,1)S(1)}, bf16[2,2,256,512]{3,2,0,1:T(8,128)(2,1)S(1)}, u32[]{:S(2)}, u32[]{:S(2)}) collective-permute-start(bf16[2,2,256,512]{3,2,0,1:T(8,128)(2,1)S(1)} %dynamic-slice_bitcast_fusion.8), channel_id=1, source_target_pairs={{0,16},{16,0},{1,17},{17,1},{2,18},{18,2},{3,19},{19,3},{4,20},{20... | collective-permute-start | bytes 3145736 | tf_op jit(solution)/shard_map/ppermute | solution.py:42
  899.2 110.2 %collective-permute-start.18 = (bf16[2,256,512]{2,1,0:T(8,128)(2,1)S(1)}, bf16[2,256,512]{2,1,0:T(8,128)(2,1)S(1)}, u32[]{:S(2)}, u32[]{:S(2)}) collective-permute-start(bf16[2,256,512]{2,1,0:T(8,128)(2,1)S(1)} %dynamic-slice_bitcast_fusion.11), channel_id=1, source_target_pairs={{0,8},{8,0},{4,12},{12,4},{1,9},{9,1},{5,13},{13,5},{2,10},{10,2},... | collective-permute-start | bytes 1572872 | tf_op jit(solution)/shard_map/ppermute | solution.py:46
  942.6 88.0 %collective-permute-start.28 = (bf16[1,256,2048]{2,1,0:T(8,128)(2,1)S(1)}, bf16[1,256,2048]{2,1,0:T(8,128)(2,1)}, u32[]{:S(2)}, u32[]{:S(2)}) collective-permute-start(bf16[1,256,2048]{2,1,0:T(8,128)(2,1)S(1)} %get-tuple-element.194), channel_id=1, source_target_pairs={{0,8},{8,0},{4,12},{12,4},{1,9},{9,1},{5,13},{13,5},{2,10},{10,2},... | collective-permute-start | bytes 3145736 | tf_op jit(solution)/shard_map/ppermute | solution.py:46
  1007.4 43.4 %collective-permute-start.25 = (bf16[1,256,2048]{2,1,0:T(8,128)(2,1)}, bf16[1,256,2048]{2,1,0:T(8,128)(2,1)}, u32[]{:S(2)}, u32[]{:S(2)}) collective-permute-start(bf16[1,256,2048]{2,1,0:T(8,128)(2,1)} %get-tuple-element.196), channel_id=1, source_target_pairs={{0,8},{8,0},{4,12},{12,4},{1,9},{9,1},{5,13},{13,5},{2,10},{10,2},... | collective-permute-start | bytes 3145736 | tf_op jit(solution)/shard_map/ppermute | solution.py:46
  1020.8 33.8 %collective-permute-start.22 = (bf16[2,256,512]{2,1,0:T(8,128)(2,1)}, bf16[2,256,512]{2,1,0:T(8,128)(2,1)}, u32[]{:S(2)}, u32[]{:S(2)}) collective-permute-start(bf16[2,256,512]{2,1,0:T(8,128)(2,1)} %fusion.40), channel_id=1, source_target_pairs={{0,0},{1,8},{2,16},{3,24},{4,4},{5,12},{6,20},{7,28},{8,1},{9,9},{... | collective-permute-start | bytes 1572872 | tf_op jit(solution)/shard_map/ppermute | solution.py:87
  (98 other events, 2384.9 us)
Sparse Core Ops, SparseCore 0:
  90.3 42.5 all-reduce.4
  134.5 77.2 all-gather.1
  521.9 76.0 reduce-scatter.1

commit v6 on v5

--- a/solution.py
+++ b/solution.py
@@ -54,19 +54,6 @@
     return lax.axis_size("dp") == 2 and lax.axis_size("stream") == 4
 
 
-def place_kernel(order_ref, near_ref, beside_ref, out_ref):
-    step = pl.program_id(0)
-    half = pl.num_programs(0) // 2
-
-    @pl.when(step < half)
-    def _():
-        out_ref[...] = near_ref[0]
-
-    @pl.when(step >= half)
-    def _():
-        out_ref[...] = beside_ref[0]
-
-
 def gather_weight(shard, axis):
     return lax.all_gather(shard, ("dp", "stream"), axis=axis, tiled=True)
 
@@ -75,65 +62,34 @@
     return paired() and lax.axis_size("head") == 4
 
 
-def swap_head(a):
-    at = lambda x, y, core, z: (x * 4 + y * 2 + core) * 4 + z
-    pairs = [
-        (at(x, y, core, z), at(z // 2, z % 2, core, 2 * x + y))
-        for x in range(2)
-        for y in range(2)
-        for core in range(2)
-        for z in range(4)
-    ]
-    return lax.ppermute(a, ("dp", "stream", "head"), pairs)
-
-
-def row_weight(shard, near):
-    place = lax.axis_index("dp") * 4 + lax.axis_index("stream")
-    beside = over_core(near)
-    flips = jnp.array([0, 4, 2, 6, 1, 5, 3, 7], jnp.int32)
-    count, rows, columns = shard.shape
-    piece = (1, count, rows, columns)
-    inner = (0, 0, 0)
-    return pl.pallas_call(
-        place_kernel,
-        grid_spec=pltpu.PrefetchScalarGridSpec(
-            num_scalar_prefetch=1,
-            grid=(8,),
-            in_specs=[
-                pl.BlockSpec(piece, lambda k, order: (jnp.minimum(k, 3),) + inner),
-                pl.BlockSpec(piece, lambda k, order: (jnp.maximum(k - 4, 0),) + inner),
-            ],
-            out_specs=pl.BlockSpec(
-                shard.shape,
-                lambda k, order: (0, lax.rem(order[k], 2), lax.div(order[k], 2)),
-            ),
-        ),
-        out_shape=jax.ShapeDtypeStruct((count, 2 * rows, 4 * columns), shard.dtype),
-        compiler_params=pltpu.CompilerParams(vmem_limit_bytes=40 * 1024 * 1024),
-        cost_estimate=pl.CostEstimate(flops=0, bytes_accessed=32 * shard.size, transcendentals=0),
-        name="weight_in_order",
-    )(place ^ flips, near, beside)
+def take(a, index, axis):
+    return lax.dynamic_index_in_dim(a, index, axis, keepdims=False)
+
+
+def add_bf(a, b):
+    return (a.astype(F32) + b.astype(F32)).astype(BF16)
+
+
+def chip_parts(partial):
+    count, rows, columns = partial.shape
+    core, x = lax.axis_index("stream") % 2, lax.axis_index("dp")
+    split = partial.reshape(count, 4, 2, rows // 8, columns)
+    chip = add_bf(take(split, core, 2), over_core(take(split, 1 - core, 2)))
+    chip = chip.reshape(count, 2, 2, rows // 8, columns)
+    return take(chip, x, 1), take(chip, 1 - x, 1)
+
+
+def plane_parts(stays, leaves):
+    y = lax.axis_index("stream") // 2
+    line = add_bf(stays, over_x(leaves))
+    return take(line, y, 1), over_y(take(line, 1 - y, 1))
 
 
 def scatter_parts(partial):
     if not paired():
         whole = lax.psum_scatter(partial, ("dp", "stream"), scatter_dimension=1, tiled=True)
         return whole, jnp.zeros_like(whole)
-    count, rows, columns = partial.shape
-    stream = lax.axis_index("stream")
-    x, y, core = lax.axis_index("dp"), stream // 2, stream % 2
-
-    def pick(a, index, axis):
-        return lax.dynamic_index_in_dim(a, index, axis, keepdims=False)
-
-    def add(a, b):
-        return (a.astype(F32) + b.astype(F32)).astype(BF16)
-
-    split = partial.reshape(count, 4, 2, rows // 8, columns)
-    chip = add(pick(split, core, 2), over_core(pick(split, 1 - core, 2)))
-    chip = chip.reshape(count, 2, 2, rows // 8, columns)
-    line = add(pick(chip, x, 1), over_x(pick(chip, 1 - x, 1)))
-    return pick(line, y, 1), over_y(pick(line, 1 - y, 1))
+    return plane_parts(*chip_parts(partial))
 
 
 def add_kernel(turned, a_ref, b_ref, out_ref):
@@ -178,18 +134,22 @@
     beside = lambda at: at + 1 - 2 * core
 
     barrier = pltpu.get_barrier_semaphore()
-    peers = line + ((to_x, to_y, to_core) if count else ())
+    peers = (line if units else ()) + ((to_x, to_y, to_core) if count else ())
     for peer in peers:
         pl.semaphore_signal(barrier, inc=1, device_id=peer, device_id_type=pl.DeviceIdType.MESH)
     pl.semaphore_wait(barrier, len(peers))
 
     def region(w, at, part=None):
-        full, width = fulls[w], shard_refs[w].shape[axes[w]]
-        rows = shard_refs[w].shape[0]
+        full, width = fulls[w], shard_refs[w].shape[min(axes[w], 1)]
+        rows, columns = shard_refs[w].shape
         start, size = (0, rows) if part is None else (part * (rows // 2), rows // 2)
         if axes[w] == 0:
             return full.at[pl.ds(pl.multiple_of(at * width + start, size), size)]
-        return full.at[pl.ds(start, size), pl.ds(pl.multiple_of(at * width, width), width)]
+        column = at * width
+        if axes[w] == 2:
+            start = lax.rem(at, 2) * rows + start
+            start, column = pl.multiple_of(start, size), lax.div(at, 2) * width
+        return full.at[pl.ds(start, size), pl.ds(pl.multiple_of(column, width), width)]
 
     def near(w, index, source, target, peer):
         return pltpu.make_async_remote_copy(
@@ -306,6 +266,9 @@
         return 3 - step + z if way == 0 else step + z - 3
 
     def line_step(step):
+        if not units:
+            return
+
         def body(c, carry):
             for way, rank in ways:
 
@@ -367,7 +330,8 @@
 
         return carry
 
-    lax.fori_loop(0, chunk, finish, 0)
+    if units:
+        lax.fori_loop(0, chunk, finish, 0)
     for w in range(count):
         last(w)
 
@@ -387,17 +351,19 @@
 
         return carry
 
-    lax.fori_loop(0, chunk, drain, 0)
+    if units:
+        lax.fori_loop(0, chunk, drain, 0)
     for v in range(whole):
         keep(v).wait()
 
 
 def exchange(partials, pieces, shards_in, axes, collective_id):
     units, whole, count = len(partials), len(pieces), len(shards_in)
-    tokens, feats = partials[0].shape[0], partials[0].shape[1] // 4
+    tokens, feats = (partials[0].shape[0], partials[0].shape[1] // 4) if units else (64, 128)
     chunk = 4
+    grown = ((8, 1), (1, 8), (2, 4))
     full = [
-        jax.ShapeDtypeStruct(tuple(n * 8 if i == axis else n for i, n in enumerate(w.shape)), BF16)
+        jax.ShapeDtypeStruct(tuple(n * k for n, k in zip(w.shape, grown[axis])), BF16)
         for w, axis in zip(shards_in, axes)
     ]
     anywhere = pl.BlockSpec(memory_space=pl.ANY)
@@ -410,17 +376,17 @@
         + [jax.ShapeDtypeStruct((tokens, 4 * feats), BF16)] * whole
         + full,
         scratch_shapes=[
-            pltpu.VMEM((units, 4, tokens, feats), BF16),
-            pltpu.VMEM((2, units, 3, tokens, feats), BF16),
-            sems((units, 4)),
-            sems((2, units, 3, chunk)),
-            sems((2, units, 3, chunk)),
+            pltpu.VMEM((max(units, 1), 4, tokens, feats), BF16),
+            pltpu.VMEM((2, max(units, 1), 3, tokens, feats), BF16),
+            sems((max(units, 1), 4)),
+            sems((2, max(units, 1), 3, chunk)),
+            sems((2, max(units, 1), 3, chunk)),
             sems((max(count, 1),)),
             sems((max(count, 1), 9)),
             sems((max(count, 1), 9)),
-            sems((whole,)),
-            sems((2, whole, 3, chunk)),
-            sems((2, whole, 3, chunk)),
+            sems((max(whole, 1),)),
+            sems((2, max(whole, 1), 3, chunk)),
+            sems((2, max(whole, 1), 3, chunk)),
         ],
         compiler_params=pltpu.CompilerParams(
             collective_id=collective_id,
@@ -428,7 +394,7 @@
             vmem_limit_bytes=48 * 1024 * 1024,
         ),
         cost_estimate=pl.CostEstimate(
-            flops=0, bytes_accessed=600 * 1024 * 1024, transcendentals=0
+            flops=0, bytes_accessed=(1 if units else 240) * 1024 * 1024, transcendentals=0
         ),
         name="exchange",
     )(*partials, *pieces, *shards_in)
@@ -484,50 +450,6 @@
     )(x)
 
 
-def plane_sum_kernel(x_ref, out_ref, got, send_sem, recv_sem):
-    x, stream = lax.axis_index("dp"), lax.axis_index("stream")
-    peers = (
-        {"stream": stream + 1 - 2 * lax.rem(stream, 2)},
-        {"stream": lax.rem(stream + 2, 4)},
-        {"dp": 1 - x},
-    )
-    barrier = pltpu.get_barrier_semaphore()
-    for peer in peers:
-        pl.semaphore_signal(barrier, inc=1, device_id=peer, device_id_type=pl.DeviceIdType.MESH)
-    pl.semaphore_wait(barrier, 3)
-    out_ref[...] = x_ref[...]
-    for step, peer in enumerate(peers):
-        copy = pltpu.make_async_remote_copy(
-            src_ref=out_ref,
-            dst_ref=got.at[step],
-            send_sem=send_sem.at[step],
-            recv_sem=recv_sem.at[step],
-            device_id=peer,
-            device_id_type=pl.DeviceIdType.MESH,
-        )
-        copy.start()
-        copy.wait()
-        out_ref[...] += got[step]
-
-
-def plane_sum(x, collective_id):
-    if not paired():
-        return lax.psum(x.astype(BF16), ("dp", "stream")).astype(F32)
-    return pl.pallas_call(
-        plane_sum_kernel,
-        out_shape=jax.ShapeDtypeStruct(x.shape, F32),
-        in_specs=[pl.BlockSpec(memory_space=pltpu.VMEM)],
-        out_specs=pl.BlockSpec(memory_space=pltpu.VMEM),
-        scratch_shapes=[
-            pltpu.VMEM((3,) + x.shape, F32),
-            pltpu.SemaphoreType.DMA((3,)),
-            pltpu.SemaphoreType.DMA((3,)),
-        ],
-        compiler_params=pltpu.CompilerParams(collective_id=collective_id, has_side_effects=True),
-        name="sum_over_plane",
-    )(x)
-
-
 def turn(v, keep, left, right):
     h = ROT // 2
     return v * keep + pltpu.roll(v, HD - h, 1) * left + pltpu.roll(v, h, 1) * right
@@ -559,15 +481,55 @@
     )(values_in, *tables)
 
 
+def feed_kernel(x_ref, d_ref, up_ref, down_ref, gated_ref, d_up_ref, grad_up_ref, grad_down_ref):
+    tokens, model_width = x_ref.shape
+    step = min(256, tokens)
+    for r in range(0, tokens, step):
+        rows = slice(r, r + step)
+        up_pre = dot(x_ref[rows], up_ref[...])
+        d_gated = dot_nt(d_ref[rows], down_ref[...])
+        below = 0.5 * (1.0 + lax.erf(up_pre * 0.5**0.5))
+        density = jnp.exp(-0.5 * up_pre * up_pre) * (2.0 * jnp.pi) ** -0.5
+        gated_ref[rows] = (up_pre * below).astype(BF16)
+        d_up_ref[rows] = (d_gated * (below + up_pre * density)).astype(BF16)
+    wide = min(512, model_width)
+    for c in range(0, model_width, wide):
+        part = slice(c, c + wide)
+        grad_up_ref[part] = dot_tn(x_ref[:, part], d_up_ref[...]).astype(BF16)
+        grad_down_ref[part] = dot_tn(d_ref[:, part], gated_ref[...]).astype(BF16)
+
+
+def feed_forward(x, d_out, up, down):
+    tokens, model_width = x.shape
+    hidden = up.shape[1]
+    block = min(512, hidden)
+    fixed = pl.BlockSpec((tokens, model_width), lambda i: (0, 0), pipeline_mode=pl.Buffered(1))
+    narrow = pl.BlockSpec((tokens, block), lambda i: (0, i))
+    column = pl.BlockSpec((model_width, block), lambda i: (0, i))
+    shape = lambda rows: jax.ShapeDtypeStruct((rows, hidden), BF16)
+    return pl.pallas_call(
+        feed_kernel,
+        grid=(hidden // block,),
+        in_specs=[fixed, fixed, column, pl.BlockSpec((block, model_width), lambda i: (i, 0))],
+        out_specs=[narrow, narrow, column, column],
+        out_shape=[shape(tokens), shape(tokens), shape(model_width), shape(model_width)],
+        compiler_params=pltpu.CompilerParams(vmem_limit_bytes=56 * 1024 * 1024),
+        cost_estimate=pl.CostEstimate(
+            flops=8 * tokens * model_width * hidden,
+            bytes_accessed=4 * model_width * (2 * hidden + tokens),
+            transcendentals=0,
+        ),
+        name="feed_forward",
+    )(x, d_out, up, down)
+
+
 def attention_kernel(
     place_ref, q_ref, do_ref, start_ref, valid_ref, keep_ref, left_ref, right_ref, *refs
 ):
-    blocks = (len(refs) - 4) // 4
+    blocks = (len(refs) - 6) // 2
     k_refs, v_refs = refs[:blocks], refs[blocks : 2 * blocks]
-    o_ref, dq_ref = refs[2 * blocks : 2 * blocks + 2]
-    dk_refs = refs[2 * blocks + 2 : 3 * blocks + 2]
-    dv_refs = refs[3 * blocks + 2 : 4 * blocks + 2]
-    s_ref, dp_ref = refs[4 * blocks + 2 :]
+    o_ref, dq_ref, near_ref, beside_ref, s_ref, dp_ref = refs[2 * blocks :]
+    grad_ref = lambda j: (beside_ref if j % 2 else near_ref).at[j // 2]
     rows = q_ref.shape[1]
     scale = HD ** (-0.5)
     member = place_ref[0]
@@ -595,7 +557,7 @@
         s_ref[j] = p
         p_bf = p.astype(BF16)
         out = out + dot(p_bf, v_refs[j][0])
-        dv_refs[j][0] = dot_tn(p_bf, d_out).astype(BF16)
+        grad_ref(j)[1] = dot_tn(p_bf, d_out).astype(BF16)
         d_p = dot_nt(d_out, v_refs[j][0])
         dp_ref[j] = d_p
         delta = delta + jnp.sum(p * d_p, axis=1, keepdims=True)
@@ -604,33 +566,36 @@
     for j in range(blocks):
         d_s = (s_ref[j] * (dp_ref[j] - delta)).astype(BF16)
         d_q = d_q + dot(d_s, k_refs[j][0])
-        dk_refs[j][0] = (dot_tn(d_s, q) * scale).astype(BF16)
+        grad_ref(j)[0] = (dot_tn(d_s, q) * scale).astype(BF16)
     dq_ref[0] = turn(d_q * scale, keep, -left, -right).astype(BF16)
 
 
-def attention(places, queries, d_attended, starts, valid, tables, keys, values):
-    micro, rows, feats = queries.shape
+def attention(index, places, queries, d_attended, starts, valid, tables, keys, values):
+    _, rows, feats = queries.shape
     blocks = len(keys)
-    tile = pl.BlockSpec((1, rows, HD), lambda b, h: (b, 0, h))
-    like = lambda dtype: jax.ShapeDtypeStruct((micro, rows, feats), dtype)
+    tile = pl.BlockSpec((1, rows, HD), lambda h: (index, 0, h))
+    fixed = lambda width: pl.BlockSpec((1, rows, width), lambda h: (index, 0, 0))
+    out_tile = pl.BlockSpec((1, rows, HD), lambda h: (0, 0, h))
+    grad_tile = pl.BlockSpec((blocks // 2, 2, rows, HD), lambda h: (0, 0, 0, h))
+    shape = lambda *lead: jax.ShapeDtypeStruct(lead + (rows, feats), BF16)
     return pl.pallas_call(
         attention_kernel,
-        grid=(micro, feats // HD),
+        grid=(feats // HD,),
         in_specs=[pl.BlockSpec(memory_space=pltpu.SMEM), tile, tile]
-        + [pl.BlockSpec((1, rows, 1), lambda b, h: (b, 0, 0))] * 2
-        + [pl.BlockSpec((1, rows, HD), lambda b, h: (b, 0, 0))] * 3
+        + [fixed(1)] * 2
+        + [fixed(HD)] * 3
         + [tile] * (2 * blocks),
-        out_specs=[tile] * (2 + 2 * blocks),
-        out_shape=[like(BF16)] * (2 + 2 * blocks),
+        out_specs=[out_tile] * 2 + [grad_tile] * 2,
+        out_shape=[shape(1)] * 2 + [shape(blocks // 2, 2)] * 2,
         scratch_shapes=[
             pltpu.VMEM((blocks, rows, rows), F32),
             pltpu.VMEM((blocks, rows, rows), F32),
         ],
         compiler_params=pltpu.CompilerParams(vmem_limit_bytes=40 * 1024 * 1024),
         cost_estimate=pl.CostEstimate(
-            flops=12 * micro * feats * rows * rows * blocks,
-            bytes_accessed=micro * rows * feats * 2 * (4 + 4 * blocks),
-            transcendentals=micro * rows * rows * blocks * feats // HD,
+            flops=0,
+            bytes_accessed=1024,
+            transcendentals=0,
         ),
         name="attention_both_ways",
     )(places, queries, d_attended, starts, valid, *tables, *keys, *values)
@@ -644,12 +609,12 @@
     return (local, beside, across, over_core(across))
 
 
-def reduce_rows(parts):
-    add = lambda a, b: a.astype(F32) + b.astype(F32)
-    across = add(parts[2], over_core(parts[3])).astype(BF16)
-    return add(
-        add(parts[0], over_core(parts[1])), lax.ppermute(across, "stream", [(2, 0), (3, 1)])
-    )
+def add_f32(a, b):
+    return a.astype(F32) + b.astype(F32)
+
+
+def over_line(a):
+    return lax.ppermute(a, "stream", [(2, 0), (3, 1)])
 
 
 def columns_of(pieces, rows):
@@ -675,7 +640,7 @@
         streams_ref[s] = total
         sums.append(row_sum(total))
         squares.append(row_sum(total * total))
-    stats_ref[...] = columns_of(sums + squares, weights.shape[0])
+    stats_ref[...] = columns_of(sums + squares, weights.shape[0]).T[:8]
 
 
 def mix_streams(weights, history):
@@ -690,11 +655,11 @@
         ],
         out_specs=[
             pl.BlockSpec((4, block, feats), lambda i: (0, i, 0)),
-            pl.BlockSpec((block, 128), lambda i: (i, 0)),
+            pl.BlockSpec((8, block), lambda i: (0, i)),
         ],
         out_shape=[
             jax.ShapeDtypeStruct((4, tokens, feats), F32),
-            jax.ShapeDtypeStruct((tokens, 128), F32),
+            jax.ShapeDtypeStruct((8, tokens), F32),
         ],
         compiler_params=pltpu.CompilerParams(vmem_limit_bytes=40 * 1024 * 1024),
         cost_estimate=pl.CostEstimate(
@@ -714,7 +679,7 @@
     for s in range(4):
         for layer in layers:
             crossed.append(row_sum(streams_ref[s] * layer))
-    out_ref[...] = columns_of(crossed + plain + direct, cot.shape[0])
+    out_ref[...] = columns_of(crossed + plain + direct, cot.shape[0]).T[:56]
 
 
 def early_sums(streams, cot, history):
@@ -728,8 +693,8 @@
             pl.BlockSpec((block, feats), lambda i: (i, 0)),
             pl.BlockSpec((HIST, block, feats), lambda i: (0, i, 0)),
         ],
-        out_specs=pl.BlockSpec((block, 128), lambda i: (i, 0)),
-        out_shape=jax.ShapeDtypeStruct((tokens, 128), F32),
+        out_specs=pl.BlockSpec((56, block), lambda i: (0, i)),
+        out_shape=jax.ShapeDtypeStruct((56, tokens), F32),
         compiler_params=pltpu.CompilerParams(vmem_limit_bytes=40 * 1024 * 1024),
         cost_estimate=pl.CostEstimate(
             flops=110 * tokens * feats, bytes_accessed=36 * tokens * feats, transcendentals=0
@@ -757,14 +722,14 @@
         seconds.append(row_sum(scaled * centered))
         for j in range(HIST):
             dots.append(row_sum(scaled * history_ref[j].astype(F32)))
-    out_ref[...] = columns_of(dots + firsts + seconds, rows)
+    out_ref[...] = columns_of(dots + firsts + seconds, rows).T[:48]
 
 
 def gradient_sums(grads, streams, stats, gain, history):
     _, tokens, feats = streams.shape
     block = min(128, tokens)
     wide = pl.BlockSpec((block, feats), lambda i: (i, 0))
-    sums, edges = pl.pallas_call(
+    return pl.pallas_call(
         sums_kernel,
         grid=(tokens // block,),
         in_specs=[wide] * 4
@@ -775,11 +740,11 @@
             pl.BlockSpec((HIST, block, feats), lambda i: (0, i, 0)),
         ],
         out_specs=[
-            pl.BlockSpec((block, 128), lambda i: (i, 0)),
+            pl.BlockSpec((48, block), lambda i: (0, i)),
             pl.BlockSpec((8, feats), lambda i: (0, 0)),
         ],
         out_shape=[
-            jax.ShapeDtypeStruct((tokens, 128), F32),
+            jax.ShapeDtypeStruct((48, tokens), F32),
             jax.ShapeDtypeStruct((8, feats), F32),
         ],
         compiler_params=pltpu.CompilerParams(vmem_limit_bytes=40 * 1024 * 1024),
@@ -788,48 +753,170 @@
         ),
         name="gradient_sums",
     )(*grads, streams, stats, gain, history)
-    return sums[:, : 4 * HIST + 8], edges
-
-
-def mix_gradient(sums, early, stats, model_width):
+
+
+def small_kernel(
+    members,
+    plane,
+    sums_ref,
+    early_ref,
+    stats_ref,
+    pre_ref,
+    slope_ref,
+    hidden_ref,
+    rms_ref,
+    w_ref,
+    current_ref,
+    edge_ref,
+    small_ref,
+    scaled_ref,
+    coef_ref,
+    slots,
+    got,
+    d_mix_ref,
+    rows_ref,
+    send_sem,
+    recv_sem,
+    plane_send,
+    plane_recv,
+):
+    x, stream, z = lax.axis_index("dp"), lax.axis_index("stream"), lax.axis_index("head")
+    line = [{"head": lax.rem(z + k, members)} for k in range(1, members)]
+    near = (
+        {"stream": stream + 1 - 2 * lax.rem(stream, 2)},
+        {"stream": lax.rem(stream + 2, 4)},
+        {"dp": 1 - x},
+    )
+    near = near if plane else ()
+    barrier = pltpu.get_barrier_semaphore()
+    for peer in line + list(near):
+        pl.semaphore_signal(barrier, inc=1, device_id=peer, device_id_type=pl.DeviceIdType.MESH)
+    pl.semaphore_wait(barrier, len(line) + len(near))
+    copies = []
+    for k, peer in enumerate(line):
+        copy = pltpu.make_async_remote_copy(
+            src_ref=sums_ref,
+            dst_ref=slots.at[z],
+            send_sem=send_sem.at[k],
+            recv_sem=recv_sem.at[k],
+            device_id=peer,
+            device_id_type=pl.DeviceIdType.MESH,
+        )
+        copy.start()
+        copies.append(copy)
+    slots[z] = sums_ref[...]
+    for copy in copies:
+        copy.wait()
+    total = slots[0]
+    for k in range(1, members):
+        total = total + slots[k]
+    slots[0] = total
     n = 4 * HIST
-    first, second = sums[n : n + 4] / model_width, sums[n + 4 : n + 8] / model_width
-    spread = lambda a: jnp.repeat(a, HIST, axis=0)
-    crossed, plain, direct = early[:n], early[n : n + HIST], early[n + HIST : n + 2 * HIST]
-    means, inverse = spread(stats.T[:4]), spread(stats.T[4:])
-    plain = jnp.tile(plain, (4, 1))
-    crossed = (crossed - means * plain) * inverse
-    d_mix = inverse * (sums[:n] - spread(first) * plain - spread(second) * crossed)
-    d_mix = d_mix + jnp.concatenate([jnp.zeros_like(d_mix[: 3 * HIST]), direct])
-    return d_mix, jnp.concatenate([first, second])
+    model_width = members * small_ref.shape[1]
+    plain = early_ref[n : n + HIST]
+    rows_ref[...] = jnp.zeros_like(rows_ref)
+    rows_ref[0:8] = slots[0, n : n + 8] / model_width
+    for s in range(4):
+        part = slice(s * HIST, (s + 1) * HIST)
+        mean, inverse = stats_ref[s : s + 1], stats_ref[4 + s : 5 + s]
+        crossed = (early_ref[part] - mean * plain) * inverse
+        d_part = inverse * (
+            slots[0, part] - rows_ref[s : s + 1] * plain - rows_ref[4 + s : 5 + s] * crossed
+        )
+        if s == 3:
+            d_part = d_part + early_ref[n + HIST : n + 2 * HIST]
+        d_mix_ref[part] = d_part
+    d_mix = d_mix_ref[...]
+    high = dict(precision=HIGHEST, preferred_element_type=F32)
+    d_pre = jnp.dot(w_ref[...], d_mix, **high) * slope_ref[...]
+    rms = rms_ref[...]
+    cross = jnp.sum(d_pre * pre_ref[...], axis=0, keepdims=True)
+    rows_ref[8:9] = rms * rms * cross / model_width
+    coef_ref[...] = rows_ref[...].T
+    scaled = d_pre * rms
+    scaled_ref[...] = scaled
+    small_ref[...] = jnp.zeros_like(small_ref)
+    small_ref[0:n] = jnp.dot(scaled, current_ref[...].astype(F32), **high)
+    small_ref[n : n + 8] = edge_ref[...]
+    small_ref[n + 8 : 2 * n + 8, 0:n] = lax.dot_general(
+        hidden_ref[...], d_mix, (((1,), (1,)), ((), ())), **high
+    )
+    small_ref[n + 8 : 2 * n + 8, n : n + 1] = jnp.sum(d_mix, axis=1, keepdims=True)
+    for step, peer in enumerate(near):
+        copy = pltpu.make_async_remote_copy(
+            src_ref=small_ref,
+            dst_ref=got.at[step],
+            send_sem=plane_send.at[step],
+            recv_sem=plane_recv.at[step],
+            device_id=peer,
+            device_id_type=pl.DeviceIdType.MESH,
+        )
+        copy.start()
+        copy.wait()
+        small_ref[...] += got[step]
+
+
+def small_gradients(sums, early, stats, pre, slope, hidden, rms, w_out, current, edges):
+    members, plane = lax.axis_size("head"), paired()
+    tokens, feats = current.shape
+    n = 4 * HIST
+    shape = jax.ShapeDtypeStruct
+    sems = pltpu.SemaphoreType.DMA
+    small, scaled, coefs = pl.pallas_call(
+        functools.partial(small_kernel, members, plane),
+        in_specs=[pl.BlockSpec(memory_space=pltpu.VMEM)] * 10,
+        out_specs=[pl.BlockSpec(memory_space=pltpu.VMEM)] * 3,
+        out_shape=[shape((80, feats), F32), shape((n, tokens), F32), shape((tokens, 128), F32)],
+        scratch_shapes=[
+            pltpu.VMEM((members, 48, tokens), F32),
+            pltpu.VMEM((3, 80, feats), F32),
+            pltpu.VMEM((n, tokens), F32),
+            pltpu.VMEM((128, tokens), F32),
+            sems((members - 1,)),
+            sems((members - 1,)),
+            sems((3,)),
+            sems((3,)),
+        ],
+        compiler_params=pltpu.CompilerParams(
+            collective_id=3, has_side_effects=True, vmem_limit_bytes=40 * 1024 * 1024
+        ),
+        name="small_gradients",
+    )(sums, early, stats, pre, slope, hidden, rms, w_out, current, edges)
+    if not plane:
+        small = lax.psum(small.astype(BF16), ("dp", "stream")).astype(F32)
+    return small, scaled, coefs
 
 
 def history_kernel(
-    g0, g1, g2, g3, streams_ref, stats_ref, gain_ref, cot_ref, current_ref, columns_ref, d_ref, w_ref, out_ref
+    g0, g1, g2, g3, streams_ref, stats_ref, gain_ref, cot_ref, current_ref, weights_ref, coef_ref, d_ref, w_ref, out_ref
 ):
-    n = 4 * HIST
-    stats, columns = stats_ref[...], columns_ref[...]
-    column = lambda i: columns[:, i : i + 1]
+    stats, weights, coefs = stats_ref[...], weights_ref[...], coef_ref[...]
     d_streams = []
     for s, g_ref in enumerate((g0, g1, g2, g3)):
         inverse = stats[:, 4 + s : 5 + s]
         centered = (streams_ref[s] - stats[:, s : s + 1]) * inverse
         scaled = g_ref[...].astype(F32) * gain_ref[s : s + 1]
-        d_streams.append(inverse * (scaled - column(n + s) - centered * column(n + 4 + s)))
+        d_streams.append(
+            inverse * (scaled - coefs[:, s : s + 1] - centered * coefs[:, 4 + s : 5 + s])
+        )
     d_streams[3] = d_streams[3] + cot_ref[...].astype(F32)
     for j in range(HIST):
-        total = column(j) * d_streams[0]
+        total = weights[:, j : j + 1] * d_streams[0]
         for s in range(1, 4):
-            total = total + column(s * HIST + j) * d_streams[s]
+            total = total + weights[:, s * HIST + j : s * HIST + j + 1] * d_streams[s]
         if j == HIST - 1:
-            total = total + jnp.dot(
-                d_ref[...], w_ref[...], precision=HIGHEST, preferred_element_type=F32
+            total = total + lax.dot_general(
+                d_ref[...],
+                w_ref[...],
+                (((0,), (0,)), ((), ())),
+                precision=HIGHEST,
+                preferred_element_type=F32,
             )
-            total = total - current_ref[...].astype(F32) * column(n + 9)
+            total = total - current_ref[...].astype(F32) * coefs[:, 8:9]
         out_ref[j] = total
 
 
-def history_gradient(grads, streams, stats, gain, cot, current, columns, d_scaled, w_rows):
+def history_gradient(grads, streams, stats, gain, cot, current, weights, coefs, d_scaled, w_rows):
     _, tokens, feats = streams.shape
     block = min(128, tokens)
     wide = pl.BlockSpec((block, feats), lambda i: (i, 0))
@@ -845,8 +932,9 @@
             fixed(gain),
             wide,
             wide,
-            narrow(columns),
-            narrow(d_scaled),
+            narrow(weights),
+            narrow(coefs),
+            pl.BlockSpec((d_scaled.shape[0], block), lambda i: (0, i)),
             fixed(w_rows),
         ],
         out_specs=pl.BlockSpec((HIST, block, feats), lambda i: (0, i, 0)),
@@ -856,7 +944,7 @@
             flops=110 * tokens * feats, bytes_accessed=64 * tokens * feats, transcendentals=0
         ),
         name="history_gradient",
-    )(*grads, streams, stats, gain, cot, current, columns, d_scaled, w_rows)
+    )(*grads, streams, stats, gain, cot, current, weights, coefs, d_scaled, w_rows)
 
 
 def shards(
@@ -908,9 +996,7 @@
 
     cot_rows = cotangent.reshape(tokens, feats).astype(F32) * valid
     cot_bf = cot_rows.astype(BF16)
-    w_both = jnp.concatenate([w_attn_out, w_down])
     duplex = lined()
-    kv_near = swap_head(w_qkv[1:]) if duplex else w_qkv[:1]
 
     history = history.reshape(HIST, tokens, feats)
     current = history[HIST - 1]
@@ -918,172 +1004,150 @@
     mixed = lax.dot_general(w_mix_in, current, (((0,), (1,)), ((), ())), preferred_element_type=F32)
     square = jnp.sum(current_f * current_f, axis=1)[None]
     mixed = head_sum(jnp.concatenate([mixed, square]), 0).T
-    mixed, kv_near, cot_bf = lax.optimization_barrier((mixed, kv_near, cot_bf))
+    mixed, cot_bf, w_up = lax.optimization_barrier((mixed, cot_bf, w_up))
     out_full = lax.all_gather(cot_bf, "head", axis=1, tiled=True)
     if duplex:
-        kv_near = jnp.stack([kv_near, over_x(kv_near)])
-        kv_near = jnp.concatenate([kv_near, over_y(kv_near)])
+        _, _, (up_full, wk) = exchange([], [], [w_up, w_qkv[1]], (0, 0), 4)
+        mixed, up_full = lax.optimization_barrier((mixed, up_full))
     rms_scale = lax.rsqrt(mixed[:, 4 * HIST :] / model_width + EPSILON)
     mix_pre = mixed[:, : 4 * HIST] * rms_scale
+    below_mix = 0.5 * (1.0 + lax.erf(mix_pre * 0.5**0.5))
     mix_hidden = gelu_exact(mix_pre)
+    slope_mix = below_mix + mix_pre * jnp.exp(-0.5 * mix_pre * mix_pre) * (2.0 * jnp.pi) ** -0.5
     mix_weights = jnp.dot(mix_hidden, w_mix_out_f, precision=HIGHEST) + mix_bias.reshape(-1)
     streams, stats = mix_streams(mix_weights, history)
-    stats = head_sum(stats[:, :8].T, 1)
+    stats = head_sum(stats, 1)
     stat_sum, stat_square = stats[:4], stats[4:]
-    early = early_sums(streams, cot_bf, history)
-    stat_sum, stat_square, kv_near = lax.optimization_barrier((stat_sum, stat_square, kv_near))
     row_means = (stat_sum / model_width)[:, :, None]
     inv_std = lax.rsqrt(stat_square[:, :, None] / model_width - row_means * row_means + EPSILON)
     centered = (streams - row_means) * inv_std
     row_stats = jnp.concatenate([row_means[..., 0], inv_std[..., 0]]).T
-    early = lax.psum(early[:, : 6 * HIST].T, "head")
     normed = (centered * ln_gain[:, None, :] + ln_bias[:, None, :]).astype(BF16)
 
-    def all_features(stream):
-        return lax.all_gather(normed[stream], "head", axis=1, tiled=True)
+    def all_features(a):
+        return lax.all_gather(a, "head", axis=1, tiled=True)
 
     if duplex:
-        w_kv = row_weight(w_qkv[1:], kv_near)
-        k_in, v_in = normed[1], normed[2]
-        partials = [dot(k_in, w_kv[0]).astype(BF16), dot(v_in, w_kv[1]).astype(BF16)]
-        partials, out_full = lax.optimization_barrier((partials, out_full))
-        (key_pre, value_pre), (up_in, q_in), (wq, up_full, both_full) = exchange(
-            partials,
-            [normed[3], normed[0]],
-            [w_qkv[0], w_up, w_both],
-            (0, 0, 1),
-            4,
+        w_down, normed = lax.optimization_barrier((w_down, normed))
+        _, _, (down_full, w_out_full, wv, wq) = exchange(
+            [], [], [w_down, w_attn_out, w_qkv[2], w_qkv[0]], (1, 1, 0, 0), 6
         )
     else:
         wq, wk, wv = gather_weight(w_qkv, 1)
-        both_full = gather_weight(w_both, 1)
+        w_out_full, down_full = gather_weight(w_attn_out, 1), gather_weight(w_down, 1)
         up_full = gather_weight(w_up, 0)
-        k_in, v_in, q_in, up_in = (all_features(s) for s in (1, 2, 0, 3))
-        key_pre, value_pre = dot(k_in, wk), dot(v_in, wv)
-    w_out_full, down_full = both_full[:feats], both_full[feats:]
-
-    keys = rotate(key_pre, tables, 1.0)
-    values = value_pre.astype(BF16)
-    queries = dot(q_in, wq)
-    d_attended = dot_nt(out_full, w_out_full).astype(BF16) * valid.astype(BF16)
-    by_micro = lambda a: a.reshape(micro, quarter, feats)
-    key_blocks = exchange_rows(by_micro(keys))
-    value_blocks = exchange_rows(by_micro(values))
-    places = member ^ jnp.arange(4, dtype=jnp.int32)
 
     def to_owner(partial):
         return lax.psum_scatter(
             partial.astype(BF16), "head", scatter_dimension=1, tiled=True
         ).astype(F32)
 
-    up_pre = dot(up_in, up_full)
-    below = 0.5 * (1.0 + lax.erf(up_pre * 0.5**0.5))
-    slope = below + up_pre * jnp.exp(-0.5 * up_pre * up_pre) * (2.0 * jnp.pi) ** -0.5
-    gated_up, slope = lax.optimization_barrier(((up_pre * below).astype(BF16), slope))
-    d_up = (dot_nt(out_full, down_full) * slope).astype(BF16)
+    up_out, out_full = lax.optimization_barrier((normed[3], out_full))
+    up_in, k_out, down_full = lax.optimization_barrier(
+        (all_features(up_out), normed[1], down_full)
+    )
+    k_in, v_out = lax.optimization_barrier((all_features(k_out), normed[2]))
+    gated_up, d_up, product_up, product_down = feed_forward(up_in, out_full, up_full, down_full)
+    feed_products = [product_up[None], product_down[None]]
+    feed_parts = [chip_parts(a) if paired() else a for a in feed_products]
+    streams_late, v_out, d_up, feed_parts = lax.optimization_barrier(
+        (streams, v_out, d_up, feed_parts)
+    )
+    early = head_sum(early_sums(streams_late, cot_bf, history), 2)
+    v_in, q_out, early = lax.optimization_barrier((all_features(v_out), normed[0], early))
+    key_pre, value_pre = dot(k_in, wk), dot(v_in, wv)
     d_up_in = dot_nt(d_up, up_full).astype(BF16)
-    queries, d_up, gated_up, d_up_in = lax.optimization_barrier((queries, d_up, gated_up, d_up_in))
+    q_in, d_up_in = lax.optimization_barrier((all_features(q_out), d_up_in))
     g_up = to_owner(d_up_in)
-
-    results = attention(
-        places,
-        by_micro(queries),
-        by_micro(d_attended),
-        starts.reshape(micro, quarter, 1),
-        valid.reshape(micro, quarter, 1),
-        tuple(a.reshape(micro, quarter, HD) for a in tables),
-        key_blocks,
-        value_blocks,
-    )
-    attended, d_query_pre = results[0].reshape(tokens, feats), results[1].reshape(tokens, feats)
-    d_keys = reduce_rows(results[2:6]).reshape(tokens, feats)
-    d_values = reduce_rows(results[6:10]).reshape(tokens, feats)
-    d_key_pre = rotate(d_keys, tables, -1.0)
-    d_value_pre = d_values.astype(BF16)
-
-    combined = dot(attended, w_out_full) + dot(gated_up, down_full)
+    product = lambda a, b: dot_tn(a, b).astype(BF16)
+    feed = dot(gated_up, down_full).astype(BF16)
+    d_attended = dot_nt(out_full, w_out_full).astype(BF16) * valid.astype(BF16)
+    feed_terms = [plane_parts(*a) if paired() else scatter_parts(a) for a in feed_parts]
+    grad_up = add_terms(feed_terms[0][0][0], feed_terms[0][1][0], False)
+    grad_down = add_terms(feed_terms[1][0][0], feed_terms[1][1][0], True)
+
+    keys = rotate(key_pre, tables, 1.0)
+    values = value_pre.astype(BF16)
+    queries = dot(q_in, wq)
+    if duplex:
+        place = lax.axis_index("dp") * 4 + member
+        own = lambda w: take(w.reshape(4, 8, feats // 8, feats), place, 1)
+        shares = lax.all_to_all(jnp.stack([own(wk), own(wv)], axis=1), "head", 0, 0)
+        shares = [shares[:, i].transpose(1, 0, 2).reshape(feats // 8, 4 * feats) for i in range(2)]
+        queries, feed, d_attended, grad_up, grad_down, early, shares = lax.optimization_barrier(
+            (queries, feed, d_attended, grad_up, grad_down, early, shares)
+        )
+    by_micro = lambda a: a.reshape((micro, quarter) + a.shape[1:])
+    key_blocks = exchange_rows(by_micro(keys))
+    value_blocks = exchange_rows(by_micro(values))
+    places = member ^ jnp.arange(4, dtype=jnp.int32)
+    attended, d_query_pre, d_rows = [], [], []
+    queries = by_micro(queries)
+    for index in range(micro):
+        results = attention(
+            index,
+            places,
+            queries,
+            by_micro(d_attended),
+            by_micro(starts[:, None]),
+            by_micro(valid),
+            tuple(by_micro(a) for a in tables),
+            key_blocks,
+            value_blocks,
+        )
+        attended.append(results[0][0])
+        d_query_pre.append(results[1][0])
+        chip = add_f32(results[2], over_core(results[3]))
+        across = chip[1].astype(BF16)
+        queries, across = lax.optimization_barrier((queries, across))
+        d_rows.append(add_f32(chip[0], over_line(across)))
+    attended, d_query_pre = jnp.concatenate(attended), jnp.concatenate(d_query_pre)
+    d_key_pre = rotate(jnp.concatenate([a[0] for a in d_rows]), tables, -1.0)
+    d_value_pre = jnp.concatenate([a[1] for a in d_rows]).astype(BF16)
+
+    combined = dot(attended, w_out_full) + feed
+    products = jnp.stack([product(q_in, d_query_pre), product(out_full, attended)])
     if duplex:
         partials = [dot_nt(d_query_pre, wq).astype(BF16), combined.astype(BF16)]
-        (g_query, branch), (d_key_full, d_value_full), _ = exchange(
-            partials, [d_key_pre, d_value_pre], [], (), 5
-        )
-        g_key, g_value = dot_nt(d_key_full, w_kv[0]), dot_nt(d_value_full, w_kv[1])
+        parts = chip_parts(products)
+        kv = jnp.stack([product(k_in, d_key_pre), product(v_in, d_value_pre)])
+        partials, parts, kv, g_up = lax.optimization_barrier((partials, parts, kv, g_up))
+        (g_query, branch), (d_key_full, d_value_full), (wk_rows, wv_rows) = exchange(
+            partials, [d_key_pre, d_value_pre], shares, (0, 0), 5
+        )
+        g_key, g_value = dot_nt(d_key_full, wk_rows), dot_nt(d_value_full, wv_rows)
+        kv_terms = scatter_parts(kv)
+        terms = plane_parts(*parts)
     else:
         g_query = to_owner(dot_nt(d_query_pre, wq))
         g_key = to_owner(dot_nt(d_key_pre, wk))
         g_value = to_owner(dot_nt(d_value_pre, wv))
         branch = to_owner(combined)
+        terms = scatter_parts(products)
+        kv_terms = scatter_parts(
+            jnp.stack([product(k_in, d_key_pre), product(v_in, d_value_pre)])
+        )
     block_out = (valid * (streams[3] + branch)).astype(BF16)
-
-    product = lambda a, b: dot_tn(a, b).astype(BF16)
-    up_terms = scatter_parts(product(up_in, d_up)[None])
-    down_terms = scatter_parts(product(out_full, gated_up)[None])
-    grad_up = add_terms(up_terms[0][0], up_terms[1][0], False)
-    grad_down = add_terms(down_terms[0][0], down_terms[1][0], True)
-    if duplex:
-        by_head = lambda a, b: jnp.concatenate(
-            [product(a, b[:, i * feats : (i + 1) * feats]) for i in range(4)]
-        )
-        terms = scatter_parts(
-            jnp.stack([by_head(k_in, d_key_full), by_head(v_in, d_value_full)])
-        )
-        kv = swap_head((terms[0].astype(F32) + terms[1].astype(F32)).astype(BF16)).astype(F32)
-        terms = scatter_parts(jnp.stack([product(q_in, d_query_pre), product(out_full, attended)]))
-        grad_query = terms[0][:1].astype(F32) + terms[1][:1].astype(F32)
-        grad_qkv = jnp.concatenate([grad_query, kv])
-    else:
-        terms = scatter_parts(
-            jnp.stack(
-                [
-                    product(q_in, d_query_pre),
-                    product(k_in, d_key_pre),
-                    product(v_in, d_value_pre),
-                    product(out_full, attended),
-                ]
-            )
-        )
-        grad_qkv = terms[0][:3].astype(F32) + terms[1][:3].astype(F32)
-    grad_attn_out = add_terms(terms[0][-1], terms[1][-1], True)
+    grad_query = terms[0][:1].astype(F32) + terms[1][:1].astype(F32)
+    grad_attn_out = add_terms(terms[0][1], terms[1][1], True)
 
     grads = (g_query, g_key, g_value, g_up)
-    sums, gain_shift = gradient_sums(grads, streams, row_stats, ln_gain, history)
-    sums = head_sum(sums.T, 3)
-    d_mix, coefs = mix_gradient(sums, early, row_stats, model_width)
-    d_hidden = jnp.dot(w_mix_out_f, d_mix, precision=HIGHEST)
-    mix_pre_t = mix_pre.T
-    below_mix = 0.5 * (1.0 + lax.erf(mix_pre_t * 0.5**0.5))
-    density = jnp.exp(-0.5 * mix_pre_t * mix_pre_t) * (2.0 * jnp.pi) ** -0.5
-    d_pre = d_hidden * (below_mix + mix_pre_t * density)
-    cross = jnp.sum(d_pre * mix_pre_t, axis=0, keepdims=True)
-    rms_row = rms_scale.T
-    grad_w1 = jnp.dot(d_pre * rms_row, current_f, precision=HIGHEST)
-    grad_w2 = jnp.dot(mix_hidden.T, d_mix.T, precision=HIGHEST)
-    grad_bias = jnp.sum(d_mix, axis=1)
-    wide = lambda a: jnp.pad(a, ((0, 0), (0, feats - a.shape[1])))
-    small = jnp.concatenate([grad_w1, gain_shift, wide(grad_w2), wide(grad_bias[None])])
-    small = plane_sum(small, 6)
+    sums, edges = gradient_sums(grads, streams, row_stats, ln_gain, history)
+    small, d_scaled, coefs = small_gradients(
+        sums, early, row_stats.T, mix_pre.T, slope_mix.T, mix_hidden.T, rms_scale.T, w_mix_out_f, current, edges
+    )
+    history_grad = history_gradient(
+        grads, streams, row_stats, ln_gain, cot_bf, current, mix_weights, coefs, d_scaled, w_mix_in_f.T
+    ).reshape(HIST, micro, quarter, feats)
+    grad_qkv = jnp.concatenate([grad_query, kv_terms[0].astype(F32) + kv_terms[1].astype(F32)])
     n = 4 * HIST
-    columns = jnp.concatenate(
-        [mix_weights.T, coefs, rms_row, rms_row * rms_row * cross / model_width]
-    ).T
-    history_grad = history_gradient(
-        grads,
-        streams,
-        row_stats,
-        ln_gain,
-        cot_bf,
-        current,
-        columns,
-        (d_pre * rms_row).T,
-        w_mix_in_f.T,
-    ).reshape(HIST, micro, quarter, feats)
     return (
         block_out.reshape(micro, quarter, feats),
         mix_weights.reshape(micro, quarter, 4 * HIST),
         history_grad,
         small[:n].T,
         small[n + 8 : 2 * n + 8, :n],
-        small[2 * n + 8, :n].reshape(mix_bias.shape),
+        small[n + 8 : 2 * n + 8, n].reshape(mix_bias.shape),
         small[n : n + 4],
         small[n + 4 : n + 8],
         grad_qkv,

time: 1190 us -> 960 us (0.81)
  waiting for transfers between devices: 231 us -> 115 us
  matrix products: 133 us -> 75.2 us
  Pallas kernels: 622 us -> 593 us
  local copies, waits for them, and re-layouts: 80 us -> 58.6 us
    ppermute x5 -> x4, waiting for transfers between devices: 120 us -> 2.94 us  [over_x(): return lax.ppermute(a, 'dp', SWAP_X)]
    pallas_call x2 -> x3, Pallas kernels: 407 us -> 317 us  [exchange(): pl.pallas_call(functools.partial(exchange_kernel, units, whole, axes), in...]
    pallas_call x3 -> x4, Pallas kernels: 68.4 us -> 123 us  [the longest x2 47 us: attention(): pl.pallas_call(attention_kernel, grid=(feats // HD,), in_specs=[pl.BlockS...]
    all_gather x1, waiting for transfers between devices: 44.5 us -> 0.01 us  [shards(): out_full = lax.all_gather(cot_bf, 'head', axis=1, tiled=True)]
    all_gather x0 -> x4, waiting for transfers between devices: none -> 24.8 us  [all_features(): return lax.all_gather(a, 'head', axis=1, tiled=True)]
    ppermute x2, waiting for transfers between devices: 0.01 us -> 21.5 us  [exchange_rows(): across = lax.ppermute(local, 'stream', [(0, 2), (1, 3)])]
    dot_general x6 -> x5, matrix products: 52.2 us -> 31.3 us  [dot(): return jnp.dot(a, b, preferred_element_type=F32)]
    dot_general x12 -> x4, matrix products: 33.7 us -> 14.5 us  [dot_tn(): lax.dot_general(a, b, (((0,), (0,)), ((), ())), preferred_element_type=F32)]
  transfers between devices with their start and end apart: 32 -> 29, of which waited for: 10 -> 12; matrix products, arithmetic and copies ran while one was open for 19% -> 17% of each run, Pallas kernels for 27% -> 58%
where the time goes in v6:
time: 960 us; the launch traced here: 953 us
  Pallas kernels  593 us (62%)
  waiting for transfers between devices  115 us (12%)
  matrix products  75.2 us (8%)
  other arithmetic  65.7 us (7%)
  local copies, waits for them, and re-layouts  58.6 us (6%)
  starting transfers between devices  29.1 us (3%)
  between operations  15.9 us (2%)
    pallas_call x3, Pallas kernels, exchange(): pl.pallas_call(functools.partial(exchange_kernel, units, whole, axes), in...  317 us
    pallas_call x3, Pallas kernels, head_sum(): pl.pallas_call(functools.partial(head_sum_kernel, members), out_shape=jax...  78.4 us
    pallas_call x2, Pallas kernels, attention(): pl.pallas_call(attention_kernel, grid=(feats // HD,), in_specs=[pl.BlockS...  47 us
    pallas_call x1, Pallas kernels, feed_forward(): pl.pallas_call(feed_kernel, grid=(hidden // block,), in_specs=[fixed, fix...  42.5 us
    pallas_call x1, Pallas kernels, small_gradients(): pl.pallas_call(functools.partial(small_kernel, members, plane), in_specs=...  33.3 us
    dot_general x5, matrix products, dot(): return jnp.dot(a, b, preferred_element_type=F32)  31.3 us
    dot_general x5, matrix products, dot_nt(): lax.dot_general(a, b, (((1,), (1,)), ((), ())), preferred_element_type=F32)  28.4 us
    ppermute x4, waiting for transfers between devices, over_y(): return lax.ppermute(a, 'stream', SWAP_Y)  25.8 us
  transfers between devices with their start and end apart: 29, of which 12 were waited for; matrix products, arithmetic and copies ran while one was open for 17% of the time, Pallas kernels for 58%

profile of v6, /device:TPU:8, one launch (start us, length us, event | category | flops | bytes accessed | tf_op | source)
XLA Modules:
  0.0 953.3 jit_solution(12554297133633610495)
XLA Ops:
  13.6 19.2 %sum_over_head.3 = f32[37,1024]{1,0:T(8,128)} custom-call(f32[37,1024]{1,0:T(8,128)} %pad_maximum_fusion.13.x_ref), custom_call_target="tpu_custom_call" | custom-call | tf_op jit(solution)/shard_map/sum_over_head/pallas_call | solution.py:438
  36.9 48.2 %exchange.3 = (bf16[2048,2048]{1,0:T(8,128)(2,1)}, bf16[2048,512]{1,0:T(8,128)(2,1)S(1)}) custom-call(bf16[256,2048]{1,0:T(8,128)(2,1)S(1)} %copy-done.20, bf16[256,512]{1,0:T(8,128)(2,1)S(1)} %get-tuple-element.245.refs_1_), custom_call_target="tpu_custom_call" | custom-call | bytes 251658240 | tf_op jit(solution)/shard_map/exchange/pallas_call | solution.py:371
  88.3 12.1 %mix_streams.1 = (f32[4,1024,512]{2,1,0:T(8,128)S(1)}, f32[8,1024]{1,0:T(8,128)S(1)}) custom-call(f32[1024,36]{1,0:T(8,128)S(1)} %convolution_add_fusion.weights_ref, bf16[9,1024,512]{2,1,0:T(8,128)(2,1)} %bitcast.238), custom_call_target="tpu_custom_call" | custom-call | flops 41943040 | bytes 17825792 | tf_op jit(solution)/shard_map/mix_streams/pallas_call | solution.py:649
  104.3 12.1 %sum_over_head.4 = f32[8,1024]{1,0:T(8,128)} custom-call(f32[8,1024]{1,0:T(8,128)} %copy-done.33), custom_call_target="tpu_custom_call" | custom-call | tf_op jit(solution)/shard_map/sum_over_head/pallas_call | solution.py:438
  123.7 63.9 %exchange.4 = (bf16[2048,2048]{1,0:T(8,128)(2,1)}, bf16[512,2048]{1,0:T(8,128)(2,1)S(1)}, bf16[2048,512]{1,0:T(8,128)(2,1)S(1)}, bf16[2048,512]{1,0:T(8,128)(2,1)}) custom-call(bf16[2048,256]{1,0:T(8,128)(2,1)S(1)} %copy-done.21, bf16[512,256]{1,0:T(8,128)(2,1)S(1)} %copy-done.27, bf16[256,512]{1,0:T(8,128)(2,1)S(1)} %get-tuple-element.246.refs_2_, ...), custom_call_target="tpu_custom_call" | custom-call | bytes 251658240 | tf_op jit(solution)/shard_map/exchange/pallas_call | solution.py:371
  190.3 11.7 %all-gather.8.cloned.1.call-done.x_ref = bf16[1024,2048]{1,0:T(8,128)(2,1)} async-done(((bf16[1024,512]{1,0:T(8,128)(2,1)}), bf16[1024,2048]{1,0:T(8,128)(2,1)}) %all-gather.8.cloned.1.call-update) | async-done | bytes 4194320 | tf_op jit(solution)/shard_map/all_gather | solution.py:1028
  202.3 42.5 %feed_forward.1 = (bf16[1024,2048]{1,0:T(8,128)(2,1)}, bf16[1024,2048]{1,0:T(8,128)(2,1)}, bf16[2048,2048]{1,0:T(8,128)(2,1)}, bf16[2048,2048]{1,0:T(8,128)(2,1)}) custom-call(bf16[1024,2048]{1,0:T(8,128)(2,1)} %all-gather.8.cloned.1.call-done.x_ref, bf16[1024,2048]{1,0:T(8,128)(2,1)} %all-gather.6.cloned.1.call-done.d_ref, ...), custom_call_target="tpu_custom_call" | custom-call | flops 34359738368 | bytes 41943040 | tf_op jit(solution)/shard_map/feed_forward/pallas_call | solution.py:510
  272.9 10.5 %all-gather.10.cloned.1.call-done = bf16[1024,2048]{1,0:T(8,128)(2,1)} async-done(((bf16[1024,512]{1,0:T(8,128)(2,1)}), bf16[1024,2048]{1,0:T(8,128)(2,1)}) %all-gather.10.cloned.1.call-update) | async-done | bytes 4194320 | tf_op jit(solution)/shard_map/all_gather | solution.py:1028
  286.3 6.7 all-to-all-start
  308.6 8.7 all-to-all-done
  328.2 11.7 %early_sums.1.x_ref = f32[56,1024]{1,0:T(8,128)S(1)} custom-call(f32[4,1024,512]{2,1,0:T(8,128)S(1)} %copy-done.1, bf16[1024,512]{1,0:T(8,128)(2,1)S(1)} %copy-done.2, bf16[9,1024,512]{2,1,0:T(8,128)(2,1)} %bitcast.239), custom_call_target="tpu_custom_call" | custom-call | flops 57671680 | bytes 18874368 | tf_op jit(solution)/shard_map/early_sums/pallas_call | solution.py:688
  340.6 47.1 %sum_over_head.5.early_ref = f32[56,1024]{1,0:T(8,128)} custom-call(f32[56,1024]{1,0:T(8,128)} %copy-done.23), custom_call_target="tpu_custom_call" | custom-call | tf_op jit(solution)/shard_map/sum_over_head/pallas_call | solution.py:438
  419.8 10.5 %convolution_convert_fusion.1 = bf16[1024,2048]{1,0:T(8,128)(2,1)} fusion(bf16[1024,2048]{1,0:T(8,128)(2,1)S(1)} %copy-done.72, bf16[2048,2048]{1,0:T(8,128)(2,1)S(1)} %bitcast.281), kind=kOutput, calls=%fused_computation.22 | convolution fusion | flops 8592031744 | bytes 16777216 | tf_op jit(solution)/shard_map/dot_general | solution.py:26
  439.2 13.3 %collective-permute-done.5 = bf16[1,256,2048]{2,1,0:T(8,128)(2,1)S(1)} collective-permute-done((bf16[1,256,2048]{2,1,0:T(8,128)(2,1)S(1)}, bf16[1,256,2048]{2,1,0:T(8,128)(2,1)S(1)}, u32[]{:S(2)}, u32[]{:S(2)}) %collective-permute-start.5) | collective-permute-done | bytes 1048608 | tf_op jit(solution)/shard_map/ppermute | solution.py:46
  453.5 21.5 %collective-permute-done.10.refs_6_ = bf16[2,512,512]{2,1,0:T(8,128)(2,1)} collective-permute-done((bf16[2,512,512]{2,1,0:T(8,128)(2,1)}, bf16[2,512,512]{2,1,0:T(8,128)(2,1)}, u32[]{:S(2)}, u32[]{:S(2)}) %collective-permute-start.10) | collective-permute-done | bytes 1048608 | tf_op jit(solution)/shard_map/ppermute | solution.py:607
  475.1 10.5 %convolution_convert_fusion.2 = bf16[1024,2048]{1,0:T(8,128)(2,1)} fusion(bf16[1024,2048]{1,0:T(8,128)(2,1)S(1)} %copy-done.73, bf16[2048,2048]{1,0:T(8,128)(2,1)S(1)} %bitcast.279), kind=kOutput, calls=%fused_computation.23 | convolution fusion | flops 8592031744 | bytes 16777216 | tf_op jit(solution)/shard_map/dot_general | solution.py:30
  489.7 7.0 collective-permute-done.3
  507.2 23.6 %attention_both_ways.2 = (bf16[1,512,512]{2,1,0:T(8,128)(2,1)S(1)}, bf16[1,512,512]{2,1,0:T(8,128)(2,1)S(1)}, bf16[2,2,512,512]{3,2,1,0:T(8,128)(2,1)}, bf16[2,2,512,512]{3,2,1,0:T(8,128)(2,1)}) custom-call(s32[4]{0:T(128)S(1)} %iota_xor_fusion.place_ref, f32[2,512,512]{2,1,0:T(8,128)} %bitcast.257, bf16[2,512,512]{2,1,0:T(8,128)(2,1)S(1)} %bitcast.223, ...), custom_call_target="tpu_custom_call" | custom-call | bytes 1024 | tf_op jit(solution)/shard_map/attention_both_ways/pallas_call | solution.py:581
  542.5 23.4 %attention_both_ways.3 = (bf16[1,512,512]{2,1,0:T(8,128)(2,1)S(1)}, bf16[1,512,512]{2,1,0:T(8,128)(2,1)S(1)}, bf16[2,2,512,512]{3,2,1,0:T(8,128)(2,1)}, bf16[2,2,512,512]{3,2,1,0:T(8,128)(2,1)}) custom-call(s32[4]{0:T(128)S(1)} %iota_xor_fusion.place_ref, f32[2,512,512]{2,1,0:T(8,128)} %bitcast.258, bf16[2,512,512]{2,1,0:T(8,128)(2,1)S(1)} %bitcast.224, ...), custom_call_target="tpu_custom_call" | custom-call | bytes 1024 | tf_op jit(solution)/shard_map/attention_both_ways/pallas_call | solution.py:581
  592.0 24.0 %collective-permute-done.16 = bf16[2,512,512]{2,1,0:T(8,128)(2,1)S(1)} collective-permute-done((bf16[2,512,512]{2,1,0:T(8,128)(2,1)S(1)}, bf16[2,512,512]{2,1,0:T(8,128)(2,1)S(1)}, u32[]{:S(2)}, u32[]{:S(2)}) %collective-permute-start.16) | collective-permute-done | bytes 1048608 | tf_op jit(solution)/shard_map/ppermute | solution.py:617
  641.1 205.3 %exchange.5 = (f32[1024,512]{1,0:T(8,128)S(1)}, f32[1024,512]{1,0:T(8,128)}, bf16[1024,2048]{1,0:T(8,128)(2,1)}, bf16[1024,2048]{1,0:T(8,128)(2,1)}, bf16[512,20...) custom-call(bf16[1024,2048]{1,0:T(8,128)(2,1)} %convolution_convert_fusion.refs_0_, ...), custom_call_target="tpu_custom_call" | custom-call | bytes 1048576 | tf_op jit(solution)/shard_map/exchange/pallas_call | solution.py:371
  854.2 15.1 %gradient_sums.1 = (f32[48,1024]{1,0:T(8,128)S(1)}, f32[8,512]{1,0:T(8,128)S(1)}) custom-call(f32[1024,512]{1,0:T(8,128)S(1)} %get-tuple-element.143.g0, f32[1024,512]{1,0:T(8,128)S(1)} %fusion.56.g1, f32[1024,512]{1,0:T(8,128)S(1)} %fusion.57.g2, f32[1024,512]{1,0:T(8,128)S(1)} %convert_element_type.307.g3, f32[4,1024,512]{2,1,0:T(8,128)} %copy-done, ...), custom_call_target="tpu_custom_call" | custom-call | flops 57671680 | bytes 22020096 | tf_op jit(solution)/shard_map/gradient_sums/pallas_call | solution.py:732
  869.3 33.3 %small_gradients.1 = (f32[80,512]{1,0:T(8,128)S(1)}, f32[36,1024]{1,0:T(8,128)S(1)}, f32[1024,128]{1,0:T(8,128)S(1)}) custom-call(f32[48,1024]{1,0:T(8,128)S(1)} %get-tuple-element.149.sums_ref, f32[56,1024]{1,0:T(8,128)S(1)} %copy-done.24, f32[8,1024]{1,0:T(8,128)S(1)} %pad_maximum_fusion.14.stats_ref, f32[36,1024]{1,0:T(8,128)S(1)} %copy-done.26, ...), custom_call_target="tpu_custom_call" | custom-call | tf_op jit(solution)/shard_map/small_gradients/pallas_call | solution.py:865
  912.7 16.9 %history_gradient.1 = f32[9,1024,512]{2,1,0:T(8,128)} custom-call(f32[1024,512]{1,0:T(8,128)S(1)} %get-tuple-element.143.g0, f32[1024,512]{1,0:T(8,128)S(1)} %fusion.56.g1, f32[1024,512]{1,0:T(8,128)S(1)} %fusion.57.g2, f32[1024,512]{1,0:T(8,128)S(1)} %convert_element_type.307.g3, f32[4,1024,512]{2,1,0:T(8,128)} %copy-done, f32[1024,8]{1,0:T(8,128)S(1)} %bitcast.222, ...), custom_call_target="tpu_custom_call" | custom-call | flops 57671680 | bytes 33554432 | tf_op jit(solution)/shard_map/history_gradient/pallas_call | solution.py:925
  (336 shorter events, 238.7 us)
Async XLA Ops:
  7.2 116.4 %all-gather.6.cloned.1.call-start = ((), (), s32[]{:S(2)}) async-start(), calls=%async_computation.2 | async-start | bytes 5242880 | tf_op jit(solution)/shard_map/all_gather | solution.py:1008
  35.6 166.4 %all-gather.8.cloned.1.call-start = ((), (), s32[]{:S(2)}) async-start(), calls=%async_computation.3 | async-start | bytes 5242880 | tf_op jit(solution)/shard_map/all_gather | solution.py:1028
  123.6 159.8 %all-gather.10.cloned.1.call-start = ((), (), s32[]{:S(2)}) async-start(), calls=%async_computation.4 | async-start | bytes 5242880 | tf_op jit(solution)/shard_map/all_gather | solution.py:1028
  202.0 189.8 %all-gather.12.cloned.1.call-start = ((), (), s32[]{:S(2)}) async-start(), calls=%async_computation.5 | async-start | bytes 5242880 | tf_op jit(solution)/shard_map/all_gather | solution.py:1028
  286.3 31.0 %all-to-all-start = ((bf16[4,2,64,512]{3,2,1,0:T(8,128)(2,1)}), bf16[4,2,64,512]{3,2,1,0:T(8,128)(2,1)S(1)}, u32[]{:S(2)}, u32[]{:S(2)}) async-start(bf16[4,2,64,512]{3,2,1,0:T(8,128)(2,1)} %pad_maximum_fusion.12), calls=%async_computation | async-start | bytes 1048576 | tf_op jit(solution)/shard_map/all_to_all | solution.py:1075
  293.0 207.5 %all-gather.14.cloned.1.call-start = ((), (), s32[]{:S(2)}) async-start(), calls=%async_computation.6 | async-start | bytes 5242880 | tf_op jit(solution)/shard_map/all_gather | solution.py:1028
  302.5 104.7 %collective-permute-start.4 = (bf16[1,2,256,2048]{3,2,1,0:T(8,128)(2,1)}, bf16[1,2,256,2048]{3,2,1,0:T(8,128)(2,1)}, u32[]{:S(2)}, u32[]{:S(2)}) collective-permute-start(bf16[1,2,256,2048]{3,2,1,0:T(8,128)(2,1)} %get-tuple-element.117), channel_id=1, source_target_pairs={{0,16},{16,0},{1,17},{17,1},{2,18},{18,2},{3,19},{19,3},{4,20},{20... | collective-permute-start | bytes 6291464 | tf_op jit(solution)/shard_map/ppermute | solution.py:42
  387.7 46.1 %collective-permute-start.2 = (bf16[1,2,256,2048]{3,2,1,0:T(8,128)(2,1)}, bf16[1,2,256,2048]{3,2,1,0:T(8,128)(2,1)}, u32[]{:S(2)}, u32[]{:S(2)}) collective-permute-start(bf16[1,2,256,2048]{3,2,1,0:T(8,128)(2,1)} %get-tuple-element.115), channel_id=1, source_target_pairs={{0,16},{16,0},{1,17},{17,1},{2,18},{18,2},{3,19},{19,3},{4,20},{20... | collective-permute-start | bytes 6291464 | tf_op jit(solution)/shard_map/ppermute | solution.py:42
  391.8 243.3 %reduce-scatter.2.cloned.1.call-start = ((), (), s32[]{:S(2)}) async-start(), calls=%async_computation.7 | async-start | bytes 5242880 | tf_op jit(solution)/shard_map/reduce_scatter | solution.py:1041
  402.9 27.5 %collective-permute-start.7 = (bf16[2,512,512]{2,1,0:T(8,128)(2,1)}, bf16[2,512,512]{2,1,0:T(8,128)(2,1)}, u32[]{:S(2)}, u32[]{:S(2)}) collective-permute-start(bf16[2,512,512]{2,1,0:T(8,128)(2,1)} %bitcast.216), channel_id=1, source_target_pairs={{0,8},{4,12},{1,9},{5,13},{2,10},{6,14},{3,11},{7,15},{16,24},{20,... | collective-permute-start | bytes 3145736 | tf_op jit(solution)/shard_map/ppermute | solution.py:607
  411.5 40.9 %collective-permute-start.5 = (bf16[1,256,2048]{2,1,0:T(8,128)(2,1)S(1)}, bf16[1,256,2048]{2,1,0:T(8,128)(2,1)S(1)}, u32[]{:S(2)}, u32[]{:S(2)}) collective-permute-start(bf16[1,256,2048]{2,1,0:T(8,128)(2,1)S(1)} %get-tuple-element.240), channel_id=1, source_target_pairs={{0,8},{8,0},{4,12},{12,4},{1,9},{9,1},{5,13},{13,5},{2,10},{10,2},... | collective-permute-start | bytes 3145736 | tf_op jit(solution)/shard_map/ppermute | solution.py:46
  415.8 59.3 %collective-permute-start.10 = (bf16[2,512,512]{2,1,0:T(8,128)(2,1)}, bf16[2,512,512]{2,1,0:T(8,128)(2,1)}, u32[]{:S(2)}, u32[]{:S(2)}) collective-permute-start(bf16[2,512,512]{2,1,0:T(8,128)(2,1)} %bitcast.52.refs_4_), channel_id=1, source_target_pairs={{0,8},{4,12},{1,9},{5,13},{2,10},{6,14},{3,11},{7,15},{16,24},{20,... | collective-permute-start | bytes 3145736 | tf_op jit(solution)/shard_map/ppermute | solution.py:607
  430.4 76.7 %collective-permute-start.6 = (bf16[2,512,512]{2,1,0:T(8,128)(2,1)S(1)}, bf16[2,512,512]{2,1,0:T(8,128)(2,1)}, u32[]{:S(2)}, u32[]{:S(2)}) collective-permute-start(bf16[2,512,512]{2,1,0:T(8,128)(2,1)S(1)} %bitcast.217), channel_id=1, source_target_pairs={{0,4},{4,0},{8,12},{12,8},{1,5},{5,1},{9,13},{13,9},{2,6},{6,2},{1... | collective-permute-start | bytes 3145736 | tf_op jit(solution)/shard_map/ppermute | solution.py:50
  430.4 76.7 %collective-permute-start.8 = (bf16[2,512,512]{2,1,0:T(8,128)(2,1)}, bf16[2,512,512]{2,1,0:T(8,128)(2,1)}, u32[]{:S(2)}, u32[]{:S(2)}) collective-permute-start(bf16[2,512,512]{2,1,0:T(8,128)(2,1)} %collective-permute-done.7.refs_2_), channel_id=1, source_target_pairs={{0,4},{4,0},{8,12},{12,8},{1,5},{5,1},{9,13},{13,9},{2,6},{6,2},{1... | collective-permute-start | bytes 3145736 | tf_op jit(solution)/shard_map/ppermute | solution.py:50
  437.7 58.9 %collective-permute-start.3 = (bf16[1,256,2048]{2,1,0:T(8,128)(2,1)}, bf16[1,256,2048]{2,1,0:T(8,128)(2,1)}, u32[]{:S(2)}, u32[]{:S(2)}) collective-permute-start(bf16[1,256,2048]{2,1,0:T(8,128)(2,1)} %get-tuple-element.242), channel_id=1, source_target_pairs={{0,8},{8,0},{4,12},{12,4},{1,9},{9,1},{5,13},{13,5},{2,10},{10,2},... | collective-permute-start | bytes 3145736 | tf_op jit(solution)/shard_map/ppermute | solution.py:46
  453.5 53.6 %collective-permute-start.9 = (bf16[2,512,512]{2,1,0:T(8,128)(2,1)}, bf16[2,512,512]{2,1,0:T(8,128)(2,1)}, u32[]{:S(2)}, u32[]{:S(2)}) collective-permute-start(bf16[2,512,512]{2,1,0:T(8,128)(2,1)} %bitcast.52.refs_4_), channel_id=1, source_target_pairs={{0,4},{4,0},{8,12},{12,8},{1,5},{5,1},{9,13},{13,9},{2,6},{6,2},{1... | collective-permute-start | bytes 3145736 | tf_op jit(solution)/shard_map/ppermute | solution.py:50
  475.0 32.1 %collective-permute-start.11 = (bf16[2,512,512]{2,1,0:T(8,128)(2,1)}, bf16[2,512,512]{2,1,0:T(8,128)(2,1)}, u32[]{:S(2)}, u32[]{:S(2)}) collective-permute-start(bf16[2,512,512]{2,1,0:T(8,128)(2,1)} %collective-permute-done.10.refs_6_), channel_id=1, source_target_pairs={{0,4},{4,0},{8,12},{12,8},{1,5},{5,1},{9,13},{13,9},{2,6},{6,2},{1... | collective-permute-start | bytes 3145736 | tf_op jit(solution)/shard_map/ppermute | solution.py:50
  541.0 43.9 %collective-permute-start.14 = (bf16[2,512,512]{2,1,0:T(8,128)(2,1)}, bf16[2,512,512]{2,1,0:T(8,128)(2,1)}, u32[]{:S(2)}, u32[]{:S(2)}) collective-permute-start(bf16[2,512,512]{2,1,0:T(8,128)(2,1)} %fusion.17), channel_id=1, source_target_pairs={{8,0},{12,4},{9,1},{13,5},{10,2},{14,6},{11,3},{15,7},{24,16},{28,... | collective-permute-start | bytes 3145736 | tf_op jit(solution)/shard_map/ppermute | solution.py:617
  565.9 20.8 %collective-permute-start.15 = (bf16[2,2,512,512]{3,2,1,0:T(8,128)(2,1)}, bf16[2,2,512,512]{3,2,1,0:T(8,128)(2,1)S(1)}, u32[]{:S(2)}, u32[]{:S(2)}) collective-permute-start(bf16[2,2,512,512]{3,2,1,0:T(8,128)(2,1)} %get-tuple-element.135), channel_id=1, source_target_pairs={{0,4},{4,0},{8,12},{12,8},{1,5},{5,1},{9,13},{13,9},{2,6},{6,2},{1... | collective-permute-start | bytes 6291464 | tf_op jit(solution)/shard_map/ppermute | solution.py:50
  587.5 28.5 %collective-permute-start.16 = (bf16[2,512,512]{2,1,0:T(8,128)(2,1)S(1)}, bf16[2,512,512]{2,1,0:T(8,128)(2,1)S(1)}, u32[]{:S(2)}, u32[]{:S(2)}) collective-permute-start(bf16[2,512,512]{2,1,0:T(8,128)(2,1)S(1)} %fusion.18), channel_id=1, source_target_pairs={{8,0},{12,4},{9,1},{13,5},{10,2},{14,6},{11,3},{15,7},{24,16},{28,... | collective-permute-start | bytes 3145736 | tf_op jit(solution)/shard_map/ppermute | solution.py:617
  638.6 264.7 %collective-permute-start.19 = (bf16[2,4,256,512]{3,2,1,0:T(8,128)(2,1)S(1)}, bf16[2,4,256,512]{3,2,1,0:T(8,128)(2,1)S(1)}, u32[]{:S(2)}, u32[]{:S(2)}) collective-permute-start(bf16[2,4,256,512]{3,2,1,0:T(8,128)(2,1)S(1)} %dynamic-slice_bitcast_fusion.2), channel_id=1, source_target_pairs={{0,4},{4,0},{8,12},{12,8},{1,5},{5,1},{9,13},{13,9},{2,6},{6,2},{1... | collective-permute-start | bytes 6291464 | tf_op jit(solution)/shard_map/ppermute | solution.py:50
  639.5 270.6 %collective-permute-start.17 = (bf16[2,2,256,512]{3,2,1,0:T(8,128)(2,1)}, bf16[2,2,256,512]{3,2,1,0:T(8,128)(2,1)}, u32[]{:S(2)}, u32[]{:S(2)}) collective-permute-start(bf16[2,2,256,512]{3,2,1,0:T(8,128)(2,1)} %get-tuple-element.156), channel_id=1, source_target_pairs={{0,16},{16,0},{1,17},{17,1},{2,18},{18,2},{3,19},{19,3},{4,20},{20... | collective-permute-start | bytes 3145736 | tf_op jit(solution)/shard_map/ppermute | solution.py:42
  904.2 25.4 %collective-permute-start.20 = (bf16[2,2,256,512]{3,2,0,1:T(8,128)(2,1)S(1)}, bf16[2,2,256,512]{3,2,0,1:T(8,128)(2,1)S(1)}, u32[]{:S(2)}, u32[]{:S(2)}) collective-permute-start(bf16[2,2,256,512]{3,2,0,1:T(8,128)(2,1)S(1)} %dynamic-slice_bitcast_fusion.7), channel_id=1, source_target_pairs={{0,16},{16,0},{1,17},{17,1},{2,18},{18,2},{3,19},{19,3},{4,20},{20... | collective-permute-start | bytes 3145736 | tf_op jit(solution)/shard_map/ppermute | solution.py:42
  911.8 20.9 %collective-permute-start.18 = (bf16[2,256,512]{2,1,0:T(8,128)(2,1)S(1)}, bf16[2,256,512]{2,1,0:T(8,128)(2,1)S(1)}, u32[]{:S(2)}, u32[]{:S(2)}) collective-permute-start(bf16[2,256,512]{2,1,0:T(8,128)(2,1)S(1)} %dynamic-slice_bitcast_fusion.15), channel_id=1, source_target_pairs={{0,8},{8,0},{4,12},{12,4},{1,9},{9,1},{5,13},{13,5},{2,10},{10,2},... | collective-permute-start | bytes 1572872 | tf_op jit(solution)/shard_map/ppermute | solution.py:46
  (83 other events, 1021.2 us)
Sparse Core Ops, SparseCore 0:
  35.7 81.1 all-gather.5
  123.8 78.1 all-gather.7
  204.1 79.2 all-gather.9
  285.5 106.3 all-gather.11
  393.8 80.1 all-gather.13
  532.5 80.0 reduce-scatter.1

commit v7 on v6

--- a/solution.py
+++ b/solution.py
@@ -79,10 +79,17 @@
     return take(chip, x, 1), take(chip, 1 - x, 1)
 
 
+def line_parts(stays, leaves):
+    return add_bf(stays, over_x(leaves))
+
+
+def last_parts(line):
+    y = lax.axis_index("stream") // 2
+    return take(line, y, 1), over_y(take(line, 1 - y, 1))
+
+
 def plane_parts(stays, leaves):
-    y = lax.axis_index("stream") // 2
-    line = add_bf(stays, over_x(leaves))
-    return take(line, y, 1), over_y(take(line, 1 - y, 1))
+    return last_parts(line_parts(stays, leaves))
 
 
 def scatter_parts(partial):
@@ -115,14 +122,22 @@
     )(a, b)
 
 
-def exchange_kernel(units, whole, axes, *refs):
-    count = len(axes)
-    inputs, refs = refs[: units + whole + count], refs[units + whole + count :]
-    partials, pieces, shard_refs = inputs[:units], inputs[units : units + whole], inputs[units + whole :]
+def exchange_kernel(units, spread, axes, *refs):
+    count, whole = len(axes), 2 if units else 0
+    inputs, refs = refs[: units + count], refs[units + count :]
+    partials, shard_refs = inputs[:units], inputs[units:]
+    if units:
+        done_in, near_in, beside_in = refs[:2], refs[2], refs[3]
+        keep_ref, left_ref, right_ref = refs[4:7]
+        refs = refs[7:]
     outputs, refs = refs[: units + whole + count], refs[units + whole + count :]
     outs, wides, fulls = outputs[:units], outputs[units : units + whole], outputs[units + whole :]
-    held, got, load_sem, send_sem, recv_sem, own_sem, near_send, near_recv = refs[:8]
-    piece_own, piece_send, piece_recv = refs[8:]
+    shares, refs = refs[:spread], refs[spread:]
+    own_sem, near_send, near_recv = refs[:3]
+    if units:
+        held, got, load_sem, send_sem, recv_sem = refs[3:8]
+        mine, theirs, below, pieces, piece_own, piece_send, piece_recv = refs[8:15]
+        mine_sem, done_sem, core_send, core_recv, y_send, y_recv = refs[15:]
     x, stream, z = lax.axis_index("dp"), lax.axis_index("stream"), lax.axis_index("head")
     core = lax.rem(stream, 2)
     other_x, other_y, other_core = 1 - x, lax.rem(stream + 2, 4), stream + 1 - 2 * core
@@ -134,7 +149,8 @@
     beside = lambda at: at + 1 - 2 * core
 
     barrier = pltpu.get_barrier_semaphore()
-    peers = (line if units else ()) + ((to_x, to_y, to_core) if count else ())
+    peers = (line if units or spread else ()) + ((to_x, to_y, to_core) if count else ())
+    peers = peers + (({"head": lax.rem(z + 2, 4)},) if spread else ())
     for peer in peers:
         pl.semaphore_signal(barrier, inc=1, device_id=peer, device_id_type=pl.DeviceIdType.MESH)
     pl.semaphore_wait(barrier, len(peers))
@@ -206,32 +222,101 @@
         ):
             pass_on(w, index, at, to_core, part).wait_send()
 
+    for w in range(count):
+        first(w)
+    if not units:
+        moves = []
+        for i in range(spread):
+            second(i)
+        for i in range(spread):
+            third(i)
+        for i in range(spread):
+            last(i)
+            spread_own, spread_send, spread_recv = refs[3:6]
+            rows, columns = shares[i].shape[0], fulls[i].shape[1]
+            target = shares[i].at[:, pl.ds(pl.multiple_of(z * columns, columns), columns)]
+
+            def source(at):
+                start = (at * 8 + place) * rows
+                return fulls[i].at[pl.ds(pl.multiple_of(start, rows), rows)]
+
+            moves.append(pltpu.make_async_copy(source(z), target, spread_own.at[i]))
+            for k in range(1, 4):
+                to = lax.rem(z + k, 4)
+                moves.append(
+                    pltpu.make_async_remote_copy(
+                        src_ref=source(to),
+                        dst_ref=target,
+                        send_sem=spread_send.at[i, k - 1],
+                        recv_sem=spread_recv.at[i, k - 1],
+                        device_id={"head": to},
+                        device_id_type=pl.DeviceIdType.MESH,
+                    )
+                )
+        for move in moves:
+            move.start()
+        for w in range(spread, count):
+            second(w)
+        for w in range(spread, count):
+            third(w)
+        for w in range(spread, count):
+            last(w)
+        for move in moves:
+            move.wait()
+        return
+
     feats = held.shape[-1]
     chunk = send_sem.shape[-1]
-    step_rows = held.shape[2] // chunk
+    tokens = held.shape[2]
+    step_rows = tokens // chunk
+    y = lax.div(stream, 2)
 
     def load(u, b):
         return pltpu.make_async_copy(
             partials[u].at[:, b * feats : (b + 1) * feats], held.at[u, b], load_sem.at[u, b]
         )
 
+    def to_beside(v):
+        return pltpu.make_async_remote_copy(
+            src_ref=beside_in.at[:, v],
+            dst_ref=theirs.at[v],
+            send_sem=core_send.at[v],
+            recv_sem=core_recv.at[v],
+            device_id=to_core,
+            device_id_type=pl.DeviceIdType.MESH,
+        )
+
+    def load_done(v):
+        return pltpu.make_async_copy(
+            done_in[v], pieces.at[v, pl.ds(0, done_in[v].shape[0])], done_sem.at[v]
+        )
+
+    def load_mine(v):
+        return pltpu.make_async_copy(near_in.at[:, v], mine.at[v], mine_sem.at[v])
+
+    def to_below(v):
+        return pltpu.make_async_remote_copy(
+            src_ref=mine.at[v, 1],
+            dst_ref=below.at[v],
+            send_sem=y_send.at[v],
+            recv_sem=y_recv.at[v],
+            device_id=to_y,
+            device_id_type=pl.DeviceIdType.MESH,
+        )
+
+    for v in range(2):
+        to_beside(v).start()
+        load_mine(v).start()
+        load_done(v).start()
     for u in range(units):
         for b in range(4):
             load(u, b).start()
-    for w in range(count):
-        first(w)
-
-    def columns(block):
-        return pl.ds(pl.multiple_of(block * feats, feats), feats)
-
-    def keep(v):
-        return pltpu.make_async_copy(pieces[v], wides[v].at[:, columns(z)], piece_own.at[v])
-
-    for v in range(whole):
-        keep(v).start()
     for u in range(units):
         for b in range(4):
             load(u, b).wait()
+
+    def columns(block):
+        return pl.ds(pl.multiple_of(block * feats, feats), feats)
 
     def part(c):
         return pl.ds(pl.multiple_of(c * step_rows, step_rows), step_rows)
@@ -251,7 +336,7 @@
     def relay(way, v, step, block, c):
         target = wides[v].at[part(c), columns(block)]
         return pltpu.make_async_remote_copy(
-            src_ref=pieces[v].at[part(c)] if step == 0 else target,
+            src_ref=pieces.at[v, part(c)] if step == 0 else target,
             dst_ref=target,
             send_sem=piece_send.at[way, v, step, c],
             recv_sem=piece_recv.at[way, v, step, c],
@@ -265,11 +350,21 @@
     def block_at(way, step):
         return 3 - step + z if way == 0 else step + z - 3
 
-    def line_step(step):
-        if not units:
-            return
-
-        def body(c, carry):
+    def keep(v):
+        return pltpu.make_async_copy(pieces.at[v], wides[v].at[:, columns(z)], piece_own.at[v])
+
+    def over_parts(body, start=0, stop=None):
+        def step(c, carry):
+            body(c)
+            return carry
+
+        lax.fori_loop(start, chunk if stop is None else stop, step, 0)
+
+    ready = done_in[0].shape[0] // step_rows
+    early, late = (0, ready), (ready, chunk)
+
+    def sum_step(step):
+        def body(c):
             for way, rank in ways:
 
                 @pl.when(rank <= step)
@@ -288,29 +383,83 @@
 
                         hop(way, u, step, block, c).start()
 
+        over_parts(body)
+
+    def gather_step(v, step, span):
+        def body(c):
+            for way, rank in ways:
+
                 @pl.when((rank >= step) & (rank < 3))
                 def _():
                     block = piece_at(way, step)
-                    for v in range(whole):
-                        if step > 0:
-                            relay(way, v, step - 1, block, c).wait_recv()
-                        relay(way, v, step, block, c).start()
-
-            return carry
-
-        lax.fori_loop(0, chunk, body, 0)
-
-    line_step(0)
-    for w in range(min(count, 2)):
+                    if step > 0:
+                        relay(way, v, step - 1, block, c).wait_recv()
+                    relay(way, v, step, block, c).start()
+
+        over_parts(body, *span)
+
+    def chip_sum(v):
+        load_mine(v).wait()
+        to_beside(v).wait()
+
+        @pl.when(y == 1)
+        def _():
+            def body(c):
+                total = mine[v, 1, part(c)].astype(F32) + theirs[v, 1, part(c)].astype(F32)
+                mine[v, 1, part(c)] = total.astype(BF16)
+
+            over_parts(body, 0, chunk - ready)
+            to_below(v).start()
+
+    def bring(v):
+        def body(c, from_y):
+            rows, out = part(c), part(c + ready)
+            total = mine[v, 0, rows].astype(F32) + theirs[v, 0, rows].astype(F32)
+            if from_y:
+                total = total + below[v, rows].astype(F32)
+            if v == 1:
+                pieces[v, out] = total.astype(BF16)
+            else:
+                for head in range(feats // HD):
+                    lanes = slice(head * HD, (head + 1) * HD)
+                    pieces[v, out, lanes] = turn(
+                        total[:, lanes], keep_ref[rows], -left_ref[rows], -right_ref[rows]
+                    ).astype(BF16)
+
+        @pl.when(y == 0)
+        def _():
+            to_below(v).wait_recv()
+            over_parts(lambda c: body(c, True), 0, chunk - ready)
+
+        @pl.when(y == 1)
+        def _():
+            over_parts(lambda c: body(c, False), 0, chunk - ready)
+
+        keep(v).start()
+
+    sum_step(0)
+    for v in range(whole):
+        load_done(v).wait()
+        gather_step(v, 0, early)
+    for v in range(whole):
+        chip_sum(v)
+    for w in range(count):
         second(w)
-    line_step(1)
-    for w in range(2, count):
-        second(w)
-    line_step(2)
+    for v in range(whole):
+        bring(v)
+        gather_step(v, 0, late)
+    sum_step(1)
+    for v in range(whole):
+        gather_step(v, 1, early)
     for w in range(count):
         third(w)
-
-    def finish(c, carry):
+    for v in range(whole):
+        gather_step(v, 1, late)
+    sum_step(2)
+    for v in range(whole):
+        gather_step(v, 2, early)
+
+    def finish(c):
         for u in range(units):
             outs[u][part(c)] = held[u, z, part(c)].astype(F32)
             for way, rank in ways:
@@ -320,6 +469,13 @@
                     hop(way, u, 2, z, c).wait_recv()
                     outs[u][part(c)] += got[way, u, 2, part(c)].astype(F32)
 
+    for v in range(whole):
+        gather_step(v, 2, late)
+    over_parts(finish)
+    for w in range(count):
+        last(w)
+
+    def drain(c):
         for way, rank in ways:
 
             @pl.when(rank == 3)
@@ -328,14 +484,6 @@
                     for step in range(3):
                         relay(way, v, step, piece_at(way, step + 1), c).wait_recv()
 
-        return carry
-
-    if units:
-        lax.fori_loop(0, chunk, finish, 0)
-    for w in range(count):
-        last(w)
-
-    def drain(c, carry):
         for step in range(3):
             for way, rank in ways:
 
@@ -349,56 +497,82 @@
                     for v in range(whole):
                         relay(way, v, step, piece_at(way, step), c).wait_send()
 
-        return carry
-
-    if units:
-        lax.fori_loop(0, chunk, drain, 0)
+    over_parts(drain)
     for v in range(whole):
         keep(v).wait()
 
-
-def exchange(partials, pieces, shards_in, axes, collective_id):
-    units, whole, count = len(partials), len(pieces), len(shards_in)
-    tokens, feats = (partials[0].shape[0], partials[0].shape[1] // 4) if units else (64, 128)
-    chunk = 4
+        @pl.when(y == 1)
+        def _():
+            to_below(v).wait_send()
+
+
+def exchange(partials, rows, shards_in, axes, collective_id, spread=0):
+    units, count = len(partials), len(shards_in)
     grown = ((8, 1), (1, 8), (2, 4))
+    shape = jax.ShapeDtypeStruct
     full = [
-        jax.ShapeDtypeStruct(tuple(n * k for n, k in zip(w.shape, grown[axis])), BF16)
+        shape(tuple(n * k for n, k in zip(w.shape, grown[axis])), BF16)
         for w, axis in zip(shards_in, axes)
     ]
-    anywhere = pl.BlockSpec(memory_space=pl.ANY)
+    anywhere, local = pl.BlockSpec(memory_space=pl.ANY), pl.BlockSpec(memory_space=pltpu.VMEM)
     sems = pltpu.SemaphoreType.DMA
+    out_specs, out_shape = [anywhere] * count, full
+    in_specs = [anywhere] * (units + count)
+    scratch = [sems((count,)), sems((count, 9)), sems((count, 9))]
+    if units:
+        tokens, feats = partials[0].shape[0], partials[0].shape[1] // 4
+        chunk = 4
+        in_specs = in_specs + [anywhere] * 4 + [local] * 3
+        last = rows[2].shape[2]
+        out_specs = [local] * units + [anywhere] * 2 + out_specs
+        out_shape = (
+            [shape((tokens, feats), F32)] * units + [shape((tokens, 4 * feats), BF16)] * 2 + out_shape
+        )
+        scratch = scratch + [
+            pltpu.VMEM((units, 4, tokens, feats), BF16),
+            pltpu.VMEM((2, units, 3, tokens, feats), BF16),
+            sems((units, 4)),
+            sems((2, units, 3, chunk)),
+            sems((2, units, 3, chunk)),
+            pltpu.VMEM((2, 2, last, feats), BF16),
+            pltpu.VMEM((2, 2, last, feats), BF16),
+            pltpu.VMEM((2, last, feats), BF16),
+            pltpu.VMEM((2, tokens, feats), BF16),
+            sems((2,)),
+            sems((2, 2, 3, chunk)),
+            sems((2, 2, 3, chunk)),
+            sems((2,)),
+            sems((2,)),
+            sems((2,)),
+            sems((2,)),
+            sems((2,)),
+            sems((2,)),
+        ]
+    if spread:
+        out_specs = out_specs + [anywhere] * spread
+        out_shape = out_shape + [
+            shape((w.shape[0] // 4, w.shape[1] * 4), BF16) for w in shards_in[:spread]
+        ]
+        scratch = scratch + [sems((spread,))] + [sems((spread, 3))] * 2
     results = pl.pallas_call(
-        functools.partial(exchange_kernel, units, whole, axes),
-        in_specs=[anywhere] * (units + whole + count),
-        out_specs=[pl.BlockSpec(memory_space=pltpu.VMEM)] * units + [anywhere] * (whole + count),
-        out_shape=[jax.ShapeDtypeStruct((tokens, feats), F32)] * units
-        + [jax.ShapeDtypeStruct((tokens, 4 * feats), BF16)] * whole
-        + full,
-        scratch_shapes=[
-            pltpu.VMEM((max(units, 1), 4, tokens, feats), BF16),
-            pltpu.VMEM((2, max(units, 1), 3, tokens, feats), BF16),
-            sems((max(units, 1), 4)),
-            sems((2, max(units, 1), 3, chunk)),
-            sems((2, max(units, 1), 3, chunk)),
-            sems((max(count, 1),)),
-            sems((max(count, 1), 9)),
-            sems((max(count, 1), 9)),
-            sems((max(whole, 1),)),
-            sems((2, max(whole, 1), 3, chunk)),
-            sems((2, max(whole, 1), 3, chunk)),
-        ],
+        functools.partial(exchange_kernel, units, spread, axes),
+        in_specs=in_specs,
+        out_specs=out_specs,
+        out_shape=out_shape,
+        scratch_shapes=scratch,
         compiler_params=pltpu.CompilerParams(
             collective_id=collective_id,
             has_side_effects=True,
-            vmem_limit_bytes=48 * 1024 * 1024,
+            vmem_limit_bytes=(56 if units else 8) * 1024 * 1024,
         ),
         cost_estimate=pl.CostEstimate(
-            flops=0, bytes_accessed=(1 if units else 240) * 1024 * 1024, transcendentals=0
+            flops=0, bytes_accessed=(600 if units else 240) * 1024 * 1024, transcendentals=0
         ),
         name="exchange",
-    )(*partials, *pieces, *shards_in)
-    return results[:units], results[units : units + whole], results[units + whole :]
+    )(*partials, *shards_in, *rows)
+    if not units:
+        return results
+    return results[:units], results[units : len(results) - count], results[len(results) - count :]
 
 
 def head_sum_kernel(members, x_ref, out_ref, slots, send_sem, recv_sem):
@@ -593,8 +767,8 @@
         ],
         compiler_params=pltpu.CompilerParams(vmem_limit_bytes=40 * 1024 * 1024),
         cost_estimate=pl.CostEstimate(
-            flops=0,
-            bytes_accessed=1024,
+            flops=6 * feats * rows * rows * blocks,
+            bytes_accessed=rows * feats * 2 * (4 + 4 * blocks),
             transcendentals=0,
         ),
         name="attention_both_ways",
@@ -679,7 +853,7 @@
     for s in range(4):
         for layer in layers:
             crossed.append(row_sum(streams_ref[s] * layer))
-    out_ref[...] = columns_of(crossed + plain + direct, cot.shape[0]).T[:56]
+    out_ref[...] = columns_of(crossed + plain + direct, cot.shape[0]).T[:64].astype(BF16)
 
 
 def early_sums(streams, cot, history):
@@ -693,8 +867,8 @@
             pl.BlockSpec((block, feats), lambda i: (i, 0)),
             pl.BlockSpec((HIST, block, feats), lambda i: (0, i, 0)),
         ],
-        out_specs=pl.BlockSpec((56, block), lambda i: (0, i)),
-        out_shape=jax.ShapeDtypeStruct((56, tokens), F32),
+        out_specs=pl.BlockSpec((64, block), lambda i: (0, i)),
+        out_shape=jax.ShapeDtypeStruct((64, tokens), BF16),
         compiler_params=pltpu.CompilerParams(vmem_limit_bytes=40 * 1024 * 1024),
         cost_estimate=pl.CostEstimate(
             flops=110 * tokens * feats, bytes_accessed=36 * tokens * feats, transcendentals=0
@@ -703,7 +877,9 @@
     )(streams, cot, history)
 
 
-def sums_kernel(g0, g1, g2, g3, streams_ref, stats_ref, gain_ref, history_ref, out_ref, edge_ref):
+def sums_kernel(
+    g0, g1, g2, g3, streams_ref, stats_ref, gain_ref, history_ref, dots_ref, out_ref, edge_ref
+):
     stats = stats_ref[...]
     rows = stats.shape[0]
 
@@ -722,7 +898,8 @@
         seconds.append(row_sum(scaled * centered))
         for j in range(HIST):
             dots.append(row_sum(scaled * history_ref[j].astype(F32)))
-    out_ref[...] = columns_of(dots + firsts + seconds, rows).T[:48]
+    dots_ref[...] = columns_of(dots, rows).T[:48].astype(BF16)
+    out_ref[...] = columns_of(firsts + seconds, rows).T[:8]
 
 
 def gradient_sums(grads, streams, stats, gain, history):
@@ -741,10 +918,12 @@
         ],
         out_specs=[
             pl.BlockSpec((48, block), lambda i: (0, i)),
+            pl.BlockSpec((8, block), lambda i: (0, i)),
             pl.BlockSpec((8, feats), lambda i: (0, 0)),
         ],
         out_shape=[
-            jax.ShapeDtypeStruct((48, tokens), F32),
+            jax.ShapeDtypeStruct((48, tokens), BF16),
+            jax.ShapeDtypeStruct((8, tokens), F32),
             jax.ShapeDtypeStruct((8, feats), F32),
         ],
         compiler_params=pltpu.CompilerParams(vmem_limit_bytes=40 * 1024 * 1024),
@@ -758,8 +937,9 @@
 def small_kernel(
     members,
     plane,
+    dots_ref,
     sums_ref,
-    early_ref,
+    early_in,
     stats_ref,
     pre_ref,
     slope_ref,
@@ -771,10 +951,17 @@
     small_ref,
     scaled_ref,
     coef_ref,
+    dot_slots,
+    early_slots,
     slots,
     got,
     d_mix_ref,
+    early_ref,
     rows_ref,
+    dot_send,
+    dot_recv,
+    early_send,
+    early_recv,
     send_sem,
     recv_sem,
     plane_send,
@@ -793,35 +980,43 @@
         pl.semaphore_signal(barrier, inc=1, device_id=peer, device_id_type=pl.DeviceIdType.MESH)
     pl.semaphore_wait(barrier, len(line) + len(near))
     copies = []
-    for k, peer in enumerate(line):
-        copy = pltpu.make_async_remote_copy(
-            src_ref=sums_ref,
-            dst_ref=slots.at[z],
-            send_sem=send_sem.at[k],
-            recv_sem=recv_sem.at[k],
-            device_id=peer,
-            device_id_type=pl.DeviceIdType.MESH,
-        )
-        copy.start()
-        copies.append(copy)
-    slots[z] = sums_ref[...]
+    for source, target, sends, receives in (
+        (dots_ref, dot_slots, dot_send, dot_recv),
+        (early_in, early_slots, early_send, early_recv),
+        (sums_ref, slots, send_sem, recv_sem),
+    ):
+        for k, peer in enumerate(line):
+            copy = pltpu.make_async_remote_copy(
+                src_ref=source,
+                dst_ref=target.at[z],
+                send_sem=sends.at[k],
+                recv_sem=receives.at[k],
+                device_id=peer,
+                device_id_type=pl.DeviceIdType.MESH,
+            )
+            copy.start()
+            copies.append(copy)
+        target[z] = source[...]
     for copy in copies:
         copy.wait()
-    total = slots[0]
+    total, dots = slots[0], dot_slots[0].astype(F32)
+    early_ref[...] = early_slots[0].astype(F32)
     for k in range(1, members):
+        early_ref[...] += early_slots[k].astype(F32)
         total = total + slots[k]
-    slots[0] = total
+        dots = dots + dot_slots[k].astype(F32)
+    d_mix_ref[...] = dots[: 4 * HIST]
     n = 4 * HIST
     model_width = members * small_ref.shape[1]
     plain = early_ref[n : n + HIST]
     rows_ref[...] = jnp.zeros_like(rows_ref)
-    rows_ref[0:8] = slots[0, n : n + 8] / model_width
+    rows_ref[0:8] = total / model_width
     for s in range(4):
         part = slice(s * HIST, (s + 1) * HIST)
         mean, inverse = stats_ref[s : s + 1], stats_ref[4 + s : 5 + s]
         crossed = (early_ref[part] - mean * plain) * inverse
         d_part = inverse * (
-            slots[0, part] - rows_ref[s : s + 1] * plain - rows_ref[4 + s : 5 + s] * crossed
+            d_mix_ref[part] - rows_ref[s : s + 1] * plain - rows_ref[4 + s : 5 + s] * crossed
         )
         if s == 3:
             d_part = d_part + early_ref[n + HIST : n + 2 * HIST]
@@ -856,7 +1051,7 @@
         small_ref[...] += got[step]
 
 
-def small_gradients(sums, early, stats, pre, slope, hidden, rms, w_out, current, edges):
+def small_gradients(dots, sums, early, stats, pre, slope, hidden, rms, w_out, current, edges):
     members, plane = lax.axis_size("head"), paired()
     tokens, feats = current.shape
     n = 4 * HIST
@@ -864,14 +1059,21 @@
     sems = pltpu.SemaphoreType.DMA
     small, scaled, coefs = pl.pallas_call(
         functools.partial(small_kernel, members, plane),
-        in_specs=[pl.BlockSpec(memory_space=pltpu.VMEM)] * 10,
+        in_specs=[pl.BlockSpec(memory_space=pltpu.VMEM)] * 11,
         out_specs=[pl.BlockSpec(memory_space=pltpu.VMEM)] * 3,
         out_shape=[shape((80, feats), F32), shape((n, tokens), F32), shape((tokens, 128), F32)],
         scratch_shapes=[
-            pltpu.VMEM((members, 48, tokens), F32),
+            pltpu.VMEM((members, 48, tokens), BF16),
+            pltpu.VMEM((members, 64, tokens), BF16),
+            pltpu.VMEM((members, 8, tokens), F32),
             pltpu.VMEM((3, 80, feats), F32),
             pltpu.VMEM((n, tokens), F32),
+            pltpu.VMEM((64, tokens), F32),
             pltpu.VMEM((128, tokens), F32),
+            sems((members - 1,)),
+            sems((members - 1,)),
+            sems((members - 1,)),
+            sems((members - 1,)),
             sems((members - 1,)),
             sems((members - 1,)),
             sems((3,)),
@@ -881,7 +1083,7 @@
             collective_id=3, has_side_effects=True, vmem_limit_bytes=40 * 1024 * 1024
         ),
         name="small_gradients",
-    )(sums, early, stats, pre, slope, hidden, rms, w_out, current, edges)
+    )(dots, sums, early, stats, pre, slope, hidden, rms, w_out, current, edges)
     if not plane:
         small = lax.psum(small.astype(BF16), ("dp", "stream")).astype(F32)
     return small, scaled, coefs
@@ -1007,7 +1209,7 @@
     mixed, cot_bf, w_up = lax.optimization_barrier((mixed, cot_bf, w_up))
     out_full = lax.all_gather(cot_bf, "head", axis=1, tiled=True)
     if duplex:
-        _, _, (up_full, wk) = exchange([], [], [w_up, w_qkv[1]], (0, 0), 4)
+        (up_full,) = exchange([], (), [w_up], (0,), 4)
         mixed, up_full = lax.optimization_barrier((mixed, up_full))
     rms_scale = lax.rsqrt(mixed[:, 4 * HIST :] / model_width + EPSILON)
     mix_pre = mixed[:, : 4 * HIST] * rms_scale
@@ -1029,8 +1231,8 @@
 
     if duplex:
         w_down, normed = lax.optimization_barrier((w_down, normed))
-        _, _, (down_full, w_out_full, wv, wq) = exchange(
-            [], [], [w_down, w_attn_out, w_qkv[2], w_qkv[0]], (1, 1, 0, 0), 6
+        wk, wv, down_full, w_out_full, wq, *shares = exchange(
+            [], (), [w_qkv[1], w_qkv[2], w_down, w_attn_out, w_qkv[0]], (0, 0, 1, 1, 0), 6, 2
         )
     else:
         wq, wk, wv = gather_weight(w_qkv, 1)
@@ -1050,36 +1252,28 @@
     gated_up, d_up, product_up, product_down = feed_forward(up_in, out_full, up_full, down_full)
     feed_products = [product_up[None], product_down[None]]
     feed_parts = [chip_parts(a) if paired() else a for a in feed_products]
-    streams_late, v_out, d_up, feed_parts = lax.optimization_barrier(
-        (streams, v_out, d_up, feed_parts)
-    )
-    early = head_sum(early_sums(streams_late, cot_bf, history), 2)
-    v_in, q_out, early = lax.optimization_barrier((all_features(v_out), normed[0], early))
-    key_pre, value_pre = dot(k_in, wk), dot(v_in, wv)
-    d_up_in = dot_nt(d_up, up_full).astype(BF16)
-    q_in, d_up_in = lax.optimization_barrier((all_features(q_out), d_up_in))
-    g_up = to_owner(d_up_in)
-    product = lambda a, b: dot_tn(a, b).astype(BF16)
+    v_out, d_up, feed_parts = lax.optimization_barrier((v_out, d_up, feed_parts))
+    feed_lines = [line_parts(*a) for a in feed_parts] if paired() else feed_parts
+    streams_late, feed_lines[0] = lax.optimization_barrier((streams, feed_lines[0]))
+    early = early_sums(streams_late, cot_bf, history)
     feed = dot(gated_up, down_full).astype(BF16)
     d_attended = dot_nt(out_full, w_out_full).astype(BF16) * valid.astype(BF16)
-    feed_terms = [plane_parts(*a) if paired() else scatter_parts(a) for a in feed_parts]
-    grad_up = add_terms(feed_terms[0][0][0], feed_terms[0][1][0], False)
-    grad_down = add_terms(feed_terms[1][0][0], feed_terms[1][1][0], True)
-
-    keys = rotate(key_pre, tables, 1.0)
-    values = value_pre.astype(BF16)
-    queries = dot(q_in, wq)
-    if duplex:
-        place = lax.axis_index("dp") * 4 + member
-        own = lambda w: take(w.reshape(4, 8, feats // 8, feats), place, 1)
-        shares = lax.all_to_all(jnp.stack([own(wk), own(wv)], axis=1), "head", 0, 0)
-        shares = [shares[:, i].transpose(1, 0, 2).reshape(feats // 8, 4 * feats) for i in range(2)]
-        queries, feed, d_attended, grad_up, grad_down, early, shares = lax.optimization_barrier(
-            (queries, feed, d_attended, grad_up, grad_down, early, shares)
-        )
+    d_up_in = dot_nt(d_up, up_full).astype(BF16)
+    keys = rotate(dot(k_in, wk), tables, 1.0)
+    v_in, q_out, early, feed, d_attended, d_up_in, keys, wk, wv = lax.optimization_barrier(
+        (all_features(v_out), normed[0], early, feed, d_attended, d_up_in, keys, wk, wv)
+    )
+    values = dot(v_in, wv).astype(BF16)
     by_micro = lambda a: a.reshape((micro, quarter) + a.shape[1:])
     key_blocks = exchange_rows(by_micro(keys))
     value_blocks = exchange_rows(by_micro(values))
+    q_in, d_up_in, key_blocks, value_blocks, feed_lines[1], early = lax.optimization_barrier(
+        (all_features(q_out), d_up_in, key_blocks, value_blocks, feed_lines[1], early)
+    )
+    g_up = to_owner(d_up_in)
+    product = lambda a, b: dot_tn(a, b).astype(BF16)
+
+    queries = dot(q_in, wq)
     places = member ^ jnp.arange(4, dtype=jnp.int32)
     attended, d_query_pre, d_rows = [], [], []
     queries = by_micro(queries)
@@ -1097,45 +1291,73 @@
         )
         attended.append(results[0][0])
         d_query_pre.append(results[1][0])
+        if duplex and index == micro - 1:
+            continue
         chip = add_f32(results[2], over_core(results[3]))
         across = chip[1].astype(BF16)
         queries, across = lax.optimization_barrier((queries, across))
         d_rows.append(add_f32(chip[0], over_line(across)))
     attended, d_query_pre = jnp.concatenate(attended), jnp.concatenate(d_query_pre)
-    d_key_pre = rotate(jnp.concatenate([a[0] for a in d_rows]), tables, -1.0)
-    d_value_pre = jnp.concatenate([a[1] for a in d_rows]).astype(BF16)
-
-    combined = dot(attended, w_out_full) + feed
+    d_key_rows = jnp.concatenate([a[0] for a in d_rows])
+    done = d_key_rows.shape[0]
+    d_key_rows = rotate(d_key_rows, tuple(a[:done] for a in tables), -1.0)
+    d_value_rows = jnp.concatenate([a[1] for a in d_rows]).astype(BF16)
+    attended, d_query_pre, d_key_rows, d_value_rows = lax.optimization_barrier(
+        (attended, d_query_pre, d_key_rows, d_value_rows)
+    )
+
     products = jnp.stack([product(q_in, d_query_pre), product(out_full, attended)])
     if duplex:
-        partials = [dot_nt(d_query_pre, wq).astype(BF16), combined.astype(BF16)]
+        partials = [dot_nt(d_query_pre, wq).astype(BF16)]
         parts = chip_parts(products)
-        kv = jnp.stack([product(k_in, d_key_pre), product(v_in, d_value_pre)])
-        partials, parts, kv, g_up = lax.optimization_barrier((partials, parts, kv, g_up))
-        (g_query, branch), (d_key_full, d_value_full), (wk_rows, wv_rows) = exchange(
-            partials, [d_key_pre, d_value_pre], shares, (0, 0), 5
-        )
+        partials, parts, g_up, feed_lines = lax.optimization_barrier(
+            (partials, parts, g_up, feed_lines)
+        )
+        feed_terms = [last_parts(a) for a in feed_lines]
+        (g_query,), (d_key_full, d_value_full), (wk_rows, wv_rows) = exchange(
+            partials,
+            [d_key_rows, d_value_rows, results[2], results[3], *(a[done:] for a in tables)],
+            shares,
+            (0, 0),
+            5,
+        )
+        attended_late, g_query = lax.optimization_barrier((attended, g_query))
+        pair = lambda a: (a[: tokens // 2], a[tokens // 2 :])
+        halves = [
+            (dot(a, w_out_full) + b).astype(BF16) for a, b in zip(pair(attended_late), pair(feed))
+        ]
+        branch = to_owner(halves[0])
         g_key, g_value = dot_nt(d_key_full, wk_rows), dot_nt(d_value_full, wv_rows)
-        kv_terms = scatter_parts(kv)
         terms = plane_parts(*parts)
     else:
         g_query = to_owner(dot_nt(d_query_pre, wq))
-        g_key = to_owner(dot_nt(d_key_pre, wk))
-        g_value = to_owner(dot_nt(d_value_pre, wv))
-        branch = to_owner(combined)
+        branch = to_owner(dot(attended, w_out_full) + feed)
         terms = scatter_parts(products)
+        feed_terms = [scatter_parts(a) for a in feed_products]
+        g_key = to_owner(dot_nt(d_key_rows, wk))
+        g_value = to_owner(dot_nt(d_value_rows, wv))
         kv_terms = scatter_parts(
-            jnp.stack([product(k_in, d_key_pre), product(v_in, d_value_pre)])
-        )
+            jnp.stack([product(k_in, d_key_rows), product(v_in, d_value_rows)])
+        )
+    grad_up = add_terms(feed_terms[0][0][0], feed_terms[0][1][0], False)
+    grad_down = add_terms(feed_terms[1][0][0], feed_terms[1][1][0], True)
+    grad_attn_out = add_terms(terms[0][1], terms[1][1], True)
+
+    grads = (g_query, g_key, g_value, g_up)
+    dots, sums, edges = gradient_sums(grads, streams, row_stats, ln_gain, history)
+    if duplex:
+        sums, d_key_full, d_value_full = lax.optimization_barrier((sums, d_key_full, d_value_full))
+        own = lambda a: lax.dynamic_slice_in_dim(a, lax.axis_index("head") * feats, feats, 1)
+        kv = jnp.stack([product(k_in, own(d_key_full)), product(v_in, own(d_value_full))])
+        kv_terms = scatter_parts(kv)
+    grad_query = terms[0][:1].astype(F32) + terms[1][:1].astype(F32)
+    small, d_scaled, coefs = small_gradients(
+        dots, sums, early, row_stats.T, mix_pre.T, slope_mix.T, mix_hidden.T, rms_scale.T, w_mix_out_f, current, edges
+    )
+    if duplex:
+        coefs, second_half = lax.optimization_barrier((coefs, halves[1]))
+        branch = jnp.concatenate([branch, to_owner(second_half)])
     block_out = (valid * (streams[3] + branch)).astype(BF16)
-    grad_query = terms[0][:1].astype(F32) + terms[1][:1].astype(F32)
-    grad_attn_out = add_terms(terms[0][1], terms[1][1], True)
-
-    grads = (g_query, g_key, g_value, g_up)
-    sums, edges = gradient_sums(grads, streams, row_stats, ln_gain, history)
-    small, d_scaled, coefs = small_gradients(
-        sums, early, row_stats.T, mix_pre.T, slope_mix.T, mix_hidden.T, rms_scale.T, w_mix_out_f, current, edges
-    )
     history_grad = history_gradient(
         grads, streams, row_stats, ln_gain, cot_bf, current, mix_weights, coefs, d_scaled, w_mix_in_f.T
     ).reshape(HIST, micro, quarter, feats)

time: 960 us -> 924 us (0.963)
  Pallas kernels: 593 us -> 533 us
  local copies, waits for them, and re-layouts: 58.6 us -> 79.3 us
  waiting for transfers between devices: 115 us -> 129 us
    pallas_call x3 -> x2, Pallas kernels: 78.4 us -> 31 us  [head_sum(): pl.pallas_call(functools.partial(head_sum_kernel, members), out_shape=jax...]
    ppermute x4, waiting for transfers between devices: 2.94 us -> 39.1 us  [over_x(): return lax.ppermute(a, 'dp', SWAP_X)]
    ppermute x4, waiting for transfers between devices: 25.8 us -> 1.34 us  [over_y(): return lax.ppermute(a, 'stream', SWAP_Y)]
    ppermute x2 -> x1, waiting for transfers between devices: 24 us -> 0.01 us  [over_line(): return lax.ppermute(a, 'stream', [(2, 0), (3, 1)])]
    pallas_call x3, Pallas kernels: 317 us -> 294 us  [exchange(): pl.pallas_call(functools.partial(exchange_kernel, units, spread, axes), i...]
    reduce_scatter x1 -> x3, waiting for transfers between devices: 0.01 us -> 22.1 us  [to_owner(): lax.psum_scatter(partial.astype(BF16), 'head', scatter_dimension=1, tiled...]
    unnamed x160 -> x219, local copies, waits for them, and re-layouts: 23.2 us -> 40.8 us
    ppermute x2, waiting for transfers between devices: 21.5 us -> 37 us  [exchange_rows(): across = lax.ppermute(local, 'stream', [(0, 2), (1, 3)])]
  transfers between devices with their start and end apart: 29 -> 28, of which waited for: 12 -> 12; matrix products, arithmetic and copies ran while one was open for 17% -> 17% of each run, Pallas kernels for 58% -> 35%
where the time goes in v7:
time: 924 us; the launch traced here: 915 us
  Pallas kernels  533 us (58%)
  waiting for transfers between devices  129 us (14%)
  matrix products  79.5 us (9%)
  local copies, waits for them, and re-layouts  79.3 us (9%)
  other arithmetic  58.4 us (6%)
  starting transfers between devices  19.6 us (2%)
  between operations  15.7 us (2%)
    pallas_call x3, Pallas kernels, exchange(): pl.pallas_call(functools.partial(exchange_kernel, units, spread, axes), i...  294 us
    pallas_call x2, Pallas kernels, attention(): pl.pallas_call(attention_kernel, grid=(feats // HD,), in_specs=[pl.BlockS...  46.5 us
    pallas_call x1, Pallas kernels, small_gradients(): pl.pallas_call(functools.partial(small_kernel, members, plane), in_specs=...  45 us
    pallas_call x1, Pallas kernels, feed_forward(): pl.pallas_call(feed_kernel, grid=(hidden // block,), in_specs=[fixed, fix...  42.5 us
    unnamed x219, local copies, waits for them, and re-layouts  40.8 us
    ppermute x4, waiting for transfers between devices, over_x(): return lax.ppermute(a, 'dp', SWAP_X)  39.1 us
    ppermute x2, waiting for transfers between devices, exchange_rows(): across = lax.ppermute(local, 'stream', [(0, 2), (1, 3)])  37 us
    dot_general x6, matrix products, dot(): return jnp.dot(a, b, preferred_element_type=F32)  33.2 us
  transfers between devices with their start and end apart: 28, of which 12 were waited for; matrix products, arithmetic and copies ran while one was open for 17% of the time, Pallas kernels for 35%

profile of v7, /device:TPU:8, one launch (start us, length us, event | category | flops | bytes accessed | tf_op | source)
XLA Modules:
  0.0 914.9 jit_solution(8726569667426466242)
XLA Ops:
  14.1 19.2 %sum_over_head.2 = f32[37,1024]{1,0:T(8,128)} custom-call(f32[37,1024]{1,0:T(8,128)} %pad_maximum_fusion.4.x_ref), custom_call_target="tpu_custom_call" | custom-call | tf_op jit(solution)/shard_map/sum_over_head/pallas_call | solution.py:612
  34.8 41.1 %exchange.3.up_ref = bf16[2048,2048]{1,0:T(8,128)(2,1)S(1)} custom-call(bf16[256,2048]{1,0:T(8,128)(2,1)S(1)} %copy-done.36), custom_call_target="tpu_custom_call" | custom-call | bytes 251658240 | tf_op jit(solution)/shard_map/exchange/pallas_call | solution.py:557
  80.5 12.3 %mix_streams.1 = (f32[4,1024,512]{2,1,0:T(8,128)S(1)}, f32[8,1024]{1,0:T(8,128)S(1)}) custom-call(f32[1024,36]{1,0:T(8,128)S(1)} %convolution_add_fusion.weights_ref, bf16[9,1024,512]{2,1,0:T(8,128)(2,1)} %bitcast.208), custom_call_target="tpu_custom_call" | custom-call | flops 41943040 | bytes 17825792 | tf_op jit(solution)/shard_map/mix_streams/pallas_call | solution.py:823
  96.8 11.8 %sum_over_head.3 = f32[8,1024]{1,0:T(8,128)} custom-call(f32[8,1024]{1,0:T(8,128)} %copy-done.55), custom_call_target="tpu_custom_call" | custom-call | tf_op jit(solution)/shard_map/sum_over_head/pallas_call | solution.py:612
  117.1 85.8 %exchange.4 = (bf16[2048,512]{1,0:T(8,128)(2,1)S(1)}, bf16[2048,512]{1,0:T(8,128)(2,1)S(1)}, bf16[2048,2048]{1,0:T(8,128)(2,1)S(1)}, bf16[512,2048]{1,0:T(8,128)...) custom-call(bf16[256,512]{1,0:T(8,128)(2,1)S(1)} %get-tuple-element.283.refs_0_, ...), custom_call_target="tpu_custom_call" | custom-call | bytes 251658240 | tf_op jit(solution)/shard_map/exchange/pallas_call | solution.py:557
  213.3 42.5 %feed_forward.1 = (bf16[1024,2048]{1,0:T(8,128)(2,1)}, bf16[1024,2048]{1,0:T(8,128)(2,1)}, bf16[2048,2048]{1,0:T(8,128)(2,1)}, bf16[2048,2048]{1,0:T(8,128)(2,1)}) custom-call(bf16[1024,2048]{1,0:T(8,128)(2,1)} %all-gather.8.cloned.1.call-done.x_ref, bf16[1024,2048]{1,0:T(8,128)(2,1)} %all-gather.6.cloned.1.call-done.d_ref, bf16[2048,2048]{1,0:T(8,128)(2,1)} %copy-done.15, ...), custom_call_target="tpu_custom_call" | custom-call | flops 34359738368 | bytes 41943040 | tf_op jit(solution)/shard_map/feed_forward/pallas_call | solution.py:684
  283.3 6.9 all-gather.10.cloned.1.call-done
  294.9 5.7 fusion.17
  300.6 10.7 %convolution_convert_fusion.2 = bf16[1024,2048]{1,0:T(8,128)(2,1)} fusion(bf16[1024,2048]{1,0:T(8,128)(2,1)S(1)} %copy-done.105, bf16[2048,2048]{1,0:T(8,128)(2,1)S(1)} %bitcast.207), kind=kOutput, calls=%fused_computation.26 | convolution fusion | flops 8592031744 | bytes 16777216 | tf_op jit(solution)/shard_map/dot_general | solution.py:26
  321.1 13.9 %convolution_convert_fusion.1 = bf16[1024,2048]{1,0:T(8,128)(2,1)} fusion(bf16[1024,2048]{1,0:T(8,128)(2,1)} %get-tuple-element.130, bf16[2048,2048]{1,0:T(8,128)(2,1)} %copy-done.15), kind=kOutput, calls=%fused_computation.25 | convolution fusion | flops 8592031744 | bytes 16777216 | tf_op jit(solution)/shard_map/dot_general | solution.py:30
  335.1 24.1 %collective-permute-done.2 = bf16[1,2,256,2048]{3,2,1,0:T(8,128)(2,1)} collective-permute-done((bf16[1,2,256,2048]{3,2,1,0:T(8,128)(2,1)}, bf16[1,2,256,2048]{3,2,1,0:T(8,128)(2,1)}, u32[]{:S(2)}, u32[]{:S(2)}) %collective-permute-start.2) | collective-permute-done | bytes 2097184 | tf_op jit(solution)/shard_map/ppermute | solution.py:42
  366.3 11.9 %early_sums.1.early_in = bf16[64,1024]{1,0:T(8,128)(2,1)S(1)} custom-call(f32[4,1024,512]{2,1,0:T(8,128)S(1)} %copy-done.1, bf16[1024,512]{1,0:T(8,128)(2,1)S(1)} %copy-done.4, bf16[9,1024,512]{2,1,0:T(8,128)(2,1)} %bitcast.209), custom_call_target="tpu_custom_call" | custom-call | flops 57671680 | bytes 18874368 | tf_op jit(solution)/shard_map/early_sums/pallas_call | solution.py:862
  396.2 17.0 %collective-permute-done.7.refs_6_ = bf16[2,512,512]{2,1,0:T(8,128)(2,1)} collective-permute-done((bf16[2,512,512]{2,1,0:T(8,128)(2,1)}, bf16[2,512,512]{2,1,0:T(8,128)(2,1)}, u32[]{:S(2)}, u32[]{:S(2)}) %collective-permute-start.7) | collective-permute-done | bytes 1048608 | tf_op jit(solution)/shard_map/ppermute | solution.py:781
  413.2 20.0 %collective-permute-done.4.refs_2_ = bf16[2,512,512]{2,1,0:T(8,128)(2,1)} collective-permute-done((bf16[2,512,512]{2,1,0:T(8,128)(2,1)S(1)}, bf16[2,512,512]{2,1,0:T(8,128)(2,1)}, u32[]{:S(2)}, u32[]{:S(2)}) %collective-permute-start.4) | collective-permute-done | bytes 1048608 | tf_op jit(solution)/shard_map/ppermute | solution.py:781
  442.6 15.6 %all-gather.14.cloned.1.call-done = bf16[1024,2048]{1,0:T(8,128)(2,1)} async-done(((bf16[1024,512]{1,0:T(8,128)(2,1)}), bf16[1024,2048]{1,0:T(8,128)(2,1)}) %all-gather.14.cloned.1.call-update) | async-done | bytes 4194320 | tf_op jit(solution)/shard_map/all_gather | solution.py:1230
  458.2 6.6 fusion.59
  464.9 23.3 %attention_both_ways.2 = (bf16[1,512,512]{2,1,0:T(8,128)(2,1)S(1)}, bf16[1,512,512]{2,1,0:T(8,128)(2,1)S(1)}, bf16[2,2,512,512]{3,2,1,0:T(8,128)(2,1)}, bf16[2,2,512,512]{3,2,1,0:T(8,128)(2,1)}) custom-call(s32[4]{0:T(128)S(1)} %iota_xor_fusion.place_ref, f32[2,512,512]{2,1,0:T(8,128)} %bitcast.230, bf16[2,512,512]{2,1,0:T(8,128)(2,1)S(1)} %bitcast.199, ...), custom_call_target="tpu_custom_call" | custom-call | flops 3221225472 | bytes 10485760 | tf_op jit(solution)/shard_map/attention_both_ways/pallas_call | solution.py:755
  501.0 23.2 %attention_both_ways.3 = (bf16[1,512,512]{2,1,0:T(8,128)(2,1)S(1)}, bf16[1,512,512]{2,1,0:T(8,128)(2,1)S(1)}, bf16[2,2,512,512]{3,2,1,0:T(8,128)(2,1)}, bf16[2,2,512,512]{3,2,1,0:T(8,128)(2,1)}) custom-call(s32[4]{0:T(128)S(1)} %iota_xor_fusion.place_ref, f32[2,512,512]{2,1,0:T(8,128)} %bitcast.231, bf16[2,512,512]{2,1,0:T(8,128)(2,1)S(1)} %bitcast.200, ...), custom_call_target="tpu_custom_call" | custom-call | flops 3221225472 | bytes 10485760 | tf_op jit(solution)/shard_map/attention_both_ways/pallas_call | solution.py:755
  546.0 22.1 %reduce-scatter.4.cloned.1.call-done = bf16[1024,512]{1,0:T(8,128)(2,1)} async-done(((bf16[1024,2048]{1,0:T(8,128)(2,1)}), bf16[1024,512]{1,0:T(8,128)(2,1)}) %reduce-scatter.4.cloned.1.call-update) | async-done | bytes 1048592 | tf_op jit(solution)/shard_map/reduce_scatter | solution.py:1243
  569.6 166.8 %exchange.5 = (f32[1024,512]{1,0:T(8,128)}, bf16[1024,2048]{1,0:T(8,128)(2,1)}, bf16[1024,2048]{1,0:T(8,128)(2,1)}, bf16[512,2048]{1,0:T(8,128)(2,1)}, bf16[512,2048]{1,0:T(8,128)(2,1)}) custom-call(bf16[1024,2048]{1,0:T(8,128)(2,1)} %convolution_convert_fusion.refs_0_, bf16[64,2048]{1,0:T(8,128)(2,1)} %copy-done.47, bf16[64,2048]{1,0:T(8,128)(2,1)} %copy-done.48, ...), custom_call_target="tpu_custom_call" | custom-call | bytes 629145600 | tf_op jit(solution)/shard_map/exchange/pallas_call | solution.py:557
  749.5 16.6 %gradient_sums.1 = (bf16[48,1024]{1,0:T(8,128)(2,1)S(1)}, f32[8,1024]{1,0:T(8,128)S(1)}, f32[8,512]{1,0:T(8,128)S(1)}) custom-call(f32[1024,512]{1,0:T(8,128)S(1)} %copy-done.9, f32[1024,512]{1,0:T(8,128)S(1)} %fusion.60.g1, f32[1024,512]{1,0:T(8,128)S(1)} %fusion.61.g2, f32[1024,512]{1,0:T(8,128)S(1)} %convert_element_type.307.g3, f32[4,1024,512]{2,1,0:T(8,128)} %copy-done, ...), custom_call_target="tpu_custom_call" | custom-call | flops 57671680 | bytes 22020096 | tf_op jit(solution)/shard_map/gradient_sums/pallas_call | solution.py:909
  776.1 45.0 %small_gradients.1 = (f32[80,512]{1,0:T(8,128)S(1)}, f32[36,1024]{1,0:T(8,128)S(1)}, f32[1024,128]{1,0:T(8,128)S(1)}) custom-call(bf16[48,1024]{1,0:T(8,128)(2,1)S(1)} %get-tuple-element.182.dots_ref, f32[8,1024]{1,0:T(8,128)S(1)} %get-tuple-element.184.sums_ref, bf16[64,1024]{1,0:T(8,128)(2,1)S(1)} %copy-done.41, ...), custom_call_target="tpu_custom_call" | custom-call | tf_op jit(solution)/shard_map/small_gradients/pallas_call | solution.py:1060
  846.4 15.0 %collective-permute-done.13 = bf16[2,2,256,512]{3,2,1,0:T(8,128)(2,1)} collective-permute-done((bf16[2,2,256,512]{3,2,1,0:T(8,128)(2,1)}, bf16[2,2,256,512]{3,2,1,0:T(8,128)(2,1)}, u32[]{:S(2)}, u32[]{:S(2)}) %collective-permute-start.13) | collective-permute-done | bytes 1048608 | tf_op jit(solution)/shard_map/ppermute | solution.py:42
  869.7 17.0 %history_gradient.1 = f32[9,1024,512]{2,1,0:T(8,128)} custom-call(f32[1024,512]{1,0:T(8,128)S(1)} %copy-done.10, f32[1024,512]{1,0:T(8,128)S(1)} %copy-done.14, f32[1024,512]{1,0:T(8,128)S(1)} %copy-done.12, f32[1024,512]{1,0:T(8,128)S(1)} %convert_element_type.307.g3, f32[4,1024,512]{2,1,0:T(8,128)} %copy-done, f32[1024,8]{1,0:T(8,128)S(1)} %bitcast.198, ...), custom_call_target="tpu_custom_call" | custom-call | flops 57671680 | bytes 33554432 | tf_op jit(solution)/shard_map/history_gradient/pallas_call | solution.py:1127
  (390 shorter events, 225.2 us)
Async XLA Ops:
  7.2 108.9 %all-gather.6.cloned.1.call-start = ((), (), s32[]{:S(2)}) async-start(), calls=%async_computation.3 | async-start | bytes 5242880 | tf_op jit(solution)/shard_map/all_gather | solution.py:1210
  34.8 178.2 %all-gather.8.cloned.1.call-start = ((), (), s32[]{:S(2)}) async-start(), calls=%async_computation.4 | async-start | bytes 5242880 | tf_op jit(solution)/shard_map/all_gather | solution.py:1230
  116.1 174.2 %all-gather.10.cloned.1.call-start = ((), (), s32[]{:S(2)}) async-start(), calls=%async_computation.5 | async-start | bytes 5242880 | tf_op jit(solution)/shard_map/all_gather | solution.py:1230
  213.0 165.8 %all-gather.12.cloned.1.call-start = ((), (), s32[]{:S(2)}) async-start(), calls=%async_computation.6 | async-start | bytes 5242880 | tf_op jit(solution)/shard_map/all_gather | solution.py:1230
  264.4 11.8 %collective-permute-start = (bf16[1,4,256,2048]{3,2,1,0:T(8,128)(2,1)}, bf16[1,4,256,2048]{3,2,1,0:T(8,128)(2,1)}, u32[]{:S(2)}, u32[]{:S(2)}) collective-permute-start(bf16[1,4,256,2048]{3,2,1,0:T(8,128)(2,1)} %dynamic-slice_bitcast_fusion.1), channel_id=1, source_target_pairs={{0,4},{4,0},{8,12},{12,8},{1,5},{5,1},{9,13},{13,9},{2,6},{6,2},{1... | collective-permute-start | bytes 12582920 | tf_op jit(solution)/shard_map/ppermute | solution.py:50
  290.3 167.9 %all-gather.14.cloned.1.call-start = ((), (), s32[]{:S(2)}) async-start(), calls=%async_computation.7 | async-start | bytes 5242880 | tf_op jit(solution)/shard_map/all_gather | solution.py:1230
  311.3 47.8 %collective-permute-start.2 = (bf16[1,2,256,2048]{3,2,1,0:T(8,128)(2,1)}, bf16[1,2,256,2048]{3,2,1,0:T(8,128)(2,1)}, u32[]{:S(2)}, u32[]{:S(2)}) collective-permute-start(bf16[1,2,256,2048]{3,2,1,0:T(8,128)(2,1)} %get-tuple-element.126), channel_id=1, source_target_pairs={{0,16},{16,0},{1,17},{17,1},{2,18},{18,2},{3,19},{19,3},{4,20},{20... | collective-permute-start | bytes 6291464 | tf_op jit(solution)/shard_map/ppermute | solution.py:42
  378.8 189.3 %reduce-scatter.4.cloned.1.call-start = ((), (), s32[]{:S(2)}) async-start(), calls=%async_computation.8 | async-start | bytes 5242880 | tf_op jit(solution)/shard_map/reduce_scatter | solution.py:1243
  378.9 55.8 %collective-permute-start.9 = (bf16[1,2,256,2048]{3,2,1,0:T(8,128)(2,1)}, bf16[1,2,256,2048]{3,2,1,0:T(8,128)(2,1)}, u32[]{:S(2)}, u32[]{:S(2)}) collective-permute-start(bf16[1,2,256,2048]{3,2,1,0:T(8,128)(2,1)} %get-tuple-element.140), channel_id=1, source_target_pairs={{0,16},{16,0},{1,17},{17,1},{2,18},{18,2},{3,19},{19,3},{4,20},{20... | collective-permute-start | bytes 6291464 | tf_op jit(solution)/shard_map/ppermute | solution.py:42
  385.9 27.3 %collective-permute-start.7 = (bf16[2,512,512]{2,1,0:T(8,128)(2,1)}, bf16[2,512,512]{2,1,0:T(8,128)(2,1)}, u32[]{:S(2)}, u32[]{:S(2)}) collective-permute-start(bf16[2,512,512]{2,1,0:T(8,128)(2,1)} %bitcast.32.refs_4_), channel_id=1, source_target_pairs={{0,8},{4,12},{1,9},{5,13},{2,10},{6,14},{3,11},{7,15},{16,24},{20,... | collective-permute-start | bytes 3145736 | tf_op jit(solution)/shard_map/ppermute | solution.py:781
  390.3 42.9 %collective-permute-start.4 = (bf16[2,512,512]{2,1,0:T(8,128)(2,1)S(1)}, bf16[2,512,512]{2,1,0:T(8,128)(2,1)}, u32[]{:S(2)}, u32[]{:S(2)}) collective-permute-start(bf16[2,512,512]{2,1,0:T(8,128)(2,1)S(1)} %bitcast.192), channel_id=1, source_target_pairs={{0,8},{4,12},{1,9},{5,13},{2,10},{6,14},{3,11},{7,15},{16,24},{20,... | collective-permute-start | bytes 3145736 | tf_op jit(solution)/shard_map/ppermute | solution.py:781
  395.6 43.0 %collective-permute-start.6 = (bf16[2,512,512]{2,1,0:T(8,128)(2,1)}, bf16[2,512,512]{2,1,0:T(8,128)(2,1)S(1)}, u32[]{:S(2)}, u32[]{:S(2)}) collective-permute-start(bf16[2,512,512]{2,1,0:T(8,128)(2,1)} %bitcast.32.refs_4_), channel_id=1, source_target_pairs={{0,4},{4,0},{8,12},{12,8},{1,5},{5,1},{9,13},{13,9},{2,6},{6,2},{1... | collective-permute-start | bytes 3145736 | tf_op jit(solution)/shard_map/ppermute | solution.py:50
  395.7 43.9 %collective-permute-start.3 = (bf16[2,512,512]{2,1,0:T(8,128)(2,1)S(1)}, bf16[2,512,512]{2,1,0:T(8,128)(2,1)S(1)}, u32[]{:S(2)}, u32[]{:S(2)}) collective-permute-start(bf16[2,512,512]{2,1,0:T(8,128)(2,1)S(1)} %bitcast.193), channel_id=1, source_target_pairs={{0,4},{4,0},{8,12},{12,8},{1,5},{5,1},{9,13},{13,9},{2,6},{6,2},{1... | collective-permute-start | bytes 3145736 | tf_op jit(solution)/shard_map/ppermute | solution.py:50
  413.2 27.4 %collective-permute-start.8 = (bf16[2,512,512]{2,1,0:T(8,128)(2,1)}, bf16[2,512,512]{2,1,0:T(8,128)(2,1)S(1)}, u32[]{:S(2)}, u32[]{:S(2)}) collective-permute-start(bf16[2,512,512]{2,1,0:T(8,128)(2,1)} %collective-permute-done.7.refs_6_), channel_id=1, source_target_pairs={{0,4},{4,0},{8,12},{12,8},{1,5},{5,1},{9,13},{13,9},{2,6},{6,2},{1... | collective-permute-start | bytes 3145736 | tf_op jit(solution)/shard_map/ppermute | solution.py:50
  489.8 415.5 %reduce-scatter.6.cloned.1.call-start = ((), (), s32[]{:S(2)}) async-start(), calls=%async_computation.9 | async-start | bytes 2621440 | tf_op jit(solution)/shard_map/reduce_scatter | solution.py:1243
  497.5 28.0 %collective-permute-start.11 = (bf16[2,512,512]{2,1,0:T(8,128)(2,1)S(1)}, bf16[2,512,512]{2,1,0:T(8,128)(2,1)S(1)}, u32[]{:S(2)}, u32[]{:S(2)}) collective-permute-start(bf16[2,512,512]{2,1,0:T(8,128)(2,1)S(1)} %fusion.18), channel_id=1, source_target_pairs={{8,0},{12,4},{9,1},{13,5},{10,2},{14,6},{11,3},{15,7},{24,16},{28,... | collective-permute-start | bytes 3145736 | tf_op jit(solution)/shard_map/ppermute | solution.py:791
  740.6 164.7 %reduce-scatter.8.cloned.1.call-start = ((), (), s32[]{:S(2)}) async-start(), calls=%async_computation.10 | async-start | bytes 2621440 | tf_op jit(solution)/shard_map/reduce_scatter | solution.py:1243
  774.6 61.1 %collective-permute-start.15 = (bf16[2,4,256,512]{3,2,1,0:T(8,128)(2,1)}, bf16[2,4,256,512]{3,2,1,0:T(8,128)(2,1)}, u32[]{:S(2)}, u32[]{:S(2)}) collective-permute-start(bf16[2,4,256,512]{3,2,1,0:T(8,128)(2,1)} %fusion.5), channel_id=1, source_target_pairs={{0,4},{4,0},{8,12},{12,8},{1,5},{5,1},{9,13},{13,9},{2,6},{6,2},{1... | collective-permute-start | bytes 6291464 | tf_op jit(solution)/shard_map/ppermute | solution.py:50
  834.3 55.5 %collective-permute-start.19 = (bf16[1,256,2048]{2,1,0:T(8,128)(2,1)}, bf16[1,256,2048]{2,1,0:T(8,128)(2,1)}, u32[]{:S(2)}, u32[]{:S(2)}) collective-permute-start(bf16[1,256,2048]{2,1,0:T(8,128)(2,1)} %get-tuple-element.276), channel_id=1, source_target_pairs={{0,8},{8,0},{4,12},{12,4},{1,9},{9,1},{5,13},{13,5},{2,10},{10,2},... | collective-permute-start | bytes 3145736 | tf_op jit(solution)/shard_map/ppermute | solution.py:46
  834.9 26.4 %collective-permute-start.13 = (bf16[2,2,256,512]{3,2,1,0:T(8,128)(2,1)}, bf16[2,2,256,512]{3,2,1,0:T(8,128)(2,1)}, u32[]{:S(2)}, u32[]{:S(2)}) collective-permute-start(bf16[2,2,256,512]{3,2,1,0:T(8,128)(2,1)} %get-tuple-element.193), channel_id=1, source_target_pairs={{0,16},{16,0},{1,17},{17,1},{2,18},{18,2},{3,19},{19,3},{4,20},{20... | collective-permute-start | bytes 3145736 | tf_op jit(solution)/shard_map/ppermute | solution.py:42
  839.2 47.6 %collective-permute-start.16 = (bf16[2,2,256,512]{3,2,0,1:T(8,128)(2,1)}, bf16[2,2,256,512]{3,2,0,1:T(8,128)(2,1)}, u32[]{:S(2)}, u32[]{:S(2)}) collective-permute-start(bf16[2,2,256,512]{3,2,0,1:T(8,128)(2,1)} %dynamic-slice_bitcast_fusion.10), channel_id=1, source_target_pairs={{0,16},{16,0},{1,17},{17,1},{2,18},{18,2},{3,19},{19,3},{4,20},{20... | collective-permute-start | bytes 3145736 | tf_op jit(solution)/shard_map/ppermute | solution.py:42
  842.3 53.8 %collective-permute-start.18 = (bf16[1,256,2048]{2,1,0:T(8,128)(2,1)}, bf16[1,256,2048]{2,1,0:T(8,128)(2,1)}, u32[]{:S(2)}, u32[]{:S(2)}) collective-permute-start(bf16[1,256,2048]{2,1,0:T(8,128)(2,1)} %get-tuple-element.278), channel_id=1, source_target_pairs={{0,8},{8,0},{4,12},{12,4},{1,9},{9,1},{5,13},{13,5},{2,10},{10,2},... | collective-permute-start | bytes 3145736 | tf_op jit(solution)/shard_map/ppermute | solution.py:46
  864.1 30.3 %collective-permute-start.14 = (bf16[2,256,512]{2,1,0:T(8,128)(2,1)}, bf16[2,256,512]{2,1,0:T(8,128)(2,1)}, u32[]{:S(2)}, u32[]{:S(2)}) collective-permute-start(bf16[2,256,512]{2,1,0:T(8,128)(2,1)} %dynamic-slice_bitcast_fusion.14), channel_id=1, source_target_pairs={{0,8},{8,0},{4,12},{12,4},{1,9},{9,1},{5,13},{13,5},{2,10},{10,2},... | collective-permute-start | bytes 1572872 | tf_op jit(solution)/shard_map/ppermute | solution.py:46
  888.3 15.5 %collective-permute-start.17 = (bf16[2,256,512]{2,1,0:T(8,128)(2,1)S(1)}, bf16[2,256,512]{2,1,0:T(8,128)(2,1)S(1)}, u32[]{:S(2)}, u32[]{:S(2)}) collective-permute-start(bf16[2,256,512]{2,1,0:T(8,128)(2,1)S(1)} %dynamic-slice_bitcast_fusion.13), channel_id=1, source_target_pairs={{0,8},{8,0},{4,12},{12,4},{1,9},{9,1},{5,13},{13,5},{2,10},{10,2},... | collective-permute-start | bytes 1572872 | tf_op jit(solution)/shard_map/ppermute | solution.py:46
  (112 other events, 1375.1 us)
Sparse Core Ops, SparseCore 0:
  34.9 81.1 all-gather.5
  117.6 89.6 all-gather.7
  213.1 77.1 all-gather.9
  292.3 79.2 all-gather.11
  378.9 79.2 all-gather.13
  489.9 78.1 reduce-scatter.3
  740.8 48.6 reduce-scatter.5
  826.0 39.7 reduce-scatter.7

commit v8 on v7

--- a/solution.py
+++ b/solution.py
@@ -129,15 +129,20 @@
     if units:
         done_in, near_in, beside_in = refs[:2], refs[2], refs[3]
         keep_ref, left_ref, right_ref = refs[4:7]
-        refs = refs[7:]
+        lines_in, stays_in, leaves_in, streams_in = refs[7:9], refs[9], refs[10], refs[11:13]
+        refs = refs[13:]
     outputs, refs = refs[: units + whole + count], refs[units + whole + count :]
     outs, wides, fulls = outputs[:units], outputs[units : units + whole], outputs[units + whole :]
     shares, refs = refs[:spread], refs[spread:]
+    if units:
+        grad_refs, refs = refs[:6], refs[6:]
     own_sem, near_send, near_recv = refs[:3]
     if units:
         held, got, load_sem, send_sem, recv_sem = refs[3:8]
         mine, theirs, below, pieces, piece_own, piece_send, piece_recv = refs[8:15]
-        mine_sem, done_sem, core_send, core_recv, y_send, y_recv = refs[15:]
+        mine_sem, done_sem, core_send, core_recv, y_send, y_recv = refs[15:21]
+        feed_own, feed_got, pair_own, pair_x, pair_y, wide_in, full_grad, from_core = refs[21:29]
+        job_load, job_send, job_recv = refs[29:]
     x, stream, z = lax.axis_index("dp"), lax.axis_index("stream"), lax.axis_index("head")
     core = lax.rem(stream, 2)
     other_x, other_y, other_core = 1 - x, lax.rem(stream + 2, 4), stream + 1 - 2 * core
@@ -437,6 +442,88 @@
 
         keep(v).start()
 
+    def job(index, source, target, peer):
+        return pltpu.make_async_remote_copy(
+            src_ref=source,
+            dst_ref=target,
+            send_sem=job_send.at[index],
+            recv_sem=job_recv.at[index],
+            device_id=peer,
+            device_id_type=pl.DeviceIdType.MESH,
+        )
+
+    def job_in(index):
+        source, target = (
+            (lines_in[index].at[y], feed_own.at[index])
+            if index < 2
+            else (stays_in, pair_own.at[0])
+            if index == 2
+            else (streams_in[index - 3], wide_in.at[index - 3])
+        )
+        return pltpu.make_async_copy(source, target, job_load.at[index])
+
+    def feed_job(f):
+        return job(f, lines_in[f].at[1 - y], feed_got.at[f], to_y)
+
+    def pair_x_job(i):
+        source = full_grad.at[:, pl.ds(other_x * 2, 2), core] if i else leaves_in
+        return job(2 + 4 * i, source, pair_x.at[i], to_x)
+
+    def pair_y_job(i):
+        return job(3 + 4 * i, pair_own.at[i, :, 1 - y], pair_y.at[i], to_y)
+
+    def core_job(i):
+        return job(4 + i, full_grad.at[i, :, 1 - core], from_core.at[i], to_core)
+
+    def product(i):
+        job_in(3 + i).wait()
+        rows = full_grad.shape[3]
+        for b in range(4):
+            part_in = wide_in[i, :, b * 2 * rows : (b + 1) * 2 * rows]
+            block = dot_tn(part_in, pieces[i]).astype(BF16)
+            full_grad[i, b, 0] = block[:rows]
+            full_grad[i, b, 1] = block[rows:]
+        core_job(i).start()
+
+    def both(a, b):
+        return a.astype(F32) + b.astype(F32)
+
+    def chip_grad():
+        for i in range(2):
+            core_job(i).wait()
+            for b in range(4):
+                full_grad[i, b, core] = both(full_grad[i, b, core], from_core[i, b]).astype(BF16)
+        pair_x_job(1).start()
+
+    def pair_line(i):
+        pair_x_job(i).wait()
+        for n in range(2):
+            for k in range(2):
+                stays = pair_own[i, n, k] if i == 0 else full_grad[n, x * 2 + k, core]
+                pair_own[i, n, k] = both(stays, pair_x[i, n, k]).astype(BF16)
+        pair_y_job(i).start()
+
+    def pair_finish(i):
+        pair_y_job(i).wait()
+        total = [both(pair_own[i, n, y], pair_y[i, n]) for n in range(2)]
+        grad_refs[2 + 2 * i][...] = total[0]
+        grad_refs[3 + 2 * i][...] = total[1].T if i == 0 else total[1]
+
+    def feed_finish():
+        wide = min(512, feed_own.shape[2])
+        for f in range(2):
+            feed_job(f).wait()
+            for c in range(0, feed_own.shape[2], wide):
+                span = slice(c, c + wide)
+                total = both(feed_own[f, :, span], feed_got[f, :, span])
+                if f == 0:
+                    grad_refs[0][:, span] = total
+                else:
+                    grad_refs[1][span] = total.T
+
+    pair_x_job(0).start()
+    for index in range(5):
+        job_in(index).start()
     sum_step(0)
     for v in range(whole):
         load_done(v).wait()
@@ -448,16 +535,27 @@
     for v in range(whole):
         bring(v)
         gather_step(v, 0, late)
+    for f in range(2):
+        feed_job(f).start()
     sum_step(1)
     for v in range(whole):
         gather_step(v, 1, early)
     for w in range(count):
         third(w)
+    for i in range(2):
+        product(i)
     for v in range(whole):
         gather_step(v, 1, late)
+    job_in(2).wait()
+    pair_line(0)
     sum_step(2)
     for v in range(whole):
         gather_step(v, 2, early)
+    chip_grad()
+    for f in range(2):
+        job_in(f).wait()
+    feed_finish()
+    pair_finish(0)
 
     def finish(c):
         for u in range(units):
@@ -471,9 +569,11 @@
 
     for v in range(whole):
         gather_step(v, 2, late)
+    pair_line(1)
     over_parts(finish)
     for w in range(count):
         last(w)
+    pair_finish(1)
 
     def drain(c):
         for way, rank in ways:
@@ -522,8 +622,9 @@
     if units:
         tokens, feats = partials[0].shape[0], partials[0].shape[1] // 4
         chunk = 4
-        in_specs = in_specs + [anywhere] * 4 + [local] * 3
+        in_specs = in_specs + [anywhere] * 4 + [local] * 3 + [anywhere] * 6
         last = rows[2].shape[2]
+        line, stays = rows[7], rows[9]
         out_specs = [local] * units + [anywhere] * 2 + out_specs
         out_shape = (
             [shape((tokens, feats), F32)] * units + [shape((tokens, 4 * feats), BF16)] * 2 + out_shape
@@ -547,6 +648,22 @@
             sems((2,)),
             sems((2,)),
             sems((2,)),
+            pltpu.VMEM((2,) + line.shape[1:], BF16),
+            pltpu.VMEM((2,) + line.shape[1:], BF16),
+            pltpu.VMEM((2,) + stays.shape, BF16),
+            pltpu.VMEM((2,) + stays.shape, BF16),
+            pltpu.VMEM((2, 2) + stays.shape[2:], BF16),
+            pltpu.VMEM((2,) + rows[11].shape, BF16),
+            pltpu.VMEM((2, 4, 2) + stays.shape[2:], BF16),
+            pltpu.VMEM((2, 4) + stays.shape[2:], BF16),
+            sems((5,)),
+            sems((8,)),
+            sems((8,)),
+        ]
+        wide, narrow = line.shape[1:], stays.shape[2:]
+        out_specs = out_specs + [local] * 6
+        out_shape = out_shape + [
+            shape(s, F32) for s in (wide, wide[::-1], narrow, narrow[::-1], narrow, narrow)
         ]
     if spread:
         out_specs = out_specs + [anywhere] * spread
@@ -572,7 +689,8 @@
     )(*partials, *shards_in, *rows)
     if not units:
         return results
-    return results[:units], results[units : len(results) - count], results[len(results) - count :]
+    end = units + 2 + count
+    return results[:units], results[units : units + 2], results[units + 2 : end], results[end:]
 
 
 def head_sum_kernel(members, x_ref, out_ref, slots, send_sem, recv_sem):
@@ -1313,10 +1431,11 @@
         partials, parts, g_up, feed_lines = lax.optimization_barrier(
             (partials, parts, g_up, feed_lines)
         )
-        feed_terms = [last_parts(a) for a in feed_lines]
-        (g_query,), (d_key_full, d_value_full), (wk_rows, wv_rows) = exchange(
+        (g_query,), (d_key_full, d_value_full), (wk_rows, wv_rows), plane_grads = exchange(
             partials,
-            [d_key_rows, d_value_rows, results[2], results[3], *(a[done:] for a in tables)],
+            [d_key_rows, d_value_rows, results[2], results[3], *(a[done:] for a in tables)]
+            + [a[0] for a in feed_lines]
+            + [*parts, k_in, v_in],
             shares,
             (0, 0),
             5,
@@ -1328,7 +1447,6 @@
         ]
         branch = to_owner(halves[0])
         g_key, g_value = dot_nt(d_key_full, wk_rows), dot_nt(d_value_full, wv_rows)
-        terms = plane_parts(*parts)
     else:
         g_query = to_owner(dot_nt(d_query_pre, wq))
         branch = to_owner(dot(attended, w_out_full) + feed)
@@ -1339,18 +1457,16 @@
         kv_terms = scatter_parts(
             jnp.stack([product(k_in, d_key_rows), product(v_in, d_value_rows)])
         )
-    grad_up = add_terms(feed_terms[0][0][0], feed_terms[0][1][0], False)
-    grad_down = add_terms(feed_terms[1][0][0], feed_terms[1][1][0], True)
-    grad_attn_out = add_terms(terms[0][1], terms[1][1], True)
-
     grads = (g_query, g_key, g_value, g_up)
     dots, sums, edges = gradient_sums(grads, streams, row_stats, ln_gain, history)
     if duplex:
-        sums, d_key_full, d_value_full = lax.optimization_barrier((sums, d_key_full, d_value_full))
-        own = lambda a: lax.dynamic_slice_in_dim(a, lax.axis_index("head") * feats, feats, 1)
-        kv = jnp.stack([product(k_in, own(d_key_full)), product(v_in, own(d_value_full))])
-        kv_terms = scatter_parts(kv)
-    grad_query = terms[0][:1].astype(F32) + terms[1][:1].astype(F32)
+        grad_up, grad_down, grad_query, grad_attn_out, grad_key, grad_value = plane_grads
+        grad_qkv = jnp.stack([grad_query, grad_key, grad_value])
+    else:
+        grad_up = add_terms(feed_terms[0][0][0], feed_terms[0][1][0], False)
+        grad_down = add_terms(feed_terms[1][0][0], feed_terms[1][1][0], True)
+        grad_attn_out = add_terms(terms[0][1], terms[1][1], True)
+        grad_qkv = jnp.concatenate([add_f32(terms[0][:1], terms[1][:1]), add_f32(*kv_terms)])
     small, d_scaled, coefs = small_gradients(
         dots, sums, early, row_stats.T, mix_pre.T, slope_mix.T, mix_hidden.T, rms_scale.T, w_mix_out_f, current, edges
     )
@@ -1361,7 +1477,6 @@
     history_grad = history_gradient(
         grads, streams, row_stats, ln_gain, cot_bf, current, mix_weights, coefs, d_scaled, w_mix_in_f.T
     ).reshape(HIST, micro, quarter, feats)
-    grad_qkv = jnp.concatenate([grad_query, kv_terms[0].astype(F32) + kv_terms[1].astype(F32)])
     n = 4 * HIST
     return (
         block_out.reshape(micro, quarter, feats),

time: 924 us -> 893 us (0.966)
  waiting for transfers between devices: 129 us -> 114 us
    ppermute x4 -> x2, waiting for transfers between devices: 39.1 us -> 24 us  [over_x(): return lax.ppermute(a, 'dp', SWAP_X)]
    pallas_call x3 -> x0, Pallas kernels: 9.91 us -> none  [add_terms(): pl.pallas_call(functools.partial(add_kernel, turned), grid=(columns // bl...]
    unnamed x219 -> x216, local copies, waits for them, and re-layouts: 40.8 us -> 49.8 us
    squeeze x10 -> x5, local copies, waits for them, and re-layouts: 19.7 us -> 13 us  [take(): return lax.dynamic_index_in_dim(a, index, axis, keepdims=False)]
    convert_element_type x8 -> x5, other arithmetic: 24.5 us -> 18.9 us  [add_bf(): return (a.astype(F32) + b.astype(F32)).astype(BF16)]
  transfers between devices with their start and end apart: 28 -> 21, of which waited for: 12 -> 10; matrix products, arithmetic and copies ran while one was open for 17% -> 15% of each run, Pallas kernels for 35% -> 37%
where the time goes in v8:
time: 893 us; the launch traced here: 882 us
  Pallas kernels  534 us (60%)
  waiting for transfers between devices  114 us (13%)
  local copies, waits for them, and re-layouts  81.4 us (9%)
  matrix products  73.3 us (8%)
  other arithmetic  50 us (6%)
  between operations  15.7 us (2%)
  starting transfers between devices  13.7 us (2%)
    pallas_call x3, Pallas kernels, exchange(): pl.pallas_call(functools.partial(exchange_kernel, units, spread, axes), i...  296 us
    pallas_call x1, Pallas kernels, small_gradients(): pl.pallas_call(functools.partial(small_kernel, members, plane), in_specs=...  53.2 us
    unnamed x216, local copies, waits for them, and re-layouts  49.8 us
    pallas_call x2, Pallas kernels, attention(): pl.pallas_call(attention_kernel, grid=(feats // HD,), in_specs=[pl.BlockS...  46.6 us
    pallas_call x1, Pallas kernels, feed_forward(): pl.pallas_call(feed_kernel, grid=(hidden // block,), in_specs=[fixed, fix...  42.4 us
    ppermute x2, waiting for transfers between devices, exchange_rows(): across = lax.ppermute(local, 'stream', [(0, 2), (1, 3)])  37.3 us
    dot_general x6, matrix products, dot(): return jnp.dot(a, b, preferred_element_type=F32)  33.3 us
    dot_general x5, matrix products, dot_nt(): lax.dot_general(a, b, (((1,), (1,)), ((), ())), preferred_element_type=F32)  31.8 us
  transfers between devices with their start and end apart: 21, of which 10 were waited for; matrix products, arithmetic and copies ran while one was open for 15% of the time, Pallas kernels for 37%

profile of v8, /device:TPU:8, one launch (start us, length us, event | category | flops | bytes accessed | tf_op | source)
XLA Modules:
  0.0 882.1 jit_solution(4100140363429617070)
XLA Ops:
  14.1 19.2 %sum_over_head.2 = f32[37,1024]{1,0:T(8,128)} custom-call(f32[37,1024]{1,0:T(8,128)} %pad_maximum_fusion.4.x_ref), custom_call_target="tpu_custom_call" | custom-call | tf_op jit(solution)/shard_map/sum_over_head/pallas_call | solution.py:730
  34.8 41.1 %exchange.3.up_ref = bf16[2048,2048]{1,0:T(8,128)(2,1)S(1)} custom-call(bf16[256,2048]{1,0:T(8,128)(2,1)S(1)} %copy-done.36), custom_call_target="tpu_custom_call" | custom-call | bytes 251658240 | tf_op jit(solution)/shard_map/exchange/pallas_call | solution.py:674
  80.5 12.3 %mix_streams.1 = (f32[4,1024,512]{2,1,0:T(8,128)S(1)}, f32[8,1024]{1,0:T(8,128)S(1)}) custom-call(f32[1024,36]{1,0:T(8,128)S(1)} %convolution_add_fusion.weights_ref, bf16[9,1024,512]{2,1,0:T(8,128)(2,1)} %bitcast.170), custom_call_target="tpu_custom_call" | custom-call | flops 41943040 | bytes 17825792 | tf_op jit(solution)/shard_map/mix_streams/pallas_call | solution.py:941
  96.7 11.8 %sum_over_head.3 = f32[8,1024]{1,0:T(8,128)} custom-call(f32[8,1024]{1,0:T(8,128)} %copy-done.56), custom_call_target="tpu_custom_call" | custom-call | tf_op jit(solution)/shard_map/sum_over_head/pallas_call | solution.py:730
  117.0 85.9 %exchange.4 = (bf16[2048,512]{1,0:T(8,128)(2,1)S(1)}, bf16[2048,512]{1,0:T(8,128)(2,1)S(1)}, bf16[2048,2048]{1,0:T(8,128)(2,1)S(1)}, bf16[512,2048]{1,0:T(8,128)...) custom-call(bf16[256,512]{1,0:T(8,128)(2,1)S(1)} %get-tuple-element.285.refs_0_, ...), custom_call_target="tpu_custom_call" | custom-call | bytes 251658240 | tf_op jit(solution)/shard_map/exchange/pallas_call | solution.py:674
  213.3 42.4 %feed_forward.1 = (bf16[1024,2048]{1,0:T(8,128)(2,1)}, bf16[1024,2048]{1,0:T(8,128)(2,1)}, bf16[2048,2048]{1,0:T(8,128)(2,1)}, bf16[2048,2048]{1,0:T(8,128)(2,1)}) custom-call(bf16[1024,2048]{1,0:T(8,128)(2,1)} %all-gather.8.cloned.1.call-done.x_ref, bf16[1024,2048]{1,0:T(8,128)(2,1)} %all-gather.6.cloned.1.call-done.d_ref, bf16[2048,2048]{1,0:T(8,128)(2,1)} %copy-done.15, ...), custom_call_target="tpu_custom_call" | custom-call | flops 34359738368 | bytes 41943040 | tf_op jit(solution)/shard_map/feed_forward/pallas_call | solution.py:802
  283.2 7.0 all-gather.10.cloned.1.call-done.refs_14_
  294.8 5.7 fusion.11
  300.6 10.7 %convolution_convert_fusion.2 = bf16[1024,2048]{1,0:T(8,128)(2,1)} fusion(bf16[1024,2048]{1,0:T(8,128)(2,1)S(1)} %copy-done.102, bf16[2048,2048]{1,0:T(8,128)(2,1)S(1)} %bitcast.169), kind=kOutput, calls=%fused_computation.20 | convolution fusion | flops 8592031744 | bytes 16777216 | tf_op jit(solution)/shard_map/dot_general | solution.py:26
  321.2 13.9 %convolution_convert_fusion.1 = bf16[1024,2048]{1,0:T(8,128)(2,1)} fusion(bf16[1024,2048]{1,0:T(8,128)(2,1)} %get-tuple-element.133, bf16[2048,2048]{1,0:T(8,128)(2,1)} %copy-done.15), kind=kOutput, calls=%fused_computation.19 | convolution fusion | flops 8592031744 | bytes 16777216 | tf_op jit(solution)/shard_map/dot_general | solution.py:30
  335.1 24.0 %collective-permute-done.2 = bf16[1,2,256,2048]{3,2,1,0:T(8,128)(2,1)} collective-permute-done((bf16[1,2,256,2048]{3,2,1,0:T(8,128)(2,1)}, bf16[1,2,256,2048]{3,2,1,0:T(8,128)(2,1)}, u32[]{:S(2)}, u32[]{:S(2)}) %collective-permute-start.2) | collective-permute-done | bytes 2097184 | tf_op jit(solution)/shard_map/ppermute | solution.py:42
  366.2 11.9 %early_sums.1.early_in = bf16[64,1024]{1,0:T(8,128)(2,1)S(1)} custom-call(f32[4,1024,512]{2,1,0:T(8,128)S(1)} %copy-done.1, bf16[1024,512]{1,0:T(8,128)(2,1)S(1)} %copy-done.4, bf16[9,1024,512]{2,1,0:T(8,128)(2,1)} %bitcast.171), custom_call_target="tpu_custom_call" | custom-call | flops 57671680 | bytes 18874368 | tf_op jit(solution)/shard_map/early_sums/pallas_call | solution.py:980
  380.4 5.5 convolution_convert_fusion.5
  395.9 17.2 %collective-permute-done.7.refs_6_ = bf16[2,512,512]{2,1,0:T(8,128)(2,1)} collective-permute-done((bf16[2,512,512]{2,1,0:T(8,128)(2,1)}, bf16[2,512,512]{2,1,0:T(8,128)(2,1)}, u32[]{:S(2)}, u32[]{:S(2)}) %collective-permute-start.7) | collective-permute-done | bytes 1048608 | tf_op jit(solution)/shard_map/ppermute | solution.py:899
  413.2 20.0 %collective-permute-done.4.refs_2_ = bf16[2,512,512]{2,1,0:T(8,128)(2,1)} collective-permute-done((bf16[2,512,512]{2,1,0:T(8,128)(2,1)S(1)}, bf16[2,512,512]{2,1,0:T(8,128)(2,1)}, u32[]{:S(2)}, u32[]{:S(2)}) %collective-permute-start.4) | collective-permute-done | bytes 1048608 | tf_op jit(solution)/shard_map/ppermute | solution.py:899
  442.6 15.5 %all-gather.14.cloned.1.call-done = bf16[1024,2048]{1,0:T(8,128)(2,1)} async-done(((bf16[1024,512]{1,0:T(8,128)(2,1)}), bf16[1024,2048]{1,0:T(8,128)(2,1)}) %all-gather.14.cloned.1.call-update) | async-done | bytes 4194320 | tf_op jit(solution)/shard_map/all_gather | solution.py:1348
  458.1 6.6 fusion.49
  464.8 23.3 %attention_both_ways.2 = (bf16[1,512,512]{2,1,0:T(8,128)(2,1)S(1)}, bf16[1,512,512]{2,1,0:T(8,128)(2,1)S(1)}, bf16[2,2,512,512]{3,2,1,0:T(8,128)(2,1)}, bf16[2,2,512,512]{3,2,1,0:T(8,128)(2,1)}) custom-call(s32[4]{0:T(128)S(1)} %iota_xor_fusion.place_ref, f32[2,512,512]{2,1,0:T(8,128)} %bitcast.188, bf16[2,512,512]{2,1,0:T(8,128)(2,1)S(1)} %bitcast.161, ...), custom_call_target="tpu_custom_call" | custom-call | flops 3221225472 | bytes 10485760 | tf_op jit(solution)/shard_map/attention_both_ways/pallas_call | solution.py:873
  501.1 23.3 %attention_both_ways.3 = (bf16[1,512,512]{2,1,0:T(8,128)(2,1)S(1)}, bf16[1,512,512]{2,1,0:T(8,128)(2,1)S(1)}, bf16[2,2,512,512]{3,2,1,0:T(8,128)(2,1)}, bf16[2,2,512,512]{3,2,1,0:T(8,128)(2,1)}) custom-call(s32[4]{0:T(128)S(1)} %iota_xor_fusion.place_ref, f32[2,512,512]{2,1,0:T(8,128)} %bitcast.189, bf16[2,512,512]{2,1,0:T(8,128)(2,1)S(1)} %bitcast.162, ...), custom_call_target="tpu_custom_call" | custom-call | flops 3221225472 | bytes 10485760 | tf_op jit(solution)/shard_map/attention_both_ways/pallas_call | solution.py:873
  546.4 21.6 %reduce-scatter.4.cloned.1.call-done = bf16[1024,512]{1,0:T(8,128)(2,1)} async-done(((bf16[1024,2048]{1,0:T(8,128)(2,1)}), bf16[1024,512]{1,0:T(8,128)(2,1)}) %reduce-scatter.4.cloned.1.call-update) | async-done | bytes 1048592 | tf_op jit(solution)/shard_map/reduce_scatter | solution.py:1361
  569.5 169.1 %exchange.5 = (f32[1024,512]{1,0:T(8,128)}, bf16[1024,2048]{1,0:T(8,128)(2,1)}, bf16[1024,2048]{1,0:T(8,128)(2,1)}, bf16[512,2048]{1,0:T(8,128)(2,1)}, bf16[512,...) custom-call(bf16[1024,2048]{1,0:T(8,128)(2,1)} %convolution_convert_, ...), custom_call_target="tpu_custom_call" | custom-call | bytes 629145600 | tf_op jit(solution)/shard_map/exchange/pallas_call | solution.py:674
  753.2 16.7 %gradient_sums.1 = (bf16[48,1024]{1,0:T(8,128)(2,1)S(1)}, f32[8,1024]{1,0:T(8,128)S(1)}, f32[8,512]{1,0:T(8,128)S(1)}) custom-call(f32[1024,512]{1,0:T(8,128)S(1)} %copy-done.9, f32[1024,512]{1,0:T(8,128)S(1)} %fusion.50.g1, f32[1024,512]{1,0:T(8,128)S(1)} %fusion.51.g2, f32[1024,512]{1,0:T(8,128)S(1)} %convert_element_type.242.g3, f32[4,1024,512]{2,1,0:T(8,128)} %copy-done, ...), custom_call_target="tpu_custom_call" | custom-call | flops 57671680 | bytes 22020096 | tf_op jit(solution)/shard_map/gradient_sums/pallas_call | solution.py:1027
  769.9 53.2 %small_gradients.1 = (f32[80,512]{1,0:T(8,128)S(1)}, f32[36,1024]{1,0:T(8,128)S(1)}, f32[1024,128]{1,0:T(8,128)S(1)}) custom-call(bf16[48,1024]{1,0:T(8,128)(2,1)S(1)} %get-tuple-element.189.dots_ref, f32[8,1024]{1,0:T(8,128)S(1)} %get-tuple-element.190.sums_ref, bf16[64,1024]{1,0:T(8,128)(2,1)S(1)} %copy-done.41, ...), custom_call_target="tpu_custom_call" | custom-call | tf_op jit(solution)/shard_map/small_gradients/pallas_call | solution.py:1178
  847.0 16.9 %history_gradient.1 = f32[9,1024,512]{2,1,0:T(8,128)} custom-call(f32[1024,512]{1,0:T(8,128)S(1)} %copy-done.10, f32[1024,512]{1,0:T(8,128)S(1)} %copy-done.14, f32[1024,512]{1,0:T(8,128)S(1)} %copy-done.12, f32[1024,512]{1,0:T(8,128)S(1)} %convert_element_type.242.g3, f32[4,1024,512]{2,1,0:T(8,128)} %copy-done, f32[1024,8]{1,0:T(8,128)S(1)} %bitcast.160, ...), custom_call_target="tpu_custom_call" | custom-call | flops 57671680 | bytes 33554432 | tf_op jit(solution)/shard_map/history_gradient/pallas_call | solution.py:1245
  (354 shorter events, 191.6 us)
Async XLA Ops:
  7.2 108.8 %all-gather.6.cloned.1.call-start = ((), (), s32[]{:S(2)}) async-start(), calls=%async_computation.3 | async-start | bytes 5242880 | tf_op jit(solution)/shard_map/all_gather | solution.py:1328
  34.8 178.2 %all-gather.8.cloned.1.call-start = ((), (), s32[]{:S(2)}) async-start(), calls=%async_computation.4 | async-start | bytes 5242880 | tf_op jit(solution)/shard_map/all_gather | solution.py:1348
  116.1 174.2 %all-gather.10.cloned.1.call-start = ((), (), s32[]{:S(2)}) async-start(), calls=%async_computation.5 | async-start | bytes 5242880 | tf_op jit(solution)/shard_map/all_gather | solution.py:1348
  213.0 165.7 %all-gather.12.cloned.1.call-start = ((), (), s32[]{:S(2)}) async-start(), calls=%async_computation.6 | async-start | bytes 5242880 | tf_op jit(solution)/shard_map/all_gather | solution.py:1348
  260.9 7.5 collective-permute-start.1
  264.3 11.8 %collective-permute-start = (bf16[1,4,256,2048]{3,2,1,0:T(8,128)(2,1)}, bf16[1,4,256,2048]{3,2,1,0:T(8,128)(2,1)}, u32[]{:S(2)}, u32[]{:S(2)}) collective-permute-start(bf16[1,4,256,2048]{3,2,1,0:T(8,128)(2,1)} %dynamic-slice_bitcast_fusion.1), channel_id=1, source_target_pairs={{0,4},{4,0},{8,12},{12,8},{1,5},{5,1},{9,13},{13,9},{2,6},{6,2},{1... | collective-permute-start | bytes 12582920 | tf_op jit(solution)/shard_map/ppermute | solution.py:50
  290.3 167.9 %all-gather.14.cloned.1.call-start = ((), (), s32[]{:S(2)}) async-start(), calls=%async_computation.7 | async-start | bytes 5242880 | tf_op jit(solution)/shard_map/all_gather | solution.py:1348
  311.3 47.8 %collective-permute-start.2 = (bf16[1,2,256,2048]{3,2,1,0:T(8,128)(2,1)}, bf16[1,2,256,2048]{3,2,1,0:T(8,128)(2,1)}, u32[]{:S(2)}, u32[]{:S(2)}) collective-permute-start(bf16[1,2,256,2048]{3,2,1,0:T(8,128)(2,1)} %get-tuple-element.129), channel_id=1, source_target_pairs={{0,16},{16,0},{1,17},{17,1},{2,18},{18,2},{3,19},{19,3},{4,20},{20... | collective-permute-start | bytes 6291464 | tf_op jit(solution)/shard_map/ppermute | solution.py:42
  378.7 189.3 %reduce-scatter.4.cloned.1.call-start = ((), (), s32[]{:S(2)}) async-start(), calls=%async_computation.8 | async-start | bytes 5242880 | tf_op jit(solution)/shard_map/reduce_scatter | solution.py:1361
  378.8 55.8 %collective-permute-start.9 = (bf16[1,2,256,2048]{3,2,1,0:T(8,128)(2,1)}, bf16[1,2,256,2048]{3,2,1,0:T(8,128)(2,1)}, u32[]{:S(2)}, u32[]{:S(2)}) collective-permute-start(bf16[1,2,256,2048]{3,2,1,0:T(8,128)(2,1)} %get-tuple-element.143), channel_id=1, source_target_pairs={{0,16},{16,0},{1,17},{17,1},{2,18},{18,2},{3,19},{19,3},{4,20},{20... | collective-permute-start | bytes 6291464 | tf_op jit(solution)/shard_map/ppermute | solution.py:42
  385.9 27.3 %collective-permute-start.7 = (bf16[2,512,512]{2,1,0:T(8,128)(2,1)}, bf16[2,512,512]{2,1,0:T(8,128)(2,1)}, u32[]{:S(2)}, u32[]{:S(2)}) collective-permute-start(bf16[2,512,512]{2,1,0:T(8,128)(2,1)} %bitcast.32.refs_4_), channel_id=1, source_target_pairs={{0,8},{4,12},{1,9},{5,13},{2,10},{6,14},{3,11},{7,15},{16,24},{20,... | collective-permute-start | bytes 3145736 | tf_op jit(solution)/shard_map/ppermute | solution.py:899
  390.3 42.9 %collective-permute-start.4 = (bf16[2,512,512]{2,1,0:T(8,128)(2,1)S(1)}, bf16[2,512,512]{2,1,0:T(8,128)(2,1)}, u32[]{:S(2)}, u32[]{:S(2)}) collective-permute-start(bf16[2,512,512]{2,1,0:T(8,128)(2,1)S(1)} %bitcast.154), channel_id=1, source_target_pairs={{0,8},{4,12},{1,9},{5,13},{2,10},{6,14},{3,11},{7,15},{16,24},{20,... | collective-permute-start | bytes 3145736 | tf_op jit(solution)/shard_map/ppermute | solution.py:899
  395.4 43.3 %collective-permute-start.6 = (bf16[2,512,512]{2,1,0:T(8,128)(2,1)}, bf16[2,512,512]{2,1,0:T(8,128)(2,1)S(1)}, u32[]{:S(2)}, u32[]{:S(2)}) collective-permute-start(bf16[2,512,512]{2,1,0:T(8,128)(2,1)} %bitcast.32.refs_4_), channel_id=1, source_target_pairs={{0,4},{4,0},{8,12},{12,8},{1,5},{5,1},{9,13},{13,9},{2,6},{6,2},{1... | collective-permute-start | bytes 3145736 | tf_op jit(solution)/shard_map/ppermute | solution.py:50
  395.4 44.2 %collective-permute-start.3 = (bf16[2,512,512]{2,1,0:T(8,128)(2,1)S(1)}, bf16[2,512,512]{2,1,0:T(8,128)(2,1)S(1)}, u32[]{:S(2)}, u32[]{:S(2)}) collective-permute-start(bf16[2,512,512]{2,1,0:T(8,128)(2,1)S(1)} %bitcast.155), channel_id=1, source_target_pairs={{0,4},{4,0},{8,12},{12,8},{1,5},{5,1},{9,13},{13,9},{2,6},{6,2},{1... | collective-permute-start | bytes 3145736 | tf_op jit(solution)/shard_map/ppermute | solution.py:50
  413.2 27.4 %collective-permute-start.8 = (bf16[2,512,512]{2,1,0:T(8,128)(2,1)}, bf16[2,512,512]{2,1,0:T(8,128)(2,1)S(1)}, u32[]{:S(2)}, u32[]{:S(2)}) collective-permute-start(bf16[2,512,512]{2,1,0:T(8,128)(2,1)} %collective-permute-done.7.refs_6_), channel_id=1, source_target_pairs={{0,4},{4,0},{8,12},{12,8},{1,5},{5,1},{9,13},{13,9},{2,6},{6,2},{1... | collective-permute-start | bytes 3145736 | tf_op jit(solution)/shard_map/ppermute | solution.py:50
  433.2 8.4 collective-permute-start.5
  489.7 4.5 collective-permute-start.10
  489.7 376.7 %reduce-scatter.6.cloned.1.call-start = ((), (), s32[]{:S(2)}) async-start(), calls=%async_computation.9 | async-start | bytes 2621440 | tf_op jit(solution)/shard_map/reduce_scatter | solution.py:1361
  497.4 28.4 %collective-permute-start.11 = (bf16[2,512,512]{2,1,0:T(8,128)(2,1)S(1)}, bf16[2,512,512]{2,1,0:T(8,128)(2,1)S(1)}, u32[]{:S(2)}, u32[]{:S(2)}) collective-permute-start(bf16[2,512,512]{2,1,0:T(8,128)(2,1)S(1)} %fusion.12), channel_id=1, source_target_pairs={{8,0},{12,4},{9,1},{13,5},{10,2},{14,6},{11,3},{15,7},{24,16},{28,... | collective-permute-start | bytes 3145736 | tf_op jit(solution)/shard_map/ppermute | solution.py:909
  525.8 212.8 %copy-start.77 = (bf16[1024,512]{1,0:T(8,128)(2,1)}, bf16[1024,512]{1,0:T(8,128)(2,1)S(1)}, u32[]{:S(2)}) copy-start(bf16[1024,512]{1,0:T(8,128)(2,1)S(1)} %pad_maximum_fusion.1) | copy-start | bytes 3145732
  538.4 5.8 collective-permute-start.12
  569.5 169.1 %copy-start.60 = (bf16[512,2048]{1,0:T(8,128)(2,1)S(1)}, bf16[512,2048]{1,0:T(8,128)(2,1)}, u32[]{:S(2)}) copy-start(bf16[512,2048]{1,0:T(8,128)(2,1)} %copy-done.58) | copy-start | bytes 6291460
  742.8 125.1 %reduce-scatter.8.cloned.1.call-start = ((), (), s32[]{:S(2)}) async-start(), calls=%async_computation.10 | async-start | bytes 2621440 | tf_op jit(solution)/shard_map/reduce_scatter | solution.py:1361
  753.2 72.1 %copy-start.61 = (bf16[512,2048]{1,0:T(8,128)(2,1)S(1)}, bf16[512,2048]{1,0:T(8,128)(2,1)}, u32[]{:S(2)}) copy-start(bf16[512,2048]{1,0:T(8,128)(2,1)} %copy-done.58) | copy-start | bytes 6291460
  (102 other events, 885.9 us)
Sparse Core Ops, SparseCore 0:
  34.8 81.1 all-gather.5
  117.6 89.6 all-gather.7
  213.1 77.1 all-gather.9
  292.2 79.2 all-gather.11
  378.8 79.2 all-gather.13
  489.8 78.1 reduce-scatter.3
  742.9 59.9 reduce-scatter.5
  828.1 39.7 reduce-scatter.7

commit v9 on v8

--- a/solution.py
+++ b/solution.py
@@ -16,6 +16,7 @@
 MASKED = -1e30
 F32 = jnp.float32
 BF16 = jnp.bfloat16
+VMEM_LIMIT = 60 * 1024 * 1024
 
 SWAP_X = [(0, 1), (1, 0)]
 SWAP_Y = [(0, 2), (2, 0), (1, 3), (3, 1)]
@@ -680,7 +681,7 @@
         compiler_params=pltpu.CompilerParams(
             collective_id=collective_id,
             has_side_effects=True,
-            vmem_limit_bytes=(56 if units else 8) * 1024 * 1024,
+            vmem_limit_bytes=VMEM_LIMIT,
         ),
         cost_estimate=pl.CostEstimate(
             flops=0, bytes_accessed=(600 if units else 240) * 1024 * 1024, transcendentals=0
@@ -737,7 +738,9 @@
             pltpu.SemaphoreType.DMA((members - 1,)),
             pltpu.SemaphoreType.DMA((members - 1,)),
         ],
-        compiler_params=pltpu.CompilerParams(collective_id=collective_id, has_side_effects=True),
+        compiler_params=pltpu.CompilerParams(
+            collective_id=collective_id, has_side_effects=True, vmem_limit_bytes=VMEM_LIMIT
+        ),
         name="sum_over_head",
     )(x)
 
@@ -805,7 +808,7 @@
         in_specs=[fixed, fixed, column, pl.BlockSpec((block, model_width), lambda i: (i, 0))],
         out_specs=[narrow, narrow, column, column],
         out_shape=[shape(tokens), shape(tokens), shape(model_width), shape(model_width)],
-        compiler_params=pltpu.CompilerParams(vmem_limit_bytes=56 * 1024 * 1024),
+        compiler_params=pltpu.CompilerParams(vmem_limit_bytes=VMEM_LIMIT),
         cost_estimate=pl.CostEstimate(
             flops=8 * tokens * model_width * hidden,
             bytes_accessed=4 * model_width * (2 * hidden + tokens),
@@ -883,10 +886,10 @@
             pltpu.VMEM((blocks, rows, rows), F32),
             pltpu.VMEM((blocks, rows, rows), F32),
         ],
-        compiler_params=pltpu.CompilerParams(vmem_limit_bytes=40 * 1024 * 1024),
+        compiler_params=pltpu.CompilerParams(vmem_limit_bytes=VMEM_LIMIT),
         cost_estimate=pl.CostEstimate(
-            flops=6 * feats * rows * rows * blocks,
-            bytes_accessed=rows * feats * 2 * (4 + 4 * blocks),
+            flops=0,
+            bytes_accessed=1024,
             transcendentals=0,
         ),
         name="attention_both_ways",
@@ -953,7 +956,7 @@
             jax.ShapeDtypeStruct((4, tokens, feats), F32),
             jax.ShapeDtypeStruct((8, tokens), F32),
         ],
-        compiler_params=pltpu.CompilerParams(vmem_limit_bytes=40 * 1024 * 1024),
+        compiler_params=pltpu.CompilerParams(vmem_limit_bytes=VMEM_LIMIT),
         cost_estimate=pl.CostEstimate(
             flops=80 * tokens * feats, bytes_accessed=34 * tokens * feats, transcendentals=0
         ),
@@ -987,7 +990,7 @@
         ],
         out_specs=pl.BlockSpec((64, block), lambda i: (0, i)),
         out_shape=jax.ShapeDtypeStruct((64, tokens), BF16),
-        compiler_params=pltpu.CompilerParams(vmem_limit_bytes=40 * 1024 * 1024),
+        compiler_params=pltpu.CompilerParams(vmem_limit_bytes=VMEM_LIMIT),
         cost_estimate=pl.CostEstimate(
             flops=110 * tokens * feats, bytes_accessed=36 * tokens * feats, transcendentals=0
         ),
@@ -1044,7 +1047,7 @@
             jax.ShapeDtypeStruct((8, tokens), F32),
             jax.ShapeDtypeStruct((8, feats), F32),
         ],
-        compiler_params=pltpu.CompilerParams(vmem_limit_bytes=40 * 1024 * 1024),
+        compiler_params=pltpu.CompilerParams(vmem_limit_bytes=VMEM_LIMIT),
         cost_estimate=pl.CostEstimate(
             flops=110 * tokens * feats, bytes_accessed=42 * tokens * feats, transcendentals=0
         ),
@@ -1052,12 +1055,60 @@
     )(*grads, streams, stats, gain, history)
 
 
+def totals_kernel(members, *refs):
+    ins, outs, slots, sems = refs[:3], refs[3:6], refs[6:9], refs[9:]
+    z = lax.axis_index("head")
+    line = [{"head": lax.rem(z + k, members)} for k in range(1, members)]
+    barrier = pltpu.get_barrier_semaphore()
+    for peer in line:
+        pl.semaphore_signal(barrier, inc=1, device_id=peer, device_id_type=pl.DeviceIdType.MESH)
+    pl.semaphore_wait(barrier, len(line))
+    copies = []
+    for index in range(3):
+        for k, peer in enumerate(line):
+            copy = pltpu.make_async_remote_copy(
+                src_ref=ins[index],
+                dst_ref=slots[index].at[z],
+                send_sem=sems[2 * index].at[k],
+                recv_sem=sems[2 * index + 1].at[k],
+                device_id=peer,
+                device_id_type=pl.DeviceIdType.MESH,
+            )
+            copy.start()
+            copies.append(copy)
+        slots[index][z] = ins[index][...]
+    for copy in copies:
+        copy.wait()
+    for index in range(3):
+        total = slots[index][0].astype(F32)
+        for k in range(1, members):
+            total = total + slots[index][k].astype(F32)
+        outs[index][...] = total
+
+
+def head_totals(arrays, collective_id):
+    members = lax.axis_size("head")
+    local = pl.BlockSpec(memory_space=pltpu.VMEM)
+    return pl.pallas_call(
+        functools.partial(totals_kernel, members),
+        in_specs=[local] * 3,
+        out_specs=[local] * 3,
+        out_shape=[jax.ShapeDtypeStruct(a.shape, F32) for a in arrays],
+        scratch_shapes=[pltpu.VMEM((members,) + a.shape, a.dtype) for a in arrays]
+        + [pltpu.SemaphoreType.DMA((members - 1,))] * 6,
+        compiler_params=pltpu.CompilerParams(
+            collective_id=collective_id, has_side_effects=True, vmem_limit_bytes=VMEM_LIMIT
+        ),
+        name="totals_over_head",
+    )(*arrays)
+
+
 def small_kernel(
     members,
     plane,
     dots_ref,
+    early_ref,
     sums_ref,
-    early_in,
     stats_ref,
     pre_ref,
     slope_ref,
@@ -1069,72 +1120,37 @@
     small_ref,
     scaled_ref,
     coef_ref,
-    dot_slots,
-    early_slots,
-    slots,
     got,
     d_mix_ref,
-    early_ref,
     rows_ref,
-    dot_send,
-    dot_recv,
-    early_send,
-    early_recv,
-    send_sem,
-    recv_sem,
     plane_send,
     plane_recv,
 ):
-    x, stream, z = lax.axis_index("dp"), lax.axis_index("stream"), lax.axis_index("head")
-    line = [{"head": lax.rem(z + k, members)} for k in range(1, members)]
+    x, stream = lax.axis_index("dp"), lax.axis_index("stream")
     near = (
         {"stream": stream + 1 - 2 * lax.rem(stream, 2)},
         {"stream": lax.rem(stream + 2, 4)},
         {"dp": 1 - x},
     )
     near = near if plane else ()
-    barrier = pltpu.get_barrier_semaphore()
-    for peer in line + list(near):
-        pl.semaphore_signal(barrier, inc=1, device_id=peer, device_id_type=pl.DeviceIdType.MESH)
-    pl.semaphore_wait(barrier, len(line) + len(near))
-    copies = []
-    for source, target, sends, receives in (
-        (dots_ref, dot_slots, dot_send, dot_recv),
-        (early_in, early_slots, early_send, early_recv),
-        (sums_ref, slots, send_sem, recv_sem),
-    ):
-        for k, peer in enumerate(line):
-            copy = pltpu.make_async_remote_copy(
-                src_ref=source,
-                dst_ref=target.at[z],
-                send_sem=sends.at[k],
-                recv_sem=receives.at[k],
-                device_id=peer,
-                device_id_type=pl.DeviceIdType.MESH,
+    if plane:
+        barrier = pltpu.get_barrier_semaphore()
+        for peer in near:
+            pl.semaphore_signal(
+                barrier, inc=1, device_id=peer, device_id_type=pl.DeviceIdType.MESH
             )
-            copy.start()
-            copies.append(copy)
-        target[z] = source[...]
-    for copy in copies:
-        copy.wait()
-    total, dots = slots[0], dot_slots[0].astype(F32)
-    early_ref[...] = early_slots[0].astype(F32)
-    for k in range(1, members):
-        early_ref[...] += early_slots[k].astype(F32)
-        total = total + slots[k]
-        dots = dots + dot_slots[k].astype(F32)
-    d_mix_ref[...] = dots[: 4 * HIST]
+        pl.semaphore_wait(barrier, len(near))
     n = 4 * HIST
     model_width = members * small_ref.shape[1]
     plain = early_ref[n : n + HIST]
     rows_ref[...] = jnp.zeros_like(rows_ref)
-    rows_ref[0:8] = total / model_width
+    rows_ref[0:8] = sums_ref[...] / model_width
     for s in range(4):
         part = slice(s * HIST, (s + 1) * HIST)
         mean, inverse = stats_ref[s : s + 1], stats_ref[4 + s : 5 + s]
         crossed = (early_ref[part] - mean * plain) * inverse
         d_part = inverse * (
-            d_mix_ref[part] - rows_ref[s : s + 1] * plain - rows_ref[4 + s : 5 + s] * crossed
+            dots_ref[part] - rows_ref[s : s + 1] * plain - rows_ref[4 + s : 5 + s] * crossed
         )
         if s == 3:
             d_part = d_part + early_ref[n + HIST : n + 2 * HIST]
@@ -1169,7 +1185,7 @@
         small_ref[...] += got[step]
 
 
-def small_gradients(dots, sums, early, stats, pre, slope, hidden, rms, w_out, current, edges):
+def small_gradients(dots, early, sums, stats, pre, slope, hidden, rms, w_out, current, edges):
     members, plane = lax.axis_size("head"), paired()
     tokens, feats = current.shape
     n = 4 * HIST
@@ -1181,27 +1197,19 @@
         out_specs=[pl.BlockSpec(memory_space=pltpu.VMEM)] * 3,
         out_shape=[shape((80, feats), F32), shape((n, tokens), F32), shape((tokens, 128), F32)],
         scratch_shapes=[
-            pltpu.VMEM((members, 48, tokens), BF16),
-            pltpu.VMEM((members, 64, tokens), BF16),
-            pltpu.VMEM((members, 8, tokens), F32),
             pltpu.VMEM((3, 80, feats), F32),
             pltpu.VMEM((n, tokens), F32),
-            pltpu.VMEM((64, tokens), F32),
             pltpu.VMEM((128, tokens), F32),
-            sems((members - 1,)),
-            sems((members - 1,)),
-            sems((members - 1,)),
-            sems((members - 1,)),
-            sems((members - 1,)),
-            sems((members - 1,)),
             sems((3,)),
             sems((3,)),
         ],
         compiler_params=pltpu.CompilerParams(
-            collective_id=3, has_side_effects=True, vmem_limit_bytes=40 * 1024 * 1024
+            collective_id=3 if plane else None,
+            has_side_effects=plane,
+            vmem_limit_bytes=VMEM_LIMIT,
         ),
         name="small_gradients",
-    )(dots, sums, early, stats, pre, slope, hidden, rms, w_out, current, edges)
+    )(dots, early, sums, stats, pre, slope, hidden, rms, w_out, current, edges)
     if not plane:
         small = lax.psum(small.astype(BF16), ("dp", "stream")).astype(F32)
     return small, scaled, coefs
@@ -1259,7 +1267,7 @@
         ],
         out_specs=pl.BlockSpec((HIST, block, feats), lambda i: (0, i, 0)),
         out_shape=jax.ShapeDtypeStruct((HIST, tokens, feats), F32),
-        compiler_params=pltpu.CompilerParams(vmem_limit_bytes=40 * 1024 * 1024),
+        compiler_params=pltpu.CompilerParams(vmem_limit_bytes=VMEM_LIMIT),
         cost_estimate=pl.CostEstimate(
             flops=110 * tokens * feats, bytes_accessed=64 * tokens * feats, transcendentals=0
         ),
@@ -1441,7 +1449,8 @@
             5,
         )
         attended_late, g_query = lax.optimization_barrier((attended, g_query))
-        pair = lambda a: (a[: tokens // 2], a[tokens // 2 :])
+        cut = 3 * tokens // 8
+        pair = lambda a: (a[:cut], a[cut:])
         halves = [
             (dot(a, w_out_full) + b).astype(BF16) for a, b in zip(pair(attended_late), pair(feed))
         ]
@@ -1459,7 +1468,10 @@
         )
     grads = (g_query, g_key, g_value, g_up)
     dots, sums, edges = gradient_sums(grads, streams, row_stats, ln_gain, history)
+    dots, early, sums = head_totals((dots, early, sums), 7)
     if duplex:
+        sums, second_half = lax.optimization_barrier((sums, halves[1]))
+        branch = jnp.concatenate([branch, to_owner(second_half)])
         grad_up, grad_down, grad_query, grad_attn_out, grad_key, grad_value = plane_grads
         grad_qkv = jnp.stack([grad_query, grad_key, grad_value])
     else:
@@ -1468,11 +1480,8 @@
         grad_attn_out = add_terms(terms[0][1], terms[1][1], True)
         grad_qkv = jnp.concatenate([add_f32(terms[0][:1], terms[1][:1]), add_f32(*kv_terms)])
     small, d_scaled, coefs = small_gradients(
-        dots, sums, early, row_stats.T, mix_pre.T, slope_mix.T, mix_hidden.T, rms_scale.T, w_mix_out_f, current, edges
+        dots, early, sums, row_stats.T, mix_pre.T, slope_mix.T, mix_hidden.T, rms_scale.T, w_mix_out_f, current, edges
     )
-    if duplex:
-        coefs, second_half = lax.optimization_barrier((coefs, halves[1]))
-        branch = jnp.concatenate([branch, to_owner(second_half)])
     block_out = (valid * (streams[3] + branch)).astype(BF16)
     history_grad = history_gradient(
         grads, streams, row_stats, ln_gain, cot_bf, current, mix_weights, coefs, d_scaled, w_mix_in_f.T

time: 893 us -> 878 us (0.983)
  local copies, waits for them, and re-layouts: 81.4 us -> 44.1 us
  other arithmetic: 50 us -> 62.3 us
    unnamed x216 -> x118, local copies, waits for them, and re-layouts: 49.8 us -> 13.4 us
    pallas_call x1, Pallas kernels: 53.2 us -> 17.9 us  [small_gradients(): pl.pallas_call(functools.partial(small_kernel, members, plane), in_specs=...]
    pallas_call x0 -> x1, Pallas kernels: none -> 29.5 us  [head_totals(): pl.pallas_call(functools.partial(totals_kernel, members), in_specs=[local...]
  transfers between devices with their start and end apart: 21 -> 21, of which waited for: 10 -> 11; matrix products, arithmetic and copies ran while one was open for 15% -> 17% of each run, Pallas kernels for 37% -> 37%
where the time goes in v9:
time: 878 us; the launch traced here: 868 us
  Pallas kernels  537 us (61%)
  waiting for transfers between devices  117 us (13%)
  matrix products  79 us (9%)
  other arithmetic  62.3 us (7%)
  local copies, waits for them, and re-layouts  44.1 us (5%)
  between operations  15.3 us (2%)
  starting transfers between devices  13.8 us (2%)
    pallas_call x3, Pallas kernels, exchange(): pl.pallas_call(functools.partial(exchange_kernel, units, spread, axes), i...  297 us
    pallas_call x2, Pallas kernels, attention(): pl.pallas_call(attention_kernel, grid=(feats // HD,), in_specs=[pl.BlockS...  47.5 us
    pallas_call x1, Pallas kernels, feed_forward(): pl.pallas_call(feed_kernel, grid=(hidden // block,), in_specs=[fixed, fix...  42.5 us
    dot_general x6, matrix products, dot(): return jnp.dot(a, b, preferred_element_type=F32)  35.9 us
    dot_general x5, matrix products, dot_nt(): lax.dot_general(a, b, (((1,), (1,)), ((), ())), preferred_element_type=F32)  34 us
    ppermute x2, waiting for transfers between devices, exchange_rows(): across = lax.ppermute(local, 'stream', [(0, 2), (1, 3)])  32.8 us
    pallas_call x2, Pallas kernels, head_sum(): pl.pallas_call(functools.partial(head_sum_kernel, members), out_shape=jax...  31.4 us
    all_gather x4, waiting for transfers between devices, all_features(): return lax.all_gather(a, 'head', axis=1, tiled=True)  30 us
  transfers between devices with their start and end apart: 21, of which 11 were waited for; matrix products, arithmetic and copies ran while one was open for 17% of the time, Pallas kernels for 37%

profile of v9, /device:TPU:8, one launch (start us, length us, event | category | flops | bytes accessed | tf_op | source)
XLA Modules:
  0.0 868.3 jit_solution(4837058802803581878)
XLA Ops:
  14.1 19.2 %sum_over_head.2 = f32[37,1024]{1,0:T(8,128)} custom-call(f32[37,1024]{1,0:T(8,128)} %pad_maximum_fusion.4.x_ref), custom_call_target="tpu_custom_call" | custom-call | tf_op jit(solution)/shard_map/sum_over_head/pallas_call | solution.py:731
  34.8 41.9 %exchange.3.up_ref = bf16[2048,2048]{1,0:T(8,128)(2,1)} custom-call(bf16[256,2048]{1,0:T(8,128)(2,1)} %refs_0_), custom_call_target="tpu_custom_call" | custom-call | bytes 251658240 | tf_op jit(solution)/shard_map/exchange/pallas_call | solution.py:675
  80.0 14.2 %mix_streams.1 = (f32[4,1024,512]{2,1,0:T(8,128)}, f32[8,1024]{1,0:T(8,128)}) custom-call(f32[1024,36]{1,0:T(8,128)} %convolution_add_fusion.weights_ref, bf16[9,1024,512]{2,1,0:T(8,128)(2,1)} %bitcast.151), custom_call_target="tpu_custom_call" | custom-call | flops 41943040 | bytes 17825792 | tf_op jit(solution)/shard_map/mix_streams/pallas_call | solution.py:944
  94.2 12.2 %sum_over_head.3 = f32[8,1024]{1,0:T(8,128)} custom-call(f32[8,1024]{1,0:T(8,128)} %get-tuple-element.115.x_ref), custom_call_target="tpu_custom_call" | custom-call | tf_op jit(solution)/shard_map/sum_over_head/pallas_call | solution.py:731
  117.0 86.8 %exchange.4 = (bf16[2048,512]{1,0:T(8,128)(2,1)}, bf16[2048,512]{1,0:T(8,128)(2,1)}, bf16[2048,2048]{1,0:T(8,128)(2,1)}, bf16[512,2048]{1,0:T(8,128)(2,1)}, bf16...) custom-call(bf16[256,512]{1,0:T(8,128)(2,1)} %get-tuple-element.291.refs_0_, ...), custom_call_target="tpu_custom_call" | custom-call | bytes 251658240 | tf_op jit(solution)/shard_map/exchange/pallas_call | solution.py:675
  208.2 42.5 %feed_forward.1 = (bf16[1024,2048]{1,0:T(8,128)(2,1)}, bf16[1024,2048]{1,0:T(8,128)(2,1)}, bf16[2048,2048]{1,0:T(8,128)(2,1)}, bf16[2048,2048]{1,0:T(8,128)(2,1)}) custom-call(bf16[1024,2048]{1,0:T(8,128)(2,1)} %all-gather.8.cloned.1.call-done.x_ref, bf16[1024,2048]{1,0:T(8,128)(2,1)} %all-gather.6.cloned.1.call-done.d_ref, ...), custom_call_target="tpu_custom_call" | custom-call | flops 34359738368 | bytes 41943040 | tf_op jit(solution)/shard_map/feed_forward/pallas_call | solution.py:805
  278.4 12.2 %all-gather.10.cloned.1.call-done.refs_14_ = bf16[1024,2048]{1,0:T(8,128)(2,1)} async-done(((bf16[1024,512]{1,0:T(8,128)(2,1)}), bf16[1024,2048]{1,0:T(8,128)(2,1)}) %all-gather.10.cloned.1.call-update) | async-done | bytes 4194320 | tf_op jit(solution)/shard_map/all_gather | solution.py:1356
  300.4 10.6 %convolution_convert_fusion.2 = bf16[1024,2048]{1,0:T(8,128)(2,1)} fusion(bf16[1024,2048]{1,0:T(8,128)(2,1)S(1)} %copy-done.53, bf16[2048,2048]{1,0:T(8,128)(2,1)S(1)} %bitcast.212), kind=kOutput, calls=%fused_computation.19 | convolution fusion | flops 8592031744 | bytes 16777216 | tf_op jit(solution)/shard_map/dot_general | solution.py:27
  320.9 13.9 %convolution_convert_fusion.1 = bf16[1024,2048]{1,0:T(8,128)(2,1)} fusion(bf16[1024,2048]{1,0:T(8,128)(2,1)} %get-tuple-element.136, bf16[2048,2048]{1,0:T(8,128)(2,1)} %exchange.3.up_ref), kind=kOutput, calls=%fused_computation.18 | convolution fusion | flops 8592031744 | bytes 16777216 | tf_op jit(solution)/shard_map/dot_general | solution.py:31
  334.8 24.1 %collective-permute-done.2 = bf16[1,2,256,2048]{3,2,1,0:T(8,128)(2,1)} collective-permute-done((bf16[1,2,256,2048]{3,2,1,0:T(8,128)(2,1)}, bf16[1,2,256,2048]{3,2,1,0:T(8,128)(2,1)}, u32[]{:S(2)}, u32[]{:S(2)}) %collective-permute-start.2) | collective-permute-done | bytes 2097184 | tf_op jit(solution)/shard_map/ppermute | solution.py:43
  363.3 13.5 %early_sums.1.refs_1_ = bf16[64,1024]{1,0:T(8,128)(2,1)} custom-call(f32[4,1024,512]{2,1,0:T(8,128)} %get-tuple-element.133.streams_ref, bf16[1024,512]{1,0:T(8,128)(2,1)} %fusion.10.cot_ref, bf16[9,1024,512]{2,1,0:T(8,128)(2,1)} %bitcast.152), custom_call_target="tpu_custom_call" | custom-call | flops 57671680 | bytes 18874368 | tf_op jit(solution)/shard_map/early_sums/pallas_call | solution.py:983
  399.2 12.8 %collective-permute-done.7.refs_6_ = bf16[2,512,512]{2,1,0:T(8,128)(2,1)} collective-permute-done((bf16[2,512,512]{2,1,0:T(8,128)(2,1)}, bf16[2,512,512]{2,1,0:T(8,128)(2,1)}, u32[]{:S(2)}, u32[]{:S(2)}) %collective-permute-start.7) | collective-permute-done | bytes 1048608 | tf_op jit(solution)/shard_map/ppermute | solution.py:902
  412.0 20.0 %collective-permute-done.4.refs_2_ = bf16[2,512,512]{2,1,0:T(8,128)(2,1)} collective-permute-done((bf16[2,512,512]{2,1,0:T(8,128)(2,1)S(1)}, bf16[2,512,512]{2,1,0:T(8,128)(2,1)}, u32[]{:S(2)}, u32[]{:S(2)}) %collective-permute-start.4) | collective-permute-done | bytes 1048608 | tf_op jit(solution)/shard_map/ppermute | solution.py:902
  442.5 13.7 %all-gather.14.cloned.1.call-done = bf16[1024,2048]{1,0:T(8,128)(2,1)} async-done(((bf16[1024,512]{1,0:T(8,128)(2,1)}), bf16[1024,2048]{1,0:T(8,128)(2,1)}) %all-gather.14.cloned.1.call-update) | async-done | bytes 4194320 | tf_op jit(solution)/shard_map/all_gather | solution.py:1356
  456.2 6.5 fusion.49
  462.7 23.7 %attention_both_ways.2 = (bf16[1,512,512]{2,1,0:T(8,128)(2,1)}, bf16[1,512,512]{2,1,0:T(8,128)(2,1)}, bf16[2,2,512,512]{3,2,1,0:T(8,128)(2,1)}, bf16[2,2,512,512]{3,2,1,0:T(8,128)(2,1)}) custom-call(s32[4]{0:T(128)} %iota_xor_fusion.place_ref, f32[2,512,512]{2,1,0:T(8,128)} %bitcast.177, bf16[2,512,512]{2,1,0:T(8,128)(2,1)} %bitcast.182, ...), custom_call_target="tpu_custom_call" | custom-call | bytes 1024 | tf_op jit(solution)/shard_map/attention_both_ways/pallas_call | solution.py:876
  500.1 23.8 %attention_both_ways.3 = (bf16[1,512,512]{2,1,0:T(8,128)(2,1)}, bf16[1,512,512]{2,1,0:T(8,128)(2,1)}, bf16[2,2,512,512]{3,2,1,0:T(8,128)(2,1)}, bf16[2,2,512,512]{3,2,1,0:T(8,128)(2,1)}) custom-call(s32[4]{0:T(128)} %iota_xor_fusion.place_ref, f32[2,512,512]{2,1,0:T(8,128)} %bitcast.178, bf16[2,512,512]{2,1,0:T(8,128)(2,1)} %bitcast.183, ...), custom_call_target="tpu_custom_call" | custom-call | bytes 1024 | tf_op jit(solution)/shard_map/attention_both_ways/pallas_call | solution.py:876
  548.8 16.0 %reduce-scatter.4.cloned.1.call-done = bf16[1024,512]{1,0:T(8,128)(2,1)} async-done(((bf16[1024,2048]{1,0:T(8,128)(2,1)}), bf16[1024,512]{1,0:T(8,128)(2,1)}) %reduce-scatter.4.cloned.1.call-update) | async-done | bytes 1048592 | tf_op jit(solution)/shard_map/reduce_scatter | solution.py:1369
  567.7 168.7 %exchange.5 = (f32[1024,512]{1,0:T(8,128)}, bf16[1024,2048]{1,0:T(8,128)(2,1)}, bf16[1024,2048]{1,0:T(8,128)(2,1)}, bf16[512,2048]{1,0:T(8,128)(2,1)}, bf16[512,...) custom-call(bf16[1024,2048]{1,0:T(8,128)(2,1)} %convolution_convert_, ...), custom_call_target="tpu_custom_call" | custom-call | bytes 629145600 | tf_op jit(solution)/shard_map/exchange/pallas_call | solution.py:675
  742.1 6.7 fusion.51.g2
  752.4 17.1 %gradient_sums.1 = (bf16[48,1024]{1,0:T(8,128)(2,1)}, f32[8,1024]{1,0:T(8,128)}, f32[8,512]{1,0:T(8,128)}) custom-call(f32[1024,512]{1,0:T(8,128)} %get-tuple-element.186.g0, f32[1024,512]{1,0:T(8,128)} %fusion.50.g1, f32[1024,512]{1,0:T(8,128)} %fusion.51.g2, f32[1024,512]{1,0:T(8,128)} %convert_element_type.242.g3, ...), custom_call_target="tpu_custom_call" | custom-call | flops 57671680 | bytes 22020096 | tf_op jit(solution)/shard_map/gradient_sums/pallas_call | solution.py:1030
  769.5 29.5 %totals_over_head.1 = (f32[48,1024]{1,0:T(8,128)}, f32[64,1024]{1,0:T(8,128)}, f32[8,1024]{1,0:T(8,128)}) custom-call(bf16[48,1024]{1,0:T(8,128)(2,1)} %get-tuple-element.192.refs_0_, bf16[64,1024]{1,0:T(8,128)(2,1)} %early_sums.1.refs_1_, f32[8,1024]{1,0:T(8,128)} %get-tuple-element.194.refs_2_), custom_call_target="tpu_custom_call" | custom-call | tf_op jit(solution)/shard_map/totals_over_head/pallas_call | solution.py:1092
  809.7 17.9 %small_gradients.1 = (f32[80,512]{1,0:T(8,128)}, f32[36,1024]{1,0:T(8,128)}, f32[1024,128]{1,0:T(8,128)}) custom-call(f32[48,1024]{1,0:T(8,128)} %get-tuple-element.197.dots_ref, f32[64,1024]{1,0:T(8,128)} %get-tuple-element.198.early_ref, f32[8,1024]{1,0:T(8,128)} %get-tuple-element.199.sums_ref, f32[8,1024]{1,0:T(8,128)} %copy-done.28, ...), custom_call_target="tpu_custom_call" | custom-call | tf_op jit(solution)/shard_map/small_gradients/pallas_call | solution.py:1194
  830.6 18.9 %history_gradient.1 = f32[9,1024,512]{2,1,0:T(8,128)} custom-call(f32[1024,512]{1,0:T(8,128)} %get-tuple-element.186.g0, f32[1024,512]{1,0:T(8,128)} %fusion.50.g1, f32[1024,512]{1,0:T(8,128)} %fusion.51.g2, f32[1024,512]{1,0:T(8,128)} %convert_element_type.242.g3, f32[4,1024,512]{2,1,0:T(8,128)} %get-tuple-element.133.streams_ref, f32[1024,8]{1,0:T(8,128)} %bitcast.180, ...), custom_call_target="tpu_custom_call" | custom-call | flops 57671680 | bytes 33554432 | tf_op jit(solution)/shard_map/history_gradient/pallas_call | solution.py:1253
  (257 shorter events, 186.6 us)
Async XLA Ops:
  7.2 108.8 %all-gather.6.cloned.1.call-start = ((), (), s32[]{:S(2)}) async-start(), calls=%async_computation.3 | async-start | bytes 5242880 | tf_op jit(solution)/shard_map/all_gather | solution.py:1336
  34.7 42.0 %copy-start.21 = (f32[37,1024]{1,0:T(8,128)S(1)}, f32[37,1024]{1,0:T(8,128)}, u32[]{:S(2)}) copy-start(f32[37,1024]{1,0:T(8,128)} %sum_over_head.2) | copy-start | bytes 454660
  34.7 43.9 %copy-start.37 = (bf16[36,36]{1,0:T(8,128)(2,1)S(1)}, bf16[36,36]{1,0:T(8,128)(2,1)}, u32[]{:S(2)}) copy-start(bf16[36,36]{1,0:T(8,128)(2,1)} %param.17) | copy-start | bytes 7780
  34.7 173.1 %all-gather.8.cloned.1.call-start = ((), (), s32[]{:S(2)}) async-start(), calls=%async_computation.4 | async-start | bytes 5242880 | tf_op jit(solution)/shard_map/all_gather | solution.py:1356
  116.0 174.5 %all-gather.10.cloned.1.call-start = ((), (), s32[]{:S(2)}) async-start(), calls=%async_computation.5 | async-start | bytes 5242880 | tf_op jit(solution)/shard_map/all_gather | solution.py:1356
  207.9 168.9 %all-gather.12.cloned.1.call-start = ((), (), s32[]{:S(2)}) async-start(), calls=%async_computation.6 | async-start | bytes 5242880 | tf_op jit(solution)/shard_map/all_gather | solution.py:1356
  255.9 7.5 collective-permute-start.1
  259.4 11.2 %collective-permute-start = (bf16[1,4,256,2048]{3,2,1,0:T(8,128)(2,1)}, bf16[1,4,256,2048]{3,2,1,0:T(8,128)(2,1)}, u32[]{:S(2)}, u32[]{:S(2)}) collective-permute-start(bf16[1,4,256,2048]{3,2,1,0:T(8,128)(2,1)} %dynamic-slice_bitcast_fusion.1), channel_id=1, source_target_pairs={{0,4},{4,0},{8,12},{12,8},{1,5},{5,1},{9,13},{13,9},{2,6},{6,2},{1... | collective-permute-start | bytes 12582920 | tf_op jit(solution)/shard_map/ppermute | solution.py:51
  290.5 165.7 %all-gather.14.cloned.1.call-start = ((), (), s32[]{:S(2)}) async-start(), calls=%async_computation.7 | async-start | bytes 5242880 | tf_op jit(solution)/shard_map/all_gather | solution.py:1356
  311.0 47.8 %collective-permute-start.2 = (bf16[1,2,256,2048]{3,2,1,0:T(8,128)(2,1)}, bf16[1,2,256,2048]{3,2,1,0:T(8,128)(2,1)}, u32[]{:S(2)}, u32[]{:S(2)}) collective-permute-start(bf16[1,2,256,2048]{3,2,1,0:T(8,128)(2,1)} %get-tuple-element.132), channel_id=1, source_target_pairs={{0,16},{16,0},{1,17},{17,1},{2,18},{18,2},{3,19},{19,3},{4,20},{20... | collective-permute-start | bytes 6291464 | tf_op jit(solution)/shard_map/ppermute | solution.py:43
  376.8 188.0 %reduce-scatter.4.cloned.1.call-start = ((), (), s32[]{:S(2)}) async-start(), calls=%async_computation.8 | async-start | bytes 5242880 | tf_op jit(solution)/shard_map/reduce_scatter | solution.py:1369
  376.9 58.9 %collective-permute-start.9 = (bf16[1,2,256,2048]{3,2,1,0:T(8,128)(2,1)}, bf16[1,2,256,2048]{3,2,1,0:T(8,128)(2,1)}, u32[]{:S(2)}, u32[]{:S(2)}) collective-permute-start(bf16[1,2,256,2048]{3,2,1,0:T(8,128)(2,1)} %get-tuple-element.146), channel_id=1, source_target_pairs={{0,16},{16,0},{1,17},{17,1},{2,18},{18,2},{3,19},{19,3},{4,20},{20... | collective-permute-start | bytes 6291464 | tf_op jit(solution)/shard_map/ppermute | solution.py:43
  384.7 27.3 %collective-permute-start.7 = (bf16[2,512,512]{2,1,0:T(8,128)(2,1)}, bf16[2,512,512]{2,1,0:T(8,128)(2,1)}, u32[]{:S(2)}, u32[]{:S(2)}) collective-permute-start(bf16[2,512,512]{2,1,0:T(8,128)(2,1)} %bitcast.32.refs_4_), channel_id=1, source_target_pairs={{0,8},{4,12},{1,9},{5,13},{2,10},{6,14},{3,11},{7,15},{16,24},{20,... | collective-permute-start | bytes 3145736 | tf_op jit(solution)/shard_map/ppermute | solution.py:902
  389.1 42.9 %collective-permute-start.4 = (bf16[2,512,512]{2,1,0:T(8,128)(2,1)S(1)}, bf16[2,512,512]{2,1,0:T(8,128)(2,1)}, u32[]{:S(2)}, u32[]{:S(2)}) collective-permute-start(bf16[2,512,512]{2,1,0:T(8,128)(2,1)S(1)} %bitcast.162), channel_id=1, source_target_pairs={{0,8},{4,12},{1,9},{5,13},{2,10},{6,14},{3,11},{7,15},{16,24},{20,... | collective-permute-start | bytes 3145736 | tf_op jit(solution)/shard_map/ppermute | solution.py:902
  398.6 40.9 %collective-permute-start.6 = (bf16[2,512,512]{2,1,0:T(8,128)(2,1)}, bf16[2,512,512]{2,1,0:T(8,128)(2,1)S(1)}, u32[]{:S(2)}, u32[]{:S(2)}) collective-permute-start(bf16[2,512,512]{2,1,0:T(8,128)(2,1)} %bitcast.32.refs_4_), channel_id=1, source_target_pairs={{0,4},{4,0},{8,12},{12,8},{1,5},{5,1},{9,13},{13,9},{2,6},{6,2},{1... | collective-permute-start | bytes 3145736 | tf_op jit(solution)/shard_map/ppermute | solution.py:51
  398.7 40.8 %collective-permute-start.3 = (bf16[2,512,512]{2,1,0:T(8,128)(2,1)S(1)}, bf16[2,512,512]{2,1,0:T(8,128)(2,1)S(1)}, u32[]{:S(2)}, u32[]{:S(2)}) collective-permute-start(bf16[2,512,512]{2,1,0:T(8,128)(2,1)S(1)} %bitcast.163), channel_id=1, source_target_pairs={{0,4},{4,0},{8,12},{12,8},{1,5},{5,1},{9,13},{13,9},{2,6},{6,2},{1... | collective-permute-start | bytes 3145736 | tf_op jit(solution)/shard_map/ppermute | solution.py:51
  412.0 28.5 %collective-permute-start.8 = (bf16[2,512,512]{2,1,0:T(8,128)(2,1)}, bf16[2,512,512]{2,1,0:T(8,128)(2,1)S(1)}, u32[]{:S(2)}, u32[]{:S(2)}) collective-permute-start(bf16[2,512,512]{2,1,0:T(8,128)(2,1)} %collective-permute-done.7.refs_6_), channel_id=1, source_target_pairs={{0,4},{4,0},{8,12},{12,8},{1,5},{5,1},{9,13},{13,9},{2,6},{6,2},{1... | collective-permute-start | bytes 3145736 | tf_op jit(solution)/shard_map/ppermute | solution.py:51
  432.0 10.5 %collective-permute-start.5 = (bf16[2,512,512]{2,1,0:T(8,128)(2,1)}, bf16[2,512,512]{2,1,0:T(8,128)(2,1)}, u32[]{:S(2)}, u32[]{:S(2)}) collective-permute-start(bf16[2,512,512]{2,1,0:T(8,128)(2,1)} %collective-permute-done.4.refs_2_), channel_id=1, source_target_pairs={{0,4},{4,0},{8,12},{12,8},{1,5},{5,1},{9,13},{13,9},{2,6},{6,2},{1... | collective-permute-start | bytes 3145736 | tf_op jit(solution)/shard_map/ppermute | solution.py:51
  486.5 4.6 collective-permute-start.10
  486.6 365.4 %reduce-scatter.6.cloned.1.call-start = ((), (), s32[]{:S(2)}) async-start(), calls=%async_computation.9 | async-start | bytes 1966080 | tf_op jit(solution)/shard_map/reduce_scatter | solution.py:1369
  495.6 32.6 %collective-permute-start.11 = (bf16[2,512,512]{2,1,0:T(8,128)(2,1)S(1)}, bf16[2,512,512]{2,1,0:T(8,128)(2,1)S(1)}, u32[]{:S(2)}, u32[]{:S(2)}) collective-permute-start(bf16[2,512,512]{2,1,0:T(8,128)(2,1)S(1)} %fusion.12), channel_id=1, source_target_pairs={{8,0},{12,4},{9,1},{13,5},{10,2},{14,6},{11,3},{15,7},{24,16},{28,... | collective-permute-start | bytes 3145736 | tf_op jit(solution)/shard_map/ppermute | solution.py:912
  540.7 5.8 collective-permute-start.12
  740.7 114.4 %reduce-scatter.8.cloned.1.call-start = ((), (), s32[]{:S(2)}) async-start(), calls=%async_computation.10 | async-start | bytes 3276800 | tf_op jit(solution)/shard_map/reduce_scatter | solution.py:1369
  752.4 46.5 %copy-start.49 = (bf16[512,2048]{1,0:T(8,128)(2,1)S(1)}, bf16[512,2048]{1,0:T(8,128)(2,1)}, u32[]{:S(2)}) copy-start(bf16[512,2048]{1,0:T(8,128)(2,1)} %get-tuple-element.135) | copy-start | bytes 6291460
  (53 other events, 482.9 us)
Sparse Core Ops, SparseCore 0:
  34.8 81.1 all-gather.5
  118.1 89.6 all-gather.7
  210.0 80.4 all-gather.9
  292.5 79.2 all-gather.11
  376.9 79.2 all-gather.13
  486.7 78.0 reduce-scatter.3
  740.8 37.4 reduce-scatter.5
  803.9 51.1 reduce-scatter.7

commit v10 on v9

--- a/solution.py
+++ b/solution.py
@@ -819,11 +819,11 @@
 
 
 def attention_kernel(
-    place_ref, q_ref, do_ref, start_ref, valid_ref, keep_ref, left_ref, right_ref, *refs
+    extra, place_ref, q_ref, do_ref, start_ref, valid_ref, keep_ref, left_ref, right_ref, *refs
 ):
-    blocks = (len(refs) - 6) // 2
+    blocks = (len(refs) - 6 - extra) // 2
     k_refs, v_refs = refs[:blocks], refs[blocks : 2 * blocks]
-    o_ref, dq_ref, near_ref, beside_ref, s_ref, dp_ref = refs[2 * blocks :]
+    o_ref, dq_ref, near_ref, beside_ref, s_ref, dp_ref = refs[2 * blocks + extra :]
     grad_ref = lambda j: (beside_ref if j % 2 else near_ref).at[j // 2]
     rows = q_ref.shape[1]
     scale = HD ** (-0.5)
@@ -865,23 +865,24 @@
     dq_ref[0] = turn(d_q * scale, keep, -left, -right).astype(BF16)
 
 
-def attention(index, places, queries, d_attended, starts, valid, tables, keys, values):
-    _, rows, feats = queries.shape
+def attention(index, places, queries, d_attended, starts, valid, tables, keys, values, earlier):
+    micro, rows, feats = queries.shape
     blocks = len(keys)
     tile = pl.BlockSpec((1, rows, HD), lambda h: (index, 0, h))
     fixed = lambda width: pl.BlockSpec((1, rows, width), lambda h: (index, 0, 0))
-    out_tile = pl.BlockSpec((1, rows, HD), lambda h: (0, 0, h))
     grad_tile = pl.BlockSpec((blocks // 2, 2, rows, HD), lambda h: (0, 0, 0, h))
     shape = lambda *lead: jax.ShapeDtypeStruct(lead + (rows, feats), BF16)
     return pl.pallas_call(
-        attention_kernel,
+        functools.partial(attention_kernel, len(earlier)),
         grid=(feats // HD,),
         in_specs=[pl.BlockSpec(memory_space=pltpu.SMEM), tile, tile]
         + [fixed(1)] * 2
         + [fixed(HD)] * 3
-        + [tile] * (2 * blocks),
-        out_specs=[out_tile] * 2 + [grad_tile] * 2,
-        out_shape=[shape(1)] * 2 + [shape(blocks // 2, 2)] * 2,
+        + [tile] * (2 * blocks)
+        + [pl.BlockSpec(memory_space=pl.ANY)] * len(earlier),
+        out_specs=[tile] * 2 + [grad_tile] * 2,
+        out_shape=[shape(micro)] * 2 + [shape(blocks // 2, 2)] * 2,
+        input_output_aliases={8 + 2 * blocks + i: i for i in range(len(earlier))},
         scratch_shapes=[
             pltpu.VMEM((blocks, rows, rows), F32),
             pltpu.VMEM((blocks, rows, rows), F32),
@@ -893,7 +894,7 @@
             transcendentals=0,
         ),
         name="attention_both_ways",
-    )(places, queries, d_attended, starts, valid, *tables, *keys, *values)
+    )(places, queries, d_attended, starts, valid, *tables, *keys, *values, *earlier)
 
 
 def exchange_rows(local):
@@ -1393,15 +1394,18 @@
     by_micro = lambda a: a.reshape((micro, quarter) + a.shape[1:])
     key_blocks = exchange_rows(by_micro(keys))
     value_blocks = exchange_rows(by_micro(values))
-    q_in, d_up_in, key_blocks, value_blocks, feed_lines[1], early = lax.optimization_barrier(
-        (all_features(q_out), d_up_in, key_blocks, value_blocks, feed_lines[1], early)
+    d_up_in, key_blocks, value_blocks = lax.optimization_barrier(
+        (d_up_in, key_blocks, value_blocks)
+    )
+    q_in, key_blocks, value_blocks, feed_lines[1], early = lax.optimization_barrier(
+        (all_features(q_out), key_blocks, value_blocks, feed_lines[1], early)
     )
     g_up = to_owner(d_up_in)
     product = lambda a, b: dot_tn(a, b).astype(BF16)
 
     queries = dot(q_in, wq)
     places = member ^ jnp.arange(4, dtype=jnp.int32)
-    attended, d_query_pre, d_rows = [], [], []
+    earlier, d_rows = (), []
     queries = by_micro(queries)
     for index in range(micro):
         results = attention(
@@ -1414,16 +1418,16 @@
             tuple(by_micro(a) for a in tables),
             key_blocks,
             value_blocks,
-        )
-        attended.append(results[0][0])
-        d_query_pre.append(results[1][0])
+            earlier,
+        )
+        earlier = results[:2]
         if duplex and index == micro - 1:
             continue
         chip = add_f32(results[2], over_core(results[3]))
         across = chip[1].astype(BF16)
         queries, across = lax.optimization_barrier((queries, across))
         d_rows.append(add_f32(chip[0], over_line(across)))
-    attended, d_query_pre = jnp.concatenate(attended), jnp.concatenate(d_query_pre)
+    attended, d_query_pre = (a.reshape(tokens, feats) for a in earlier)
     d_key_rows = jnp.concatenate([a[0] for a in d_rows])
     done = d_key_rows.shape[0]
     d_key_rows = rotate(d_key_rows, tuple(a[:done] for a in tables), -1.0)

time: 878 us -> 863 us (0.983)
  waiting for transfers between devices: 117 us -> 101 us
    reduce_scatter x3, waiting for transfers between devices: 19.1 us -> 3.59 us  [to_owner(): lax.psum_scatter(partial.astype(BF16), 'head', scatter_dimension=1, tiled...]
  transfers between devices with their start and end apart: 21 -> 21, of which waited for: 11 -> 10; matrix products, arithmetic and copies ran while one was open for 17% -> 18% of each run, Pallas kernels for 37% -> 41%
where the time goes in v10:
time: 863 us; the launch traced here: 854 us
  Pallas kernels  539 us (62%)
  waiting for transfers between devices  101 us (12%)
  matrix products  79.3 us (9%)
  other arithmetic  62.5 us (7%)
  local copies, waits for them, and re-layouts  43.2 us (5%)
  between operations  15.2 us (2%)
  starting transfers between devices  13.7 us (2%)
    pallas_call x3, Pallas kernels, exchange(): pl.pallas_call(functools.partial(exchange_kernel, units, spread, axes), i...  300 us
    pallas_call x2, Pallas kernels, attention(): pl.pallas_call(functools.partial(attention_kernel, len(earlier)), grid=(f...  47.5 us
    pallas_call x1, Pallas kernels, feed_forward(): pl.pallas_call(feed_kernel, grid=(hidden // block,), in_specs=[fixed, fix...  42.2 us
    dot_general x6, matrix products, dot(): return jnp.dot(a, b, preferred_element_type=F32)  36.2 us
    dot_general x5, matrix products, dot_nt(): lax.dot_general(a, b, (((1,), (1,)), ((), ())), preferred_element_type=F32)  34 us
    ppermute x2, waiting for transfers between devices, exchange_rows(): across = lax.ppermute(local, 'stream', [(0, 2), (1, 3)])  33 us
    pallas_call x2, Pallas kernels, head_sum(): pl.pallas_call(functools.partial(head_sum_kernel, members), out_shape=jax...  31.4 us
    all_gather x4, waiting for transfers between devices, all_features(): return lax.all_gather(a, 'head', axis=1, tiled=True)  30 us
  transfers between devices with their start and end apart: 21, of which 10 were waited for; matrix products, arithmetic and copies ran while one was open for 18% of the time, Pallas kernels for 41%

profile of v10, /device:TPU:8, one launch (start us, length us, event | category | flops | bytes accessed | tf_op | source)
XLA Modules:
  0.0 854.4 jit_solution(7998064045307946956)
XLA Ops:
  14.1 19.2 %sum_over_head.2 = f32[37,1024]{1,0:T(8,128)} custom-call(f32[37,1024]{1,0:T(8,128)} %pad_maximum_fusion.2.x_ref), custom_call_target="tpu_custom_call" | custom-call | tf_op jit(solution)/shard_map/sum_over_head/pallas_call | solution.py:731
  34.8 41.9 %exchange.3.up_ref = bf16[2048,2048]{1,0:T(8,128)(2,1)} custom-call(bf16[256,2048]{1,0:T(8,128)(2,1)} %refs_0_), custom_call_target="tpu_custom_call" | custom-call | bytes 251658240 | tf_op jit(solution)/shard_map/exchange/pallas_call | solution.py:675
  80.0 14.2 %mix_streams.1 = (f32[4,1024,512]{2,1,0:T(8,128)}, f32[8,1024]{1,0:T(8,128)}) custom-call(f32[1024,36]{1,0:T(8,128)} %convolution_add_fusion.weights_ref, bf16[9,1024,512]{2,1,0:T(8,128)(2,1)} %bitcast.149), custom_call_target="tpu_custom_call" | custom-call | flops 41943040 | bytes 17825792 | tf_op jit(solution)/shard_map/mix_streams/pallas_call | solution.py:945
  94.2 12.2 %sum_over_head.3 = f32[8,1024]{1,0:T(8,128)} custom-call(f32[8,1024]{1,0:T(8,128)} %get-tuple-element.123.x_ref), custom_call_target="tpu_custom_call" | custom-call | tf_op jit(solution)/shard_map/sum_over_head/pallas_call | solution.py:731
  117.0 86.8 %exchange.4 = (bf16[2048,512]{1,0:T(8,128)(2,1)}, bf16[2048,512]{1,0:T(8,128)(2,1)}, bf16[2048,2048]{1,0:T(8,128)(2,1)}, bf16[512,2048]{1,0:T(8,128)(2,1)}, bf16...) custom-call(bf16[256,512]{1,0:T(8,128)(2,1)} %get-tuple-element.307.refs_0_, ...), custom_call_target="tpu_custom_call" | custom-call | bytes 251658240 | tf_op jit(solution)/shard_map/exchange/pallas_call | solution.py:675
  208.2 42.2 %feed_forward.1 = (bf16[1024,2048]{1,0:T(8,128)(2,1)}, bf16[1024,2048]{1,0:T(8,128)(2,1)}, bf16[2048,2048]{1,0:T(8,128)(2,1)}, bf16[2048,2048]{1,0:T(8,128)(2,1)}) custom-call(bf16[1024,2048]{1,0:T(8,128)(2,1)} %all-gather.8.cloned.1.call-done.x_ref, bf16[1024,2048]{1,0:T(8,128)(2,1)} %all-gather.6.cloned.1.call-done.d_ref, ...), custom_call_target="tpu_custom_call" | custom-call | flops 34359738368 | bytes 41943040 | tf_op jit(solution)/shard_map/feed_forward/pallas_call | solution.py:805
  278.0 12.5 %all-gather.10.cloned.1.call-done.refs_14_ = bf16[1024,2048]{1,0:T(8,128)(2,1)} async-done(((bf16[1024,512]{1,0:T(8,128)(2,1)}), bf16[1024,2048]{1,0:T(8,128)(2,1)}) %all-gather.10.cloned.1.call-update) | async-done | bytes 4194320 | tf_op jit(solution)/shard_map/all_gather | solution.py:1357
  300.5 10.9 %convolution_convert_fusion.2 = bf16[1024,2048]{1,0:T(8,128)(2,1)} fusion(bf16[1024,2048]{1,0:T(8,128)(2,1)S(1)} %copy-done.51, bf16[2048,2048]{1,0:T(8,128)(2,1)S(1)} %bitcast.211), kind=kOutput, calls=%fused_computation.19 | convolution fusion | flops 8592031744 | bytes 16777216 | tf_op jit(solution)/shard_map/dot_general | solution.py:27
  321.2 13.9 %convolution_convert_fusion.1 = bf16[1024,2048]{1,0:T(8,128)(2,1)} fusion(bf16[1024,2048]{1,0:T(8,128)(2,1)} %get-tuple-element.144, bf16[2048,2048]{1,0:T(8,128)(2,1)} %exchange.3.up_ref), kind=kOutput, calls=%fused_computation.18 | convolution fusion | flops 8592031744 | bytes 16777216 | tf_op jit(solution)/shard_map/dot_general | solution.py:31
  335.1 24.0 %collective-permute-done.2 = bf16[1,2,256,2048]{3,2,1,0:T(8,128)(2,1)} collective-permute-done((bf16[1,2,256,2048]{3,2,1,0:T(8,128)(2,1)}, bf16[1,2,256,2048]{3,2,1,0:T(8,128)(2,1)}, u32[]{:S(2)}, u32[]{:S(2)}) %collective-permute-start.2) | collective-permute-done | bytes 2097184 | tf_op jit(solution)/shard_map/ppermute | solution.py:43
  363.6 13.5 %early_sums.1.refs_1_ = bf16[64,1024]{1,0:T(8,128)(2,1)} custom-call(f32[4,1024,512]{2,1,0:T(8,128)} %get-tuple-element.141.streams_ref, bf16[1024,512]{1,0:T(8,128)(2,1)} %fusion.10.cot_ref, bf16[9,1024,512]{2,1,0:T(8,128)(2,1)} %bitcast.150), custom_call_target="tpu_custom_call" | custom-call | flops 57671680 | bytes 18874368 | tf_op jit(solution)/shard_map/early_sums/pallas_call | solution.py:984
  379.0 6.2 convolution_convert_fusion.5
  399.5 13.0 %collective-permute-done.7.refs_6_ = bf16[2,512,512]{2,1,0:T(8,128)(2,1)} collective-permute-done((bf16[2,512,512]{2,1,0:T(8,128)(2,1)}, bf16[2,512,512]{2,1,0:T(8,128)(2,1)}, u32[]{:S(2)}, u32[]{:S(2)}) %collective-permute-start.7) | collective-permute-done | bytes 1048608 | tf_op jit(solution)/shard_map/ppermute | solution.py:903
  412.5 20.0 %collective-permute-done.4.refs_2_ = bf16[2,512,512]{2,1,0:T(8,128)(2,1)} collective-permute-done((bf16[2,512,512]{2,1,0:T(8,128)(2,1)S(1)}, bf16[2,512,512]{2,1,0:T(8,128)(2,1)}, u32[]{:S(2)}, u32[]{:S(2)}) %collective-permute-start.4) | collective-permute-done | bytes 1048608 | tf_op jit(solution)/shard_map/ppermute | solution.py:903
  443.2 13.4 %all-gather.14.cloned.1.call-done = bf16[1024,2048]{1,0:T(8,128)(2,1)} async-done(((bf16[1024,512]{1,0:T(8,128)(2,1)}), bf16[1024,2048]{1,0:T(8,128)(2,1)}) %all-gather.14.cloned.1.call-update) | async-done | bytes 4194320 | tf_op jit(solution)/shard_map/all_gather | solution.py:1357
  456.5 5.8 fusion.49
  462.4 23.7 %attention_both_ways.2 = (bf16[2,512,512]{2,1,0:T(8,128)(2,1)}, bf16[2,512,512]{2,1,0:T(8,128)(2,1)}, bf16[2,2,512,512]{3,2,1,0:T(8,128)(2,1)}, bf16[2,2,512,512]{3,2,1,0:T(8,128)(2,1)}) custom-call(s32[4]{0:T(128)} %iota_xor_fusion.place_ref, f32[2,512,512]{2,1,0:T(8,128)} %bitcast.170, bf16[2,512,512]{2,1,0:T(8,128)(2,1)} %bitcast.180, ...), custom_call_target="tpu_custom_call" | custom-call | bytes 1024 | tf_op jit(solution)/shard_map/attention_both_ways/pallas_call | solution.py:875
  499.1 23.8 %attention_both_ways.3 = (bf16[2,512,512]{2,1,0:T(8,128)(2,1)}, bf16[2,512,512]{2,1,0:T(8,128)(2,1)}, bf16[2,2,512,512]{3,2,1,0:T(8,128)(2,1)}, bf16[2,2,512,512]{3,2,1,0:T(8,128)(2,1)}) custom-call(s32[4]{0:T(128)} %iota_xor_fusion.place_ref, f32[2,512,512]{2,1,0:T(8,128)} %bitcast.171, ...), custom_call_target="tpu_custom_call", output_to_operand_aliasing={{0}: (16, {}), {1}: (17, {})} | custom-call | bytes 1024 | tf_op jit(solution)/shard_map/attention_both_ways/pallas_call | solution.py:875
  551.4 171.2 %exchange.5 = (f32[1024,512]{1,0:T(8,128)}, bf16[1024,2048]{1,0:T(8,128)(2,1)}, bf16[1024,2048]{1,0:T(8,128)(2,1)}, bf16[512,2048]{1,0:T(8,128)(2,1)}, bf16[512,...) custom-call(bf16[1024,2048]{1,0:T(8,128)(2,1)} %convolution_convert_, ...), custom_call_target="tpu_custom_call" | custom-call | bytes 629145600 | tf_op jit(solution)/shard_map/exchange/pallas_call | solution.py:675
  728.2 6.7 fusion.51.g2
  738.6 16.9 %gradient_sums.1 = (bf16[48,1024]{1,0:T(8,128)(2,1)}, f32[8,1024]{1,0:T(8,128)}, f32[8,512]{1,0:T(8,128)}) custom-call(f32[1024,512]{1,0:T(8,128)} %get-tuple-element.202.g0, f32[1024,512]{1,0:T(8,128)} %fusion.50.g1, f32[1024,512]{1,0:T(8,128)} %fusion.51.g2, f32[1024,512]{1,0:T(8,128)} %convert_element_type.242.g3, ...), custom_call_target="tpu_custom_call" | custom-call | flops 57671680 | bytes 22020096 | tf_op jit(solution)/shard_map/gradient_sums/pallas_call | solution.py:1031
  755.5 29.1 %totals_over_head.1 = (f32[48,1024]{1,0:T(8,128)}, f32[64,1024]{1,0:T(8,128)}, f32[8,1024]{1,0:T(8,128)}) custom-call(bf16[48,1024]{1,0:T(8,128)(2,1)} %get-tuple-element.208.refs_0_, bf16[64,1024]{1,0:T(8,128)(2,1)} %early_sums.1.refs_1_, f32[8,1024]{1,0:T(8,128)} %get-tuple-element.210.refs_2_), custom_call_target="tpu_custom_call" | custom-call | tf_op jit(solution)/shard_map/totals_over_head/pallas_call | solution.py:1093
  795.3 18.1 %small_gradients.1 = (f32[80,512]{1,0:T(8,128)}, f32[36,1024]{1,0:T(8,128)}, f32[1024,128]{1,0:T(8,128)}) custom-call(f32[48,1024]{1,0:T(8,128)} %get-tuple-element.213.dots_ref, f32[64,1024]{1,0:T(8,128)} %get-tuple-element.214.early_ref, f32[8,1024]{1,0:T(8,128)} %get-tuple-element.215.sums_ref, f32[8,1024]{1,0:T(8,128)} %copy-done.26, ...), custom_call_target="tpu_custom_call" | custom-call | tf_op jit(solution)/shard_map/small_gradients/pallas_call | solution.py:1195
  816.3 18.9 %history_gradient.1 = f32[9,1024,512]{2,1,0:T(8,128)} custom-call(f32[1024,512]{1,0:T(8,128)} %get-tuple-element.202.g0, f32[1024,512]{1,0:T(8,128)} %fusion.50.g1, f32[1024,512]{1,0:T(8,128)} %fusion.51.g2, f32[1024,512]{1,0:T(8,128)} %convert_element_type.242.g3, f32[4,1024,512]{2,1,0:T(8,128)} %get-tuple-element.141.streams_ref, f32[1024,8]{1,0:T(8,128)} %bitcast.178, ...), custom_call_target="tpu_custom_call" | custom-call | flops 57671680 | bytes 33554432 | tf_op jit(solution)/shard_map/history_gradient/pallas_call | solution.py:1254
  (251 shorter events, 181.1 us)
Async XLA Ops:
  7.2 108.8 %all-gather.6.cloned.1.call-start = ((), (), s32[]{:S(2)}) async-start(), calls=%async_computation.3 | async-start | bytes 5242880 | tf_op jit(solution)/shard_map/all_gather | solution.py:1337
  8.7 68.0 %copy-start = (bf16[1,2,512,512]{3,2,1,0:T(8,128)(2,1)}, bf16[1,2,512,512]{3,2,1,0:T(8,128)(2,1)S(1)}, u32[]{:S(2)}) copy-start(bf16[1,2,512,512]{3,2,1,0:T(8,128)(2,1)S(1)} %slice.99) | copy-start | bytes 3145732
  34.7 42.0 %copy-start.21 = (f32[37,1024]{1,0:T(8,128)S(1)}, f32[37,1024]{1,0:T(8,128)}, u32[]{:S(2)}) copy-start(f32[37,1024]{1,0:T(8,128)} %sum_over_head.2) | copy-start | bytes 454660
  34.7 43.9 %copy-start.35 = (bf16[36,36]{1,0:T(8,128)(2,1)S(1)}, bf16[36,36]{1,0:T(8,128)(2,1)}, u32[]{:S(2)}) copy-start(bf16[36,36]{1,0:T(8,128)(2,1)} %param.17) | copy-start | bytes 7780
  34.8 173.2 %all-gather.8.cloned.1.call-start = ((), (), s32[]{:S(2)}) async-start(), calls=%async_computation.4 | async-start | bytes 5242880 | tf_op jit(solution)/shard_map/all_gather | solution.py:1357
  116.1 174.5 %all-gather.10.cloned.1.call-start = ((), (), s32[]{:S(2)}) async-start(), calls=%async_computation.5 | async-start | bytes 5242880 | tf_op jit(solution)/shard_map/all_gather | solution.py:1357
  207.9 169.2 %all-gather.12.cloned.1.call-start = ((), (), s32[]{:S(2)}) async-start(), calls=%async_computation.6 | async-start | bytes 5242880 | tf_op jit(solution)/shard_map/all_gather | solution.py:1357
  255.6 7.5 collective-permute-start.1
  259.0 11.2 %collective-permute-start = (bf16[1,4,256,2048]{3,2,1,0:T(8,128)(2,1)}, bf16[1,4,256,2048]{3,2,1,0:T(8,128)(2,1)}, u32[]{:S(2)}, u32[]{:S(2)}) collective-permute-start(bf16[1,4,256,2048]{3,2,1,0:T(8,128)(2,1)} %dynamic-slice_bitcast_fusion.1), channel_id=1, source_target_pairs={{0,4},{4,0},{8,12},{12,8},{1,5},{5,1},{9,13},{13,9},{2,6},{6,2},{1... | collective-permute-start | bytes 12582920 | tf_op jit(solution)/shard_map/ppermute | solution.py:51
  290.6 166.0 %all-gather.14.cloned.1.call-start = ((), (), s32[]{:S(2)}) async-start(), calls=%async_computation.7 | async-start | bytes 5242880 | tf_op jit(solution)/shard_map/all_gather | solution.py:1357
  311.3 47.8 %collective-permute-start.2 = (bf16[1,2,256,2048]{3,2,1,0:T(8,128)(2,1)}, bf16[1,2,256,2048]{3,2,1,0:T(8,128)(2,1)}, u32[]{:S(2)}, u32[]{:S(2)}) collective-permute-start(bf16[1,2,256,2048]{3,2,1,0:T(8,128)(2,1)} %get-tuple-element.140), channel_id=1, source_target_pairs={{0,16},{16,0},{1,17},{17,1},{2,18},{18,2},{3,19},{19,3},{4,20},{20... | collective-permute-start | bytes 6291464 | tf_op jit(solution)/shard_map/ppermute | solution.py:43
  377.1 167.5 %reduce-scatter.4.cloned.1.call-start = ((), (), s32[]{:S(2)}) async-start(), calls=%async_computation.8 | async-start | bytes 5242880 | tf_op jit(solution)/shard_map/reduce_scatter | solution.py:1370
  377.4 58.8 %collective-permute-start.9 = (bf16[1,2,256,2048]{3,2,1,0:T(8,128)(2,1)}, bf16[1,2,256,2048]{3,2,1,0:T(8,128)(2,1)}, u32[]{:S(2)}, u32[]{:S(2)}) collective-permute-start(bf16[1,2,256,2048]{3,2,1,0:T(8,128)(2,1)} %get-tuple-element.162), channel_id=1, source_target_pairs={{0,16},{16,0},{1,17},{17,1},{2,18},{18,2},{3,19},{19,3},{4,20},{20... | collective-permute-start | bytes 6291464 | tf_op jit(solution)/shard_map/ppermute | solution.py:43
  385.2 27.3 %collective-permute-start.7 = (bf16[2,512,512]{2,1,0:T(8,128)(2,1)}, bf16[2,512,512]{2,1,0:T(8,128)(2,1)}, u32[]{:S(2)}, u32[]{:S(2)}) collective-permute-start(bf16[2,512,512]{2,1,0:T(8,128)(2,1)} %bitcast.32.refs_4_), channel_id=1, source_target_pairs={{0,8},{4,12},{1,9},{5,13},{2,10},{6,14},{3,11},{7,15},{16,24},{20,... | collective-permute-start | bytes 3145736 | tf_op jit(solution)/shard_map/ppermute | solution.py:903
  389.6 42.9 %collective-permute-start.4 = (bf16[2,512,512]{2,1,0:T(8,128)(2,1)S(1)}, bf16[2,512,512]{2,1,0:T(8,128)(2,1)}, u32[]{:S(2)}, u32[]{:S(2)}) collective-permute-start(bf16[2,512,512]{2,1,0:T(8,128)(2,1)S(1)} %bitcast.160), channel_id=1, source_target_pairs={{0,8},{4,12},{1,9},{5,13},{2,10},{6,14},{3,11},{7,15},{16,24},{20,... | collective-permute-start | bytes 3145736 | tf_op jit(solution)/shard_map/ppermute | solution.py:903
  398.9 41.0 %collective-permute-start.6 = (bf16[2,512,512]{2,1,0:T(8,128)(2,1)}, bf16[2,512,512]{2,1,0:T(8,128)(2,1)S(1)}, u32[]{:S(2)}, u32[]{:S(2)}) collective-permute-start(bf16[2,512,512]{2,1,0:T(8,128)(2,1)} %bitcast.32.refs_4_), channel_id=1, source_target_pairs={{0,4},{4,0},{8,12},{12,8},{1,5},{5,1},{9,13},{13,9},{2,6},{6,2},{1... | collective-permute-start | bytes 3145736 | tf_op jit(solution)/shard_map/ppermute | solution.py:51
  399.0 40.9 %collective-permute-start.3 = (bf16[2,512,512]{2,1,0:T(8,128)(2,1)S(1)}, bf16[2,512,512]{2,1,0:T(8,128)(2,1)S(1)}, u32[]{:S(2)}, u32[]{:S(2)}) collective-permute-start(bf16[2,512,512]{2,1,0:T(8,128)(2,1)S(1)} %bitcast.161), channel_id=1, source_target_pairs={{0,4},{4,0},{8,12},{12,8},{1,5},{5,1},{9,13},{13,9},{2,6},{6,2},{1... | collective-permute-start | bytes 3145736 | tf_op jit(solution)/shard_map/ppermute | solution.py:51
  412.5 28.4 %collective-permute-start.8 = (bf16[2,512,512]{2,1,0:T(8,128)(2,1)}, bf16[2,512,512]{2,1,0:T(8,128)(2,1)S(1)}, u32[]{:S(2)}, u32[]{:S(2)}) collective-permute-start(bf16[2,512,512]{2,1,0:T(8,128)(2,1)} %collective-permute-done.7.refs_6_), channel_id=1, source_target_pairs={{0,4},{4,0},{8,12},{12,8},{1,5},{5,1},{9,13},{13,9},{2,6},{6,2},{1... | collective-permute-start | bytes 3145736 | tf_op jit(solution)/shard_map/ppermute | solution.py:51
  432.5 10.4 %collective-permute-start.5 = (bf16[2,512,512]{2,1,0:T(8,128)(2,1)}, bf16[2,512,512]{2,1,0:T(8,128)(2,1)}, u32[]{:S(2)}, u32[]{:S(2)}) collective-permute-start(bf16[2,512,512]{2,1,0:T(8,128)(2,1)} %collective-permute-done.4.refs_2_), channel_id=1, source_target_pairs={{0,4},{4,0},{8,12},{12,8},{1,5},{5,1},{9,13},{13,9},{2,6},{6,2},{1... | collective-permute-start | bytes 3145736 | tf_op jit(solution)/shard_map/ppermute | solution.py:51
  442.9 394.9 %reduce-scatter.6.cloned.1.call-start = ((), (), s32[]{:S(2)}) async-start(), calls=%async_computation.9 | async-start | bytes 1966080 | tf_op jit(solution)/shard_map/reduce_scatter | solution.py:1370
  486.1 4.4 collective-permute-start.10
  494.8 28.0 %collective-permute-start.11 = (bf16[2,512,512]{2,1,0:T(8,128)(2,1)S(1)}, bf16[2,512,512]{2,1,0:T(8,128)(2,1)S(1)}, u32[]{:S(2)}, u32[]{:S(2)}) collective-permute-start(bf16[2,512,512]{2,1,0:T(8,128)(2,1)S(1)} %fusion.12), channel_id=1, source_target_pairs={{8,0},{12,4},{9,1},{13,5},{10,2},{14,6},{11,3},{15,7},{24,16},{28,... | collective-permute-start | bytes 3145736 | tf_op jit(solution)/shard_map/ppermute | solution.py:913
  539.2 8.4 collective-permute-start.12
  726.9 114.5 %reduce-scatter.8.cloned.1.call-start = ((), (), s32[]{:S(2)}) async-start(), calls=%async_computation.10 | async-start | bytes 3276800 | tf_op jit(solution)/shard_map/reduce_scatter | solution.py:1370
  (51 other events, 431.4 us)
Sparse Core Ops, SparseCore 0:
  34.8 81.1 all-gather.5
  118.2 89.6 all-gather.7
  210.1 80.4 all-gather.9
  292.5 79.2 all-gather.11
  377.3 79.2 all-gather.13
  458.7 77.9 reduce-scatter.3
  727.0 37.0 reduce-scatter.5
  790.1 51.1 reduce-scatter.7

commit v11 on v10

--- a/solution.py
+++ b/solution.py
@@ -941,7 +941,7 @@
 
 def mix_streams(weights, history):
     _, tokens, feats = history.shape
-    block = min(128, tokens)
+    block = min(256, tokens)
     return pl.pallas_call(
         streams_kernel,
         grid=(tokens // block,),
@@ -980,7 +980,7 @@
 
 def early_sums(streams, cot, history):
     _, tokens, feats = streams.shape
-    block = min(128, tokens)
+    block = min(256, tokens)
     return pl.pallas_call(
         early_kernel,
         grid=(tokens // block,),
@@ -1026,7 +1026,7 @@
 
 def gradient_sums(grads, streams, stats, gain, history):
     _, tokens, feats = streams.shape
-    block = min(128, tokens)
+    block = min(256, tokens)
     wide = pl.BlockSpec((block, feats), lambda i: (i, 0))
     return pl.pallas_call(
         sums_kernel,
@@ -1247,7 +1247,7 @@
 
 def history_gradient(grads, streams, stats, gain, cot, current, weights, coefs, d_scaled, w_rows):
     _, tokens, feats = streams.shape
-    block = min(128, tokens)
+    block = min(256, tokens)
     wide = pl.BlockSpec((block, feats), lambda i: (i, 0))
     narrow = lambda a: pl.BlockSpec((block, a.shape[1]), lambda i: (i, 0))
     fixed = lambda a: pl.BlockSpec(a.shape, lambda i: (0, 0))

time: 863 us -> 864 us (level)
  no operation moved by 1% of the time
where the time goes in v11:
time: 864 us; the launch traced here: 855 us
  Pallas kernels  539 us (62%)
  waiting for transfers between devices  103 us (12%)
  matrix products  79.2 us (9%)
  other arithmetic  62.5 us (7%)
  local copies, waits for them, and re-layouts  43.2 us (5%)
  between operations  15.2 us (2%)
  starting transfers between devices  12.9 us (1%)
    pallas_call x3, Pallas kernels, exchange(): pl.pallas_call(functools.partial(exchange_kernel, units, spread, axes), i...  300 us
    pallas_call x2, Pallas kernels, attention(): pl.pallas_call(functools.partial(attention_kernel, len(earlier)), grid=(f...  47.7 us
    pallas_call x1, Pallas kernels, feed_forward(): pl.pallas_call(feed_kernel, grid=(hidden // block,), in_specs=[fixed, fix...  42.2 us
    dot_general x6, matrix products, dot(): return jnp.dot(a, b, preferred_element_type=F32)  36.1 us
    dot_general x5, matrix products, dot_nt(): lax.dot_general(a, b, (((1,), (1,)), ((), ())), preferred_element_type=F32)  34 us
    ppermute x2, waiting for transfers between devices, exchange_rows(): across = lax.ppermute(local, 'stream', [(0, 2), (1, 3)])  33 us
    pallas_call x2, Pallas kernels, head_sum(): pl.pallas_call(functools.partial(head_sum_kernel, members), out_shape=jax...  31.8 us
    all_gather x4, waiting for transfers between devices, all_features(): return lax.all_gather(a, 'head', axis=1, tiled=True)  30.5 us
  transfers between devices with their start and end apart: 21, of which 10 were waited for; matrix products, arithmetic and copies ran while one was open for 18% of the time, Pallas kernels for 41%

profile of v11, /device:TPU:8, one launch (start us, length us, event | category | flops | bytes accessed | tf_op | source)
XLA Modules:
  0.0 854.7 jit_solution(7722230754974475683)
XLA Ops:
  14.1 19.2 %sum_over_head.2 = f32[37,1024]{1,0:T(8,128)} custom-call(f32[37,1024]{1,0:T(8,128)} %pad_maximum_fusion.2.x_ref), custom_call_target="tpu_custom_call" | custom-call | tf_op jit(solution)/shard_map/sum_over_head/pallas_call | solution.py:731
  34.8 41.9 %exchange.3.up_ref = bf16[2048,2048]{1,0:T(8,128)(2,1)} custom-call(bf16[256,2048]{1,0:T(8,128)(2,1)} %refs_0_), custom_call_target="tpu_custom_call" | custom-call | bytes 251658240 | tf_op jit(solution)/shard_map/exchange/pallas_call | solution.py:675
  80.0 13.2 %mix_streams.1 = (f32[4,1024,512]{2,1,0:T(8,128)}, f32[8,1024]{1,0:T(8,128)}) custom-call(f32[1024,36]{1,0:T(8,128)} %convolution_add_fusion.weights_ref, bf16[9,1024,512]{2,1,0:T(8,128)(2,1)} %bitcast.149), custom_call_target="tpu_custom_call" | custom-call | flops 41943040 | bytes 17825792 | tf_op jit(solution)/shard_map/mix_streams/pallas_call | solution.py:945
  93.3 12.6 %sum_over_head.3 = f32[8,1024]{1,0:T(8,128)} custom-call(f32[8,1024]{1,0:T(8,128)} %get-tuple-element.123.x_ref), custom_call_target="tpu_custom_call" | custom-call | tf_op jit(solution)/shard_map/sum_over_head/pallas_call | solution.py:731
  117.1 86.7 %exchange.4 = (bf16[2048,512]{1,0:T(8,128)(2,1)}, bf16[2048,512]{1,0:T(8,128)(2,1)}, bf16[2048,2048]{1,0:T(8,128)(2,1)}, bf16[512,2048]{1,0:T(8,128)(2,1)}, bf16...) custom-call(bf16[256,512]{1,0:T(8,128)(2,1)} %get-tuple-element.307.refs_0_, ...), custom_call_target="tpu_custom_call" | custom-call | bytes 251658240 | tf_op jit(solution)/shard_map/exchange/pallas_call | solution.py:675
  208.2 42.2 %feed_forward.1 = (bf16[1024,2048]{1,0:T(8,128)(2,1)}, bf16[1024,2048]{1,0:T(8,128)(2,1)}, bf16[2048,2048]{1,0:T(8,128)(2,1)}, bf16[2048,2048]{1,0:T(8,128)(2,1)}) custom-call(bf16[1024,2048]{1,0:T(8,128)(2,1)} %all-gather.8.cloned.1.call-done.x_ref, bf16[1024,2048]{1,0:T(8,128)(2,1)} %all-gather.6.cloned.1.call-done.d_ref, ...), custom_call_target="tpu_custom_call" | custom-call | flops 34359738368 | bytes 41943040 | tf_op jit(solution)/shard_map/feed_forward/pallas_call | solution.py:805
  277.9 12.6 %all-gather.10.cloned.1.call-done.refs_14_ = bf16[1024,2048]{1,0:T(8,128)(2,1)} async-done(((bf16[1024,512]{1,0:T(8,128)(2,1)}), bf16[1024,2048]{1,0:T(8,128)(2,1)}) %all-gather.10.cloned.1.call-update) | async-done | bytes 4194320 | tf_op jit(solution)/shard_map/all_gather | solution.py:1357
  300.5 10.8 %convolution_convert_fusion.2 = bf16[1024,2048]{1,0:T(8,128)(2,1)} fusion(bf16[1024,2048]{1,0:T(8,128)(2,1)S(1)} %copy-done.51, bf16[2048,2048]{1,0:T(8,128)(2,1)S(1)} %bitcast.211), kind=kOutput, calls=%fused_computation.19 | convolution fusion | flops 8592031744 | bytes 16777216 | tf_op jit(solution)/shard_map/dot_general | solution.py:27
  321.1 13.9 %convolution_convert_fusion.1 = bf16[1024,2048]{1,0:T(8,128)(2,1)} fusion(bf16[1024,2048]{1,0:T(8,128)(2,1)} %get-tuple-element.144, bf16[2048,2048]{1,0:T(8,128)(2,1)} %exchange.3.up_ref), kind=kOutput, calls=%fused_computation.18 | convolution fusion | flops 8592031744 | bytes 16777216 | tf_op jit(solution)/shard_map/dot_general | solution.py:31
  335.1 24.0 %collective-permute-done.2 = bf16[1,2,256,2048]{3,2,1,0:T(8,128)(2,1)} collective-permute-done((bf16[1,2,256,2048]{3,2,1,0:T(8,128)(2,1)}, bf16[1,2,256,2048]{3,2,1,0:T(8,128)(2,1)}, u32[]{:S(2)}, u32[]{:S(2)}) %collective-permute-start.2) | collective-permute-done | bytes 2097184 | tf_op jit(solution)/shard_map/ppermute | solution.py:43
  363.6 14.0 %early_sums.1.refs_1_ = bf16[64,1024]{1,0:T(8,128)(2,1)} custom-call(f32[4,1024,512]{2,1,0:T(8,128)} %get-tuple-element.141.streams_ref, bf16[1024,512]{1,0:T(8,128)(2,1)} %fusion.10.cot_ref, bf16[9,1024,512]{2,1,0:T(8,128)(2,1)} %bitcast.150), custom_call_target="tpu_custom_call" | custom-call | flops 57671680 | bytes 18874368 | tf_op jit(solution)/shard_map/early_sums/pallas_call | solution.py:984
  379.2 6.2 convolution_convert_fusion.5
  399.7 13.0 %collective-permute-done.7.refs_6_ = bf16[2,512,512]{2,1,0:T(8,128)(2,1)} collective-permute-done((bf16[2,512,512]{2,1,0:T(8,128)(2,1)}, bf16[2,512,512]{2,1,0:T(8,128)(2,1)}, u32[]{:S(2)}, u32[]{:S(2)}) %collective-permute-start.7) | collective-permute-done | bytes 1048608 | tf_op jit(solution)/shard_map/ppermute | solution.py:903
  412.7 20.0 %collective-permute-done.4.refs_2_ = bf16[2,512,512]{2,1,0:T(8,128)(2,1)} collective-permute-done((bf16[2,512,512]{2,1,0:T(8,128)(2,1)S(1)}, bf16[2,512,512]{2,1,0:T(8,128)(2,1)}, u32[]{:S(2)}, u32[]{:S(2)}) %collective-permute-start.4) | collective-permute-done | bytes 1048608 | tf_op jit(solution)/shard_map/ppermute | solution.py:903
  443.2 13.8 %all-gather.14.cloned.1.call-done = bf16[1024,2048]{1,0:T(8,128)(2,1)} async-done(((bf16[1024,512]{1,0:T(8,128)(2,1)}), bf16[1024,2048]{1,0:T(8,128)(2,1)}) %all-gather.14.cloned.1.call-update) | async-done | bytes 4194320 | tf_op jit(solution)/shard_map/all_gather | solution.py:1357
  456.9 5.8 fusion.49
  462.8 23.9 %attention_both_ways.2 = (bf16[2,512,512]{2,1,0:T(8,128)(2,1)}, bf16[2,512,512]{2,1,0:T(8,128)(2,1)}, bf16[2,2,512,512]{3,2,1,0:T(8,128)(2,1)}, bf16[2,2,512,512]{3,2,1,0:T(8,128)(2,1)}) custom-call(s32[4]{0:T(128)} %iota_xor_fusion.place_ref, f32[2,512,512]{2,1,0:T(8,128)} %bitcast.170, bf16[2,512,512]{2,1,0:T(8,128)(2,1)} %bitcast.180, ...), custom_call_target="tpu_custom_call" | custom-call | bytes 1024 | tf_op jit(solution)/shard_map/attention_both_ways/pallas_call | solution.py:875
  499.4 23.8 %attention_both_ways.3 = (bf16[2,512,512]{2,1,0:T(8,128)(2,1)}, bf16[2,512,512]{2,1,0:T(8,128)(2,1)}, bf16[2,2,512,512]{3,2,1,0:T(8,128)(2,1)}, bf16[2,2,512,512]{3,2,1,0:T(8,128)(2,1)}) custom-call(s32[4]{0:T(128)} %iota_xor_fusion.place_ref, f32[2,512,512]{2,1,0:T(8,128)} %bitcast.171, ...), custom_call_target="tpu_custom_call", output_to_operand_aliasing={{0}: (16, {}), {1}: (17, {})} | custom-call | bytes 1024 | tf_op jit(solution)/shard_map/attention_both_ways/pallas_call | solution.py:875
  551.7 171.1 %exchange.5 = (f32[1024,512]{1,0:T(8,128)}, bf16[1024,2048]{1,0:T(8,128)(2,1)}, bf16[1024,2048]{1,0:T(8,128)(2,1)}, bf16[512,2048]{1,0:T(8,128)(2,1)}, bf16[512,...) custom-call(bf16[1024,2048]{1,0:T(8,128)(2,1)} %convolution_convert_, ...), custom_call_target="tpu_custom_call" | custom-call | bytes 629145600 | tf_op jit(solution)/shard_map/exchange/pallas_call | solution.py:675
  728.2 6.7 fusion.51.g2
  738.6 16.2 %gradient_sums.1 = (bf16[48,1024]{1,0:T(8,128)(2,1)}, f32[8,1024]{1,0:T(8,128)}, f32[8,512]{1,0:T(8,128)}) custom-call(f32[1024,512]{1,0:T(8,128)} %get-tuple-element.202.g0, f32[1024,512]{1,0:T(8,128)} %fusion.50.g1, f32[1024,512]{1,0:T(8,128)} %fusion.51.g2, f32[1024,512]{1,0:T(8,128)} %convert_element_type.242.g3, ...), custom_call_target="tpu_custom_call" | custom-call | flops 57671680 | bytes 22020096 | tf_op jit(solution)/shard_map/gradient_sums/pallas_call | solution.py:1031
  754.8 30.0 %totals_over_head.1 = (f32[48,1024]{1,0:T(8,128)}, f32[64,1024]{1,0:T(8,128)}, f32[8,1024]{1,0:T(8,128)}) custom-call(bf16[48,1024]{1,0:T(8,128)(2,1)} %get-tuple-element.208.refs_0_, bf16[64,1024]{1,0:T(8,128)(2,1)} %early_sums.1.refs_1_, f32[8,1024]{1,0:T(8,128)} %get-tuple-element.210.refs_2_), custom_call_target="tpu_custom_call" | custom-call | tf_op jit(solution)/shard_map/totals_over_head/pallas_call | solution.py:1093
  795.6 18.1 %small_gradients.1 = (f32[80,512]{1,0:T(8,128)}, f32[36,1024]{1,0:T(8,128)}, f32[1024,128]{1,0:T(8,128)}) custom-call(f32[48,1024]{1,0:T(8,128)} %get-tuple-element.213.dots_ref, f32[64,1024]{1,0:T(8,128)} %get-tuple-element.214.early_ref, f32[8,1024]{1,0:T(8,128)} %get-tuple-element.215.sums_ref, f32[8,1024]{1,0:T(8,128)} %copy-done.26, ...), custom_call_target="tpu_custom_call" | custom-call | tf_op jit(solution)/shard_map/small_gradients/pallas_call | solution.py:1195
  816.6 18.7 %history_gradient.1 = f32[9,1024,512]{2,1,0:T(8,128)} custom-call(f32[1024,512]{1,0:T(8,128)} %get-tuple-element.202.g0, f32[1024,512]{1,0:T(8,128)} %fusion.50.g1, f32[1024,512]{1,0:T(8,128)} %fusion.51.g2, f32[1024,512]{1,0:T(8,128)} %convert_element_type.242.g3, f32[4,1024,512]{2,1,0:T(8,128)} %get-tuple-element.141.streams_ref, f32[1024,8]{1,0:T(8,128)} %bitcast.178, ...), custom_call_target="tpu_custom_call" | custom-call | flops 57671680 | bytes 33554432 | tf_op jit(solution)/shard_map/history_gradient/pallas_call | solution.py:1254
  (251 shorter events, 181.0 us)
Async XLA Ops:
  7.2 108.9 %all-gather.6.cloned.1.call-start = ((), (), s32[]{:S(2)}) async-start(), calls=%async_computation.3 | async-start | bytes 5242880 | tf_op jit(solution)/shard_map/all_gather | solution.py:1337
  8.7 68.0 %copy-start = (bf16[1,2,512,512]{3,2,1,0:T(8,128)(2,1)}, bf16[1,2,512,512]{3,2,1,0:T(8,128)(2,1)S(1)}, u32[]{:S(2)}) copy-start(bf16[1,2,512,512]{3,2,1,0:T(8,128)(2,1)S(1)} %slice.99) | copy-start | bytes 3145732
  34.7 42.1 %copy-start.21 = (f32[37,1024]{1,0:T(8,128)S(1)}, f32[37,1024]{1,0:T(8,128)}, u32[]{:S(2)}) copy-start(f32[37,1024]{1,0:T(8,128)} %sum_over_head.2) | copy-start | bytes 454660
  34.7 43.9 %copy-start.35 = (bf16[36,36]{1,0:T(8,128)(2,1)S(1)}, bf16[36,36]{1,0:T(8,128)(2,1)}, u32[]{:S(2)}) copy-start(bf16[36,36]{1,0:T(8,128)(2,1)} %param.17) | copy-start | bytes 7780
  34.8 173.2 %all-gather.8.cloned.1.call-start = ((), (), s32[]{:S(2)}) async-start(), calls=%async_computation.4 | async-start | bytes 5242880 | tf_op jit(solution)/shard_map/all_gather | solution.py:1357
  116.1 174.5 %all-gather.10.cloned.1.call-start = ((), (), s32[]{:S(2)}) async-start(), calls=%async_computation.5 | async-start | bytes 5242880 | tf_op jit(solution)/shard_map/all_gather | solution.py:1357
  207.9 169.6 %all-gather.12.cloned.1.call-start = ((), (), s32[]{:S(2)}) async-start(), calls=%async_computation.6 | async-start | bytes 5242880 | tf_op jit(solution)/shard_map/all_gather | solution.py:1357
  255.5 7.5 collective-permute-start.1
  259.0 11.2 %collective-permute-start = (bf16[1,4,256,2048]{3,2,1,0:T(8,128)(2,1)}, bf16[1,4,256,2048]{3,2,1,0:T(8,128)(2,1)}, u32[]{:S(2)}, u32[]{:S(2)}) collective-permute-start(bf16[1,4,256,2048]{3,2,1,0:T(8,128)(2,1)} %dynamic-slice_bitcast_fusion.1), channel_id=1, source_target_pairs={{0,4},{4,0},{8,12},{12,8},{1,5},{5,1},{9,13},{13,9},{2,6},{6,2},{1... | collective-permute-start | bytes 12582920 | tf_op jit(solution)/shard_map/ppermute | solution.py:51
  290.6 166.4 %all-gather.14.cloned.1.call-start = ((), (), s32[]{:S(2)}) async-start(), calls=%async_computation.7 | async-start | bytes 5242880 | tf_op jit(solution)/shard_map/all_gather | solution.py:1357
  311.3 47.8 %collective-permute-start.2 = (bf16[1,2,256,2048]{3,2,1,0:T(8,128)(2,1)}, bf16[1,2,256,2048]{3,2,1,0:T(8,128)(2,1)}, u32[]{:S(2)}, u32[]{:S(2)}) collective-permute-start(bf16[1,2,256,2048]{3,2,1,0:T(8,128)(2,1)} %get-tuple-element.140), channel_id=1, source_target_pairs={{0,16},{16,0},{1,17},{17,1},{2,18},{18,2},{3,19},{19,3},{4,20},{20... | collective-permute-start | bytes 6291464 | tf_op jit(solution)/shard_map/ppermute | solution.py:43
  377.6 167.4 %reduce-scatter.4.cloned.1.call-start = ((), (), s32[]{:S(2)}) async-start(), calls=%async_computation.8 | async-start | bytes 5242880 | tf_op jit(solution)/shard_map/reduce_scatter | solution.py:1370
  377.6 58.8 %collective-permute-start.9 = (bf16[1,2,256,2048]{3,2,1,0:T(8,128)(2,1)}, bf16[1,2,256,2048]{3,2,1,0:T(8,128)(2,1)}, u32[]{:S(2)}, u32[]{:S(2)}) collective-permute-start(bf16[1,2,256,2048]{3,2,1,0:T(8,128)(2,1)} %get-tuple-element.162), channel_id=1, source_target_pairs={{0,16},{16,0},{1,17},{17,1},{2,18},{18,2},{3,19},{19,3},{4,20},{20... | collective-permute-start | bytes 6291464 | tf_op jit(solution)/shard_map/ppermute | solution.py:43
  385.4 27.3 %collective-permute-start.7 = (bf16[2,512,512]{2,1,0:T(8,128)(2,1)}, bf16[2,512,512]{2,1,0:T(8,128)(2,1)}, u32[]{:S(2)}, u32[]{:S(2)}) collective-permute-start(bf16[2,512,512]{2,1,0:T(8,128)(2,1)} %bitcast.32.refs_4_), channel_id=1, source_target_pairs={{0,8},{4,12},{1,9},{5,13},{2,10},{6,14},{3,11},{7,15},{16,24},{20,... | collective-permute-start | bytes 3145736 | tf_op jit(solution)/shard_map/ppermute | solution.py:903
  389.8 42.9 %collective-permute-start.4 = (bf16[2,512,512]{2,1,0:T(8,128)(2,1)S(1)}, bf16[2,512,512]{2,1,0:T(8,128)(2,1)}, u32[]{:S(2)}, u32[]{:S(2)}) collective-permute-start(bf16[2,512,512]{2,1,0:T(8,128)(2,1)S(1)} %bitcast.160), channel_id=1, source_target_pairs={{0,8},{4,12},{1,9},{5,13},{2,10},{6,14},{3,11},{7,15},{16,24},{20,... | collective-permute-start | bytes 3145736 | tf_op jit(solution)/shard_map/ppermute | solution.py:903
  399.1 41.0 %collective-permute-start.6 = (bf16[2,512,512]{2,1,0:T(8,128)(2,1)}, bf16[2,512,512]{2,1,0:T(8,128)(2,1)S(1)}, u32[]{:S(2)}, u32[]{:S(2)}) collective-permute-start(bf16[2,512,512]{2,1,0:T(8,128)(2,1)} %bitcast.32.refs_4_), channel_id=1, source_target_pairs={{0,4},{4,0},{8,12},{12,8},{1,5},{5,1},{9,13},{13,9},{2,6},{6,2},{1... | collective-permute-start | bytes 3145736 | tf_op jit(solution)/shard_map/ppermute | solution.py:51
  399.2 40.9 %collective-permute-start.3 = (bf16[2,512,512]{2,1,0:T(8,128)(2,1)S(1)}, bf16[2,512,512]{2,1,0:T(8,128)(2,1)S(1)}, u32[]{:S(2)}, u32[]{:S(2)}) collective-permute-start(bf16[2,512,512]{2,1,0:T(8,128)(2,1)S(1)} %bitcast.161), channel_id=1, source_target_pairs={{0,4},{4,0},{8,12},{12,8},{1,5},{5,1},{9,13},{13,9},{2,6},{6,2},{1... | collective-permute-start | bytes 3145736 | tf_op jit(solution)/shard_map/ppermute | solution.py:51
  412.7 28.4 %collective-permute-start.8 = (bf16[2,512,512]{2,1,0:T(8,128)(2,1)}, bf16[2,512,512]{2,1,0:T(8,128)(2,1)S(1)}, u32[]{:S(2)}, u32[]{:S(2)}) collective-permute-start(bf16[2,512,512]{2,1,0:T(8,128)(2,1)} %collective-permute-done.7.refs_6_), channel_id=1, source_target_pairs={{0,4},{4,0},{8,12},{12,8},{1,5},{5,1},{9,13},{13,9},{2,6},{6,2},{1... | collective-permute-start | bytes 3145736 | tf_op jit(solution)/shard_map/ppermute | solution.py:51
  432.7 10.4 %collective-permute-start.5 = (bf16[2,512,512]{2,1,0:T(8,128)(2,1)}, bf16[2,512,512]{2,1,0:T(8,128)(2,1)}, u32[]{:S(2)}, u32[]{:S(2)}) collective-permute-start(bf16[2,512,512]{2,1,0:T(8,128)(2,1)} %collective-permute-done.4.refs_2_), channel_id=1, source_target_pairs={{0,4},{4,0},{8,12},{12,8},{1,5},{5,1},{9,13},{13,9},{2,6},{6,2},{1... | collective-permute-start | bytes 3145736 | tf_op jit(solution)/shard_map/ppermute | solution.py:51
  443.1 394.7 %reduce-scatter.6.cloned.1.call-start = ((), (), s32[]{:S(2)}) async-start(), calls=%async_computation.9 | async-start | bytes 1966080 | tf_op jit(solution)/shard_map/reduce_scatter | solution.py:1370
  486.7 4.4 collective-permute-start.10
  495.5 27.7 %collective-permute-start.11 = (bf16[2,512,512]{2,1,0:T(8,128)(2,1)S(1)}, bf16[2,512,512]{2,1,0:T(8,128)(2,1)S(1)}, u32[]{:S(2)}, u32[]{:S(2)}) collective-permute-start(bf16[2,512,512]{2,1,0:T(8,128)(2,1)S(1)} %fusion.12), channel_id=1, source_target_pairs={{8,0},{12,4},{9,1},{13,5},{10,2},{14,6},{11,3},{15,7},{24,16},{28,... | collective-permute-start | bytes 3145736 | tf_op jit(solution)/shard_map/ppermute | solution.py:913
  539.5 8.4 collective-permute-start.12
  727.1 114.5 %reduce-scatter.8.cloned.1.call-start = ((), (), s32[]{:S(2)}) async-start(), calls=%async_computation.10 | async-start | bytes 3276800 | tf_op jit(solution)/shard_map/reduce_scatter | solution.py:1370
  (51 other events, 429.1 us)
Sparse Core Ops, SparseCore 0:
  34.8 81.1 all-gather.5
  118.2 89.6 all-gather.7
  210.1 80.4 all-gather.9
  292.6 79.2 all-gather.11
  377.7 79.2 all-gather.13
  459.1 77.9 reduce-scatter.3
  727.2 39.3 reduce-scatter.5
  790.4 51.1 reduce-scatter.7

commit v12 on v11

--- a/solution.py
+++ b/solution.py
@@ -1453,7 +1453,7 @@
             5,
         )
         attended_late, g_query = lax.optimization_barrier((attended, g_query))
-        cut = 3 * tokens // 8
+        cut = 5 * tokens // 16
         pair = lambda a: (a[:cut], a[cut:])
         halves = [
             (dot(a, w_out_full) + b).astype(BF16) for a, b in zip(pair(attended_late), pair(feed))

time: 864 us -> 866 us (level)
  no operation moved by 1% of the time
where the time goes in v12:
time: 866 us; the launch traced here: 857 us
  Pallas kernels  538 us (62%)
  waiting for transfers between devices  107 us (12%)
  matrix products  78.6 us (9%)
  other arithmetic  62.5 us (7%)
  local copies, waits for them, and re-layouts  43.8 us (5%)
  between operations  15.2 us (2%)
  starting transfers between devices  12.9 us (1%)
    pallas_call x3, Pallas kernels, exchange(): pl.pallas_call(functools.partial(exchange_kernel, units, spread, axes), i...  300 us
    pallas_call x2, Pallas kernels, attention(): pl.pallas_call(functools.partial(attention_kernel, len(earlier)), grid=(f...  47.7 us
    pallas_call x1, Pallas kernels, feed_forward(): pl.pallas_call(feed_kernel, grid=(hidden // block,), in_specs=[fixed, fix...  42.1 us
    dot_general x6, matrix products, dot(): return jnp.dot(a, b, preferred_element_type=F32)  35.5 us
    dot_general x5, matrix products, dot_nt(): lax.dot_general(a, b, (((1,), (1,)), ((), ())), preferred_element_type=F32)  34.1 us
    ppermute x2, waiting for transfers between devices, exchange_rows(): across = lax.ppermute(local, 'stream', [(0, 2), (1, 3)])  33.1 us
    pallas_call x2, Pallas kernels, head_sum(): pl.pallas_call(functools.partial(head_sum_kernel, members), out_shape=jax...  31.7 us
    all_gather x4, waiting for transfers between devices, all_features(): return lax.all_gather(a, 'head', axis=1, tiled=True)  30.5 us
  transfers between devices with their start and end apart: 21, of which 10 were waited for; matrix products, arithmetic and copies ran while one was open for 18% of the time, Pallas kernels for 41%

profile of v12, /device:TPU:8, one launch (start us, length us, event | category | flops | bytes accessed | tf_op | source)
XLA Modules:
  0.0 857.1 jit_solution(5607789953150881106)
XLA Ops:
  14.1 19.2 %sum_over_head.2 = f32[37,1024]{1,0:T(8,128)} custom-call(f32[37,1024]{1,0:T(8,128)} %pad_maximum_fusion.2.x_ref), custom_call_target="tpu_custom_call" | custom-call | tf_op jit(solution)/shard_map/sum_over_head/pallas_call | solution.py:731
  34.8 41.9 %exchange.3.up_ref = bf16[2048,2048]{1,0:T(8,128)(2,1)} custom-call(bf16[256,2048]{1,0:T(8,128)(2,1)} %refs_0_), custom_call_target="tpu_custom_call" | custom-call | bytes 251658240 | tf_op jit(solution)/shard_map/exchange/pallas_call | solution.py:675
  80.0 13.2 %mix_streams.1 = (f32[4,1024,512]{2,1,0:T(8,128)}, f32[8,1024]{1,0:T(8,128)}) custom-call(f32[1024,36]{1,0:T(8,128)} %convolution_add_fusion.1.weights_ref, bf16[9,1024,512]{2,1,0:T(8,128)(2,1)} %bitcast.149), custom_call_target="tpu_custom_call" | custom-call | flops 41943040 | bytes 17825792 | tf_op jit(solution)/shard_map/mix_streams/pallas_call | solution.py:945
  93.2 12.6 %sum_over_head.3 = f32[8,1024]{1,0:T(8,128)} custom-call(f32[8,1024]{1,0:T(8,128)} %get-tuple-element.123.x_ref), custom_call_target="tpu_custom_call" | custom-call | tf_op jit(solution)/shard_map/sum_over_head/pallas_call | solution.py:731
  117.1 86.7 %exchange.4 = (bf16[2048,512]{1,0:T(8,128)(2,1)}, bf16[2048,512]{1,0:T(8,128)(2,1)}, bf16[2048,2048]{1,0:T(8,128)(2,1)}, bf16[512,2048]{1,0:T(8,128)(2,1)}, bf16...) custom-call(bf16[256,512]{1,0:T(8,128)(2,1)} %get-tuple-element.307.refs_0_, ...), custom_call_target="tpu_custom_call" | custom-call | bytes 251658240 | tf_op jit(solution)/shard_map/exchange/pallas_call | solution.py:675
  208.1 42.1 %feed_forward.1 = (bf16[1024,2048]{1,0:T(8,128)(2,1)}, bf16[1024,2048]{1,0:T(8,128)(2,1)}, bf16[2048,2048]{1,0:T(8,128)(2,1)}, bf16[2048,2048]{1,0:T(8,128)(2,1)}) custom-call(bf16[1024,2048]{1,0:T(8,128)(2,1)} %all-gather.8.cloned.1.call-done.x_ref, bf16[1024,2048]{1,0:T(8,128)(2,1)} %all-gather.6.cloned.1.call-done.d_ref, ...), custom_call_target="tpu_custom_call" | custom-call | flops 34359738368 | bytes 41943040 | tf_op jit(solution)/shard_map/feed_forward/pallas_call | solution.py:805
  277.9 12.6 %all-gather.10.cloned.1.call-done.refs_14_ = bf16[1024,2048]{1,0:T(8,128)(2,1)} async-done(((bf16[1024,512]{1,0:T(8,128)(2,1)}), bf16[1024,2048]{1,0:T(8,128)(2,1)}) %all-gather.10.cloned.1.call-update) | async-done | bytes 4194320 | tf_op jit(solution)/shard_map/all_gather | solution.py:1357
  300.4 10.8 %convolution_convert_fusion.2 = bf16[1024,2048]{1,0:T(8,128)(2,1)} fusion(bf16[1024,2048]{1,0:T(8,128)(2,1)S(1)} %copy-done.52, bf16[2048,2048]{1,0:T(8,128)(2,1)S(1)} %bitcast.211), kind=kOutput, calls=%fused_computation.19 | convolution fusion | flops 8592031744 | bytes 16777216 | tf_op jit(solution)/shard_map/dot_general | solution.py:27
  321.1 14.0 %convolution_convert_fusion.1 = bf16[1024,2048]{1,0:T(8,128)(2,1)} fusion(bf16[1024,2048]{1,0:T(8,128)(2,1)} %get-tuple-element.144, bf16[2048,2048]{1,0:T(8,128)(2,1)} %exchange.3.up_ref), kind=kOutput, calls=%fused_computation.18 | convolution fusion | flops 8592031744 | bytes 16777216 | tf_op jit(solution)/shard_map/dot_general | solution.py:31
  335.1 24.0 %collective-permute-done.2 = bf16[1,2,256,2048]{3,2,1,0:T(8,128)(2,1)} collective-permute-done((bf16[1,2,256,2048]{3,2,1,0:T(8,128)(2,1)}, bf16[1,2,256,2048]{3,2,1,0:T(8,128)(2,1)}, u32[]{:S(2)}, u32[]{:S(2)}) %collective-permute-start.2) | collective-permute-done | bytes 2097184 | tf_op jit(solution)/shard_map/ppermute | solution.py:43
  363.5 14.0 %early_sums.1.refs_1_ = bf16[64,1024]{1,0:T(8,128)(2,1)} custom-call(f32[4,1024,512]{2,1,0:T(8,128)} %get-tuple-element.141.streams_ref, bf16[1024,512]{1,0:T(8,128)(2,1)} %fusion.11.cot_ref, bf16[9,1024,512]{2,1,0:T(8,128)(2,1)} %bitcast.150), custom_call_target="tpu_custom_call" | custom-call | flops 57671680 | bytes 18874368 | tf_op jit(solution)/shard_map/early_sums/pallas_call | solution.py:984
  379.2 6.2 convolution_convert_fusion.5
  399.7 13.0 %collective-permute-done.7.refs_6_ = bf16[2,512,512]{2,1,0:T(8,128)(2,1)} collective-permute-done((bf16[2,512,512]{2,1,0:T(8,128)(2,1)}, bf16[2,512,512]{2,1,0:T(8,128)(2,1)}, u32[]{:S(2)}, u32[]{:S(2)}) %collective-permute-start.7) | collective-permute-done | bytes 1048608 | tf_op jit(solution)/shard_map/ppermute | solution.py:903
  412.7 20.0 %collective-permute-done.4.refs_2_ = bf16[2,512,512]{2,1,0:T(8,128)(2,1)} collective-permute-done((bf16[2,512,512]{2,1,0:T(8,128)(2,1)S(1)}, bf16[2,512,512]{2,1,0:T(8,128)(2,1)}, u32[]{:S(2)}, u32[]{:S(2)}) %collective-permute-start.4) | collective-permute-done | bytes 1048608 | tf_op jit(solution)/shard_map/ppermute | solution.py:903
  443.2 13.7 %all-gather.14.cloned.1.call-done = bf16[1024,2048]{1,0:T(8,128)(2,1)} async-done(((bf16[1024,512]{1,0:T(8,128)(2,1)}), bf16[1024,2048]{1,0:T(8,128)(2,1)}) %all-gather.14.cloned.1.call-update) | async-done | bytes 4194320 | tf_op jit(solution)/shard_map/all_gather | solution.py:1357
  462.7 23.9 %attention_both_ways.2 = (bf16[2,512,512]{2,1,0:T(8,128)(2,1)}, bf16[2,512,512]{2,1,0:T(8,128)(2,1)}, bf16[2,2,512,512]{3,2,1,0:T(8,128)(2,1)}, bf16[2,2,512,512]{3,2,1,0:T(8,128)(2,1)}) custom-call(s32[4]{0:T(128)} %iota_xor_fusion.place_ref, f32[2,512,512]{2,1,0:T(8,128)} %bitcast.170, bf16[2,512,512]{2,1,0:T(8,128)(2,1)} %bitcast.180, ...), custom_call_target="tpu_custom_call" | custom-call | bytes 1024 | tf_op jit(solution)/shard_map/attention_both_ways/pallas_call | solution.py:875
  499.4 23.7 %attention_both_ways.3 = (bf16[2,512,512]{2,1,0:T(8,128)(2,1)}, bf16[2,512,512]{2,1,0:T(8,128)(2,1)}, bf16[2,2,512,512]{3,2,1,0:T(8,128)(2,1)}, bf16[2,2,512,512]{3,2,1,0:T(8,128)(2,1)}) custom-call(s32[4]{0:T(128)} %iota_xor_fusion.place_ref, f32[2,512,512]{2,1,0:T(8,128)} %bitcast.171, ...), custom_call_target="tpu_custom_call", output_to_operand_aliasing={{0}: (16, {}), {1}: (17, {})} | custom-call | bytes 1024 | tf_op jit(solution)/shard_map/attention_both_ways/pallas_call | solution.py:875
  551.6 171.1 %exchange.5 = (f32[1024,512]{1,0:T(8,128)}, bf16[1024,2048]{1,0:T(8,128)(2,1)}, bf16[1024,2048]{1,0:T(8,128)(2,1)}, bf16[512,2048]{1,0:T(8,128)(2,1)}, bf16[512,...) custom-call(bf16[1024,2048]{1,0:T(8,128)(2,1)} %convolution_convert_, ...), custom_call_target="tpu_custom_call" | custom-call | bytes 629145600 | tf_op jit(solution)/shard_map/exchange/pallas_call | solution.py:675
  727.8 6.7 fusion.52.g2
  738.2 16.3 %gradient_sums.1 = (bf16[48,1024]{1,0:T(8,128)(2,1)}, f32[8,1024]{1,0:T(8,128)}, f32[8,512]{1,0:T(8,128)}) custom-call(f32[1024,512]{1,0:T(8,128)} %get-tuple-element.202.g0, f32[1024,512]{1,0:T(8,128)} %fusion.51.g1, f32[1024,512]{1,0:T(8,128)} %fusion.52.g2, f32[1024,512]{1,0:T(8,128)} %convert_element_type.242.g3, ...), custom_call_target="tpu_custom_call" | custom-call | flops 57671680 | bytes 22020096 | tf_op jit(solution)/shard_map/gradient_sums/pallas_call | solution.py:1031
  754.5 26.8 %totals_over_head.1 = (f32[48,1024]{1,0:T(8,128)}, f32[64,1024]{1,0:T(8,128)}, f32[8,1024]{1,0:T(8,128)}) custom-call(bf16[48,1024]{1,0:T(8,128)(2,1)} %get-tuple-element.208.refs_0_, bf16[64,1024]{1,0:T(8,128)(2,1)} %early_sums.1.refs_1_, f32[8,1024]{1,0:T(8,128)} %get-tuple-element.210.refs_2_), custom_call_target="tpu_custom_call" | custom-call | tf_op jit(solution)/shard_map/totals_over_head/pallas_call | solution.py:1093
  792.3 19.8 %small_gradients.1 = (f32[80,512]{1,0:T(8,128)}, f32[36,1024]{1,0:T(8,128)}, f32[1024,128]{1,0:T(8,128)}) custom-call(f32[48,1024]{1,0:T(8,128)} %get-tuple-element.213.dots_ref, f32[64,1024]{1,0:T(8,128)} %get-tuple-element.214.early_ref, f32[8,1024]{1,0:T(8,128)} %get-tuple-element.215.sums_ref, f32[8,1024]{1,0:T(8,128)} %copy-done.26, ...), custom_call_target="tpu_custom_call" | custom-call | tf_op jit(solution)/shard_map/small_gradients/pallas_call | solution.py:1195
  815.1 18.7 %history_gradient.1 = f32[9,1024,512]{2,1,0:T(8,128)} custom-call(f32[1024,512]{1,0:T(8,128)} %get-tuple-element.202.g0, f32[1024,512]{1,0:T(8,128)} %fusion.51.g1, f32[1024,512]{1,0:T(8,128)} %fusion.52.g2, f32[1024,512]{1,0:T(8,128)} %convert_element_type.242.g3, f32[4,1024,512]{2,1,0:T(8,128)} %get-tuple-element.141.streams_ref, f32[1024,8]{1,0:T(8,128)} %bitcast.178, ...), custom_call_target="tpu_custom_call" | custom-call | flops 57671680 | bytes 33554432 | tf_op jit(solution)/shard_map/history_gradient/pallas_call | solution.py:1254
  836.4 7.6 reduce-scatter.8.cloned.1.call-done
  (253 shorter events, 183.0 us)
Async XLA Ops:
  7.2 108.8 %all-gather.6.cloned.1.call-start = ((), (), s32[]{:S(2)}) async-start(), calls=%async_computation.3 | async-start | bytes 5242880 | tf_op jit(solution)/shard_map/all_gather | solution.py:1337
  34.7 42.0 %copy-start.21 = (f32[37,1024]{1,0:T(8,128)S(1)}, f32[37,1024]{1,0:T(8,128)}, u32[]{:S(2)}) copy-start(f32[37,1024]{1,0:T(8,128)} %sum_over_head.2) | copy-start | bytes 454660
  34.7 43.8 %copy-start.35 = (bf16[36,36]{1,0:T(8,128)(2,1)S(1)}, bf16[36,36]{1,0:T(8,128)(2,1)}, u32[]{:S(2)}) copy-start(bf16[36,36]{1,0:T(8,128)(2,1)} %param.17) | copy-start | bytes 7780
  34.8 173.1 %all-gather.8.cloned.1.call-start = ((), (), s32[]{:S(2)}) async-start(), calls=%async_computation.4 | async-start | bytes 5242880 | tf_op jit(solution)/shard_map/all_gather | solution.py:1357
  116.1 174.4 %all-gather.10.cloned.1.call-start = ((), (), s32[]{:S(2)}) async-start(), calls=%async_computation.5 | async-start | bytes 5242880 | tf_op jit(solution)/shard_map/all_gather | solution.py:1357
  207.9 169.6 %all-gather.12.cloned.1.call-start = ((), (), s32[]{:S(2)}) async-start(), calls=%async_computation.6 | async-start | bytes 5242880 | tf_op jit(solution)/shard_map/all_gather | solution.py:1357
  255.4 7.5 collective-permute-start.1
  258.9 11.2 %collective-permute-start = (bf16[1,4,256,2048]{3,2,1,0:T(8,128)(2,1)}, bf16[1,4,256,2048]{3,2,1,0:T(8,128)(2,1)}, u32[]{:S(2)}, u32[]{:S(2)}) collective-permute-start(bf16[1,4,256,2048]{3,2,1,0:T(8,128)(2,1)} %dynamic-slice_bitcast_fusion.1), channel_id=1, source_target_pairs={{0,4},{4,0},{8,12},{12,8},{1,5},{5,1},{9,13},{13,9},{2,6},{6,2},{1... | collective-permute-start | bytes 12582920 | tf_op jit(solution)/shard_map/ppermute | solution.py:51
  290.6 166.4 %all-gather.14.cloned.1.call-start = ((), (), s32[]{:S(2)}) async-start(), calls=%async_computation.7 | async-start | bytes 5242880 | tf_op jit(solution)/shard_map/all_gather | solution.py:1357
  311.3 47.8 %collective-permute-start.2 = (bf16[1,2,256,2048]{3,2,1,0:T(8,128)(2,1)}, bf16[1,2,256,2048]{3,2,1,0:T(8,128)(2,1)}, u32[]{:S(2)}, u32[]{:S(2)}) collective-permute-start(bf16[1,2,256,2048]{3,2,1,0:T(8,128)(2,1)} %get-tuple-element.140), channel_id=1, source_target_pairs={{0,16},{16,0},{1,17},{17,1},{2,18},{18,2},{3,19},{19,3},{4,20},{20... | collective-permute-start | bytes 6291464 | tf_op jit(solution)/shard_map/ppermute | solution.py:43
  377.5 167.4 %reduce-scatter.4.cloned.1.call-start = ((), (), s32[]{:S(2)}) async-start(), calls=%async_computation.8 | async-start | bytes 5242880 | tf_op jit(solution)/shard_map/reduce_scatter | solution.py:1370
  377.6 58.9 %collective-permute-start.9 = (bf16[1,2,256,2048]{3,2,1,0:T(8,128)(2,1)}, bf16[1,2,256,2048]{3,2,1,0:T(8,128)(2,1)}, u32[]{:S(2)}, u32[]{:S(2)}) collective-permute-start(bf16[1,2,256,2048]{3,2,1,0:T(8,128)(2,1)} %get-tuple-element.162), channel_id=1, source_target_pairs={{0,16},{16,0},{1,17},{17,1},{2,18},{18,2},{3,19},{19,3},{4,20},{20... | collective-permute-start | bytes 6291464 | tf_op jit(solution)/shard_map/ppermute | solution.py:43
  385.4 27.3 %collective-permute-start.7 = (bf16[2,512,512]{2,1,0:T(8,128)(2,1)}, bf16[2,512,512]{2,1,0:T(8,128)(2,1)}, u32[]{:S(2)}, u32[]{:S(2)}) collective-permute-start(bf16[2,512,512]{2,1,0:T(8,128)(2,1)} %bitcast.32.refs_4_), channel_id=1, source_target_pairs={{0,8},{4,12},{1,9},{5,13},{2,10},{6,14},{3,11},{7,15},{16,24},{20,... | collective-permute-start | bytes 3145736 | tf_op jit(solution)/shard_map/ppermute | solution.py:903
  389.8 42.9 %collective-permute-start.4 = (bf16[2,512,512]{2,1,0:T(8,128)(2,1)S(1)}, bf16[2,512,512]{2,1,0:T(8,128)(2,1)}, u32[]{:S(2)}, u32[]{:S(2)}) collective-permute-start(bf16[2,512,512]{2,1,0:T(8,128)(2,1)S(1)} %bitcast.160), channel_id=1, source_target_pairs={{0,8},{4,12},{1,9},{5,13},{2,10},{6,14},{3,11},{7,15},{16,24},{20,... | collective-permute-start | bytes 3145736 | tf_op jit(solution)/shard_map/ppermute | solution.py:903
  399.1 41.0 %collective-permute-start.6 = (bf16[2,512,512]{2,1,0:T(8,128)(2,1)}, bf16[2,512,512]{2,1,0:T(8,128)(2,1)S(1)}, u32[]{:S(2)}, u32[]{:S(2)}) collective-permute-start(bf16[2,512,512]{2,1,0:T(8,128)(2,1)} %bitcast.32.refs_4_), channel_id=1, source_target_pairs={{0,4},{4,0},{8,12},{12,8},{1,5},{5,1},{9,13},{13,9},{2,6},{6,2},{1... | collective-permute-start | bytes 3145736 | tf_op jit(solution)/shard_map/ppermute | solution.py:51
  399.2 41.0 %collective-permute-start.3 = (bf16[2,512,512]{2,1,0:T(8,128)(2,1)S(1)}, bf16[2,512,512]{2,1,0:T(8,128)(2,1)S(1)}, u32[]{:S(2)}, u32[]{:S(2)}) collective-permute-start(bf16[2,512,512]{2,1,0:T(8,128)(2,1)S(1)} %bitcast.161), channel_id=1, source_target_pairs={{0,4},{4,0},{8,12},{12,8},{1,5},{5,1},{9,13},{13,9},{2,6},{6,2},{1... | collective-permute-start | bytes 3145736 | tf_op jit(solution)/shard_map/ppermute | solution.py:51
  412.7 28.4 %collective-permute-start.8 = (bf16[2,512,512]{2,1,0:T(8,128)(2,1)}, bf16[2,512,512]{2,1,0:T(8,128)(2,1)S(1)}, u32[]{:S(2)}, u32[]{:S(2)}) collective-permute-start(bf16[2,512,512]{2,1,0:T(8,128)(2,1)} %collective-permute-done.7.refs_6_), channel_id=1, source_target_pairs={{0,4},{4,0},{8,12},{12,8},{1,5},{5,1},{9,13},{13,9},{2,6},{6,2},{1... | collective-permute-start | bytes 3145736 | tf_op jit(solution)/shard_map/ppermute | solution.py:51
  432.7 10.4 %collective-permute-start.5 = (bf16[2,512,512]{2,1,0:T(8,128)(2,1)}, bf16[2,512,512]{2,1,0:T(8,128)(2,1)}, u32[]{:S(2)}, u32[]{:S(2)}) collective-permute-start(bf16[2,512,512]{2,1,0:T(8,128)(2,1)} %collective-permute-done.4.refs_2_), channel_id=1, source_target_pairs={{0,4},{4,0},{8,12},{12,8},{1,5},{5,1},{9,13},{13,9},{2,6},{6,2},{1... | collective-permute-start | bytes 3145736 | tf_op jit(solution)/shard_map/ppermute | solution.py:51
  443.1 393.3 %reduce-scatter.6.cloned.1.call-start = ((), (), s32[]{:S(2)}) async-start(), calls=%async_computation.9 | async-start | bytes 1638400 | tf_op jit(solution)/shard_map/reduce_scatter | solution.py:1370
  486.7 4.4 collective-permute-start.10
  495.4 27.7 %collective-permute-start.11 = (bf16[2,512,512]{2,1,0:T(8,128)(2,1)S(1)}, bf16[2,512,512]{2,1,0:T(8,128)(2,1)S(1)}, u32[]{:S(2)}, u32[]{:S(2)}) collective-permute-start(bf16[2,512,512]{2,1,0:T(8,128)(2,1)S(1)} %fusion.13), channel_id=1, source_target_pairs={{8,0},{12,4},{9,1},{13,5},{10,2},{14,6},{11,3},{15,7},{24,16},{28,... | collective-permute-start | bytes 3145736 | tf_op jit(solution)/shard_map/ppermute | solution.py:913
  539.5 8.4 collective-permute-start.12
  726.7 117.3 %reduce-scatter.8.cloned.1.call-start = ((), (), s32[]{:S(2)}) async-start(), calls=%async_computation.10 | async-start | bytes 3604480 | tf_op jit(solution)/shard_map/reduce_scatter | solution.py:1370
  738.2 43.1 %copy-start.47 = (bf16[512,2048]{1,0:T(8,128)(2,1)S(1)}, bf16[512,2048]{1,0:T(8,128)(2,1)}, u32[]{:S(2)}) copy-start(bf16[512,2048]{1,0:T(8,128)(2,1)} %get-tuple-element.143) | copy-start | bytes 6291460
  (52 other events, 454.2 us)
Sparse Core Ops, SparseCore 0:
  34.8 81.1 all-gather.5
  118.2 89.6 all-gather.7
  210.0 80.4 all-gather.9
  292.5 79.2 all-gather.11
  377.6 79.2 all-gather.13
  459.1 77.9 reduce-scatter.3
  726.8 30.2 reduce-scatter.5
  786.5 57.4 reduce-scatter.7
